TPU v7x, 32 devices: a whole 2x2x4 slice. The times are simulated.
32 devices in a mesh: section: 8 (over z, core), expert: 4 (over y, x).
Axes of the slice: x: 2, y: 2, z: 4, core: 2. Of those that a mesh axis runs over, the one named last changes fastest.
Arguments:
- tokens: bfloat16 [256, 3072], P(('section', 'expert')), may hold values from -6 to 6
- upstream: bfloat16 [256, 3072], P(('section', 'expert')), may hold values from -2 to 2
- route_ids: int32 [256, 2], P(('section', 'expert')), may hold values from 0 to 3, all different within a row; in each aligned block of 8 rows (0 to 7, 8 to 15, ...) at most 8 rows name the same one
- route_gates: bfloat16 [256, 2], P(('section', 'expert')), may hold values from 0.099609375 to 0.8984375
- w_gate: bfloat16 [4, 3072, 2048], P('expert', None, 'section'), may hold values from -0.109375 to 0.109375
- w_up: bfloat16 [4, 3072, 2048], P('expert', None, 'section'), may hold values from -0.109375 to 0.109375
- w_down: bfloat16 [4, 2048, 3072], P('expert', 'section'), may hold values from -0.125 to 0.125
Outputs:
- grad_tokens: bfloat16 [256, 3072], P(('section', 'expert'))
- grad_gates: float32 [256, 2], P(('section', 'expert'))
- grad_w_gate: bfloat16 [4, 3072, 2048], P('expert', None, 'section')
- grad_w_up: bfloat16 [4, 3072, 2048], P('expert', None, 'section')
- grad_w_down: bfloat16 [4, 2048, 3072], P('expert', 'section')
Inputs may be any that keep to these rules, and one draw needn't show every extreme that they name: `route_ids`: the two experts of a token differ. Among the 16 choices of the tokens of one device, each expert is named at most 8 times, and in some device's tokens some expert is named exactly 8 times.
All inputs are finite; a program needn't handle non-finite values.
Results may differ from a plain program's by a relative error of at most 0.0058.
Values may be sent and summed in bfloat16 or wider, within the bound.
No kernel may reach another device: no remote copies, remote signals or barrier semaphores. Data moves between devices by JAX's collectives and lax.ppermute only.
A program may use at most 128 MiB of HBM per device.

v0:
```python
import jax
import jax.numpy as jnp
from jax import lax
from jax.sharding import PartitionSpec as P


def slot_matrix(route_ids, experts, capacity):
    flattened = route_ids.reshape(-1)
    onehot = (flattened[:, None] == jnp.arange(experts, dtype=jnp.int32)[None, :]).astype(jnp.int32)
    before = jnp.cumsum(onehot, axis=0) - onehot
    position = jnp.sum(before * onehot, axis=1)
    target = flattened * capacity + position
    columns = jnp.arange(experts * capacity, dtype=jnp.int32)
    return target[:, None] == columns[None, :]


def contract_last(left, right):
    return lax.dot_general(
        left, right, (((1,), (1,)), ((), ())), preferred_element_type=jnp.float32
    )


def contract_first(left, right):
    return lax.dot_general(
        left, right, (((0,), (0,)), ((), ())), preferred_element_type=jnp.float32
    )


def local(tokens, upstream, route_ids, route_gates, w_gate, w_up, w_down):
    experts = lax.axis_size("expert")
    tok_count, features = tokens.shape
    capacity = min(tok_count, max(2, 4 * tok_count // experts))
    chosen_slots = slot_matrix(route_ids, experts, capacity)
    placement = chosen_slots.astype(jnp.bfloat16)
    tokens_twice = jnp.repeat(tokens, 2, axis=0)
    upstream_twice = jnp.repeat(upstream, 2, axis=0)
    send_x = (
        contract_first(placement, tokens_twice)
        .astype(jnp.bfloat16)
        .reshape(experts, capacity, features)
    )
    send_dy = (
        contract_first(placement, upstream_twice)
        .astype(jnp.bfloat16)
        .reshape(experts, capacity, features)
    )
    send_weight = (
        jnp.dot(
            route_gates.reshape(-1).astype(jnp.float32),
            chosen_slots.astype(jnp.float32),
            precision=lax.Precision.HIGHEST,
        )
        .astype(jnp.bfloat16)
        .reshape(experts, capacity)
    )
    recv_x, recv_dy, recv_weight = (
        lax.all_to_all(send_x, "expert", split_axis=0, concat_axis=0, tiled=True),
        lax.all_to_all(send_dy, "expert", split_axis=0, concat_axis=0, tiled=True),
        lax.all_to_all(send_weight, "expert", split_axis=0, concat_axis=0, tiled=True),
    )
    every_x, every_dy, every_weight = (
        lax.all_gather(recv_x, "section", axis=0, tiled=True),
        lax.all_gather(recv_dy, "section", axis=0, tiled=True),
        lax.all_gather(recv_weight, "section", axis=0, tiled=True),
    )
    row_count = every_x.shape[0] * capacity
    rows_x = every_x.reshape(row_count, features)
    rows_dy = every_dy.reshape(row_count, features)
    weight = every_weight.reshape(row_count, 1).astype(jnp.float32)
    gate_slab = w_gate[0]
    up_slab = w_up[0]
    down_slab = w_down[0]
    pre_gate = jnp.dot(rows_x, gate_slab, preferred_element_type=jnp.float32)
    pre_up = jnp.dot(rows_x, up_slab, preferred_element_type=jnp.float32)
    sigmoid_gate = jax.nn.sigmoid(pre_gate)
    active = pre_gate * sigmoid_gate
    hidden = (active * pre_up).astype(jnp.bfloat16)
    back_proj = contract_last(rows_dy, down_slab)
    d_hidden = weight * back_proj
    d_gate = (d_hidden * pre_up * (sigmoid_gate * (1.0 + pre_gate * (1.0 - sigmoid_gate)))).astype(
        jnp.bfloat16
    )
    d_up = (d_hidden * active).astype(jnp.bfloat16)
    scaled_up = (weight * rows_dy.astype(jnp.float32)).astype(jnp.bfloat16)
    grad_down = contract_first(hidden, scaled_up)
    grad_gate = contract_first(rows_x, d_gate)
    grad_up = contract_first(rows_x, d_up)
    input_part = contract_last(d_gate, gate_slab) + contract_last(d_up, up_slab)
    own_rows = experts * capacity
    product_part = jnp.sum(hidden.astype(jnp.float32) * back_proj, axis=1)
    input_mine, gate_mine = (
        lax.psum_scatter(input_part, "section", scatter_dimension=0, tiled=True),
        lax.psum_scatter(product_part, "section", scatter_dimension=0, tiled=True),
    )
    back_input, back_gate = (
        lax.all_to_all(
            input_mine.reshape(experts, capacity, features),
            "expert",
            split_axis=0,
            concat_axis=0,
            tiled=True,
        ),
        lax.all_to_all(
            gate_mine.reshape(experts, capacity), "expert", split_axis=0, concat_axis=0, tiled=True
        ),
    )
    selector = chosen_slots.astype(jnp.float32)
    choice_grads = jnp.dot(
        selector, back_input.reshape(own_rows, features), precision=lax.Precision.HIGHEST
    )
    grad_tokens = jnp.sum(choice_grads.reshape(tok_count, 2, features), axis=1).astype(jnp.bfloat16)
    grad_gates = jnp.dot(
        selector, back_gate.reshape(own_rows), precision=lax.Precision.HIGHEST
    ).reshape(tok_count, 2)
    return (
        grad_tokens,
        grad_gates,
        grad_gate.astype(jnp.bfloat16)[None],
        grad_up.astype(jnp.bfloat16)[None],
        grad_down.astype(jnp.bfloat16)[None],
    )


def solution(mesh):
    placed = (
        P(("section", "expert"), None),
        P(("section", "expert"), None),
        P(("section", "expert"), None),
        P(("section", "expert"), None),
        P("expert", None, "section"),
        P("expert", None, "section"),
        P("expert", "section", None),
    )
    return jax.shard_map(
        local,
        mesh=mesh,
        in_specs=placed,
        out_specs=(
            P(("section", "expert"), None),
            P(("section", "expert"), None),
            P("expert", None, "section"),
            P("expert", None, "section"),
            P("expert", "section", None),
        ),
        check_vma=False,
    )
```

profile of v0, /device:TPU:0, one launch (start us, length us, event | category | flops | bytes accessed | tf_op | source)
XLA Modules:
  0.0 135.6 jit_solution(1604582558926547329)
XLA Ops:
  7.2 0.0 copy-start
  7.2 0.0 copy-start.5
  7.2 0.0 all-gather.6.cloned.1.call-start
  7.2 0.9 copy.20
  8.1 0.1 eq.55
  8.2 0.1 fusion.24
  8.3 0.2 select_reduce_fusion
  8.5 0.9 broadcast_in_dim.19
  9.4 0.3 fusion.4
  9.7 10.6 %all_to_all.37 = bf16[4,8,3072]{2,1,0:T(8,128)(2,1)} all-to-all(bf16[4,8,3072]{2,1,0:T(8,128)(2,1)S(1)} %fusion.4), channel_id=1, replica_groups=mesh['section'=8,'expert'=4] {'expert'}, dimensions={0} | all-to-all | bytes 393216 | tf_op jit(solution)/shard_map/all_to_all | solution.py:57
  20.3 0.0 all-gather.6.cloned.1.call-update
  20.4 0.0 all-gather.4.cloned.1.call-start
  20.4 0.9 broadcast_in_dim.18
  21.3 0.3 fusion.3
  21.6 8.6 %all_to_all.38 = bf16[4,8,3072]{2,1,0:T(8,128)(2,1)} all-to-all(bf16[4,8,3072]{2,1,0:T(8,128)(2,1)S(1)} %fusion.3), channel_id=1, replica_groups=mesh['section'=8,'expert'=4] {'expert'}, dimensions={0} | all-to-all | bytes 393216 | tf_op jit(solution)/shard_map/all_to_all | solution.py:58
  30.2 0.0 all-gather.4.cloned.1.call-update
  30.3 0.0 reduce-scatter.2.cloned.1.call-start
  30.3 0.0 copy-done.5
  30.3 0.1 copy.23
  30.4 0.1 reshape.123
  30.5 0.2 fusion.21
  30.7 0.1 all_to_all.31
  30.8 7.0 %all_to_all.39 = bf16[4,1,8]{2,1,0:T(2,128)(2,1)S(1)} all-to-all(bf16[4,1,8]{2,1,0:T(2,128)(2,1)S(1)} %all_to_all.31), channel_id=1, replica_groups=mesh['section'=8,'expert'=4] {'expert'}, dimensions={0} | all-to-all | bytes 128 | tf_op jit(solution)/shard_map/all_to_all | solution.py:59
  37.8 12.9 %all-gather = bf16[32,1,8]{2,1,0:T(2,128)(2,1)S(1)} all-gather(bf16[4,1,8]{2,1,0:T(2,128)(2,1)S(1)} %all_to_all.39), channel_id=2, replica_groups=mesh['section'=8,'expert'=4] {'section'}, dimensions={0}, use_global_device_ids=true | all-gather | bytes 576 | tf_op jit(solution)/shard_map/all_gather | solution.py:64
  50.7 0.1 convert_reduce_fusion
  50.8 0.1 reshape.119
  50.8 0.0 all-gather.6.cloned.1.call-done
  50.9 0.0 copy-start.1
  50.9 2.7 %fusion.10 = f32[256,256]{0,1:T(8,128)S(1)} fusion(bf16[1,3072,256]{2,1,0:T(8,128)(2,1)} %param.12, bf16[32,8,3072]{2,1,0:T(8,128)(2,1)} %all-gather.6.cloned.1.call-done), kind=kOutput, calls=%fused_computation.17 | convolution fusion | flops 402653184 | bytes 3407872 | tf_op jit(solution)/shard_map/dot_general | solution.py:74
  53.6 0.0 copy-done
  53.7 0.0 copy-done.1
  53.7 1.4 %fusion.7 = f32[256,256]{0,1:T(8,128)} fusion(bf16[1,3072,256]{2,1,0:T(8,128)(2,1)S(1)} %copy-done, bf16[32,8,3072]{2,1,0:T(8,128)(2,1)S(1)} %copy-done.1), kind=kOutput, calls=%fused_computation.14 | convolution fusion | flops 402653184 | bytes 3407872 | tf_op jit(solution)/shard_map/dot_general | solution.py:73
  55.1 16.3 %all-gather.4.cloned.1.call-done = bf16[32,8,3072]{2,1,0:T(8,128)(2,1)} async-done(((bf16[4,8,3072]{2,1,0:T(8,128)(2,1)}), bf16[32,8,3072]{2,1,0:T(8,128)(2,1)}) %all-gather.4.cloned.1.call-update) | async-done | bytes 1572880 | tf_op jit(solution)/shard_map/all_gather | solution.py:63
  71.4 3.2 %multiply_reduce_fusion = (f32[256]{0:T(256)S(1)}, bf16[256,256]{0,1:T(8,128)(2,1)}, bf16[256,256]{0,1:T(8,128)(2,1)S(1)}, bf16[256,256]{0,1:T(8,128)(2,1)S(1)}) fusion(f32[256,256]{0,1:T(8,128)S(1)} %fusion.10, f32[256,256]{0,1:T(8,128)} %fusion.7, f32[256]{0:T(256)S(1)} %reshape.119, bf16[1,256,3072]{2,1,0:T(8,128)(2,1)} %param.13, ...), kind=kOutput, calls=%fused_computation.32 | convolution fusion | flops 403898112 | bytes 4065280 | tf_op jit(solution)/shard_map/dot_general | solution.py:18
  74.6 0.0 copy-start.3
  74.6 0.0 copy-start.2
  74.6 0.6 fusion.5
  75.2 0.0 copy-done.3
  75.2 0.8 copy-done.2
  76.0 2.3 %convolution_add_fusion = f32[256,3072]{1,0:T(8,128)} fusion(f32[256,3072]{1,0:T(8,128)S(1)} %fusion.5, bf16[256,256]{0,1:T(8,128)(2,1)S(1)} %get-tuple-element.8, bf16[1,3072,256]{2,1,0:T(8,128)(2,1)S(1)} %copy-done.2), kind=kOutput, calls=%fused_computation | convolution fusion | flops 403439616 | bytes 7995392 | tf_op jit(solution)/shard_map/dot_general | solution.py:18
  78.3 0.0 copy-start.6
  78.3 0.0 copy-start.4
  78.3 0.0 reduce-scatter.2.cloned.1.call-update
  78.4 0.1 reduce_sum.30
  78.4 0.1 copy.22
  78.5 0.5 copy-done.6
  79.0 0.6 dynamic-slice
  80.2 15.8 %all-reduce = f32[256]{0:T(256)S(1)} all-reduce(f32[256]{0:T(256)S(1)} %get-tuple-element.5), channel_id=4, replica_groups=mesh['section'=8,'expert'=4] {'section'}, use_global_device_ids=true, to_apply=%region_5.6.clone | all-reduce | flops 256 | bytes 2048
  96.0 0.1 dynamic-slice.1
  96.1 0.7 all_to_all.29
  96.8 3.6 %all-to-all-start.4 = ((f32[4,1,8]{2,1,0:T(1,128)}), f32[4,1,8]{2,1,0:T(1,128)S(1)}, u32[]{:S(2)}, u32[]{:S(2)}) async-start(f32[4,1,8]{2,1,0:T(1,128)} %bitcast.12), calls=%async_computation.5 | async-start | bytes 4096 | tf_op jit(solution)/shard_map/all_to_all | solution.py:103
  100.4 0.0 copy-done.4
  100.4 3.2 %fusion.2 = bf16[1,256,3072]{2,1,0:T(8,128)(2,1)} fusion(bf16[256,256]{0,1:T(8,128)(2,1)S(1)} %copy-done.4, bf16[32,8,3072]{2,1,0:T(8,128)(2,1)} %all-gather.4.cloned.1.call-done, f32[256]{0:T(256)S(1)} %reshape.119), kind=kOutput, calls=%fused_computation.6 | convolution fusion | flops 405798912 | bytes 3277824 | tf_op jit(solution)/shard_map/dot_general | solution.py:24
  103.6 1.8 %fusion = bf16[1,3072,256]{2,1,0:T(8,128)(2,1)} fusion(bf16[256,256]{0,1:T(8,128)(2,1)S(1)} %get-tuple-element.7, bf16[32,8,3072]{2,1,0:T(8,128)(2,1)S(1)} %copy-done.1), kind=kOutput, calls=%fused_computation.4 | convolution fusion | flops 403439616 | bytes 3276800 | tf_op jit(solution)/shard_map/dot_general | solution.py:24
  105.4 0.0 all-to-all-done.4
  105.4 13.2 %reduce-scatter.2.cloned.1.call-done = f32[32,3072]{1,0:T(8,128)} async-done(((f32[256,3072]{1,0:T(8,128)}), f32[32,3072]{1,0:T(8,128)}) %reduce-scatter.2.cloned.1.call-update) | async-done | bytes 393232 | tf_op jit(solution)/shard_map/reduce_scatter | solution.py:92
  118.6 3.6 %all-to-all-start.3 = ((f32[4,8,3072]{2,1,0:T(8,128)}), f32[4,8,3072]{2,1,0:T(8,128)S(1)}, u32[]{:S(2)}, u32[]{:S(2)}) async-start(f32[4,8,3072]{2,1,0:T(8,128)} %bitcast.71), calls=%async_computation.4 | async-start | bytes 786432 | tf_op jit(solution)/shard_map/all_to_all | solution.py:96
  122.2 2.7 %fusion.1 = bf16[1,3072,256]{2,1,0:T(8,128)(2,1)} fusion(bf16[256,256]{0,1:T(8,128)(2,1)} %copy-done.3, bf16[32,8,3072]{2,1,0:T(8,128)(2,1)S(1)} %copy-done.1), kind=kOutput, calls=%fused_computation.5 | convolution fusion | flops 403439616 | bytes 3276800 | tf_op jit(solution)/shard_map/dot_general | solution.py:24
  124.9 0.5 broadcast.64
  125.4 0.7 reduce.7
  126.1 0.1 reshape.126
  126.2 0.8 fusion.26
  127.0 1.1 all-to-all-done.3
  128.1 0.9 convolution_reduce_fusion
  (5 shorter events, 0.1 us)
Async XLA Ops:
  7.2 46.5 %copy-start = (bf16[1,3072,256]{2,1,0:T(8,128)(2,1)S(1)}, bf16[1,3072,256]{2,1,0:T(8,128)(2,1)}, u32[]{:S(2)}) copy-start(bf16[1,3072,256]{2,1,0:T(8,128)(2,1)} %param.11) | copy-start | bytes 4718596
  7.2 23.1 %copy-start.5 = (bf16[8,2]{0,1:T(2,128)(2,1)S(1)}, bf16[8,2]{0,1:T(2,128)(2,1)}, u32[]{:S(2)}) copy-start(bf16[8,2]{0,1:T(2,128)(2,1)} %param.10) | copy-start | bytes 100
  7.2 43.7 %all-gather.6.cloned.1.call-start = ((), (), s32[]{:S(2)}) async-start(), calls=%async_computation.7 | async-start | bytes 1769472 | tf_op jit(solution)/shard_map/all_gather | solution.py:62
  20.4 51.0 %all-gather.4.cloned.1.call-start = ((), (), s32[]{:S(2)}) async-start(), calls=%async_computation.6 | async-start | bytes 1769472 | tf_op jit(solution)/shard_map/all_gather | solution.py:63
  30.3 88.3 %reduce-scatter.2.cloned.1.call-start = ((), (), s32[]{:S(2)}) async-start(), calls=%async_computation.8 | async-start | bytes 3538944 | tf_op jit(solution)/shard_map/reduce_scatter | solution.py:92
  50.9 2.8 %copy-start.1 = (bf16[32,8,3072]{2,1,0:T(8,128)(2,1)S(1)}, bf16[32,8,3072]{2,1,0:T(8,128)(2,1)}, u32[]{:S(2)}) copy-start(bf16[32,8,3072]{2,1,0:T(8,128)(2,1)} %all-gather.6.cloned.1.call-done) | copy-start | bytes 4718596
  74.6 0.7 copy-start.3
  74.6 1.5 %copy-start.2 = (bf16[1,3072,256]{2,1,0:T(8,128)(2,1)S(1)}, bf16[1,3072,256]{2,1,0:T(8,128)(2,1)}, u32[]{:S(2)}) copy-start(bf16[1,3072,256]{2,1,0:T(8,128)(2,1)} %param.12) | copy-start | bytes 4718596
  78.3 0.7 copy-start.6
  78.3 22.0 %copy-start.4 = (bf16[256,256]{0,1:T(8,128)(2,1)S(1)}, bf16[256,256]{0,1:T(8,128)(2,1)}, u32[]{:S(2)}) copy-start(bf16[256,256]{0,1:T(8,128)(2,1)} %get-tuple-element.6) | copy-start | bytes 393220
  96.8 8.6 %all-to-all-start.4 = ((f32[4,1,8]{2,1,0:T(1,128)}), f32[4,1,8]{2,1,0:T(1,128)S(1)}, u32[]{:S(2)}, u32[]{:S(2)}) async-start(f32[4,1,8]{2,1,0:T(1,128)} %bitcast.12), calls=%async_computation.5 | async-start | bytes 4096 | tf_op jit(solution)/shard_map/all_to_all | solution.py:103
  118.6 9.5 %all-to-all-start.3 = ((f32[4,8,3072]{2,1,0:T(8,128)}), f32[4,8,3072]{2,1,0:T(8,128)S(1)}, u32[]{:S(2)}, u32[]{:S(2)}) async-start(f32[4,8,3072]{2,1,0:T(8,128)} %bitcast.71), calls=%async_computation.4 | async-start | bytes 786432 | tf_op jit(solution)/shard_map/all_to_all | solution.py:96
Sparse Core Ops, SparseCore 0:
  20.5 24.6 all-gather.5
  46.8 24.5 all-gather.3
  78.5 40.0 reduce-scatter.1
where the time goes:
time: 136 us
  blocking collectives  55 us (40%)
  waiting for transfers between devices  30.7 us (23%)
  matrix products  20.6 us (15%)
  between operations  14.5 us (11%)
  starting transfers between devices  7.37 us (5%)
  local copies, waits for them, and re-layouts  6.48 us (5%)
    all_gather x1, waiting for transfers between devices, local(): lax.all_gather(recv_dy, 'section', axis=0, tiled=True)  16.3 us
    unnamed x1, blocking collectives  15.8 us
    reduce_scatter x1, waiting for transfers between devices, local(): lax.psum_scatter(input_part, 'section', scatter_dimension=0, tiled=True)  13.2 us
    all_gather x1, blocking collectives, local(): lax.all_gather(recv_weight, 'section', axis=0, tiled=True)  12.9 us
    all_to_all x1, blocking collectives, local(): lax.all_to_all(send_x, 'expert', split_axis=0, concat_axis=0, tiled=True)  10.6 us
    all_to_all x1, blocking collectives, local(): lax.all_to_all(send_dy, 'expert', split_axis=0, concat_axis=0, tiled=True)  8.61 us
    dot_general x5, matrix products, contract_first(): lax.dot_general(left, right, (((0,), (0,)), ((), ())), preferred_element_...  8.32 us
    all_to_all x1, blocking collectives, local(): lax.all_to_all(send_weight, 'expert', split_axis=0, concat_axis=0, tiled=...  6.98 us
  transfers between devices with their start and end apart: 5, of which 3 were waited for; matrix products, arithmetic and copies ran while one was open for 12% of the time, Pallas kernels for 0%

commit v1 on v0

v1 whole, which is shorter than its diff:
```python
import jax
import jax.numpy as jnp
from jax import lax
from jax.sharding import PartitionSpec as P

PAD = 128


def contract_last(left, right):
    return lax.dot_general(
        left, right, (((1,), (1,)), ((), ())), preferred_element_type=jnp.float32
    )


def contract_first(left, right):
    return lax.dot_general(
        left, right, (((0,), (0,)), ((), ())), preferred_element_type=jnp.float32
    )


def swap(value, axis, mask):
    size = lax.axis_size(axis)
    return lax.ppermute(value, axis, [(i, i ^ mask) for i in range(size)])


def to_wire(total, features, experts):
    product = total[..., features : features + experts] + total[..., features + experts : features + 2 * experts]
    high = lax.reduce_precision(product, 8, 7)
    rest = jnp.zeros(total.shape[:-1] + (PAD - 2 * experts,), jnp.float32)
    return jnp.concatenate(
        [total[..., :features], high, product - high, rest], axis=-1
    ).astype(jnp.bfloat16)


def local(tokens, upstream, route_ids, route_gates, w_gate, w_up, w_down):
    experts = lax.axis_size("expert")
    groups = lax.axis_size("section") // 2
    tok_count, features = tokens.shape
    core = lax.axis_index("section") % 2
    own_expert = lax.axis_index("expert")
    first_core = core == 0

    chosen = route_ids[:, :, None] == jnp.arange(experts, dtype=jnp.int32)[None, None, :]
    dense = jnp.sum(jnp.where(chosen, route_gates[:, :, None].astype(jnp.float32), 0.0), axis=1)
    extra = jnp.pad(dense, ((0, 0), (0, PAD - experts))).astype(jnp.bfloat16)
    x_wide = jnp.concatenate([tokens, extra], axis=1)
    dy_wide = jnp.concatenate([upstream, extra], axis=1)

    got = swap(jnp.where(first_core, dy_wide, x_wide), "section", 1)
    kept = jnp.where(first_core, x_wide, dy_wide)
    block = jnp.concatenate(
        [jnp.where(first_core, kept, got), jnp.where(first_core, got, kept)], axis=0
    )
    along = [swap(block, "section", 2 * k) for k in range(1, groups)]
    near = [block] + [swap(block, "expert", d) for d in range(1, experts)]
    far_block = jnp.concatenate(along, axis=0)
    far = [far_block] + [swap(far_block, "expert", d) for d in range(1, experts)]
    pieces = [piece for pair in zip(near, far) for piece in pair]
    mine = jnp.concatenate(pieces, axis=0)
    other = jnp.concatenate([swap(piece, "section", 1) for piece in pieces], axis=0)
    rows_x = jnp.where(first_core, mine, other)
    rows_dy = jnp.where(first_core, other, mine)
    is_own = jnp.arange(experts, dtype=jnp.int32)[None, :] == own_expert
    weight = jnp.sum(
        jnp.where(is_own, rows_x[:, features : features + experts].astype(jnp.float32), 0.0),
        axis=1,
        keepdims=True,
    )
    rows_x = rows_x[:, :features]
    rows_dy = rows_dy[:, :features]

    gate_slab = w_gate[0]
    up_slab = w_up[0]
    down_slab = w_down[0]
    pre_gate = jnp.dot(rows_x, gate_slab, preferred_element_type=jnp.float32)
    pre_up = jnp.dot(rows_x, up_slab, preferred_element_type=jnp.float32)
    sigmoid_gate = jax.nn.sigmoid(pre_gate)
    active = pre_gate * sigmoid_gate
    hidden = (active * pre_up).astype(jnp.bfloat16)
    back_proj = contract_last(rows_dy, down_slab)
    d_hidden = weight * back_proj
    d_gate = (d_hidden * pre_up * (sigmoid_gate * (1.0 + pre_gate * (1.0 - sigmoid_gate)))).astype(
        jnp.bfloat16
    )
    d_up = (d_hidden * active).astype(jnp.bfloat16)
    scaled_up = (weight * rows_dy.astype(jnp.float32)).astype(jnp.bfloat16)
    product = jnp.sum(hidden.astype(jnp.float32) * back_proj, axis=1, keepdims=True)
    input_part = contract_last(d_gate, gate_slab) + contract_last(d_up, up_slab)
    grad_down = contract_first(hidden, scaled_up)
    grad_gate = contract_first(rows_x, d_gate)
    grad_up = contract_first(rows_x, d_up)

    spread = jnp.where(is_own, product, 0.0)
    wide = jnp.concatenate(
        [input_part, spread, jnp.zeros((spread.shape[0], PAD - experts), jnp.float32)], axis=1
    ).reshape(experts, groups, 2, tok_count, features + PAD)
    to_keep = jnp.where(first_core, wide[:, :, 0], wide[:, :, 1])
    to_send = jnp.where(first_core, wide[:, :, 1], wide[:, :, 0])
    total = [
        to_keep[d] + swap(to_wire(to_send[d], features, experts), "section", 1).astype(jnp.float32)
        for d in range(experts)
    ]
    plane = total[0]
    for d in range(1, experts):
        plane = plane + swap(to_wire(total[d], features, experts), "expert", d).astype(jnp.float32)
    final = plane[0]
    for k in range(1, groups):
        final = final + swap(to_wire(plane[k], features, experts), "section", 2 * k).astype(
            jnp.float32
        )
    grad_tokens = final[:, :features].astype(jnp.bfloat16)
    products = final[:, features : features + experts] + final[:, features + experts : features + 2 * experts]
    grad_gates = jnp.sum(jnp.where(chosen, products[:, None, :], 0.0), axis=2)
    return (
        grad_tokens,
        grad_gates,
        grad_gate.astype(jnp.bfloat16)[None],
        grad_up.astype(jnp.bfloat16)[None],
        grad_down.astype(jnp.bfloat16)[None],
    )


def solution(mesh):
    placed = (
        P(("section", "expert"), None),
        P(("section", "expert"), None),
        P(("section", "expert"), None),
        P(("section", "expert"), None),
        P("expert", None, "section"),
        P("expert", None, "section"),
        P("expert", "section", None),
    )
    return jax.shard_map(
        local,
        mesh=mesh,
        in_specs=placed,
        out_specs=(
            P(("section", "expert"), None),
            P(("section", "expert"), None),
            P("expert", None, "section"),
            P("expert", None, "section"),
            P("expert", "section", None),
        ),
        check_vma=False,
    )
```

time: 136 us -> 114 us (0.84)
  blocking collectives: 55 us -> 0 us
  local copies, waits for them, and re-layouts: 6.48 us -> 25.8 us
  starting transfers between devices: 7.37 us -> 25.3 us
  other arithmetic: 1.02 us -> 18 us
  between operations: 14.5 us -> 0.97 us
  matrix products: 20.6 us -> 13.4 us
    ppermute x0 -> x28, waiting for transfers between devices: none -> 29.6 us  [swap(): return lax.ppermute(value, axis, [(i, i ^ mask) for i in range(size)])]
    all_to_all x3 -> x0, blocking collectives: 26.2 us -> none  [the longest x1 10.6 us: local(): lax.all_to_all(send_x, 'expert', split_axis=0, concat_axis=0, tiled=True)]
    ppermute x0 -> x28, starting transfers between devices: none -> 25.3 us  [swap(): return lax.ppermute(value, axis, [(i, i ^ mask) for i in range(size)])]
    concatenate x0 -> x14, local copies, waits for them, and re-layouts: none -> 18 us  [the longest x10 13.7 us: to_wire(): jnp.concatenate([total[..., :features], high, product - high, rest], axis...]
    all_gather x2 -> x0, waiting for transfers between devices: 16.3 us -> none  [the longest x1 16.3 us: local(): lax.all_gather(recv_dy, 'section', axis=0, tiled=True)]
    unnamed x1 -> x0, blocking collectives: 15.8 us -> none
    reduce_scatter x1 -> x0, waiting for transfers between devices: 13.2 us -> none  [local(): lax.psum_scatter(input_part, 'section', scatter_dimension=0, tiled=True)]
    all_gather x1 -> x0, blocking collectives: 12.9 us -> none  [local(): lax.all_gather(recv_weight, 'section', axis=0, tiled=True)]
  transfers between devices with their start and end apart: 5 -> 28, of which waited for: 3 -> 10; matrix products, arithmetic and copies ran while one was open for 12% -> 21% of each run, Pallas kernels for 0% -> 0%
where the time goes in v1:
time: 114 us; the launch traced here: 113 us
  waiting for transfers between devices  29.6 us (26%)
  local copies, waits for them, and re-layouts  25.8 us (23%)
  starting transfers between devices  25.3 us (22%)
  other arithmetic  18 us (16%)
  matrix products  13.4 us (12%)
    ppermute x28, waiting for transfers between devices, swap(): return lax.ppermute(value, axis, [(i, i ^ mask) for i in range(size)])  29.6 us
    ppermute x28, starting transfers between devices, swap(): return lax.ppermute(value, axis, [(i, i ^ mask) for i in range(size)])  25.3 us
    concatenate x10, local copies, waits for them, and re-layouts, to_wire(): jnp.concatenate([total[..., :features], high, product - high, rest], axis...  13.7 us
    dot_general x3, matrix products, contract_first(): lax.dot_general(left, right, (((0,), (0,)), ((), ())), preferred_element_...  7.53 us
    another operation x10, other arithmetic  6.11 us
    dot_general x3, matrix products, contract_last(): lax.dot_general(left, right, (((1,), (1,)), ((), ())), preferred_element_...  4.37 us
    concatenate x1, local copies, waits for them, and re-layouts, local(): jnp.concatenate([input_part, spread, jnp.zeros((spread.shape[0], PAD - ex...  4.27 us
    slice x10, local copies, waits for them, and re-layouts, to_wire(): total[..., :features]  3.55 us
  transfers between devices with their start and end apart: 28, of which 10 were waited for; matrix products, arithmetic and copies ran while one was open for 21% of the time, Pallas kernels for 0%

profile of v1, /device:TPU:0, one launch (start us, length us, event | category | flops | bytes accessed | tf_op | source)
XLA Modules:
  0.0 113.0 jit_solution(2165499529322182669)
XLA Ops:
  0.7 0.8 convert_element_type.78
  1.4 0.7 select_reduce_fusion.2
  2.2 0.8 broadcast_select_fusion.4
  3.6 0.9 collective-permute-done
  4.5 0.8 constant_dynamic-update-slice_fusion.13
  5.3 0.9 constant_dynamic-update-slice_fusion.12
  6.2 3.0 %collective-permute-start.1 = (bf16[16,3200]{1,0:T(8,128)(2,1)S(1)}, bf16[16,3200]{1,0:T(8,128)(2,1)S(1)}, u32[]{:S(2)}, u32[]{:S(2)}) collective-permute-start(bf16[16,3200]{1,0:T(8,128)(2,1)S(1)} %pad_maximum_fusion), channel_id=1, source_target_pairs={{0,8},{4,12},{8,0},{12,4},{16,24},{20,28},{24,16},{28,20},{1,9},{5... | collective-permute-start | bytes 307208 | tf_op jit(solution)/shard_map/ppermute | solution.py:23
  9.2 2.6 %collective-permute-start.2 = (bf16[16,3200]{1,0:T(8,128)(2,1)S(1)}, bf16[16,3200]{1,0:T(8,128)(2,1)S(1)}, u32[]{:S(2)}, u32[]{:S(2)}) collective-permute-start(bf16[16,3200]{1,0:T(8,128)(2,1)S(1)} %pad_maximum_fusion), channel_id=1, source_target_pairs={{0,16},{4,20},{8,24},{12,28},{16,0},{20,4},{24,8},{28,12},{1,17},{... | collective-permute-start | bytes 307208 | tf_op jit(solution)/shard_map/ppermute | solution.py:23
  11.8 1.7 %collective-permute-start.4 = (bf16[16,3200]{1,0:T(8,128)(2,1)S(1)}, bf16[16,3200]{1,0:T(8,128)(2,1)S(1)}, u32[]{:S(2)}, u32[]{:S(2)}) collective-permute-start(bf16[16,3200]{1,0:T(8,128)(2,1)S(1)} %pad_maximum_fusion), channel_id=1, source_target_pairs={{0,1},{1,0},{2,3},{3,2},{4,5},{5,4},{6,7},{7,6},{8,9},{9,8},{10,11... | collective-permute-start | bytes 307208 | tf_op jit(solution)/shard_map/ppermute | solution.py:23
  13.5 1.5 %collective-permute-start.6 = (bf16[16,3200]{1,0:T(8,128)(2,1)S(1)}, bf16[16,3200]{1,0:T(8,128)(2,1)S(1)}, u32[]{:S(2)}, u32[]{:S(2)}) collective-permute-start(bf16[16,3200]{1,0:T(8,128)(2,1)S(1)} %pad_maximum_fusion), channel_id=1, source_target_pairs={{0,2},{1,3},{2,0},{3,1},{4,6},{5,7},{6,4},{7,5},{8,10},{9,11},{10,... | collective-permute-start | bytes 307208 | tf_op jit(solution)/shard_map/ppermute | solution.py:23
  15.0 5.0 %collective-permute-done.2 = bf16[16,3200]{1,0:T(8,128)(2,1)S(1)} collective-permute-done((bf16[16,3200]{1,0:T(8,128)(2,1)S(1)}, bf16[16,3200]{1,0:T(8,128)(2,1)S(1)}, u32[]{:S(2)}, u32[]{:S(2)}) %collective-permute-start.2) | collective-permute-done | bytes 102432 | tf_op jit(solution)/shard_map/ppermute | solution.py:23
  20.1 2.4 %collective-permute-start.8 = (bf16[16,3200]{1,0:T(8,128)(2,1)S(1)}, bf16[16,3200]{1,0:T(8,128)(2,1)S(1)}, u32[]{:S(2)}, u32[]{:S(2)}) collective-permute-start(bf16[16,3200]{1,0:T(8,128)(2,1)S(1)} %pad_maximum_fusion), channel_id=1, source_target_pairs={{0,3},{1,2},{2,1},{3,0},{4,7},{5,6},{6,5},{7,4},{8,11},{9,10},{10,... | collective-permute-start | bytes 307208 | tf_op jit(solution)/shard_map/ppermute | solution.py:23
  22.7 0.6 collective-permute-start.5
  24.2 2.2 %collective-permute-start.9 = (bf16[48,3200]{1,0:T(8,128)(2,1)S(1)}, bf16[48,3200]{1,0:T(8,128)(2,1)S(1)}, u32[]{:S(2)}, u32[]{:S(2)}) collective-permute-start(bf16[48,3200]{1,0:T(8,128)(2,1)S(1)} %get-tuple-element.45), channel_id=1, source_target_pairs={{0,3},{1,2},{2,1},{3,0},{4,7},{5,6},{6,5},{7,4},{8,11},{9,10},{10,... | collective-permute-start | bytes 921608 | tf_op jit(solution)/shard_map/ppermute | solution.py:23
  27.0 5.8 %collective-permute-done.5 = bf16[48,3200]{1,0:T(8,128)(2,1)S(1)} collective-permute-done((bf16[48,3200]{1,0:T(8,128)(2,1)S(1)}, bf16[48,3200]{1,0:T(8,128)(2,1)S(1)}, u32[]{:S(2)}, u32[]{:S(2)}) %collective-permute-start.5) | collective-permute-done | bytes 307232 | tf_op jit(solution)/shard_map/ppermute | solution.py:23
  32.9 6.4 %collective-permute-done.7 = bf16[48,3200]{1,0:T(8,128)(2,1)S(1)} collective-permute-done((bf16[48,3200]{1,0:T(8,128)(2,1)S(1)}, bf16[48,3200]{1,0:T(8,128)(2,1)S(1)}, u32[]{:S(2)}, u32[]{:S(2)}) %collective-permute-start.7) | collective-permute-done | bytes 307232 | tf_op jit(solution)/shard_map/ppermute | solution.py:23
  40.0 0.8 collective-permute-done.13
  42.0 0.7 fusion.5
  42.7 1.1 copy-done.5
  43.8 0.7 fusion.8
  45.2 1.4 %multiply_reduce_fusion = (f32[256]{0:T(256)S(1)}, bf16[256,256]{0,1:T(8,128)(2,1)}, bf16[256,256]{0,1:T(8,128)(2,1)S(1)}, bf16[256,256]{0,1:T(8,128)(2,1)S(1)}) fusion(f32[256,256]{0,1:T(8,128)S(1)} %fusion.8, f32[256,256]{0,1:T(8,128)S(1)} %fusion.5, f32[256]{0:T(256)S(1)} %select_reduce_fusion, bf16[1,256,3072]{2,1,0:T(8,128)(2,1)S(1)} %copy-done.10, ...), kind=kOutput, calls=%fused_computation.50 | convolution fusion | flops 404684544 | bytes 5638145 | tf_op jit(solution)/shard_map/dot_general | solution.py:10
  46.6 0.6 fusion.3
  47.3 2.4 %convolution_add_fusion = f32[256,3072]{1,0:T(8,128)} fusion(f32[256,3072]{1,0:T(8,128)S(1)} %fusion.3, bf16[256,256]{0,1:T(8,128)(2,1)S(1)} %get-tuple-element.21, bf16[1,3072,256]{2,1,0:T(8,128)(2,1)S(1)} %copy-done.5), kind=kOutput, calls=%fused_computation | convolution fusion | flops 403439616 | bytes 7995392 | tf_op jit(solution)/shard_map/dot_general | solution.py:10
  49.7 0.7 broadcast_in_dim.74
  50.4 4.3 %concatenate.68 = f32[256,3200]{1,0:T(8,128)} concatenate(f32[256,3072]{1,0:T(8,128)} %convolution_add_fusion, f32[256,4]{1,0:T(8,128)S(1)} %broadcast_select_fusion.1, f32[256,124]{1,0:T(8,128)} %broadcast_in_dim.74), dimensions={1} | concatenate | bytes 6553600 | tf_op jit(solution)/shard_map/concatenate | solution.py:94
  54.6 3.3 %fusion.13 = (f32[4,4,1,8,3200]{4,3,1,2,0:T(8,128)S(1)}, f32[4,4,1,8,3200]{4,3,1,2,0:T(8,128)}) fusion(f32[4,4,2,8,3200]{4,3,2,1,0:T(8,128)} %bitcast.83, pred[]{:T(512)S(6)} %eq.29), kind=kLoop, calls=%fused_computation.22 | loop fusion | flops 819200 | bytes 6553601 | tf_op jit(solution)/shard_map/jit(_where)/select_n | solution.py:98
  58.1 0.7 slice.452
  58.8 0.7 fusion.33
  59.4 0.7 slice.449
  60.1 0.7 fusion.36
  60.8 0.7 slice.447
  61.5 0.7 fusion.38
  62.2 0.7 fusion.34
  62.9 1.7 %concatenate.69 = bf16[4,8,3200]{2,1,0:T(8,128)(2,1)} concatenate(bf16[4,8,3072]{2,1,0:T(8,128)(2,1)} %slice.452, bf16[4,8,4]{2,1,0:T(8,128)(2,1)} %get-tuple-element.26, bf16[4,8,4]{2,1,0:T(8,128)(2,1)} %get-tuple-element.25, bf16[4,8,120]{2,1,0:T(8,128)(2,1)S(1)} %broadcast.46), dimensions={2} | concatenate | bytes 409600 | tf_op jit(solution)/shard_map/concatenate | solution.py:30
  64.8 1.7 %concatenate.72 = bf16[4,8,3200]{2,1,0:T(8,128)(2,1)} concatenate(bf16[4,8,3072]{2,1,0:T(8,128)(2,1)} %slice.449, bf16[4,8,4]{2,1,0:T(8,128)(2,1)} %get-tuple-element.34, bf16[4,8,4]{2,1,0:T(8,128)(2,1)} %get-tuple-element.33, bf16[4,8,120]{2,1,0:T(8,128)(2,1)S(1)} %broadcast.46), dimensions={2} | concatenate | bytes 409600 | tf_op jit(solution)/shard_map/concatenate | solution.py:30
  66.8 1.7 %concatenate.74 = bf16[4,8,3200]{2,1,0:T(8,128)(2,1)} concatenate(bf16[4,8,3072]{2,1,0:T(8,128)(2,1)} %slice.447, bf16[4,8,4]{2,1,0:T(8,128)(2,1)} %get-tuple-element.38, bf16[4,8,4]{2,1,0:T(8,128)(2,1)} %get-tuple-element.37, bf16[4,8,120]{2,1,0:T(8,128)(2,1)S(1)} %broadcast.46), dimensions={2} | concatenate | bytes 409600 | tf_op jit(solution)/shard_map/concatenate | solution.py:30
  68.7 1.5 %concatenate.70 = bf16[4,8,3200]{2,1,0:T(8,128)(2,1)} concatenate(bf16[4,8,3072]{2,1,0:T(8,128)(2,1)S(1)} %slice.451, bf16[4,8,4]{2,1,0:T(8,128)(2,1)} %get-tuple-element.30, bf16[4,8,4]{2,1,0:T(8,128)(2,1)S(1)} %get-tuple-element.29, bf16[4,8,120]{2,1,0:T(8,128)(2,1)S(1)} %broadcast.46), dimensions={2} | concatenate | bytes 409600 | tf_op jit(solution)/shard_map/concatenate | solution.py:30
  70.5 4.0 %fusion.2 = bf16[1,256,3072]{2,1,0:T(8,128)(2,1)} fusion(bf16[256,256]{0,1:T(8,128)(2,1)} %get-tuple-element.6, f32[256]{0:T(256)} %copy-done.9, bf16[256,3200]{1,0:T(8,128)(2,1)} %copy-done.3, bf16[256,3200]{1,0:T(8,128)(2,1)} %copy-done.2, pred[]{:T(512)S(6)} %eq.29), kind=kOutput, calls=%fused_computation.6 | convolution fusion | flops 406585344 | bytes 4850689 | tf_op jit(solution)/shard_map/dot_general | solution.py:16
  74.5 1.2 %fusion.21 = (f32[4,8,3200]{2,1,0:T(8,128)S(1)}, f32[4,8,3200]{2,1,0:T(8,128)S(1)}, f32[4,8,3200]{2,1,0:T(8,128)S(1)}) fusion(f32[4,4,1,8,3200]{4,3,1,2,0:T(8,128)S(1)} %copy-done.1, bf16[4,8,3200]{2,1,0:T(8,128)(2,1)S(1)} %collective-permute-done.19, bf16[4,8,3200]{2,1,0:T(8,128)(2,1)} %collective-permute-done.23, ...), kind=kLoop, calls=%fused_computation.36 | loop fusion | flops 614400 | bytes 3072000 | tf_op jit(solution)/shard_map/add | solution.py:100
  75.7 0.7 slice.450
  76.4 0.7 fusion.35
  77.1 0.7 slice.448
  77.8 0.7 fusion.37
  78.5 0.7 fusion.39
  79.1 1.7 %concatenate.71 = bf16[4,8,3200]{2,1,0:T(8,128)(2,1)} concatenate(bf16[4,8,3072]{2,1,0:T(8,128)(2,1)} %slice.450, bf16[4,8,4]{2,1,0:T(8,128)(2,1)} %get-tuple-element.28, bf16[4,8,4]{2,1,0:T(8,128)(2,1)} %get-tuple-element.27, bf16[4,8,120]{2,1,0:T(8,128)(2,1)S(1)} %broadcast.46), dimensions={2} | concatenate | bytes 409600 | tf_op jit(solution)/shard_map/concatenate | solution.py:30
  80.8 1.7 %collective-permute-start.20 = (bf16[4,8,3200]{2,1,0:T(8,128)(2,1)}, bf16[4,8,3200]{2,1,0:T(8,128)(2,1)}, u32[]{:S(2)}, u32[]{:S(2)}) collective-permute-start(bf16[4,8,3200]{2,1,0:T(8,128)(2,1)} %concatenate.71), channel_id=1, source_target_pairs={{0,1},{1,0},{2,3},{3,2},{4,5},{5,4},{6,7},{7,6},{8,9},{9,8},{10,11... | collective-permute-start | bytes 614408 | tf_op jit(solution)/shard_map/ppermute | solution.py:23
  82.5 1.7 %concatenate.73 = bf16[4,8,3200]{2,1,0:T(8,128)(2,1)} concatenate(bf16[4,8,3072]{2,1,0:T(8,128)(2,1)} %slice.448, bf16[4,8,4]{2,1,0:T(8,128)(2,1)} %get-tuple-element.32, bf16[4,8,4]{2,1,0:T(8,128)(2,1)} %get-tuple-element.31, bf16[4,8,120]{2,1,0:T(8,128)(2,1)S(1)} %broadcast.46), dimensions={2} | concatenate | bytes 409600 | tf_op jit(solution)/shard_map/concatenate | solution.py:30
  84.2 1.0 collective-permute-start.22
  85.3 1.5 %concatenate.75 = bf16[4,8,3200]{2,1,0:T(8,128)(2,1)} concatenate(bf16[4,8,3072]{2,1,0:T(8,128)(2,1)S(1)} %slice.446, bf16[4,8,4]{2,1,0:T(8,128)(2,1)} %get-tuple-element.36, bf16[4,8,4]{2,1,0:T(8,128)(2,1)S(1)} %get-tuple-element.35, bf16[4,8,120]{2,1,0:T(8,128)(2,1)S(1)} %broadcast.46), dimensions={2} | concatenate | bytes 409600 | tf_op jit(solution)/shard_map/concatenate | solution.py:30
  86.7 0.8 collective-permute-start.24
  87.5 1.8 %fusion.1 = bf16[1,3072,256]{2,1,0:T(8,128)(2,1)} fusion(bf16[256,256]{0,1:T(8,128)(2,1)S(1)} %get-tuple-element.21, bf16[256,3200]{1,0:T(8,128)(2,1)S(1)} %broadcast_select_fusion), kind=kOutput, calls=%fused_computation.5 | convolution fusion | flops 403439616 | bytes 3276800 | tf_op jit(solution)/shard_map/dot_general | solution.py:16
  89.3 6.6 %collective-permute-done.22 = bf16[4,8,3200]{2,1,0:T(8,128)(2,1)} collective-permute-done((bf16[4,8,3200]{2,1,0:T(8,128)(2,1)}, bf16[4,8,3200]{2,1,0:T(8,128)(2,1)}, u32[]{:S(2)}, u32[]{:S(2)}) %collective-permute-start.22) | collective-permute-done | bytes 204832 | tf_op jit(solution)/shard_map/ppermute | solution.py:23
  95.8 1.3 %fusion.25 = f32[4,8,3200]{2,1,0:T(8,128)S(1)} fusion(f32[4,4,1,8,3200]{4,3,1,2,0:T(8,128)} %get-tuple-element.12, bf16[4,8,3200]{2,1,0:T(8,128)(2,1)S(1)} %collective-permute-done.24, bf16[4,8,3200]{2,1,0:T(8,128)(2,1)} %collective-permute-done.22, bf16[4,8,3200]{2,1,0:T(8,128)(2,1)} %collective-permute-done.20, bf16[4,8,3200]{2,1,0:T(8,128)(2,1)} %collective-permute-done.18), kind=kLoop, calls=%fused_computation.42 | loop fusion | flops 819200 | bytes 1638400 | tf_op jit(solution)/shard_map/add | solution.py:105
  97.2 0.7 copy-done.4
  98.0 0.6 fusion.40
  98.6 0.7 fusion.41
  99.4 0.7 concatenate.76
  100.1 1.4 %concatenate.77 = bf16[8,3200]{1,0:T(8,128)(2,1)} concatenate(bf16[8,3072]{1,0:T(8,128)(2,1)S(1)} %slice.455, bf16[8,4]{1,0:T(8,128)(2,1)} %get-tuple-element.42, bf16[8,4]{1,0:T(8,128)(2,1)} %get-tuple-element.41, bf16[8,120]{1,0:T(8,128)(2,1)S(1)} %broadcast.47), dimensions={1} | concatenate | bytes 102400 | tf_op jit(solution)/shard_map/concatenate | solution.py:30
  101.5 3.2 %collective-permute-start.26 = (bf16[8,3200]{1,0:T(8,128)(2,1)}, bf16[8,3200]{1,0:T(8,128)(2,1)}, u32[]{:S(2)}, u32[]{:S(2)}) collective-permute-start(bf16[8,3200]{1,0:T(8,128)(2,1)} %concatenate.77), channel_id=1, source_target_pairs={{0,16},{4,20},{8,24},{12,28},{16,0},{20,4},{24,8},{28,12},{1,17},{... | collective-permute-start | bytes 153608 | tf_op jit(solution)/shard_map/ppermute | solution.py:23
  104.8 1.2 %collective-permute-start.27 = (bf16[8,3200]{1,0:T(8,128)(2,1)S(1)}, bf16[8,3200]{1,0:T(8,128)(2,1)S(1)}, u32[]{:S(2)}, u32[]{:S(2)}) collective-permute-start(bf16[8,3200]{1,0:T(8,128)(2,1)S(1)} %concatenate.78), channel_id=1, source_target_pairs={{0,24},{4,28},{8,16},{12,20},{16,8},{20,12},{24,0},{28,4},{1,25},{... | collective-permute-start | bytes 153608 | tf_op jit(solution)/shard_map/ppermute | solution.py:23
  106.0 1.8 %fusion = bf16[1,3072,256]{2,1,0:T(8,128)(2,1)} fusion(bf16[256,256]{0,1:T(8,128)(2,1)S(1)} %copy-done.7, bf16[256,3200]{1,0:T(8,128)(2,1)S(1)} %broadcast_select_fusion), kind=kOutput, calls=%fused_computation.4 | convolution fusion | flops 403439616 | bytes 3276800 | tf_op jit(solution)/shard_map/dot_general | solution.py:16
  107.8 2.9 %collective-permute-done.27 = bf16[8,3200]{1,0:T(8,128)(2,1)S(1)} collective-permute-done((bf16[8,3200]{1,0:T(8,128)(2,1)S(1)}, bf16[8,3200]{1,0:T(8,128)(2,1)S(1)}, u32[]{:S(2)}, u32[]{:S(2)}) %collective-permute-start.27) | collective-permute-done | bytes 51232 | tf_op jit(solution)/shard_map/ppermute | solution.py:23
  110.7 1.0 fusion.29
  111.7 0.6 slice.453
  (94 shorter events, 7.1 us)
Async XLA Ops:
  0.6 41.3 %copy-start = (bf16[1,3072,256]{2,1,0:T(8,128)(2,1)S(1)}, bf16[1,3072,256]{2,1,0:T(8,128)(2,1)}, u32[]{:S(2)}) copy-start(bf16[1,3072,256]{2,1,0:T(8,128)(2,1)} %param.11) | copy-start | bytes 4718596
  3.1 1.4 %collective-permute-start = (bf16[8,3200]{1,0:T(8,128)(2,1)S(1)}, bf16[8,3200]{1,0:T(8,128)(2,1)S(1)}, u32[]{:S(2)}, u32[]{:S(2)}) collective-permute-start(bf16[8,3200]{1,0:T(8,128)(2,1)S(1)} %broadcast_select_fusion.4), channel_id=1, source_target_pairs={{0,4},{4,0},{8,12},{12,8},{16,20},{20,16},{24,28},{28,24},{1,5},{5... | collective-permute-start | bytes 153608 | tf_op jit(solution)/shard_map/ppermute | solution.py:23
  6.2 7.3 %collective-permute-start.1 = (bf16[16,3200]{1,0:T(8,128)(2,1)S(1)}, bf16[16,3200]{1,0:T(8,128)(2,1)S(1)}, u32[]{:S(2)}, u32[]{:S(2)}) collective-permute-start(bf16[16,3200]{1,0:T(8,128)(2,1)S(1)} %pad_maximum_fusion), channel_id=1, source_target_pairs={{0,8},{4,12},{8,0},{12,4},{16,24},{20,28},{24,16},{28,20},{1,9},{5... | collective-permute-start | bytes 307208 | tf_op jit(solution)/shard_map/ppermute | solution.py:23
  9.2 10.9 %collective-permute-start.2 = (bf16[16,3200]{1,0:T(8,128)(2,1)S(1)}, bf16[16,3200]{1,0:T(8,128)(2,1)S(1)}, u32[]{:S(2)}, u32[]{:S(2)}) collective-permute-start(bf16[16,3200]{1,0:T(8,128)(2,1)S(1)} %pad_maximum_fusion), channel_id=1, source_target_pairs={{0,16},{4,20},{8,24},{12,28},{16,0},{20,4},{24,8},{28,12},{1,17},{... | collective-permute-start | bytes 307208 | tf_op jit(solution)/shard_map/ppermute | solution.py:23
  11.8 10.8 %collective-permute-start.3 = (bf16[16,3200]{1,0:T(8,128)(2,1)S(1)}, bf16[16,3200]{1,0:T(8,128)(2,1)S(1)}, u32[]{:S(2)}, u32[]{:S(2)}) collective-permute-start(bf16[16,3200]{1,0:T(8,128)(2,1)S(1)} %pad_maximum_fusion), channel_id=1, source_target_pairs={{0,24},{4,28},{8,16},{12,20},{16,8},{20,12},{24,0},{28,4},{1,25},{... | collective-permute-start | bytes 307208 | tf_op jit(solution)/shard_map/ppermute | solution.py:23
  11.8 10.9 %collective-permute-start.10 = (bf16[16,3200]{1,0:T(8,128)(2,1)S(1)}, bf16[16,3200]{1,0:T(8,128)(2,1)S(1)}, u32[]{:S(2)}, u32[]{:S(2)}) collective-permute-start(bf16[16,3200]{1,0:T(8,128)(2,1)S(1)} %pad_maximum_fusion), channel_id=1, source_target_pairs={{0,4},{4,0},{8,12},{12,8},{16,20},{20,16},{24,28},{28,24},{1,5},{5... | collective-permute-start | bytes 307208 | tf_op jit(solution)/shard_map/ppermute | solution.py:23
  11.8 11.5 %collective-permute-start.4 = (bf16[16,3200]{1,0:T(8,128)(2,1)S(1)}, bf16[16,3200]{1,0:T(8,128)(2,1)S(1)}, u32[]{:S(2)}, u32[]{:S(2)}) collective-permute-start(bf16[16,3200]{1,0:T(8,128)(2,1)S(1)} %pad_maximum_fusion), channel_id=1, source_target_pairs={{0,1},{1,0},{2,3},{3,2},{4,5},{5,4},{6,7},{7,6},{8,9},{9,8},{10,11... | collective-permute-start | bytes 307208 | tf_op jit(solution)/shard_map/ppermute | solution.py:23
  13.5 12.9 %collective-permute-start.6 = (bf16[16,3200]{1,0:T(8,128)(2,1)S(1)}, bf16[16,3200]{1,0:T(8,128)(2,1)S(1)}, u32[]{:S(2)}, u32[]{:S(2)}) collective-permute-start(bf16[16,3200]{1,0:T(8,128)(2,1)S(1)} %pad_maximum_fusion), channel_id=1, source_target_pairs={{0,2},{1,3},{2,0},{3,1},{4,6},{5,7},{6,4},{7,5},{8,10},{9,11},{10,... | collective-permute-start | bytes 307208 | tf_op jit(solution)/shard_map/ppermute | solution.py:23
  20.1 6.4 %collective-permute-start.8 = (bf16[16,3200]{1,0:T(8,128)(2,1)S(1)}, bf16[16,3200]{1,0:T(8,128)(2,1)S(1)}, u32[]{:S(2)}, u32[]{:S(2)}) collective-permute-start(bf16[16,3200]{1,0:T(8,128)(2,1)S(1)} %pad_maximum_fusion), channel_id=1, source_target_pairs={{0,3},{1,2},{2,1},{3,0},{4,7},{5,6},{6,5},{7,4},{8,11},{9,10},{10,... | collective-permute-start | bytes 307208 | tf_op jit(solution)/shard_map/ppermute | solution.py:23
  22.6 1.7 %collective-permute-start.11 = (bf16[48,3200]{1,0:T(8,128)(2,1)S(1)}, bf16[48,3200]{1,0:T(8,128)(2,1)S(1)}, u32[]{:S(2)}, u32[]{:S(2)}) collective-permute-start(bf16[48,3200]{1,0:T(8,128)(2,1)S(1)} %get-tuple-element.45), channel_id=1, source_target_pairs={{0,4},{4,0},{8,12},{12,8},{16,20},{20,16},{24,28},{28,24},{1,5},{5... | collective-permute-start | bytes 921608 | tf_op jit(solution)/shard_map/ppermute | solution.py:23
  22.7 10.1 %collective-permute-start.5 = (bf16[48,3200]{1,0:T(8,128)(2,1)S(1)}, bf16[48,3200]{1,0:T(8,128)(2,1)S(1)}, u32[]{:S(2)}, u32[]{:S(2)}) collective-permute-start(bf16[48,3200]{1,0:T(8,128)(2,1)S(1)} %get-tuple-element.45), channel_id=1, source_target_pairs={{0,1},{1,0},{2,3},{3,2},{4,5},{5,4},{6,7},{7,6},{8,9},{9,8},{10,11... | collective-permute-start | bytes 921608 | tf_op jit(solution)/shard_map/ppermute | solution.py:23
  23.3 16.0 %collective-permute-start.7 = (bf16[48,3200]{1,0:T(8,128)(2,1)S(1)}, bf16[48,3200]{1,0:T(8,128)(2,1)S(1)}, u32[]{:S(2)}, u32[]{:S(2)}) collective-permute-start(bf16[48,3200]{1,0:T(8,128)(2,1)S(1)} %get-tuple-element.45), channel_id=1, source_target_pairs={{0,2},{1,3},{2,0},{3,1},{4,6},{5,7},{6,4},{7,5},{8,10},{9,11},{10,... | collective-permute-start | bytes 921608 | tf_op jit(solution)/shard_map/ppermute | solution.py:23
  24.2 15.1 %collective-permute-start.9 = (bf16[48,3200]{1,0:T(8,128)(2,1)S(1)}, bf16[48,3200]{1,0:T(8,128)(2,1)S(1)}, u32[]{:S(2)}, u32[]{:S(2)}) collective-permute-start(bf16[48,3200]{1,0:T(8,128)(2,1)S(1)} %get-tuple-element.45), channel_id=1, source_target_pairs={{0,3},{1,2},{2,1},{3,0},{4,7},{5,6},{6,5},{7,4},{8,11},{9,10},{10,... | collective-permute-start | bytes 921608 | tf_op jit(solution)/shard_map/ppermute | solution.py:23
  26.4 13.5 %collective-permute-start.12 = (bf16[16,3200]{1,0:T(8,128)(2,1)S(1)}, bf16[16,3200]{1,0:T(8,128)(2,1)S(1)}, u32[]{:S(2)}, u32[]{:S(2)}) collective-permute-start(bf16[16,3200]{1,0:T(8,128)(2,1)S(1)} %collective-permute-done.4), channel_id=1, source_target_pairs={{0,4},{4,0},{8,12},{12,8},{16,20},{20,16},{24,28},{28,24},{1,5},{5... | collective-permute-start | bytes 307208 | tf_op jit(solution)/shard_map/ppermute | solution.py:23
  26.5 14.4 %collective-permute-start.14 = (bf16[16,3200]{1,0:T(8,128)(2,1)S(1)}, bf16[16,3200]{1,0:T(8,128)(2,1)S(1)}, u32[]{:S(2)}, u32[]{:S(2)}) collective-permute-start(bf16[16,3200]{1,0:T(8,128)(2,1)S(1)} %collective-permute-done.6), channel_id=1, source_target_pairs={{0,4},{4,0},{8,12},{12,8},{16,20},{20,16},{24,28},{28,24},{1,5},{5... | collective-permute-start | bytes 307208 | tf_op jit(solution)/shard_map/ppermute | solution.py:23
  32.8 8.5 %collective-permute-start.16 = (bf16[16,3200]{1,0:T(8,128)(2,1)S(1)}, bf16[16,3200]{1,0:T(8,128)(2,1)S(1)}, u32[]{:S(2)}, u32[]{:S(2)}) collective-permute-start(bf16[16,3200]{1,0:T(8,128)(2,1)S(1)} %collective-permute-done.8), channel_id=1, source_target_pairs={{0,4},{4,0},{8,12},{12,8},{16,20},{20,16},{24,28},{28,24},{1,5},{5... | collective-permute-start | bytes 307208 | tf_op jit(solution)/shard_map/ppermute | solution.py:23
  39.3 1.6 %collective-permute-start.13 = (bf16[48,3200]{1,0:T(8,128)(2,1)S(1)}, bf16[48,3200]{1,0:T(8,128)(2,1)S(1)}, u32[]{:S(2)}, u32[]{:S(2)}) collective-permute-start(bf16[48,3200]{1,0:T(8,128)(2,1)S(1)} %collective-permute-done.5), channel_id=1, source_target_pairs={{0,4},{4,0},{8,12},{12,8},{16,20},{20,16},{24,28},{28,24},{1,5},{5... | collective-permute-start | bytes 921608 | tf_op jit(solution)/shard_map/ppermute | solution.py:23
  39.3 2.0 %collective-permute-start.15 = (bf16[48,3200]{1,0:T(8,128)(2,1)S(1)}, bf16[48,3200]{1,0:T(8,128)(2,1)S(1)}, u32[]{:S(2)}, u32[]{:S(2)}) collective-permute-start(bf16[48,3200]{1,0:T(8,128)(2,1)S(1)} %collective-permute-done.7), channel_id=1, source_target_pairs={{0,4},{4,0},{8,12},{12,8},{16,20},{20,16},{24,28},{28,24},{1,5},{5... | collective-permute-start | bytes 921608 | tf_op jit(solution)/shard_map/ppermute | solution.py:23
  39.9 4.7 %copy-start.3 = (bf16[256,3200]{1,0:T(8,128)(2,1)}, bf16[256,3200]{1,0:T(8,128)(2,1)S(1)}, u32[]{:S(2)}) copy-start(bf16[256,3200]{1,0:T(8,128)(2,1)S(1)} %constant_dynamic-update-slice_fusion.3) | copy-start | bytes 4915204
  39.9 1.8 %collective-permute-start.17 = (bf16[48,3200]{1,0:T(8,128)(2,1)S(1)}, bf16[48,3200]{1,0:T(8,128)(2,1)S(1)}, u32[]{:S(2)}, u32[]{:S(2)}) collective-permute-start(bf16[48,3200]{1,0:T(8,128)(2,1)S(1)} %collective-permute-done.9), channel_id=1, source_target_pairs={{0,4},{4,0},{8,12},{12,8},{16,20},{20,16},{24,28},{28,24},{1,5},{5... | collective-permute-start | bytes 921608 | tf_op jit(solution)/shard_map/ppermute | solution.py:23
  41.8 2.9 %copy-start.2 = (bf16[256,3200]{1,0:T(8,128)(2,1)}, bf16[256,3200]{1,0:T(8,128)(2,1)S(1)}, u32[]{:S(2)}) copy-start(bf16[256,3200]{1,0:T(8,128)(2,1)S(1)} %constant_dynamic-update-slice_fusion.14) | copy-start | bytes 4915204
  42.0 1.8 %copy-start.5 = (bf16[1,3072,256]{2,1,0:T(8,128)(2,1)S(1)}, bf16[1,3072,256]{2,1,0:T(8,128)(2,1)}, u32[]{:S(2)}) copy-start(bf16[1,3072,256]{2,1,0:T(8,128)(2,1)} %param.12) | copy-start | bytes 4718596
  43.8 1.4 %copy-start.10 = (bf16[1,256,3072]{2,1,0:T(8,128)(2,1)S(1)}, bf16[1,256,3072]{2,1,0:T(8,128)(2,1)}, u32[]{:S(2)}) copy-start(bf16[1,256,3072]{2,1,0:T(8,128)(2,1)} %param.13) | copy-start | bytes 4718596
  45.2 1.4 %copy-start.9 = (f32[256]{0:T(256)}, f32[256]{0:T(256)S(1)}, u32[]{:S(2)}) copy-start(f32[256]{0:T(256)S(1)} %select_reduce_fusion) | copy-start | bytes 3076
  46.6 0.6 copy-start.6
  64.6 24.7 %collective-permute-start.18 = (bf16[4,8,3200]{2,1,0:T(8,128)(2,1)}, bf16[4,8,3200]{2,1,0:T(8,128)(2,1)}, u32[]{:S(2)}, u32[]{:S(2)}) collective-permute-start(bf16[4,8,3200]{2,1,0:T(8,128)(2,1)} %concatenate.69), channel_id=1, source_target_pairs={{0,4},{4,0},{8,12},{12,8},{16,20},{20,16},{24,28},{28,24},{1,5},{5... | collective-permute-start | bytes 614408 | tf_op jit(solution)/shard_map/ppermute | solution.py:23
  66.5 8.0 %collective-permute-start.21 = (bf16[4,8,3200]{2,1,0:T(8,128)(2,1)}, bf16[4,8,3200]{2,1,0:T(8,128)(2,1)}, u32[]{:S(2)}, u32[]{:S(2)}) collective-permute-start(bf16[4,8,3200]{2,1,0:T(8,128)(2,1)} %concatenate.72), channel_id=1, source_target_pairs={{0,4},{4,0},{8,12},{12,8},{16,20},{20,16},{24,28},{28,24},{1,5},{5... | collective-permute-start | bytes 614408 | tf_op jit(solution)/shard_map/ppermute | solution.py:23
  68.5 6.0 %collective-permute-start.23 = (bf16[4,8,3200]{2,1,0:T(8,128)(2,1)}, bf16[4,8,3200]{2,1,0:T(8,128)(2,1)}, u32[]{:S(2)}, u32[]{:S(2)}) collective-permute-start(bf16[4,8,3200]{2,1,0:T(8,128)(2,1)} %concatenate.74), channel_id=1, source_target_pairs={{0,4},{4,0},{8,12},{12,8},{16,20},{20,16},{24,28},{28,24},{1,5},{5... | collective-permute-start | bytes 614408 | tf_op jit(solution)/shard_map/ppermute | solution.py:23
  70.2 4.3 %collective-permute-start.19 = (bf16[4,8,3200]{2,1,0:T(8,128)(2,1)}, bf16[4,8,3200]{2,1,0:T(8,128)(2,1)S(1)}, u32[]{:S(2)}, u32[]{:S(2)}) collective-permute-start(bf16[4,8,3200]{2,1,0:T(8,128)(2,1)} %concatenate.70), channel_id=1, source_target_pairs={{0,4},{4,0},{8,12},{12,8},{16,20},{20,16},{24,28},{28,24},{1,5},{5... | collective-permute-start | bytes 614408 | tf_op jit(solution)/shard_map/ppermute | solution.py:23
  70.5 4.0 %copy-start.1 = (f32[4,4,1,8,3200]{4,3,1,2,0:T(8,128)S(1)}, f32[4,4,1,8,3200]{4,3,1,2,0:T(8,128)}, u32[]{:S(2)}) copy-start(f32[4,4,1,8,3200]{4,3,1,2,0:T(8,128)} %get-tuple-element.12) | copy-start | bytes 4915204
  80.8 8.4 %collective-permute-start.20 = (bf16[4,8,3200]{2,1,0:T(8,128)(2,1)}, bf16[4,8,3200]{2,1,0:T(8,128)(2,1)}, u32[]{:S(2)}, u32[]{:S(2)}) collective-permute-start(bf16[4,8,3200]{2,1,0:T(8,128)(2,1)} %concatenate.71), channel_id=1, source_target_pairs={{0,1},{1,0},{2,3},{3,2},{4,5},{5,4},{6,7},{7,6},{8,9},{9,8},{10,11... | collective-permute-start | bytes 614408 | tf_op jit(solution)/shard_map/ppermute | solution.py:23
  84.2 11.6 %collective-permute-start.22 = (bf16[4,8,3200]{2,1,0:T(8,128)(2,1)}, bf16[4,8,3200]{2,1,0:T(8,128)(2,1)}, u32[]{:S(2)}, u32[]{:S(2)}) collective-permute-start(bf16[4,8,3200]{2,1,0:T(8,128)(2,1)} %concatenate.73), channel_id=1, source_target_pairs={{0,2},{1,3},{2,0},{3,1},{4,6},{5,7},{6,4},{7,5},{8,10},{9,11},{10,... | collective-permute-start | bytes 614408 | tf_op jit(solution)/shard_map/ppermute | solution.py:23
  86.7 9.1 %collective-permute-start.24 = (bf16[4,8,3200]{2,1,0:T(8,128)(2,1)}, bf16[4,8,3200]{2,1,0:T(8,128)(2,1)S(1)}, u32[]{:S(2)}, u32[]{:S(2)}) collective-permute-start(bf16[4,8,3200]{2,1,0:T(8,128)(2,1)} %concatenate.75), channel_id=1, source_target_pairs={{0,3},{1,2},{2,1},{3,0},{4,7},{5,6},{6,5},{7,4},{8,11},{9,10},{10,... | collective-permute-start | bytes 614408 | tf_op jit(solution)/shard_map/ppermute | solution.py:23
  89.3 16.7 %copy-start.7 = (bf16[256,256]{0,1:T(8,128)(2,1)S(1)}, bf16[256,256]{0,1:T(8,128)(2,1)}, u32[]{:S(2)}) copy-start(bf16[256,256]{0,1:T(8,128)(2,1)} %copy-done.6) | copy-start | bytes 393220
  97.2 0.7 copy-start.4
  100.1 7.6 %collective-permute-start.25 = (bf16[8,3200]{1,0:T(8,128)(2,1)S(1)}, bf16[8,3200]{1,0:T(8,128)(2,1)}, u32[]{:S(2)}, u32[]{:S(2)}) collective-permute-start(bf16[8,3200]{1,0:T(8,128)(2,1)S(1)} %concatenate.76), channel_id=1, source_target_pairs={{0,8},{4,12},{8,0},{12,4},{16,24},{20,28},{24,16},{28,20},{1,9},{5... | collective-permute-start | bytes 153608 | tf_op jit(solution)/shard_map/ppermute | solution.py:23
  101.5 6.2 %collective-permute-start.26 = (bf16[8,3200]{1,0:T(8,128)(2,1)}, bf16[8,3200]{1,0:T(8,128)(2,1)}, u32[]{:S(2)}, u32[]{:S(2)}) collective-permute-start(bf16[8,3200]{1,0:T(8,128)(2,1)} %concatenate.77), channel_id=1, source_target_pairs={{0,16},{4,20},{8,24},{12,28},{16,0},{20,4},{24,8},{28,12},{1,17},{... | collective-permute-start | bytes 153608 | tf_op jit(solution)/shard_map/ppermute | solution.py:23
  104.8 7.7 %copy-start.8 = (s32[8,2]{0,1:T(2,128)S(1)}, s32[8,2]{0,1:T(2,128)}, u32[]{:S(2)}) copy-start(s32[8,2]{0,1:T(2,128)} %param.9) | copy-start | bytes 196
  104.8 5.9 %collective-permute-start.27 = (bf16[8,3200]{1,0:T(8,128)(2,1)S(1)}, bf16[8,3200]{1,0:T(8,128)(2,1)S(1)}, u32[]{:S(2)}, u32[]{:S(2)}) collective-permute-start(bf16[8,3200]{1,0:T(8,128)(2,1)S(1)} %concatenate.78), channel_id=1, source_target_pairs={{0,24},{4,28},{8,16},{12,20},{16,8},{20,12},{24,0},{28,4},{1,25},{... | collective-permute-start | bytes 153608 | tf_op jit(solution)/shard_map/ppermute | solution.py:23

commit v2 on v1

v2 whole, which is shorter than its diff:
```python
import functools

import jax
import jax.numpy as jnp
from jax import lax
from jax.experimental import pallas as pl
from jax.experimental.pallas import tpu as pltpu
from jax.sharding import PartitionSpec as P

PAD = 128
VMEM = 48 * 1024 * 1024
LARGEST = 256
BF = jnp.bfloat16
F32 = jnp.float32


def contract_last(left, right):
    return lax.dot_general(
        left, right, (((1,), (1,)), ((), ())), preferred_element_type=jnp.float32
    )


def contract_first(left, right):
    return lax.dot_general(
        left, right, (((0,), (0,)), ((), ())), preferred_element_type=jnp.float32
    )


def swap(value, axis, mask):
    size = lax.axis_size(axis)
    return lax.ppermute(value, axis, [(i, i ^ mask) for i in range(size)])


def call(body, outs, name, flops=0, moved=0):
    return pl.pallas_call(
        body,
        out_shape=outs,
        name=name,
        compiler_params=pltpu.CompilerParams(vmem_limit_bytes=VMEM),
        cost_estimate=pl.CostEstimate(flops=flops, bytes_accessed=moved, transcendentals=0),
    )


def shape(dims, dtype):
    return jax.ShapeDtypeStruct(dims, dtype)


def lanes(rows):
    return lax.broadcasted_iota(jnp.int32, (rows, PAD), 1)


def wire_pad(total, experts):
    lane = lanes(total.shape[0])
    rest = total - total.astype(BF).astype(F32)
    low = (lane >= experts) & (lane < 2 * experts)
    return jnp.where(low, total + pltpu.roll(rest, experts, 1), total).astype(BF)


def pack_body(x_ref, dy_ref, ids_ref, gates_ref, out_ref):
    count, features = x_ref.shape
    lane = lanes(count)
    gates = gates_ref[...].astype(F32)
    ids = ids_ref[...]
    dense = jnp.zeros((count, PAD), F32)
    for k in range(ids.shape[1]):
        dense = jnp.where(lane == ids[:, k : k + 1], gates[:, k : k + 1], dense)
    out_ref[:, :features] = jnp.concatenate(
        [x_ref[...].astype(F32), dy_ref[...].astype(F32)], axis=0
    ).astype(BF)
    out_ref[:, features:] = jnp.concatenate([dense, dense], axis=0).astype(BF)


def expert_body(experts, count, *refs):
    pieces, (wg_ref, wu_ref, wd_ref), rest = refs[:-12], refs[-12:-9], refs[-9:]
    x_ref, scaled_ref, hidden_ref, dg_ref, du_ref, send_ref, keep_ref, dy_ref, weight_ref = rest
    features = x_ref.shape[1]
    own = lax.axis_index("expert")
    lane = lanes(count)

    blocks = []
    for piece in pieces:
        for at in range(0, piece.shape[0], 2 * count):
            blocks.append((piece, at))
    for i in range(0, len(blocks), 2):
        halves = [ref[at : at + 2 * count, :].astype(F32) for ref, at in blocks[i : i + 2]]
        rows = pl.ds(i * count, 2 * count)
        x_ref[rows, :] = jnp.concatenate([h[:count, :features] for h in halves], axis=0).astype(BF)
        dy = jnp.concatenate([h[count:, :features] for h in halves], axis=0)
        dense = jnp.concatenate([h[:count, features:] for h in halves], axis=0)
        lane = lanes(2 * count)
        weight = jnp.sum(jnp.where(lane == own, dense, 0.0), axis=1, keepdims=True)
        weight_ref[rows, :] = jnp.broadcast_to(weight, (2 * count, PAD))
        dy_ref[rows, :] = dy.astype(BF)
        scaled_ref[rows, :] = (weight * dy).astype(BF)

    pre_gate = jnp.dot(x_ref[...], wg_ref[0], preferred_element_type=F32)
    pre_up = jnp.dot(x_ref[...], wu_ref[0], preferred_element_type=F32)
    back = contract_last(dy_ref[...], wd_ref[0])
    sig = jax.nn.sigmoid(pre_gate)
    active = pre_gate * sig
    hidden = (active * pre_up).astype(BF)
    d_hidden = weight_ref[:, :1] * back
    d_gate = (d_hidden * pre_up * (sig * (1.0 + pre_gate * (1.0 - sig)))).astype(BF)
    d_up = (d_hidden * active).astype(BF)
    hidden_ref[...] = hidden
    dg_ref[...] = d_gate
    du_ref[...] = d_up
    product = jnp.sum(hidden.astype(F32) * back, axis=1, keepdims=True)
    half = product.shape[0] // 2
    spread = jnp.where(lanes(2 * half) == own, product, 0.0)
    part = contract_last(d_gate[half:], wg_ref[0]) + contract_last(d_up[half:], wu_ref[0])
    send_ref[:, :features] = part.astype(BF)
    send_ref[:, features:] = wire_pad(spread[half:], experts)
    keep_ref[:, :features] = contract_last(d_gate[:half], wg_ref[0]) + contract_last(
        d_up[:half], wu_ref[0]
    )
    keep_ref[:, features:] = spread[:half]


def sum_body(experts, added, *refs):
    keep_ref, parts, outs = refs[0], refs[1 : 1 + added], refs[1 + added :]
    rows, width = outs[0].shape
    for i, out in enumerate(outs):
        at = pl.ds(i * rows, rows)
        total = keep_ref[at, :]
        for part in parts:
            total = total + part[at, :].astype(F32)
        if i == 0:
            out[...] = total
        else:
            out[:, : width - PAD] = total[:, : width - PAD].astype(BF)
            out[:, width - PAD :] = wire_pad(total[:, width - PAD :], experts)


def sum_parts(keep, parts, pieces, experts, name):
    rows = keep.shape[0] // pieces
    dims = (rows, keep.shape[1])
    outs = [shape(dims, F32)] + [shape(dims, BF)] * (pieces - 1)
    moved = 2 * keep.size * (2 + len(parts))
    return call(
        functools.partial(sum_body, experts, len(parts)), outs, name, keep.size * len(parts), moved
    )(keep, *parts)


def final_body(experts, added, *refs):
    keep_ref, parts, (ids_ref, tokens_ref, gates_ref) = refs[0], refs[1 : 1 + added], refs[1 + added :]
    count, features = tokens_ref.shape
    total = keep_ref[...]
    for part in parts:
        total = total + part[...].astype(F32)
    tokens_ref[...] = total[:, :features].astype(BF)
    ids = ids_ref[...]
    product = total[:, features:]
    lane = lanes(count)
    for k in range(ids.shape[1]):
        id_k = ids[:, k : k + 1]
        picked = (lane == id_k) | (lane == id_k + experts)
        gates_ref[:, k : k + 1] = jnp.sum(jnp.where(picked, product, 0.0), axis=1, keepdims=True)


def expert_plain(pieces, slabs, experts, count):
    gate_slab, up_slab, down_slab = slabs
    features = gate_slab.shape[0]
    rows = jnp.concatenate(pieces, axis=0).reshape(-1, 2, count, features + PAD)
    rows_x = rows[:, 0].reshape(-1, features + PAD)
    rows_dy = rows[:, 1, :, :features].reshape(-1, features)
    is_own = jnp.arange(PAD, dtype=jnp.int32)[None, :] == lax.axis_index("expert")
    weight = jnp.sum(
        jnp.where(is_own, rows_x[:, features:].astype(F32), 0.0), axis=1, keepdims=True
    )
    rows_x = rows_x[:, :features]
    pre_gate = jnp.dot(rows_x, gate_slab, preferred_element_type=F32)
    pre_up = jnp.dot(rows_x, up_slab, preferred_element_type=F32)
    back = contract_last(rows_dy, down_slab)
    sig = jax.nn.sigmoid(pre_gate)
    active = pre_gate * sig
    hidden = (active * pre_up).astype(BF)
    d_hidden = weight * back
    d_gate = (d_hidden * pre_up * (sig * (1.0 + pre_gate * (1.0 - sig)))).astype(BF)
    d_up = (d_hidden * active).astype(BF)
    scaled = (weight * rows_dy.astype(F32)).astype(BF)
    product = jnp.sum(hidden.astype(F32) * back, axis=1, keepdims=True)
    half = product.shape[0] // 2
    part = contract_last(d_gate, gate_slab) + contract_last(d_up, up_slab)
    wide = jnp.concatenate([part, jnp.where(is_own, product, 0.0)], axis=1)
    send = to_wire(wide[half:], experts)
    return rows_x, scaled, hidden, d_gate, d_up, send, wide[:half]


def to_wire(total, experts):
    pad = total[:, -PAD:]
    rest = jnp.roll(pad - lax.reduce_precision(pad, 8, 7), experts, 1)
    lane = jnp.arange(PAD)[None, :]
    pad = jnp.where((lane >= experts) & (lane < 2 * experts), pad + rest, pad)
    return jnp.concatenate([total[:, :-PAD], pad], axis=1).astype(BF)


def sum_plain(keep, parts, pieces, experts):
    for part in parts:
        keep = keep + part.astype(F32)
    split = jnp.split(keep, pieces, axis=0)
    return split[:1] + [to_wire(piece, experts) for piece in split[1:]]


def local(tokens, upstream, route_ids, route_gates, w_gate, w_up, w_down):
    experts = lax.axis_size("expert")
    groups = lax.axis_size("section") // 2
    count, features = tokens.shape
    width = features + PAD
    total_rows = 2 * experts * groups * count
    hidden_units = w_gate.shape[2]

    block = call(pack_body, shape((2 * count, width), BF), "pack", 0, 4 * count * width * 2)(
        tokens, upstream, route_ids, route_gates
    )
    along = [swap(block, "section", 2 * k) for k in range(1, groups)]
    near = [block] + [swap(block, "expert", d) for d in range(1, experts)]
    far_block = jnp.concatenate(along, axis=0)
    far = [far_block] + [swap(far_block, "expert", d) for d in range(1, experts)]
    mine = [piece for pair in zip(near, far) for piece in pair]
    pieces = mine + [swap(piece, "section", 1) for piece in mine]

    fits = total_rows <= LARGEST
    if fits:
        rows_x, scaled, hidden, d_gate, d_up, send, keep = pl.pallas_call(
            functools.partial(expert_body, experts, count),
            out_shape=[
                shape((total_rows, features), BF),
                shape((total_rows, features), BF),
                shape((total_rows, hidden_units), BF),
                shape((total_rows, hidden_units), BF),
                shape((total_rows, hidden_units), BF),
                shape((total_rows // 2, width), BF),
                shape((total_rows // 2, width), F32),
            ],
            scratch_shapes=[
                pltpu.VMEM((total_rows, features), BF),
                pltpu.VMEM((total_rows, PAD), F32),
            ],
            name="expert",
            compiler_params=pltpu.CompilerParams(vmem_limit_bytes=VMEM),
            cost_estimate=pl.CostEstimate(
                flops=10 * total_rows * features * hidden_units,
                bytes_accessed=16 * 1024 * 1024,
                transcendentals=total_rows * hidden_units,
            ),
        )(*pieces, w_gate, w_up, w_down)
    else:
        rows_x, scaled, hidden, d_gate, d_up, send, keep = expert_plain(
            pieces, (w_gate[0], w_up[0], w_down[0]), experts, count
        )

    def added(total, parts, pieces, name):
        if fits:
            return sum_parts(total, parts, pieces, experts, name)
        return sum_plain(total, parts, pieces, experts)

    split = added(keep, [swap(send, "section", 1)], experts, "sum_cores")
    plane = added(
        split[0], [swap(split[d], "expert", d) for d in range(1, experts)], groups, "sum_experts"
    )
    parts = [swap(plane[k], "section", 2 * k) for k in range(1, groups)]
    grad_tokens, grad_gates = call(
        functools.partial(final_body, experts, len(parts)),
        [shape((count, features), BF), shape(route_ids.shape, F32)],
        "final",
        0,
        4 * count * width * 2,
    )(plane[0], *parts, route_ids)

    grad_down = contract_first(hidden, scaled)
    grad_gate = contract_first(rows_x, d_gate)
    grad_up = contract_first(rows_x, d_up)
    return (
        grad_tokens,
        grad_gates,
        grad_gate.astype(BF)[None],
        grad_up.astype(BF)[None],
        grad_down.astype(BF)[None],
    )


def solution(mesh):
    placed = (
        P(("section", "expert"), None),
        P(("section", "expert"), None),
        P(("section", "expert"), None),
        P(("section", "expert"), None),
        P("expert", None, "section"),
        P("expert", None, "section"),
        P("expert", "section", None),
    )
    return jax.shard_map(
        local,
        mesh=mesh,
        in_specs=placed,
        out_specs=(
            P(("section", "expert"), None),
            P(("section", "expert"), None),
            P("expert", None, "section"),
            P("expert", None, "section"),
            P("expert", "section", None),
        ),
        check_vma=False,
    )
```

time: 114 us -> 78.9 us (0.69)
  local copies, waits for them, and re-layouts: 25.8 us -> 3.77 us
  other arithmetic: 18 us -> 0 us
  matrix products: 13.4 us -> 5.29 us
  Pallas kernels: 0 us -> 7.95 us
  waiting for transfers between devices: 29.6 us -> 37.4 us
  starting transfers between devices: 25.3 us -> 23.6 us
    concatenate x13 -> x0, local copies, waits for them, and re-layouts: 18 us -> none  [the longest x10 13.7 us: to_wire(): jnp.concatenate([total[..., :features], high, product - high, rest], axis...]
    pallas_call x0 -> x5, Pallas kernels: none -> 7.95 us  [the longest x1 6.84 us: local(): pl.pallas_call(functools.partial(expert_body, experts, count), out_shape=...]
    ppermute x28 -> x24, waiting for transfers between devices: 29.6 us -> 37.4 us  [swap(): return lax.ppermute(value, axis, [(i, i ^ mask) for i in range(size)])]
    another operation x10 -> x0, other arithmetic: 6.11 us -> none
    dot_general x5 -> x0, matrix products: 5.84 us -> none  [the longest x3 4.37 us: contract_last(): lax.dot_general(left, right, (((1,), (1,)), ((), ())), preferred_element_...]
    select_n x4 -> x0, other arithmetic: 4.43 us -> none  [the longest x1 3.33 us: local(): to_send = jnp.where(first_core, wide[:, :, 1], wide[:, :, 0])]
    slice x11 -> x0, local copies, waits for them, and re-layouts: 4.18 us -> none  [the longest x10 3.55 us: to_wire(): total[..., :features]]
    add x4 -> x0, other arithmetic: 3.53 us -> none  [the longest x1 1.34 us: local(): plane + swap(to_wire(total[d], features, experts), 'expert', d).astype(jn...]
  transfers between devices with their start and end apart: 28 -> 24, of which waited for: 10 -> 12; matrix products, arithmetic and copies ran while one was open for 21% -> 7% of each run, Pallas kernels for 0% -> 0%
where the time goes in v2:
time: 78.9 us; the launch traced here: 78.7 us
  waiting for transfers between devices  37.4 us (47%)
  starting transfers between devices  23.6 us (30%)
  Pallas kernels  7.95 us (10%)
  matrix products  5.29 us (7%)
  local copies, waits for them, and re-layouts  3.77 us (5%)
    ppermute x24, waiting for transfers between devices, swap(): return lax.ppermute(value, axis, [(i, i ^ mask) for i in range(size)])  37.4 us
    ppermute x24, starting transfers between devices, swap(): return lax.ppermute(value, axis, [(i, i ^ mask) for i in range(size)])  23.6 us
    pallas_call x1, Pallas kernels, local(): pl.pallas_call(functools.partial(expert_body, experts, count), out_shape=...  6.84 us
    dot_general x3, matrix products, contract_first(): lax.dot_general(left, right, (((0,), (0,)), ((), ())), preferred_element_...  5.29 us
    unnamed x13, local copies, waits for them, and re-layouts  3.76 us
  transfers between devices with their start and end apart: 24, of which 12 were waited for; matrix products, arithmetic and copies ran while one was open for 7% of the time, Pallas kernels for 0%

profile of v2, /device:TPU:0, one launch (start us, length us, event | category | flops | bytes accessed | tf_op | source)
XLA Modules:
  0.0 78.7 jit_solution(13605222190379204296)
XLA Ops:
  0.6 0.7 copy.13.gates_ref
  1.4 0.8 copy.12.ids_ref.refs_4_
  2.1 0.0 copy-start.1
  2.1 0.8 %copy-done.1 = bf16[8,3072]{1,0:T(8,128)(2,1)S(1)} copy-done((bf16[8,3072]{1,0:T(8,128)(2,1)S(1)}, bf16[8,3072]{1,0:T(8,128)(2,1)}, u32[]{:S(2)}) %copy-start.1) | copy-done | bytes 49176
  2.9 0.8 %copy-done.2 = bf16[8,3072]{1,0:T(8,128)(2,1)S(1)} copy-done((bf16[8,3072]{1,0:T(8,128)(2,1)S(1)}, bf16[8,3072]{1,0:T(8,128)(2,1)}, u32[]{:S(2)}) %copy-start.2) | copy-done | bytes 49176
  3.7 0.1 pack.1.refs_0_
  3.8 3.0 %collective-permute-start = (bf16[16,3200]{1,0:T(8,128)(2,1)S(1)}, bf16[16,3200]{1,0:T(8,128)(2,1)S(1)}, u32[]{:S(2)}, u32[]{:S(2)}) collective-permute-start(bf16[16,3200]{1,0:T(8,128)(2,1)S(1)} %pack.1.refs_0_), channel_id=1, source_target_pairs={{0,8},{4,12},{8,0},{12,4},{16,24},{20,28},{24,16},{28,20},{1,9},{5... | collective-permute-start | bytes 307208 | tf_op jit(solution)/shard_map/ppermute | solution.py:31
  6.8 2.5 %collective-permute-start.2 = (bf16[16,3200]{1,0:T(8,128)(2,1)S(1)}, bf16[16,3200]{1,0:T(8,128)(2,1)S(1)}, u32[]{:S(2)}, u32[]{:S(2)}) collective-permute-start(bf16[16,3200]{1,0:T(8,128)(2,1)S(1)} %pack.1.refs_0_), channel_id=1, source_target_pairs={{0,24},{4,28},{8,16},{12,20},{16,8},{20,12},{24,0},{28,4},{1,25},{... | collective-permute-start | bytes 307208 | tf_op jit(solution)/shard_map/ppermute | solution.py:31
  9.3 0.1 collective-permute-start.1
  9.4 0.3 collective-permute-done
  9.7 8.9 %collective-permute-done.1 = bf16[16,3200]{1,0:T(8,128)(2,1)S(1)} collective-permute-done((bf16[16,3200]{1,0:T(8,128)(2,1)S(1)}, bf16[16,3200]{1,0:T(8,128)(2,1)S(1)}, u32[]{:S(2)}, u32[]{:S(2)}) %collective-permute-start.1) | collective-permute-done | bytes 102432 | tf_op jit(solution)/shard_map/ppermute | solution.py:31
  18.6 0.0 collective-permute-done.2
  18.6 2.5 %collective-permute-start.8 = (bf16[48,3200]{1,0:T(8,128)(2,1)S(1)}, bf16[48,3200]{1,0:T(8,128)(2,1)S(1)}, u32[]{:S(2)}, u32[]{:S(2)}) collective-permute-start(bf16[48,3200]{1,0:T(8,128)(2,1)S(1)} %constant_dynamic-update-slice_fusion.refs_1_), channel_id=1, source_target_pairs={{0,3},{1,2},{2,1},{3,0},{4,7},{5,6},{6,5},{7,4},{8,11},{9,10},{10,... | collective-permute-start | bytes 921608 | tf_op jit(solution)/shard_map/ppermute | solution.py:31
  21.2 0.5 collective-permute-start.6
  21.7 0.5 collective-permute-start.4
  22.2 0.0 collective-permute-start.9
  22.2 2.4 %collective-permute-start.7 = (bf16[16,3200]{1,0:T(8,128)(2,1)S(1)}, bf16[16,3200]{1,0:T(8,128)(2,1)S(1)}, u32[]{:S(2)}, u32[]{:S(2)}) collective-permute-start(bf16[16,3200]{1,0:T(8,128)(2,1)S(1)} %pack.1.refs_0_), channel_id=1, source_target_pairs={{0,3},{1,2},{2,1},{3,0},{4,7},{5,6},{6,5},{7,4},{8,11},{9,10},{10,... | collective-permute-start | bytes 307208 | tf_op jit(solution)/shard_map/ppermute | solution.py:31
  24.7 0.0 collective-permute-done.9.refs_8_
  24.7 0.5 collective-permute-start.5
  25.2 12.1 %collective-permute-done.7.refs_6_ = bf16[16,3200]{1,0:T(8,128)(2,1)S(1)} collective-permute-done((bf16[16,3200]{1,0:T(8,128)(2,1)S(1)}, bf16[16,3200]{1,0:T(8,128)(2,1)S(1)}, u32[]{:S(2)}, u32[]{:S(2)}) %collective-permute-start.7) | collective-permute-done | bytes 102432 | tf_op jit(solution)/shard_map/ppermute | solution.py:31
  37.2 1.5 %collective-permute-start.3 = (bf16[16,3200]{1,0:T(8,128)(2,1)S(1)}, bf16[16,3200]{1,0:T(8,128)(2,1)S(1)}, u32[]{:S(2)}, u32[]{:S(2)}) collective-permute-start(bf16[16,3200]{1,0:T(8,128)(2,1)S(1)} %pack.1.refs_0_), channel_id=1, source_target_pairs={{0,1},{1,0},{2,3},{3,2},{4,5},{5,4},{6,7},{7,6},{8,9},{9,8},{10,11... | collective-permute-start | bytes 307208 | tf_op jit(solution)/shard_map/ppermute | solution.py:31
  38.7 0.6 collective-permute-done.5.refs_4_
  39.3 0.0 collective-permute-start.10
  39.3 2.6 %collective-permute-done.3.refs_2_ = bf16[16,3200]{1,0:T(8,128)(2,1)S(1)} collective-permute-done((bf16[16,3200]{1,0:T(8,128)(2,1)S(1)}, bf16[16,3200]{1,0:T(8,128)(2,1)S(1)}, u32[]{:S(2)}, u32[]{:S(2)}) %collective-permute-start.3) | collective-permute-done | bytes 102432 | tf_op jit(solution)/shard_map/ppermute | solution.py:31
  41.9 0.0 collective-permute-start.15
  41.9 0.0 collective-permute-done.8.refs_7_
  41.9 0.5 collective-permute-start.16
  42.4 0.0 collective-permute-done.6.refs_5_
  42.4 0.1 collective-permute-start.14
  42.5 0.0 collective-permute-done.4.refs_3_
  42.5 0.4 collective-permute-start.12
  42.9 0.3 collective-permute-done.15.refs_14_
  43.2 0.2 collective-permute-start.13
  43.4 1.3 %collective-permute-done.13.refs_12_ = bf16[16,3200]{1,0:T(8,128)(2,1)S(1)} collective-permute-done((bf16[16,3200]{1,0:T(8,128)(2,1)S(1)}, bf16[16,3200]{1,0:T(8,128)(2,1)S(1)}, u32[]{:S(2)}, u32[]{:S(2)}) %collective-permute-start.13) | collective-permute-done | bytes 102432 | tf_op jit(solution)/shard_map/ppermute | solution.py:31
  44.7 0.4 collective-permute-start.11
  45.0 0.9 %collective-permute-done.11.refs_10_ = bf16[16,3200]{1,0:T(8,128)(2,1)S(1)} collective-permute-done((bf16[16,3200]{1,0:T(8,128)(2,1)S(1)}, bf16[16,3200]{1,0:T(8,128)(2,1)S(1)}, u32[]{:S(2)}, u32[]{:S(2)}) %collective-permute-start.11) | collective-permute-done | bytes 102432 | tf_op jit(solution)/shard_map/ppermute | solution.py:31
  46.0 0.0 collective-permute-done.10.refs_9_
  46.0 0.0 collective-permute-done.16.refs_15_
  46.0 0.0 collective-permute-done.14.refs_13_
  46.0 0.0 collective-permute-done.12.refs_11_
  46.0 6.8 %expert.1 = (bf16[256,3072]{1,0:T(8,128)(2,1)S(1)}, bf16[256,3072]{1,0:T(8,128)(2,1)}, bf16[256,256]{1,0:T(8,128)(2,1)S(1)}, bf16[256,256]{1,0:T(8,128)(2,1)S(1)...) custom-call(bf16[16,3200]{1,0:T(8,128)(2,1)S(1)} %pack.1.refs_0_, ...), custom_call_target="tpu_custom_call" | custom-call | flops 2013265920 | bytes 16777216 | tf_op jit(solution)/shard_map/expert/pallas_call | solution.py:225
  52.8 0.4 collective-permute-start.17
  53.2 1.8 %fusion = bf16[1,3072,256]{2,1,0:T(8,128)(2,1)} fusion(bf16[256,3072]{1,0:T(8,128)(2,1)S(1)} %get-tuple-element.34, bf16[256,256]{1,0:T(8,128)(2,1)S(1)} %get-tuple-element.35), kind=kOutput, calls=%fused_computation.3 | convolution fusion | flops 403439616 | bytes 3276800 | tf_op jit(solution)/shard_map/dot_general | solution.py:24
  55.0 0.2 collective-permute-done.17.refs_1_
  55.2 0.0 copy-done
  55.2 0.2 sum_cores.1
  55.4 1.6 %collective-permute-start.18 = (bf16[32,3200]{1,0:T(8,128)(2,1)S(1)}, bf16[32,3200]{1,0:T(8,128)(2,1)S(1)}, u32[]{:S(2)}, u32[]{:S(2)}) collective-permute-start(bf16[32,3200]{1,0:T(8,128)(2,1)S(1)} %get-tuple-element.25), channel_id=1, source_target_pairs={{0,1},{1,0},{2,3},{3,2},{4,5},{5,4},{6,7},{7,6},{8,9},{9,8},{10,11... | collective-permute-start | bytes 614408 | tf_op jit(solution)/shard_map/ppermute | solution.py:31
  57.0 1.5 %collective-permute-start.19 = (bf16[32,3200]{1,0:T(8,128)(2,1)S(1)}, bf16[32,3200]{1,0:T(8,128)(2,1)S(1)}, u32[]{:S(2)}, u32[]{:S(2)}) collective-permute-start(bf16[32,3200]{1,0:T(8,128)(2,1)S(1)} %get-tuple-element.26), channel_id=1, source_target_pairs={{0,2},{1,3},{2,0},{3,1},{4,6},{5,7},{6,4},{7,5},{8,10},{9,11},{10,... | collective-permute-start | bytes 614408 | tf_op jit(solution)/shard_map/ppermute | solution.py:31
  58.5 0.5 collective-permute-start.20
  59.0 1.8 %fusion.1 = bf16[1,3072,256]{2,1,0:T(8,128)(2,1)} fusion(bf16[256,3072]{1,0:T(8,128)(2,1)S(1)} %get-tuple-element.34, bf16[256,256]{1,0:T(8,128)(2,1)S(1)} %get-tuple-element.36), kind=kOutput, calls=%fused_computation.4 | convolution fusion | flops 403439616 | bytes 3276800 | tf_op jit(solution)/shard_map/dot_general | solution.py:24
  60.8 2.6 %collective-permute-done.18.refs_1_ = bf16[32,3200]{1,0:T(8,128)(2,1)S(1)} collective-permute-done((bf16[32,3200]{1,0:T(8,128)(2,1)S(1)}, bf16[32,3200]{1,0:T(8,128)(2,1)S(1)}, u32[]{:S(2)}, u32[]{:S(2)}) %collective-permute-start.18) | collective-permute-done | bytes 204832 | tf_op jit(solution)/shard_map/ppermute | solution.py:31
  63.4 5.0 %collective-permute-done.19.refs_2_ = bf16[32,3200]{1,0:T(8,128)(2,1)S(1)} collective-permute-done((bf16[32,3200]{1,0:T(8,128)(2,1)S(1)}, bf16[32,3200]{1,0:T(8,128)(2,1)S(1)}, u32[]{:S(2)}, u32[]{:S(2)}) %collective-permute-start.19) | collective-permute-done | bytes 204832 | tf_op jit(solution)/shard_map/ppermute | solution.py:31
  68.4 0.0 collective-permute-done.20.refs_3_
  68.4 0.1 sum_experts.1
  68.5 0.1 collective-permute-start.21
  68.6 2.8 %collective-permute-start.22 = (bf16[8,3200]{1,0:T(8,128)(2,1)S(1)}, bf16[8,3200]{1,0:T(8,128)(2,1)S(1)}, u32[]{:S(2)}, u32[]{:S(2)}) collective-permute-start(bf16[8,3200]{1,0:T(8,128)(2,1)S(1)} %get-tuple-element.30), channel_id=1, source_target_pairs={{0,16},{4,20},{8,24},{12,28},{16,0},{20,4},{24,8},{28,12},{1,17},{... | collective-permute-start | bytes 153608 | tf_op jit(solution)/shard_map/ppermute | solution.py:31
  71.4 1.6 %collective-permute-start.23 = (bf16[8,3200]{1,0:T(8,128)(2,1)S(1)}, bf16[8,3200]{1,0:T(8,128)(2,1)S(1)}, u32[]{:S(2)}, u32[]{:S(2)}) collective-permute-start(bf16[8,3200]{1,0:T(8,128)(2,1)S(1)} %get-tuple-element.31), channel_id=1, source_target_pairs={{0,24},{4,28},{8,16},{12,20},{16,8},{20,12},{24,0},{28,4},{1,25},{... | collective-permute-start | bytes 153608 | tf_op jit(solution)/shard_map/ppermute | solution.py:31
  73.0 0.0 copy-done.3
  73.0 1.7 %fusion.2 = bf16[1,256,3072]{2,1,0:T(8,128)(2,1)} fusion(bf16[256,256]{1,0:T(8,128)(2,1)S(1)} %get-tuple-element.37, bf16[256,3072]{1,0:T(8,128)(2,1)S(1)} %copy-done.3), kind=kOutput, calls=%fused_computation.5 | convolution fusion | flops 403439616 | bytes 3276800 | tf_op jit(solution)/shard_map/dot_general | solution.py:24
  74.7 0.0 collective-permute-done.21.refs_1_
  74.7 0.0 collective-permute-done.22.refs_2_
  74.7 2.6 %collective-permute-done.23.refs_3_ = bf16[8,3200]{1,0:T(8,128)(2,1)S(1)} collective-permute-done((bf16[8,3200]{1,0:T(8,128)(2,1)S(1)}, bf16[8,3200]{1,0:T(8,128)(2,1)S(1)}, u32[]{:S(2)}, u32[]{:S(2)}) %collective-permute-start.23) | collective-permute-done | bytes 51232 | tf_op jit(solution)/shard_map/ppermute | solution.py:31
  77.3 0.7 final.1
  78.0 0.6 copy.15
  (6 shorter events, 0.0 us)
Async XLA Ops:
  2.1 0.8 %copy-start.1 = (bf16[8,3072]{1,0:T(8,128)(2,1)S(1)}, bf16[8,3072]{1,0:T(8,128)(2,1)}, u32[]{:S(2)}) copy-start(bf16[8,3072]{1,0:T(8,128)(2,1)} %x_ref.1) | copy-start | bytes 147460
  2.9 0.8 %copy-start.2 = (bf16[8,3072]{1,0:T(8,128)(2,1)S(1)}, bf16[8,3072]{1,0:T(8,128)(2,1)}, u32[]{:S(2)}) copy-start(bf16[8,3072]{1,0:T(8,128)(2,1)} %dy_ref.1) | copy-start | bytes 147460
  3.8 5.9 %collective-permute-start = (bf16[16,3200]{1,0:T(8,128)(2,1)S(1)}, bf16[16,3200]{1,0:T(8,128)(2,1)S(1)}, u32[]{:S(2)}, u32[]{:S(2)}) collective-permute-start(bf16[16,3200]{1,0:T(8,128)(2,1)S(1)} %pack.1.refs_0_), channel_id=1, source_target_pairs={{0,8},{4,12},{8,0},{12,4},{16,24},{20,28},{24,16},{28,20},{1,9},{5... | collective-permute-start | bytes 307208 | tf_op jit(solution)/shard_map/ppermute | solution.py:31
  6.8 11.8 %collective-permute-start.2 = (bf16[16,3200]{1,0:T(8,128)(2,1)S(1)}, bf16[16,3200]{1,0:T(8,128)(2,1)S(1)}, u32[]{:S(2)}, u32[]{:S(2)}) collective-permute-start(bf16[16,3200]{1,0:T(8,128)(2,1)S(1)} %pack.1.refs_0_), channel_id=1, source_target_pairs={{0,24},{4,28},{8,16},{12,20},{16,8},{20,12},{24,0},{28,4},{1,25},{... | collective-permute-start | bytes 307208 | tf_op jit(solution)/shard_map/ppermute | solution.py:31
  9.3 9.3 %collective-permute-start.1 = (bf16[16,3200]{1,0:T(8,128)(2,1)S(1)}, bf16[16,3200]{1,0:T(8,128)(2,1)S(1)}, u32[]{:S(2)}, u32[]{:S(2)}) collective-permute-start(bf16[16,3200]{1,0:T(8,128)(2,1)S(1)} %pack.1.refs_0_), channel_id=1, source_target_pairs={{0,16},{4,20},{8,24},{12,28},{16,0},{20,4},{24,8},{28,12},{1,17},{... | collective-permute-start | bytes 307208 | tf_op jit(solution)/shard_map/ppermute | solution.py:31
  18.6 23.3 %collective-permute-start.8 = (bf16[48,3200]{1,0:T(8,128)(2,1)S(1)}, bf16[48,3200]{1,0:T(8,128)(2,1)S(1)}, u32[]{:S(2)}, u32[]{:S(2)}) collective-permute-start(bf16[48,3200]{1,0:T(8,128)(2,1)S(1)} %constant_dynamic-update-slice_fusion.refs_1_), channel_id=1, source_target_pairs={{0,3},{1,2},{2,1},{3,0},{4,7},{5,6},{6,5},{7,4},{8,11},{9,10},{10,... | collective-permute-start | bytes 921608 | tf_op jit(solution)/shard_map/ppermute | solution.py:31
  21.2 21.3 %collective-permute-start.6 = (bf16[48,3200]{1,0:T(8,128)(2,1)S(1)}, bf16[48,3200]{1,0:T(8,128)(2,1)S(1)}, u32[]{:S(2)}, u32[]{:S(2)}) collective-permute-start(bf16[48,3200]{1,0:T(8,128)(2,1)S(1)} %constant_dynamic-update-slice_fusion.refs_1_), channel_id=1, source_target_pairs={{0,2},{1,3},{2,0},{3,1},{4,6},{5,7},{6,4},{7,5},{8,10},{9,11},{10,... | collective-permute-start | bytes 921608 | tf_op jit(solution)/shard_map/ppermute | solution.py:31
  21.7 20.8 %collective-permute-start.4 = (bf16[48,3200]{1,0:T(8,128)(2,1)S(1)}, bf16[48,3200]{1,0:T(8,128)(2,1)S(1)}, u32[]{:S(2)}, u32[]{:S(2)}) collective-permute-start(bf16[48,3200]{1,0:T(8,128)(2,1)S(1)} %constant_dynamic-update-slice_fusion.refs_1_), channel_id=1, source_target_pairs={{0,1},{1,0},{2,3},{3,2},{4,5},{5,4},{6,7},{7,6},{8,9},{9,8},{10,11... | collective-permute-start | bytes 921608 | tf_op jit(solution)/shard_map/ppermute | solution.py:31
  22.2 2.5 %collective-permute-start.9 = (bf16[16,3200]{1,0:T(8,128)(2,1)S(1)}, bf16[16,3200]{1,0:T(8,128)(2,1)S(1)}, u32[]{:S(2)}, u32[]{:S(2)}) collective-permute-start(bf16[16,3200]{1,0:T(8,128)(2,1)S(1)} %pack.1.refs_0_), channel_id=1, source_target_pairs={{0,4},{4,0},{8,12},{12,8},{16,20},{20,16},{24,28},{28,24},{1,5},{5... | collective-permute-start | bytes 307208 | tf_op jit(solution)/shard_map/ppermute | solution.py:31
  22.2 15.0 %collective-permute-start.7 = (bf16[16,3200]{1,0:T(8,128)(2,1)S(1)}, bf16[16,3200]{1,0:T(8,128)(2,1)S(1)}, u32[]{:S(2)}, u32[]{:S(2)}) collective-permute-start(bf16[16,3200]{1,0:T(8,128)(2,1)S(1)} %pack.1.refs_0_), channel_id=1, source_target_pairs={{0,3},{1,2},{2,1},{3,0},{4,7},{5,6},{6,5},{7,4},{8,11},{9,10},{10,... | collective-permute-start | bytes 307208 | tf_op jit(solution)/shard_map/ppermute | solution.py:31
  24.7 14.6 %collective-permute-start.5 = (bf16[16,3200]{1,0:T(8,128)(2,1)S(1)}, bf16[16,3200]{1,0:T(8,128)(2,1)S(1)}, u32[]{:S(2)}, u32[]{:S(2)}) collective-permute-start(bf16[16,3200]{1,0:T(8,128)(2,1)S(1)} %pack.1.refs_0_), channel_id=1, source_target_pairs={{0,2},{1,3},{2,0},{3,1},{4,6},{5,7},{6,4},{7,5},{8,10},{9,11},{10,... | collective-permute-start | bytes 307208 | tf_op jit(solution)/shard_map/ppermute | solution.py:31
  37.2 4.7 %collective-permute-start.3 = (bf16[16,3200]{1,0:T(8,128)(2,1)S(1)}, bf16[16,3200]{1,0:T(8,128)(2,1)S(1)}, u32[]{:S(2)}, u32[]{:S(2)}) collective-permute-start(bf16[16,3200]{1,0:T(8,128)(2,1)S(1)} %pack.1.refs_0_), channel_id=1, source_target_pairs={{0,1},{1,0},{2,3},{3,2},{4,5},{5,4},{6,7},{7,6},{8,9},{9,8},{10,11... | collective-permute-start | bytes 307208 | tf_op jit(solution)/shard_map/ppermute | solution.py:31
  39.3 6.7 %collective-permute-start.10 = (bf16[48,3200]{1,0:T(8,128)(2,1)S(1)}, bf16[48,3200]{1,0:T(8,128)(2,1)S(1)}, u32[]{:S(2)}, u32[]{:S(2)}) collective-permute-start(bf16[48,3200]{1,0:T(8,128)(2,1)S(1)} %constant_dynamic-update-slice_fusion.refs_1_), channel_id=1, source_target_pairs={{0,4},{4,0},{8,12},{12,8},{16,20},{20,16},{24,28},{28,24},{1,5},{5... | collective-permute-start | bytes 921608 | tf_op jit(solution)/shard_map/ppermute | solution.py:31
  41.9 1.3 %collective-permute-start.15 = (bf16[16,3200]{1,0:T(8,128)(2,1)S(1)}, bf16[16,3200]{1,0:T(8,128)(2,1)S(1)}, u32[]{:S(2)}, u32[]{:S(2)}) collective-permute-start(bf16[16,3200]{1,0:T(8,128)(2,1)S(1)} %collective-permute-done.7.refs_6_), channel_id=1, source_target_pairs={{0,4},{4,0},{8,12},{12,8},{16,20},{20,16},{24,28},{28,24},{1,5},{5... | collective-permute-start | bytes 307208 | tf_op jit(solution)/shard_map/ppermute | solution.py:31
  41.9 4.1 %collective-permute-start.16 = (bf16[48,3200]{1,0:T(8,128)(2,1)S(1)}, bf16[48,3200]{1,0:T(8,128)(2,1)S(1)}, u32[]{:S(2)}, u32[]{:S(2)}) collective-permute-start(bf16[48,3200]{1,0:T(8,128)(2,1)S(1)} %collective-permute-done.8.refs_7_), channel_id=1, source_target_pairs={{0,4},{4,0},{8,12},{12,8},{16,20},{20,16},{24,28},{28,24},{1,5},{5... | collective-permute-start | bytes 921608 | tf_op jit(solution)/shard_map/ppermute | solution.py:31
  42.4 3.6 %collective-permute-start.14 = (bf16[48,3200]{1,0:T(8,128)(2,1)S(1)}, bf16[48,3200]{1,0:T(8,128)(2,1)S(1)}, u32[]{:S(2)}, u32[]{:S(2)}) collective-permute-start(bf16[48,3200]{1,0:T(8,128)(2,1)S(1)} %collective-permute-done.6.refs_5_), channel_id=1, source_target_pairs={{0,4},{4,0},{8,12},{12,8},{16,20},{20,16},{24,28},{28,24},{1,5},{5... | collective-permute-start | bytes 921608 | tf_op jit(solution)/shard_map/ppermute | solution.py:31
  42.5 3.5 %collective-permute-start.12 = (bf16[48,3200]{1,0:T(8,128)(2,1)S(1)}, bf16[48,3200]{1,0:T(8,128)(2,1)S(1)}, u32[]{:S(2)}, u32[]{:S(2)}) collective-permute-start(bf16[48,3200]{1,0:T(8,128)(2,1)S(1)} %collective-permute-done.4.refs_3_), channel_id=1, source_target_pairs={{0,4},{4,0},{8,12},{12,8},{16,20},{20,16},{24,28},{28,24},{1,5},{5... | collective-permute-start | bytes 921608 | tf_op jit(solution)/shard_map/ppermute | solution.py:31
  43.2 1.5 %collective-permute-start.13 = (bf16[16,3200]{1,0:T(8,128)(2,1)S(1)}, bf16[16,3200]{1,0:T(8,128)(2,1)S(1)}, u32[]{:S(2)}, u32[]{:S(2)}) collective-permute-start(bf16[16,3200]{1,0:T(8,128)(2,1)S(1)} %collective-permute-done.5.refs_4_), channel_id=1, source_target_pairs={{0,4},{4,0},{8,12},{12,8},{16,20},{20,16},{24,28},{28,24},{1,5},{5... | collective-permute-start | bytes 307208 | tf_op jit(solution)/shard_map/ppermute | solution.py:31
  44.7 1.3 %collective-permute-start.11 = (bf16[16,3200]{1,0:T(8,128)(2,1)S(1)}, bf16[16,3200]{1,0:T(8,128)(2,1)S(1)}, u32[]{:S(2)}, u32[]{:S(2)}) collective-permute-start(bf16[16,3200]{1,0:T(8,128)(2,1)S(1)} %collective-permute-done.3.refs_2_), channel_id=1, source_target_pairs={{0,4},{4,0},{8,12},{12,8},{16,20},{20,16},{24,28},{28,24},{1,5},{5... | collective-permute-start | bytes 307208 | tf_op jit(solution)/shard_map/ppermute | solution.py:31
  52.8 2.3 %collective-permute-start.17 = (bf16[128,3200]{1,0:T(8,128)(2,1)S(1)}, bf16[128,3200]{1,0:T(8,128)(2,1)S(1)}, u32[]{:S(2)}, u32[]{:S(2)}) collective-permute-start(bf16[128,3200]{1,0:T(8,128)(2,1)S(1)} %get-tuple-element.23), channel_id=1, source_target_pairs={{0,4},{4,0},{8,12},{12,8},{16,20},{20,16},{24,28},{28,24},{1,5},{5... | collective-permute-start | bytes 2457608 | tf_op jit(solution)/shard_map/ppermute | solution.py:31
  53.2 2.0 %copy-start = (f32[128,3200]{1,0:T(8,128)S(1)}, f32[128,3200]{1,0:T(8,128)}, u32[]{:S(2)}) copy-start(f32[128,3200]{1,0:T(8,128)} %get-tuple-element.22.refs_0_) | copy-start | bytes 4915204
  55.4 8.0 %collective-permute-start.18 = (bf16[32,3200]{1,0:T(8,128)(2,1)S(1)}, bf16[32,3200]{1,0:T(8,128)(2,1)S(1)}, u32[]{:S(2)}, u32[]{:S(2)}) collective-permute-start(bf16[32,3200]{1,0:T(8,128)(2,1)S(1)} %get-tuple-element.25), channel_id=1, source_target_pairs={{0,1},{1,0},{2,3},{3,2},{4,5},{5,4},{6,7},{7,6},{8,9},{9,8},{10,11... | collective-permute-start | bytes 614408 | tf_op jit(solution)/shard_map/ppermute | solution.py:31
  57.0 11.4 %collective-permute-start.19 = (bf16[32,3200]{1,0:T(8,128)(2,1)S(1)}, bf16[32,3200]{1,0:T(8,128)(2,1)S(1)}, u32[]{:S(2)}, u32[]{:S(2)}) collective-permute-start(bf16[32,3200]{1,0:T(8,128)(2,1)S(1)} %get-tuple-element.26), channel_id=1, source_target_pairs={{0,2},{1,3},{2,0},{3,1},{4,6},{5,7},{6,4},{7,5},{8,10},{9,11},{10,... | collective-permute-start | bytes 614408 | tf_op jit(solution)/shard_map/ppermute | solution.py:31
  58.5 9.9 %collective-permute-start.20 = (bf16[32,3200]{1,0:T(8,128)(2,1)S(1)}, bf16[32,3200]{1,0:T(8,128)(2,1)S(1)}, u32[]{:S(2)}, u32[]{:S(2)}) collective-permute-start(bf16[32,3200]{1,0:T(8,128)(2,1)S(1)} %get-tuple-element.27), channel_id=1, source_target_pairs={{0,3},{1,2},{2,1},{3,0},{4,7},{5,6},{6,5},{7,4},{8,11},{9,10},{10,... | collective-permute-start | bytes 614408 | tf_op jit(solution)/shard_map/ppermute | solution.py:31
  59.0 14.0 %copy-start.3 = (bf16[256,3072]{1,0:T(8,128)(2,1)S(1)}, bf16[256,3072]{1,0:T(8,128)(2,1)}, u32[]{:S(2)}) copy-start(bf16[256,3072]{1,0:T(8,128)(2,1)} %get-tuple-element.38) | copy-start | bytes 4718596
  68.5 6.2 %collective-permute-start.21 = (bf16[8,3200]{1,0:T(8,128)(2,1)S(1)}, bf16[8,3200]{1,0:T(8,128)(2,1)S(1)}, u32[]{:S(2)}, u32[]{:S(2)}) collective-permute-start(bf16[8,3200]{1,0:T(8,128)(2,1)S(1)} %get-tuple-element.29), channel_id=1, source_target_pairs={{0,8},{4,12},{8,0},{12,4},{16,24},{20,28},{24,16},{28,20},{1,9},{5... | collective-permute-start | bytes 153608 | tf_op jit(solution)/shard_map/ppermute | solution.py:31
  68.6 6.1 %collective-permute-start.22 = (bf16[8,3200]{1,0:T(8,128)(2,1)S(1)}, bf16[8,3200]{1,0:T(8,128)(2,1)S(1)}, u32[]{:S(2)}, u32[]{:S(2)}) collective-permute-start(bf16[8,3200]{1,0:T(8,128)(2,1)S(1)} %get-tuple-element.30), channel_id=1, source_target_pairs={{0,16},{4,20},{8,24},{12,28},{16,0},{20,4},{24,8},{28,12},{1,17},{... | collective-permute-start | bytes 153608 | tf_op jit(solution)/shard_map/ppermute | solution.py:31
  71.4 5.9 %collective-permute-start.23 = (bf16[8,3200]{1,0:T(8,128)(2,1)S(1)}, bf16[8,3200]{1,0:T(8,128)(2,1)S(1)}, u32[]{:S(2)}, u32[]{:S(2)}) collective-permute-start(bf16[8,3200]{1,0:T(8,128)(2,1)S(1)} %get-tuple-element.31), channel_id=1, source_target_pairs={{0,24},{4,28},{8,16},{12,20},{16,8},{20,12},{24,0},{28,4},{1,25},{... | collective-permute-start | bytes 153608 | tf_op jit(solution)/shard_map/ppermute | solution.py:31

commit v3 on v2

--- a/solution.py
+++ b/solution.py
@@ -8,7 +8,8 @@
 from jax.sharding import PartitionSpec as P
 
 PAD = 128
-VMEM = 48 * 1024 * 1024
+MIB = 1024 * 1024
+VMEM = 24 * MIB
 LARGEST = 256
 BF = jnp.bfloat16
 F32 = jnp.float32
@@ -56,23 +57,52 @@
     return jnp.where(low, total + pltpu.roll(rest, experts, 1), total).astype(BF)
 
 
-def pack_body(x_ref, dy_ref, ids_ref, gates_ref, out_ref):
+def column(row):
+    count = row.shape[1]
+    here = lax.broadcasted_iota(jnp.int32, (count, count), 0)
+    there = lax.broadcasted_iota(jnp.int32, (count, count), 1)
+    return jnp.sum(jnp.where(here == there, row, 0.0), axis=1, keepdims=True)
+
+
+def as_row(col):
+    count = col.shape[0]
+    here = lax.broadcasted_iota(jnp.int32, (count, count), 0)
+    there = lax.broadcasted_iota(jnp.int32, (count, count), 1)
+    return jnp.sum(jnp.where(here == there, col, 0.0), axis=0, keepdims=True)
+
+
+def pack_body(x_hbm, dy_hbm, ids_hbm, gates_hbm, out_ref, x_ref, dy_ref, ids_ref, gates_ref, sems):
+    pairs = ((ids_hbm, ids_ref), (gates_hbm, gates_ref), (x_hbm, x_ref), (dy_hbm, dy_ref))
+    copies = [pltpu.make_async_copy(src, dst, sems.at[i]) for i, (src, dst) in enumerate(pairs)]
+    for copy in copies:
+        copy.start()
+    for copy in copies:
+        copy.wait()
     count, features = x_ref.shape
-    lane = lanes(count)
+    lane = lanes(count).astype(F32)
     gates = gates_ref[...].astype(F32)
-    ids = ids_ref[...]
+    ids = ids_ref[...].astype(F32)
     dense = jnp.zeros((count, PAD), F32)
-    for k in range(ids.shape[1]):
-        dense = jnp.where(lane == ids[:, k : k + 1], gates[:, k : k + 1], dense)
+    for k in range(ids.shape[0]):
+        dense = jnp.where(lane == column(ids[k : k + 1]), column(gates[k : k + 1]), dense)
     out_ref[:, :features] = jnp.concatenate(
         [x_ref[...].astype(F32), dy_ref[...].astype(F32)], axis=0
     ).astype(BF)
     out_ref[:, features:] = jnp.concatenate([dense, dense], axis=0).astype(BF)
 
 
-def expert_body(experts, count, *refs):
-    pieces, (wg_ref, wu_ref, wd_ref), rest = refs[:-12], refs[-12:-9], refs[-9:]
-    x_ref, scaled_ref, hidden_ref, dg_ref, du_ref, send_ref, keep_ref, dy_ref, weight_ref = rest
+def expert_body(experts, count, load, pieces_count, *refs):
+    pieces, given, rest = refs[:pieces_count], refs[pieces_count : pieces_count + 3], refs[pieces_count + 3 :]
+    x_ref, scaled_ref, hidden_ref, dg_ref, du_ref, send_ref, keep_ref = rest[:7]
+    copies = []
+    if load:
+        wg_ref, wu_ref, wd_ref, dy_ref, weight_ref, sems = rest[7:]
+        for i, (src, dst) in enumerate(zip(given, (wg_ref, wu_ref, wd_ref))):
+            copies.append(pltpu.make_async_copy(src, dst, sems.at[i]))
+            copies[i].start()
+    else:
+        wg_ref, wu_ref, wd_ref = given
+        dy_ref, weight_ref = rest[7:]
     features = x_ref.shape[1]
     own = lax.axis_index("expert")
     lane = lanes(count)
@@ -93,8 +123,14 @@
         dy_ref[rows, :] = dy.astype(BF)
         scaled_ref[rows, :] = (weight * dy).astype(BF)
 
+    if load:
+        copies[0].wait()
     pre_gate = jnp.dot(x_ref[...], wg_ref[0], preferred_element_type=F32)
+    if load:
+        copies[1].wait()
     pre_up = jnp.dot(x_ref[...], wu_ref[0], preferred_element_type=F32)
+    if load:
+        copies[2].wait()
     back = contract_last(dy_ref[...], wd_ref[0])
     sig = jax.nn.sigmoid(pre_gate)
     active = pre_gate * sig
@@ -117,7 +153,7 @@
     keep_ref[:, features:] = spread[:half]
 
 
-def sum_body(experts, added, *refs):
+def sum_body(experts, added, stays, *refs):
     keep_ref, parts, outs = refs[0], refs[1 : 1 + added], refs[1 + added :]
     rows, width = outs[0].shape
     for i, out in enumerate(outs):
@@ -125,21 +161,42 @@
         total = keep_ref[at, :]
         for part in parts:
             total = total + part[at, :].astype(F32)
-        if i == 0:
+        if i == 0 and stays:
             out[...] = total
         else:
             out[:, : width - PAD] = total[:, : width - PAD].astype(BF)
             out[:, width - PAD :] = wire_pad(total[:, width - PAD :], experts)
 
 
-def sum_parts(keep, parts, pieces, experts, name):
+def sum_parts(keep, parts, pieces, stays, experts, name):
     rows = keep.shape[0] // pieces
     dims = (rows, keep.shape[1])
-    outs = [shape(dims, F32)] + [shape(dims, BF)] * (pieces - 1)
+    outs = [shape(dims, F32 if stays and i == 0 else BF) for i in range(pieces)]
     moved = 2 * keep.size * (2 + len(parts))
     return call(
-        functools.partial(sum_body, experts, len(parts)), outs, name, keep.size * len(parts), moved
+        functools.partial(sum_body, experts, len(parts), stays),
+        outs,
+        name,
+        keep.size * len(parts),
+        moved,
     )(keep, *parts)
+
+
+def join_body(experts, count, where, keep_a, keep_b, send_a, send_b, *refs):
+    outs, total_ref = refs[:-1], refs[-1]
+    rows = keep_a.shape[0]
+    total_ref[:rows, :] = keep_a[...] + send_a[...].astype(F32)
+    total_ref[rows:, :] = keep_b[...] + send_b[...].astype(F32)
+    features = total_ref.shape[1] - PAD
+    for d, places in enumerate(where):
+        total = jnp.concatenate(
+            [total_ref[i * count : (i + 1) * count, :] for i in places], axis=0
+        )
+        if d == 0:
+            outs[d][...] = total
+        else:
+            outs[d][:, :features] = total[:, :features].astype(BF)
+            outs[d][:, features:] = wire_pad(total[:, features:], experts)
 
 
 def final_body(experts, added, *refs):
@@ -149,13 +206,15 @@
     for part in parts:
         total = total + part[...].astype(F32)
     tokens_ref[...] = total[:, :features].astype(BF)
-    ids = ids_ref[...]
     product = total[:, features:]
-    lane = lanes(count)
-    for k in range(ids.shape[1]):
-        id_k = ids[:, k : k + 1]
+    lane = lanes(count).astype(F32)
+    ids = ids_ref[...].astype(F32)
+    for k in range(ids.shape[0]):
+        id_k = column(ids[k : k + 1])
         picked = (lane == id_k) | (lane == id_k + experts)
-        gates_ref[:, k : k + 1] = jnp.sum(jnp.where(picked, product, 0.0), axis=1, keepdims=True)
+        gates_ref[k : k + 1, :] = as_row(
+            jnp.sum(jnp.where(picked, product, 0.0), axis=1, keepdims=True)
+        )
 
 
 def expert_plain(pieces, slabs, experts, count):
@@ -195,11 +254,52 @@
     return jnp.concatenate([total[:, :-PAD], pad], axis=1).astype(BF)
 
 
-def sum_plain(keep, parts, pieces, experts):
+def sum_plain(keep, parts, pieces, stays, experts):
     for part in parts:
         keep = keep + part.astype(F32)
     split = jnp.split(keep, pieces, axis=0)
-    return split[:1] + [to_wire(piece, experts) for piece in split[1:]]
+    return [
+        piece if stays and i == 0 else to_wire(piece, experts) for i, piece in enumerate(split)
+    ]
+
+
+def expert_step(pieces, weights, experts, count, limit, load):
+    w_gate, w_up, w_down = weights
+    rows = sum(piece.shape[0] for piece in pieces) // 2
+    features, hidden_units = w_gate.shape[1:]
+    width = features + PAD
+    if rows > limit:
+        return *expert_plain(pieces, (w_gate[0], w_up[0], w_down[0]), experts, count), *weights
+    outs = [
+        shape((rows, features), BF),
+        shape((rows, features), BF),
+        shape((rows, hidden_units), BF),
+        shape((rows, hidden_units), BF),
+        shape((rows, hidden_units), BF),
+        shape((rows // 2, width), BF),
+        shape((rows // 2, width), F32),
+    ]
+    scratch = [pltpu.VMEM((rows, features), BF), pltpu.VMEM((rows, PAD), F32)]
+    weight_space = pltpu.VMEM
+    if load:
+        outs += [shape(w.shape, BF) for w in weights]
+        scratch.append(pltpu.SemaphoreType.DMA((3,)))
+        weight_space = pltpu.HBM
+    specs = [pl.BlockSpec(memory_space=pltpu.VMEM)] * len(pieces)
+    result = pl.pallas_call(
+        functools.partial(expert_body, experts, count, load, len(pieces)),
+        out_shape=outs,
+        in_specs=specs + [pl.BlockSpec(memory_space=weight_space)] * 3,
+        scratch_shapes=scratch,
+        name="expert",
+        compiler_params=pltpu.CompilerParams(vmem_limit_bytes=(44 if load else 24) * MIB),
+        cost_estimate=pl.CostEstimate(
+            flops=0,
+            bytes_accessed=1024,
+            transcendentals=0,
+        ),
+    )(*pieces, *weights)
+    return result if load else [*result, *weights]
 
 
 def local(tokens, upstream, route_ids, route_gates, w_gate, w_up, w_down):
@@ -207,73 +307,103 @@
     groups = lax.axis_size("section") // 2
     count, features = tokens.shape
     width = features + PAD
-    total_rows = 2 * experts * groups * count
-    hidden_units = w_gate.shape[2]
-
-    block = call(pack_body, shape((2 * count, width), BF), "pack", 0, 4 * count * width * 2)(
-        tokens, upstream, route_ids, route_gates
-    )
-    along = [swap(block, "section", 2 * k) for k in range(1, groups)]
-    near = [block] + [swap(block, "expert", d) for d in range(1, experts)]
-    far_block = jnp.concatenate(along, axis=0)
-    far = [far_block] + [swap(far_block, "expert", d) for d in range(1, experts)]
-    mine = [piece for pair in zip(near, far) for piece in pair]
-    pieces = mine + [swap(piece, "section", 1) for piece in mine]
-
-    fits = total_rows <= LARGEST
+    fits = 2 * experts * groups * count <= LARGEST
+    ids, gates = route_ids.T, route_gates.T
+
+    block = pl.pallas_call(
+        pack_body,
+        out_shape=shape((2 * count, width), BF),
+        in_specs=[pl.BlockSpec(memory_space=pltpu.HBM)] * 4,
+        scratch_shapes=[
+            pltpu.VMEM(tokens.shape, BF),
+            pltpu.VMEM(tokens.shape, BF),
+            pltpu.VMEM(ids.shape, jnp.int32),
+            pltpu.VMEM(ids.shape, BF),
+            pltpu.SemaphoreType.DMA((4,)),
+        ],
+        name="pack",
+        compiler_params=pltpu.CompilerParams(vmem_limit_bytes=60 * MIB),
+    )(tokens, upstream, ids, gates)
+
+    def to_others(value):
+        return [value] + [swap(value, "expert", d) for d in range(1, experts)]
+
+    def added(total, parts, pieces, stays, name):
+        if fits:
+            return sum_parts(total, parts, pieces, stays, experts, name)
+        return sum_plain(total, parts, pieces, stays, experts)
+
+    along = [swap(block, "section", 2 * k) for k in range(groups - 1, 0, -1)][::-1]
+    others = sorted(range(1, experts), key=lambda d: -d.bit_count())
+    near = {0: block}
+    for d in range(1, experts):
+        near[d] = swap(near[d & (d - 1)], "expert", d & -d)
+    early = [d for d in range(1, experts) if d.bit_count() == 1]
+    late = [d for d in others if d not in early]
+    far_block = jnp.concatenate(along[1:], axis=0)
+    near_block = jnp.concatenate([near[d] for d in others], axis=0)
+    held = [along[0]] + [near[d] for d in early]
+    far_block, near_block, held = lax.optimization_barrier((far_block, near_block, held))
+    far = [swap(far_block, "expert", d) for d in others] + [swap(near_block, "section", 2)]
+
+    limit = LARGEST if fits else 0
+    order = [(0, k) for k in range(groups)] + [(d, 0) for d in early]
+    mine = jnp.concatenate([block, held[0], far_block] + held[1:], axis=0)
+    *first, w_gate, w_up, w_down = expert_step(
+        [mine, swap(mine, "section", 1)], (w_gate, w_up, w_down), experts, count, limit, True
+    )
+    order += [(d, 0) for d in late] + [(d, k) for d in others for k in range(2, groups)]
+    order += [(d, 1) for d in others]
+    mine = [near[d] for d in late] + far
+    mine, first[5] = lax.optimization_barrier((mine, first[5]))
+    second = expert_step(
+        mine + [swap(piece, "section", 1) for piece in mine],
+        (w_gate, w_up, w_down),
+        experts,
+        count,
+        limit,
+        False,
+    )[:7]
+    steps = [first, second]
+    sends = [swap(step[5], "section", 1) for step in steps]
+    keeps = [step[6] for step in steps]
+    where = [[order.index((d, k)) for k in range(groups)] for d in range(experts)]
     if fits:
-        rows_x, scaled, hidden, d_gate, d_up, send, keep = pl.pallas_call(
-            functools.partial(expert_body, experts, count),
-            out_shape=[
-                shape((total_rows, features), BF),
-                shape((total_rows, features), BF),
-                shape((total_rows, hidden_units), BF),
-                shape((total_rows, hidden_units), BF),
-                shape((total_rows, hidden_units), BF),
-                shape((total_rows // 2, width), BF),
-                shape((total_rows // 2, width), F32),
-            ],
-            scratch_shapes=[
-                pltpu.VMEM((total_rows, features), BF),
-                pltpu.VMEM((total_rows, PAD), F32),
-            ],
-            name="expert",
+        dims = (groups * count, width)
+        split = pl.pallas_call(
+            functools.partial(join_body, experts, count, where),
+            out_shape=[shape(dims, BF if d else F32) for d in range(experts)],
+            scratch_shapes=[pltpu.VMEM((experts * groups * count, width), F32)],
+            name="sum_cores",
             compiler_params=pltpu.CompilerParams(vmem_limit_bytes=VMEM),
-            cost_estimate=pl.CostEstimate(
-                flops=10 * total_rows * features * hidden_units,
-                bytes_accessed=16 * 1024 * 1024,
-                transcendentals=total_rows * hidden_units,
-            ),
-        )(*pieces, w_gate, w_up, w_down)
+            cost_estimate=pl.CostEstimate(flops=0, bytes_accessed=1024, transcendentals=0),
+        )(*keeps, *sends)
     else:
-        rows_x, scaled, hidden, d_gate, d_up, send, keep = expert_plain(
-            pieces, (w_gate[0], w_up[0], w_down[0]), experts, count
-        )
-
-    def added(total, parts, pieces, name):
-        if fits:
-            return sum_parts(total, parts, pieces, experts, name)
-        return sum_plain(total, parts, pieces, experts)
-
-    split = added(keep, [swap(send, "section", 1)], experts, "sum_cores")
-    plane = added(
-        split[0], [swap(split[d], "expert", d) for d in range(1, experts)], groups, "sum_experts"
-    )
+        total = jnp.concatenate(keeps, axis=0) + jnp.concatenate(sends, axis=0).astype(F32)
+        blocks = total.reshape(-1, count, width)
+        split = [jnp.concatenate([blocks[i] for i in places], axis=0) for places in where]
+        split = [to_wire(part, experts) if d else part for d, part in enumerate(split)]
+    arrived = [swap(part, "expert", d) if d else part for d, part in enumerate(split)]
+    plane = added(arrived[0], arrived[1:], groups, True, "sum_experts")
+    kept = plane[0]
     parts = [swap(plane[k], "section", 2 * k) for k in range(1, groups)]
     grad_tokens, grad_gates = call(
         functools.partial(final_body, experts, len(parts)),
-        [shape((count, features), BF), shape(route_ids.shape, F32)],
+        [shape((count, features), BF), shape(ids.shape, F32)],
         "final",
         0,
         4 * count * width * 2,
-    )(plane[0], *parts, route_ids)
-
+    )(kept, *parts, ids)
+
+    rows_x, scaled, hidden, d_gate, d_up = [
+        jnp.concatenate(both, axis=0) for both in list(zip(*steps))[:5]
+    ]
     grad_down = contract_first(hidden, scaled)
     grad_gate = contract_first(rows_x, d_gate)
     grad_up = contract_first(rows_x, d_up)
     return (
         grad_tokens,
-        grad_gates,
+        grad_gates.T,
         grad_gate.astype(BF)[None],
         grad_up.astype(BF)[None],
         grad_down.astype(BF)[None],

time: 78.9 us -> 63.5 us (0.80)
  waiting for transfers between devices: 37.4 us -> 23.2 us
  local copies, waits for them, and re-layouts: 3.77 us -> 1.11 us
  Pallas kernels: 7.95 us -> 10.2 us
  starting transfers between devices: 23.6 us -> 22.7 us
    ppermute x24, waiting for transfers between devices: 37.4 us -> 23.2 us  [swap(): return lax.ppermute(value, axis, [(i, i ^ mask) for i in range(size)])]
    unnamed x13 -> x9, local copies, waits for them, and re-layouts: 3.76 us -> 1.03 us
    pallas_call x4 -> x5, Pallas kernels: 7.24 us -> 9.51 us  [the longest x2 7.43 us: expert_step(): pl.pallas_call(functools.partial(expert_body, experts, count, load, len(p...]
    ppermute x24, starting transfers between devices: 23.6 us -> 22.7 us  [swap(): return lax.ppermute(value, axis, [(i, i ^ mask) for i in range(size)])]
  transfers between devices with their start and end apart: 24 -> 24, of which waited for: 12 -> 12; matrix products, arithmetic and copies ran while one was open for 7% -> 10% of each run, Pallas kernels for 0% -> 12%
where the time goes in v3:
time: 63.5 us; the launch traced here: 63.3 us
  waiting for transfers between devices  23.2 us (37%)
  starting transfers between devices  22.7 us (36%)
  Pallas kernels  10.2 us (16%)
  matrix products  5.29 us (8%)
  local copies, waits for them, and re-layouts  1.11 us (2%)
  between operations  0.78 us (1%)
    ppermute x24, waiting for transfers between devices, swap(): return lax.ppermute(value, axis, [(i, i ^ mask) for i in range(size)])  23.2 us
    ppermute x24, starting transfers between devices, swap(): return lax.ppermute(value, axis, [(i, i ^ mask) for i in range(size)])  22.7 us
    pallas_call x2, Pallas kernels, expert_step(): pl.pallas_call(functools.partial(expert_body, experts, count, load, len(p...  7.43 us
    dot_general x3, matrix products, contract_first(): lax.dot_general(left, right, (((0,), (0,)), ((), ())), preferred_element_...  5.29 us
    pallas_call x1, Pallas kernels, local(): pl.pallas_call(pack_body, out_shape=shape((2 * count, width), BF), in_spe...  1.73 us
  transfers between devices with their start and end apart: 24, of which 12 were waited for; matrix products, arithmetic and copies ran while one was open for 10% of the time, Pallas kernels for 12%

profile of v3, /device:TPU:0, one launch (start us, length us, event | category | flops | bytes accessed | tf_op | source)
XLA Modules:
  0.0 63.3 jit_solution(13378690918905677596)
XLA Ops:
  0.6 0.0 copy-start
  0.6 1.7 %pack.1 = bf16[16,3200]{1,0:T(8,128)(2,1)} custom-call(bf16[8,3072]{1,0:T(8,128)(2,1)} %x_hbm.1, bf16[8,3072]{1,0:T(8,128)(2,1)} %dy_hbm.1, s32[2,8]{1,0:T(2,128)} %bitcast.11, bf16[2,8]{1,0:T(2,128)(2,1)} %bitcast.13), custom_call_target="tpu_custom_call" | custom-call | tf_op jit(solution)/shard_map/pack/pallas_call | solution.py:313
  2.4 3.1 %collective-permute-start.5 = (bf16[16,3200]{1,0:T(8,128)(2,1)}, bf16[16,3200]{1,0:T(8,128)(2,1)S(1)}, u32[]{:S(2)}, u32[]{:S(2)}) collective-permute-start(bf16[16,3200]{1,0:T(8,128)(2,1)} %pack.1), channel_id=1, source_target_pairs={{0,8},{4,12},{8,0},{12,4},{16,24},{20,28},{24,16},{28,20},{1,9},{5... | collective-permute-start | bytes 307208 | tf_op jit(solution)/shard_map/ppermute | solution.py:32
  5.5 1.5 %collective-permute-start.4 = (bf16[16,3200]{1,0:T(8,128)(2,1)}, bf16[16,3200]{1,0:T(8,128)(2,1)S(1)}, u32[]{:S(2)}, u32[]{:S(2)}) collective-permute-start(bf16[16,3200]{1,0:T(8,128)(2,1)} %pack.1), channel_id=1, source_target_pairs={{0,1},{1,0},{2,3},{3,2},{4,5},{5,4},{6,7},{7,6},{8,9},{9,8},{10,11... | collective-permute-start | bytes 307208 | tf_op jit(solution)/shard_map/ppermute | solution.py:32
  7.0 1.5 %collective-permute-start.2 = (bf16[16,3200]{1,0:T(8,128)(2,1)}, bf16[16,3200]{1,0:T(8,128)(2,1)S(1)}, u32[]{:S(2)}, u32[]{:S(2)}) collective-permute-start(bf16[16,3200]{1,0:T(8,128)(2,1)} %pack.1), channel_id=1, source_target_pairs={{0,2},{1,3},{2,0},{3,1},{4,6},{5,7},{6,4},{7,5},{8,10},{9,11},{10,... | collective-permute-start | bytes 307208 | tf_op jit(solution)/shard_map/ppermute | solution.py:32
  8.5 2.5 %collective-permute-start.1 = (bf16[16,3200]{1,0:T(8,128)(2,1)}, bf16[16,3200]{1,0:T(8,128)(2,1)S(1)}, u32[]{:S(2)}, u32[]{:S(2)}) collective-permute-start(bf16[16,3200]{1,0:T(8,128)(2,1)} %pack.1), channel_id=1, source_target_pairs={{0,24},{4,28},{8,16},{12,20},{16,8},{20,12},{24,0},{28,4},{1,25},{... | collective-permute-start | bytes 307208 | tf_op jit(solution)/shard_map/ppermute | solution.py:32
  11.0 0.1 collective-permute-start
  11.1 0.9 %constant_dynamic-update-slice_fusion.4 = bf16[96,3200]{1,0:T(8,128)(2,1)S(1)} fusion(bf16[16,3200]{1,0:T(8,128)(2,1)} %pack.1), kind=kLoop, calls=%fused_computation.24 | loop fusion | bytes 204800
  12.0 0.0 collective-permute-done.2
  12.0 0.6 collective-permute-start.3
  12.6 3.1 %collective-permute-done.1 = bf16[16,3200]{1,0:T(8,128)(2,1)S(1)} collective-permute-done((bf16[16,3200]{1,0:T(8,128)(2,1)}, bf16[16,3200]{1,0:T(8,128)(2,1)S(1)}, u32[]{:S(2)}, u32[]{:S(2)}) %collective-permute-start.1) | collective-permute-done | bytes 102432 | tf_op jit(solution)/shard_map/ppermute | solution.py:32
  15.7 4.3 %collective-permute-done = bf16[16,3200]{1,0:T(8,128)(2,1)S(1)} collective-permute-done((bf16[16,3200]{1,0:T(8,128)(2,1)}, bf16[16,3200]{1,0:T(8,128)(2,1)S(1)}, u32[]{:S(2)}, u32[]{:S(2)}) %collective-permute-start) | collective-permute-done | bytes 102432 | tf_op jit(solution)/shard_map/ppermute | solution.py:32
  20.0 0.0 collective-permute-done.4
  20.0 0.0 collective-permute-done.3.refs_0_
  20.0 0.0 collective-permute-done.5
  20.1 0.1 collective-permute-start.6
  20.2 0.1 collective-permute-start.10
  20.3 0.6 collective-permute-start.9
  20.8 0.7 %collective-permute-start.8 = (bf16[32,3200]{1,0:T(8,128)(2,1)S(1)}, bf16[32,3200]{1,0:T(8,128)(2,1)S(1)}, u32[]{:S(2)}, u32[]{:S(2)}) collective-permute-start(bf16[32,3200]{1,0:T(8,128)(2,1)S(1)} %pad_maximum_fusion.1), channel_id=1, source_target_pairs={{0,1},{1,0},{2,3},{3,2},{4,5},{5,4},{6,7},{7,6},{8,9},{9,8},{10,11... | collective-permute-start | bytes 614408 | tf_op jit(solution)/shard_map/ppermute | solution.py:32
  21.5 2.3 %collective-permute-start.7 = (bf16[32,3200]{1,0:T(8,128)(2,1)S(1)}, bf16[32,3200]{1,0:T(8,128)(2,1)S(1)}, u32[]{:S(2)}, u32[]{:S(2)}) collective-permute-start(bf16[32,3200]{1,0:T(8,128)(2,1)S(1)} %pad_maximum_fusion.1), channel_id=1, source_target_pairs={{0,3},{1,2},{2,1},{3,0},{4,7},{5,6},{6,5},{7,4},{8,11},{9,10},{10,... | collective-permute-start | bytes 614408 | tf_op jit(solution)/shard_map/ppermute | solution.py:32
  23.8 0.0 collective-permute-done.6.refs_1_
  23.8 0.0 copy-done
  23.8 4.4 %expert.2 = (bf16[96,3072]{1,0:T(8,128)(2,1)S(1)}, bf16[96,3072]{1,0:T(8,128)(2,1)S(1)}, bf16[96,256]{1,0:T(8,128)(2,1)S(1)}, bf16[96,256]{1,0:T(8,128)(2,1)S(1)...) custom-call(bf16[96,3200]{1,0:T(8,128)(2,1)S(1)} %constant_dynamic-u, ...), custom_call_target="tpu_custom_call" | custom-call | bytes 1024 | tf_op jit(solution)/shard_map/expert/pallas_call | solution.py:289
  28.2 0.0 collective-permute-done.9.refs_3_
  28.2 0.5 collective-permute-done.8.refs_2_
  28.8 4.5 %collective-permute-done.7.refs_1_ = bf16[32,3200]{1,0:T(8,128)(2,1)S(1)} collective-permute-done((bf16[32,3200]{1,0:T(8,128)(2,1)S(1)}, bf16[32,3200]{1,0:T(8,128)(2,1)S(1)}, u32[]{:S(2)}, u32[]{:S(2)}) %collective-permute-start.7) | collective-permute-done | bytes 204832 | tf_op jit(solution)/shard_map/ppermute | solution.py:32
  33.2 0.0 collective-permute-done.10.refs_4_
  33.2 0.0 collective-permute-start.11
  33.2 0.5 collective-permute-start.12
  33.8 0.0 collective-permute-start.13
  33.8 0.5 collective-permute-start.14
  34.3 0.0 collective-permute-start.15
  34.3 0.2 collective-permute-done.11.refs_5_
  34.5 0.3 collective-permute-start.16
  34.9 0.0 collective-permute-done.12.refs_6_
  34.9 0.3 collective-permute-done.13.refs_7_
  35.2 0.3 collective-permute-done.14.refs_8_
  35.5 0.4 collective-permute-done.15.refs_9_
  35.9 3.0 %expert.3 = (bf16[160,3072]{1,0:T(8,128)(2,1)S(1)}, bf16[160,3072]{1,0:T(8,128)(2,1)S(1)}, bf16[160,256]{1,0:T(8,128)(2,1)S(1)}, bf16[160,256]{1,0:T(8,128)(2,1)...) custom-call(bf16[16,3200]{1,0:T(8,128)(2,1)S(1)} %collective-permute-done.3.refs_0_, ...), custom_call_target="tpu_custom_call" | custom-call | bytes 1024 | tf_op jit(solution)/shard_map/expert/pallas_call | solution.py:289
  39.0 0.4 collective-permute-start.17
  39.3 0.1 constant_dynamic-update-slice_fusion.5
  39.4 1.8 %fusion.1 = bf16[1,3072,256]{2,1,0:T(8,128)(2,1)} fusion(bf16[256,3072]{1,0:T(8,128)(2,1)S(1)} %constant_dynamic-update-slice_fusion.5, bf16[160,256]{1,0:T(8,128)(2,1)S(1)} %get-tuple-element.76, bf16[96,256]{1,0:T(8,128)(2,1)S(1)} %get-tuple-element.75), kind=kOutput, calls=%fused_computation.4 | convolution fusion | flops 403701760 | bytes 3276800 | tf_op jit(solution)/shard_map/dot_general | solution.py:25
  41.2 0.0 collective-permute-done.16.send_a
  41.2 0.0 collective-permute-done.17.send_b
  41.2 0.3 sum_cores.1
  41.4 0.6 collective-permute-start.18
  42.0 0.7 %collective-permute-start.19 = (bf16[32,3200]{1,0:T(8,128)(2,1)S(1)}, bf16[32,3200]{1,0:T(8,128)(2,1)S(1)}, u32[]{:S(2)}, u32[]{:S(2)}) collective-permute-start(bf16[32,3200]{1,0:T(8,128)(2,1)S(1)} %get-tuple-element.63), channel_id=1, source_target_pairs={{0,2},{1,3},{2,0},{3,1},{4,6},{5,7},{6,4},{7,5},{8,10},{9,11},{10,... | collective-permute-start | bytes 614408 | tf_op jit(solution)/shard_map/ppermute | solution.py:32
  42.7 2.3 %collective-permute-start.20 = (bf16[32,3200]{1,0:T(8,128)(2,1)S(1)}, bf16[32,3200]{1,0:T(8,128)(2,1)S(1)}, u32[]{:S(2)}, u32[]{:S(2)}) collective-permute-start(bf16[32,3200]{1,0:T(8,128)(2,1)S(1)} %get-tuple-element.64), channel_id=1, source_target_pairs={{0,3},{1,2},{2,1},{3,0},{4,7},{5,6},{6,5},{7,4},{8,11},{9,10},{10,... | collective-permute-start | bytes 614408 | tf_op jit(solution)/shard_map/ppermute | solution.py:32
  45.0 1.8 %fusion = bf16[1,3072,256]{2,1,0:T(8,128)(2,1)} fusion(bf16[256,3072]{1,0:T(8,128)(2,1)S(1)} %constant_dynamic-update-slice_fusion.5, bf16[160,256]{1,0:T(8,128)(2,1)S(1)} %get-tuple-element.74, bf16[96,256]{1,0:T(8,128)(2,1)S(1)} %get-tuple-element.73), kind=kOutput, calls=%fused_computation.3 | convolution fusion | flops 403701760 | bytes 3276800 | tf_op jit(solution)/shard_map/dot_general | solution.py:25
  46.8 2.7 %collective-permute-done.18.refs_1_ = bf16[32,3200]{1,0:T(8,128)(2,1)S(1)} collective-permute-done((bf16[32,3200]{1,0:T(8,128)(2,1)S(1)}, bf16[32,3200]{1,0:T(8,128)(2,1)S(1)}, u32[]{:S(2)}, u32[]{:S(2)}) %collective-permute-start.18) | collective-permute-done | bytes 204832 | tf_op jit(solution)/shard_map/ppermute | solution.py:32
  49.4 3.9 %collective-permute-done.19.refs_2_ = bf16[32,3200]{1,0:T(8,128)(2,1)S(1)} collective-permute-done((bf16[32,3200]{1,0:T(8,128)(2,1)S(1)}, bf16[32,3200]{1,0:T(8,128)(2,1)S(1)}, u32[]{:S(2)}, u32[]{:S(2)}) %collective-permute-start.19) | collective-permute-done | bytes 204832 | tf_op jit(solution)/shard_map/ppermute | solution.py:32
  53.4 0.0 collective-permute-done.20.refs_3_
  53.4 0.1 sum_experts.1
  53.5 1.8 %collective-permute-start.21 = (bf16[8,3200]{1,0:T(8,128)(2,1)S(1)}, bf16[8,3200]{1,0:T(8,128)(2,1)S(1)}, u32[]{:S(2)}, u32[]{:S(2)}) collective-permute-start(bf16[8,3200]{1,0:T(8,128)(2,1)S(1)} %get-tuple-element.66), channel_id=1, source_target_pairs={{0,8},{4,12},{8,0},{12,4},{16,24},{20,28},{24,16},{28,20},{1,9},{5... | collective-permute-start | bytes 153608 | tf_op jit(solution)/shard_map/ppermute | solution.py:32
  55.3 1.4 %collective-permute-start.22 = (bf16[8,3200]{1,0:T(8,128)(2,1)S(1)}, bf16[8,3200]{1,0:T(8,128)(2,1)S(1)}, u32[]{:S(2)}, u32[]{:S(2)}) collective-permute-start(bf16[8,3200]{1,0:T(8,128)(2,1)S(1)} %get-tuple-element.67), channel_id=1, source_target_pairs={{0,16},{4,20},{8,24},{12,28},{16,0},{20,4},{24,8},{28,12},{1,17},{... | collective-permute-start | bytes 153608 | tf_op jit(solution)/shard_map/ppermute | solution.py:32
  56.7 1.2 %collective-permute-start.23 = (bf16[8,3200]{1,0:T(8,128)(2,1)S(1)}, bf16[8,3200]{1,0:T(8,128)(2,1)S(1)}, u32[]{:S(2)}, u32[]{:S(2)}) collective-permute-start(bf16[8,3200]{1,0:T(8,128)(2,1)S(1)} %get-tuple-element.68), channel_id=1, source_target_pairs={{0,24},{4,28},{8,16},{12,20},{16,8},{20,12},{24,0},{28,4},{1,25},{... | collective-permute-start | bytes 153608 | tf_op jit(solution)/shard_map/ppermute | solution.py:32
  57.9 0.0 copy-start.1
  57.9 1.7 %fusion.2 = bf16[1,256,3072]{2,1,0:T(8,128)(2,1)} fusion(bf16[160,3072]{1,0:T(8,128)(2,1)S(1)} %get-tuple-element.80, bf16[96,3072]{1,0:T(8,128)(2,1)S(1)} %get-tuple-element.79, bf16[160,256]{1,0:T(8,128)(2,1)S(1)} %get-tuple-element.78, bf16[96,256]{1,0:T(8,128)(2,1)S(1)} %get-tuple-element.77), kind=kOutput, calls=%fused_computation.5 | convolution fusion | flops 406847488 | bytes 3276800 | tf_op jit(solution)/shard_map/dot_general | solution.py:25
  59.7 0.0 collective-permute-done.21.refs_1_
  59.7 1.7 %collective-permute-done.22.refs_2_ = bf16[8,3200]{1,0:T(8,128)(2,1)S(1)} collective-permute-done((bf16[8,3200]{1,0:T(8,128)(2,1)S(1)}, bf16[8,3200]{1,0:T(8,128)(2,1)S(1)}, u32[]{:S(2)}, u32[]{:S(2)}) %collective-permute-start.22) | collective-permute-done | bytes 51232 | tf_op jit(solution)/shard_map/ppermute | solution.py:32
  61.4 1.2 %collective-permute-done.23.refs_3_ = bf16[8,3200]{1,0:T(8,128)(2,1)S(1)} collective-permute-done((bf16[8,3200]{1,0:T(8,128)(2,1)S(1)}, bf16[8,3200]{1,0:T(8,128)(2,1)S(1)}, u32[]{:S(2)}, u32[]{:S(2)}) %collective-permute-start.23) | collective-permute-done | bytes 51232 | tf_op jit(solution)/shard_map/ppermute | solution.py:32
  62.6 0.0 copy-done.1
  62.6 0.7 %final.1 = (bf16[8,3072]{1,0:T(8,128)(2,1)}, f32[2,8]{1,0:T(2,128)}) custom-call(f32[8,3200]{1,0:T(8,128)S(1)} %get-tuple-element.65.refs_0_, bf16[8,3200]{1,0:T(8,128)(2,1)S(1)} %collective-permute-done.21.refs_1_, bf16[8,3200]{1,0:T(8,128)(2,1)S(1)} %collective-permute-done.22.refs_2_, bf16[8,3200]{1,0:T(8,128)(2,1)S(1)} %collective-permute-done.23.refs_3_, ...), custom_call_target="tpu_custom_call" | custom-call | bytes 204800 | tf_op jit(solution)/shard_map/final/pallas_call | solution.py:390
  (7 shorter events, 0.2 us)
Async XLA Ops:
  0.6 23.2 %copy-start = (bf16[1,3072,256]{2,1,0:T(8,128)(2,1)S(1)}, bf16[1,3072,256]{2,1,0:T(8,128)(2,1)}, u32[]{:S(2)}) copy-start(bf16[1,3072,256]{2,1,0:T(8,128)(2,1)} %refs_2_.1) | copy-start | bytes 4718596
  2.4 17.6 %collective-permute-start.5 = (bf16[16,3200]{1,0:T(8,128)(2,1)}, bf16[16,3200]{1,0:T(8,128)(2,1)S(1)}, u32[]{:S(2)}, u32[]{:S(2)}) collective-permute-start(bf16[16,3200]{1,0:T(8,128)(2,1)} %pack.1), channel_id=1, source_target_pairs={{0,8},{4,12},{8,0},{12,4},{16,24},{20,28},{24,16},{28,20},{1,9},{5... | collective-permute-start | bytes 307208 | tf_op jit(solution)/shard_map/ppermute | solution.py:32
  5.5 14.5 %collective-permute-start.4 = (bf16[16,3200]{1,0:T(8,128)(2,1)}, bf16[16,3200]{1,0:T(8,128)(2,1)S(1)}, u32[]{:S(2)}, u32[]{:S(2)}) collective-permute-start(bf16[16,3200]{1,0:T(8,128)(2,1)} %pack.1), channel_id=1, source_target_pairs={{0,1},{1,0},{2,3},{3,2},{4,5},{5,4},{6,7},{7,6},{8,9},{9,8},{10,11... | collective-permute-start | bytes 307208 | tf_op jit(solution)/shard_map/ppermute | solution.py:32
  7.0 5.1 %collective-permute-start.2 = (bf16[16,3200]{1,0:T(8,128)(2,1)}, bf16[16,3200]{1,0:T(8,128)(2,1)S(1)}, u32[]{:S(2)}, u32[]{:S(2)}) collective-permute-start(bf16[16,3200]{1,0:T(8,128)(2,1)} %pack.1), channel_id=1, source_target_pairs={{0,2},{1,3},{2,0},{3,1},{4,6},{5,7},{6,4},{7,5},{8,10},{9,11},{10,... | collective-permute-start | bytes 307208 | tf_op jit(solution)/shard_map/ppermute | solution.py:32
  8.5 7.2 %collective-permute-start.1 = (bf16[16,3200]{1,0:T(8,128)(2,1)}, bf16[16,3200]{1,0:T(8,128)(2,1)S(1)}, u32[]{:S(2)}, u32[]{:S(2)}) collective-permute-start(bf16[16,3200]{1,0:T(8,128)(2,1)} %pack.1), channel_id=1, source_target_pairs={{0,24},{4,28},{8,16},{12,20},{16,8},{20,12},{24,0},{28,4},{1,25},{... | collective-permute-start | bytes 307208 | tf_op jit(solution)/shard_map/ppermute | solution.py:32
  11.0 9.0 %collective-permute-start = (bf16[16,3200]{1,0:T(8,128)(2,1)}, bf16[16,3200]{1,0:T(8,128)(2,1)S(1)}, u32[]{:S(2)}, u32[]{:S(2)}) collective-permute-start(bf16[16,3200]{1,0:T(8,128)(2,1)} %pack.1), channel_id=1, source_target_pairs={{0,16},{4,20},{8,24},{12,28},{16,0},{20,4},{24,8},{28,12},{1,17},{... | collective-permute-start | bytes 307208 | tf_op jit(solution)/shard_map/ppermute | solution.py:32
  12.0 8.0 %collective-permute-start.3 = (bf16[16,3200]{1,0:T(8,128)(2,1)S(1)}, bf16[16,3200]{1,0:T(8,128)(2,1)S(1)}, u32[]{:S(2)}, u32[]{:S(2)}) collective-permute-start(bf16[16,3200]{1,0:T(8,128)(2,1)S(1)} %collective-permute-done.2), channel_id=1, source_target_pairs={{0,1},{1,0},{2,3},{3,2},{4,5},{5,4},{6,7},{7,6},{8,9},{9,8},{10,11... | collective-permute-start | bytes 307208 | tf_op jit(solution)/shard_map/ppermute | solution.py:32
  20.1 3.7 %collective-permute-start.6 = (bf16[96,3200]{1,0:T(8,128)(2,1)S(1)}, bf16[96,3200]{1,0:T(8,128)(2,1)S(1)}, u32[]{:S(2)}, u32[]{:S(2)}) collective-permute-start(bf16[96,3200]{1,0:T(8,128)(2,1)S(1)} %constant_dynamic-update-slice_fusion.refs_0_), channel_id=1, source_target_pairs={{0,4},{4,0},{8,12},{12,8},{16,20},{20,16},{24,28},{28,24},{1,5},{5... | collective-permute-start | bytes 1843208 | tf_op jit(solution)/shard_map/ppermute | solution.py:32
  20.2 13.1 %collective-permute-start.10 = (bf16[48,3200]{1,0:T(8,128)(2,1)S(1)}, bf16[48,3200]{1,0:T(8,128)(2,1)S(1)}, u32[]{:S(2)}, u32[]{:S(2)}) collective-permute-start(bf16[48,3200]{1,0:T(8,128)(2,1)S(1)} %pad_maximum_fusion), channel_id=1, source_target_pairs={{0,8},{4,12},{8,0},{12,4},{16,24},{20,28},{24,16},{28,20},{1,9},{5... | collective-permute-start | bytes 921608 | tf_op jit(solution)/shard_map/ppermute | solution.py:32
  20.3 8.0 %collective-permute-start.9 = (bf16[32,3200]{1,0:T(8,128)(2,1)S(1)}, bf16[32,3200]{1,0:T(8,128)(2,1)S(1)}, u32[]{:S(2)}, u32[]{:S(2)}) collective-permute-start(bf16[32,3200]{1,0:T(8,128)(2,1)S(1)} %pad_maximum_fusion.1), channel_id=1, source_target_pairs={{0,2},{1,3},{2,0},{3,1},{4,6},{5,7},{6,4},{7,5},{8,10},{9,11},{10,... | collective-permute-start | bytes 614408 | tf_op jit(solution)/shard_map/ppermute | solution.py:32
  20.8 7.9 %collective-permute-start.8 = (bf16[32,3200]{1,0:T(8,128)(2,1)S(1)}, bf16[32,3200]{1,0:T(8,128)(2,1)S(1)}, u32[]{:S(2)}, u32[]{:S(2)}) collective-permute-start(bf16[32,3200]{1,0:T(8,128)(2,1)S(1)} %pad_maximum_fusion.1), channel_id=1, source_target_pairs={{0,1},{1,0},{2,3},{3,2},{4,5},{5,4},{6,7},{7,6},{8,9},{9,8},{10,11... | collective-permute-start | bytes 614408 | tf_op jit(solution)/shard_map/ppermute | solution.py:32
  21.5 11.7 %collective-permute-start.7 = (bf16[32,3200]{1,0:T(8,128)(2,1)S(1)}, bf16[32,3200]{1,0:T(8,128)(2,1)S(1)}, u32[]{:S(2)}, u32[]{:S(2)}) collective-permute-start(bf16[32,3200]{1,0:T(8,128)(2,1)S(1)} %pad_maximum_fusion.1), channel_id=1, source_target_pairs={{0,3},{1,2},{2,1},{3,0},{4,7},{5,6},{6,5},{7,4},{8,11},{9,10},{10,... | collective-permute-start | bytes 614408 | tf_op jit(solution)/shard_map/ppermute | solution.py:32
  33.2 1.3 %collective-permute-start.11 = (bf16[16,3200]{1,0:T(8,128)(2,1)S(1)}, bf16[16,3200]{1,0:T(8,128)(2,1)S(1)}, u32[]{:S(2)}, u32[]{:S(2)}) collective-permute-start(bf16[16,3200]{1,0:T(8,128)(2,1)S(1)} %collective-permute-done.3.refs_0_), channel_id=1, source_target_pairs={{0,4},{4,0},{8,12},{12,8},{16,20},{20,16},{24,28},{28,24},{1,5},{5... | collective-permute-start | bytes 307208 | tf_op jit(solution)/shard_map/ppermute | solution.py:32
  33.2 1.7 %collective-permute-start.12 = (bf16[32,3200]{1,0:T(8,128)(2,1)S(1)}, bf16[32,3200]{1,0:T(8,128)(2,1)S(1)}, u32[]{:S(2)}, u32[]{:S(2)}) collective-permute-start(bf16[32,3200]{1,0:T(8,128)(2,1)S(1)} %collective-permute-done.7.refs_1_), channel_id=1, source_target_pairs={{0,4},{4,0},{8,12},{12,8},{16,20},{20,16},{24,28},{28,24},{1,5},{5... | collective-permute-start | bytes 614408 | tf_op jit(solution)/shard_map/ppermute | solution.py:32
  33.8 1.5 %collective-permute-start.13 = (bf16[32,3200]{1,0:T(8,128)(2,1)S(1)}, bf16[32,3200]{1,0:T(8,128)(2,1)S(1)}, u32[]{:S(2)}, u32[]{:S(2)}) collective-permute-start(bf16[32,3200]{1,0:T(8,128)(2,1)S(1)} %collective-permute-done.8.refs_2_), channel_id=1, source_target_pairs={{0,4},{4,0},{8,12},{12,8},{16,20},{20,16},{24,28},{28,24},{1,5},{5... | collective-permute-start | bytes 614408 | tf_op jit(solution)/shard_map/ppermute | solution.py:32
  33.8 1.7 %collective-permute-start.14 = (bf16[32,3200]{1,0:T(8,128)(2,1)S(1)}, bf16[32,3200]{1,0:T(8,128)(2,1)S(1)}, u32[]{:S(2)}, u32[]{:S(2)}) collective-permute-start(bf16[32,3200]{1,0:T(8,128)(2,1)S(1)} %collective-permute-done.9.refs_3_), channel_id=1, source_target_pairs={{0,4},{4,0},{8,12},{12,8},{16,20},{20,16},{24,28},{28,24},{1,5},{5... | collective-permute-start | bytes 614408 | tf_op jit(solution)/shard_map/ppermute | solution.py:32
  34.3 1.7 %collective-permute-start.15 = (bf16[48,3200]{1,0:T(8,128)(2,1)S(1)}, bf16[48,3200]{1,0:T(8,128)(2,1)S(1)}, u32[]{:S(2)}, u32[]{:S(2)}) collective-permute-start(bf16[48,3200]{1,0:T(8,128)(2,1)S(1)} %collective-permute-done.10.refs_4_), channel_id=1, source_target_pairs={{0,4},{4,0},{8,12},{12,8},{16,20},{20,16},{24,28},{28,24},{1,5},{5... | collective-permute-start | bytes 921608 | tf_op jit(solution)/shard_map/ppermute | solution.py:32
  34.5 6.6 %collective-permute-start.16 = (bf16[48,3200]{1,0:T(8,128)(2,1)S(1)}, bf16[48,3200]{1,0:T(8,128)(2,1)S(1)}, u32[]{:S(2)}, u32[]{:S(2)}) collective-permute-start(bf16[48,3200]{1,0:T(8,128)(2,1)S(1)} %get-tuple-element.59), channel_id=1, source_target_pairs={{0,4},{4,0},{8,12},{12,8},{16,20},{20,16},{24,28},{28,24},{1,5},{5... | collective-permute-start | bytes 921608 | tf_op jit(solution)/shard_map/ppermute | solution.py:32
  39.0 2.2 %collective-permute-start.17 = (bf16[80,3200]{1,0:T(8,128)(2,1)S(1)}, bf16[80,3200]{1,0:T(8,128)(2,1)S(1)}, u32[]{:S(2)}, u32[]{:S(2)}) collective-permute-start(bf16[80,3200]{1,0:T(8,128)(2,1)S(1)} %get-tuple-element.60), channel_id=1, source_target_pairs={{0,4},{4,0},{8,12},{12,8},{16,20},{20,16},{24,28},{28,24},{1,5},{5... | collective-permute-start | bytes 1536008 | tf_op jit(solution)/shard_map/ppermute | solution.py:32
  41.4 8.0 %collective-permute-start.18 = (bf16[32,3200]{1,0:T(8,128)(2,1)S(1)}, bf16[32,3200]{1,0:T(8,128)(2,1)S(1)}, u32[]{:S(2)}, u32[]{:S(2)}) collective-permute-start(bf16[32,3200]{1,0:T(8,128)(2,1)S(1)} %get-tuple-element.62), channel_id=1, source_target_pairs={{0,1},{1,0},{2,3},{3,2},{4,5},{5,4},{6,7},{7,6},{8,9},{9,8},{10,11... | collective-permute-start | bytes 614408 | tf_op jit(solution)/shard_map/ppermute | solution.py:32
  42.0 11.3 %collective-permute-start.19 = (bf16[32,3200]{1,0:T(8,128)(2,1)S(1)}, bf16[32,3200]{1,0:T(8,128)(2,1)S(1)}, u32[]{:S(2)}, u32[]{:S(2)}) collective-permute-start(bf16[32,3200]{1,0:T(8,128)(2,1)S(1)} %get-tuple-element.63), channel_id=1, source_target_pairs={{0,2},{1,3},{2,0},{3,1},{4,6},{5,7},{6,4},{7,5},{8,10},{9,11},{10,... | collective-permute-start | bytes 614408 | tf_op jit(solution)/shard_map/ppermute | solution.py:32
  42.7 10.6 %collective-permute-start.20 = (bf16[32,3200]{1,0:T(8,128)(2,1)S(1)}, bf16[32,3200]{1,0:T(8,128)(2,1)S(1)}, u32[]{:S(2)}, u32[]{:S(2)}) collective-permute-start(bf16[32,3200]{1,0:T(8,128)(2,1)S(1)} %get-tuple-element.64), channel_id=1, source_target_pairs={{0,3},{1,2},{2,1},{3,0},{4,7},{5,6},{6,5},{7,4},{8,11},{9,10},{10,... | collective-permute-start | bytes 614408 | tf_op jit(solution)/shard_map/ppermute | solution.py:32
  53.5 6.2 %collective-permute-start.21 = (bf16[8,3200]{1,0:T(8,128)(2,1)S(1)}, bf16[8,3200]{1,0:T(8,128)(2,1)S(1)}, u32[]{:S(2)}, u32[]{:S(2)}) collective-permute-start(bf16[8,3200]{1,0:T(8,128)(2,1)S(1)} %get-tuple-element.66), channel_id=1, source_target_pairs={{0,8},{4,12},{8,0},{12,4},{16,24},{20,28},{24,16},{28,20},{1,9},{5... | collective-permute-start | bytes 153608 | tf_op jit(solution)/shard_map/ppermute | solution.py:32
  55.3 6.1 %collective-permute-start.22 = (bf16[8,3200]{1,0:T(8,128)(2,1)S(1)}, bf16[8,3200]{1,0:T(8,128)(2,1)S(1)}, u32[]{:S(2)}, u32[]{:S(2)}) collective-permute-start(bf16[8,3200]{1,0:T(8,128)(2,1)S(1)} %get-tuple-element.67), channel_id=1, source_target_pairs={{0,16},{4,20},{8,24},{12,28},{16,0},{20,4},{24,8},{28,12},{1,17},{... | collective-permute-start | bytes 153608 | tf_op jit(solution)/shard_map/ppermute | solution.py:32
  56.7 5.9 %collective-permute-start.23 = (bf16[8,3200]{1,0:T(8,128)(2,1)S(1)}, bf16[8,3200]{1,0:T(8,128)(2,1)S(1)}, u32[]{:S(2)}, u32[]{:S(2)}) collective-permute-start(bf16[8,3200]{1,0:T(8,128)(2,1)S(1)} %get-tuple-element.68), channel_id=1, source_target_pairs={{0,24},{4,28},{8,16},{12,20},{16,8},{20,12},{24,0},{28,4},{1,25},{... | collective-permute-start | bytes 153608 | tf_op jit(solution)/shard_map/ppermute | solution.py:32
  57.9 4.7 %copy-start.1 = (s32[8,2]{0,1:T(2,128)S(1)}, s32[8,2]{0,1:T(2,128)}, u32[]{:S(2)}) copy-start(s32[8,2]{0,1:T(2,128)} %param.9) | copy-start | bytes 196

commit v4 on v3

--- a/solution.py
+++ b/solution.py
@@ -188,15 +188,15 @@
     total_ref[:rows, :] = keep_a[...] + send_a[...].astype(F32)
     total_ref[rows:, :] = keep_b[...] + send_b[...].astype(F32)
     features = total_ref.shape[1] - PAD
-    for d, places in enumerate(where):
+    for i, places in enumerate(where):
         total = jnp.concatenate(
             [total_ref[i * count : (i + 1) * count, :] for i in places], axis=0
         )
-        if d == 0:
-            outs[d][...] = total
+        if i < 2:
+            outs[i][...] = total
         else:
-            outs[d][:, :features] = total[:, :features].astype(BF)
-            outs[d][:, features:] = wire_pad(total[:, features:], experts)
+            outs[i][:, :features] = total[:, :features].astype(BF)
+            outs[i][:, features:] = wire_pad(total[:, features:], experts)
 
 
 def final_body(experts, added, *refs):
@@ -322,8 +322,8 @@
             pltpu.SemaphoreType.DMA((4,)),
         ],
         name="pack",
-        compiler_params=pltpu.CompilerParams(vmem_limit_bytes=60 * MIB),
-    )(tokens, upstream, ids, gates)
+        compiler_params=pltpu.CompilerParams(vmem_limit_bytes=32 * MIB),
+    )(*[pltpu.with_memory_space_constraint(v, pltpu.HBM) for v in (tokens, upstream, ids, gates)])
 
     def to_others(value):
         return [value] + [swap(value, "expert", d) for d in range(1, experts)]
@@ -333,28 +333,25 @@
             return sum_parts(total, parts, pieces, stays, experts, name)
         return sum_plain(total, parts, pieces, stays, experts)
 
-    along = [swap(block, "section", 2 * k) for k in range(groups - 1, 0, -1)][::-1]
     others = sorted(range(1, experts), key=lambda d: -d.bit_count())
-    near = {0: block}
-    for d in range(1, experts):
-        near[d] = swap(near[d & (d - 1)], "expert", d & -d)
-    early = [d for d in range(1, experts) if d.bit_count() == 1]
-    late = [d for d in others if d not in early]
-    far_block = jnp.concatenate(along[1:], axis=0)
-    near_block = jnp.concatenate([near[d] for d in others], axis=0)
-    held = [along[0]] + [near[d] for d in early]
-    far_block, near_block, held = lax.optimization_barrier((far_block, near_block, held))
-    far = [swap(far_block, "expert", d) for d in others] + [swap(near_block, "section", 2)]
+    along = [swap(block, "section", 2 * k) for k in range(groups - 1, 1, -1)][::-1]
+    near = [swap(block, "expert", d) for d in others]
+    far_block = jnp.concatenate(along, axis=0)
+    near_block = jnp.concatenate([block] + near, axis=0)
+    far_block, near_block = lax.optimization_barrier((far_block, near_block))
+    far = [swap(far_block, "expert", d) for d in others[1:]]
+    far += [swap(near_block, "section", 2), swap(far_block, "expert", others[0])]
 
     limit = LARGEST if fits else 0
-    order = [(0, k) for k in range(groups)] + [(d, 0) for d in early]
-    mine = jnp.concatenate([block, held[0], far_block] + held[1:], axis=0)
+    order = [(0, 0)] + [(d, 0) for d in others] + [(0, k) for k in range(2, groups)]
+    mine = jnp.concatenate([near_block, far_block], axis=0)
     *first, w_gate, w_up, w_down = expert_step(
         [mine, swap(mine, "section", 1)], (w_gate, w_up, w_down), experts, count, limit, True
     )
-    order += [(d, 0) for d in late] + [(d, k) for d in others for k in range(2, groups)]
-    order += [(d, 1) for d in others]
-    mine = [near[d] for d in late] + far
+    order += [(d, k) for d in others[1:] for k in range(2, groups)]
+    order += [(0, 1)] + [(d, 1) for d in others]
+    order += [(others[0], k) for k in range(2, groups)]
+    mine = far
     mine, first[5] = lax.optimization_barrier((mine, first[5]))
     second = expert_step(
         mine + [swap(piece, "section", 1) for piece in mine],
@@ -367,12 +364,19 @@
     steps = [first, second]
     sends = [swap(step[5], "section", 1) for step in steps]
     keeps = [step[6] for step in steps]
-    where = [[order.index((d, k)) for k in range(groups)] for d in range(experts)]
+    groups_of = [
+        [(d, 0) for d in range(experts)],
+        [(0, k) for k in range(2, groups)],
+        [(d, 1) for d in range(experts)],
+    ] + [[(d, k) for k in range(2, groups)] for d in others]
+    where = [[order.index(item) for item in items] for items in groups_of]
     if fits:
-        dims = (groups * count, width)
         split = pl.pallas_call(
             functools.partial(join_body, experts, count, where),
-            out_shape=[shape(dims, BF if d else F32) for d in range(experts)],
+            out_shape=[
+                shape((len(items) * count, width), F32 if i < 2 else BF)
+                for i, items in enumerate(where)
+            ],
             scratch_shapes=[pltpu.VMEM((experts * groups * count, width), F32)],
             name="sum_cores",
             compiler_params=pltpu.CompilerParams(vmem_limit_bytes=VMEM),
@@ -382,18 +386,20 @@
         total = jnp.concatenate(keeps, axis=0) + jnp.concatenate(sends, axis=0).astype(F32)
         blocks = total.reshape(-1, count, width)
         split = [jnp.concatenate([blocks[i] for i in places], axis=0) for places in where]
-        split = [to_wire(part, experts) if d else part for d, part in enumerate(split)]
-    arrived = [swap(part, "expert", d) if d else part for d, part in enumerate(split)]
-    plane = added(arrived[0], arrived[1:], groups, True, "sum_experts")
-    kept = plane[0]
-    parts = [swap(plane[k], "section", 2 * k) for k in range(1, groups)]
+        split = split[:2] + [to_wire(part, experts) for part in split[2:]]
+    crossed = [swap(part, "expert", d) for d, part in zip(others, split[3:])]
+    beside = swap(split[2], "section", 2)
+    own, *sideways = added(split[0], [beside], experts, True, "sum_near")
+    onward = added(split[1], crossed, groups - 2, False, "sum_far")
+    parts = [swap(part, "expert", d) for d, part in enumerate(sideways, 1)]
+    parts += [swap(part, "section", 2 * k) for k, part in enumerate(onward, 2)]
     grad_tokens, grad_gates = call(
         functools.partial(final_body, experts, len(parts)),
         [shape((count, features), BF), shape(ids.shape, F32)],
         "final",
         0,
         4 * count * width * 2,
-    )(kept, *parts, ids)
+    )(own, *parts, ids)
 
     rows_x, scaled, hidden, d_gate, d_up = [
         jnp.concatenate(both, axis=0) for both in list(zip(*steps))[:5]

time: 63.5 us -> 57.4 us (0.904)
  waiting for transfers between devices: 23.2 us -> 14.7 us
  starting transfers between devices: 22.7 us -> 26.6 us
  local copies, waits for them, and re-layouts: 1.11 us -> 0.16 us
    ppermute x24 -> x25, waiting for transfers between devices: 23.2 us -> 14.7 us  [swap(): return lax.ppermute(value, axis, [(i, i ^ mask) for i in range(size)])]
    ppermute x24 -> x25, starting transfers between devices: 22.7 us -> 26.6 us  [swap(): return lax.ppermute(value, axis, [(i, i ^ mask) for i in range(size)])]
    unnamed x9 -> x6, local copies, waits for them, and re-layouts: 1.03 us -> 0.08 us
    pallas_call x1, Pallas kernels: 1.73 us -> 1.1 us  [local(): pl.pallas_call(pack_body, out_shape=shape((2 * count, width), BF), in_spe...]
  transfers between devices with their start and end apart: 24 -> 25, of which waited for: 12 -> 11; matrix products, arithmetic and copies ran while one was open for 10% -> 9% of each run, Pallas kernels for 12% -> 13%
where the time goes in v4:
time: 57.4 us; the launch traced here: 57.2 us
  starting transfers between devices  26.6 us (46%)
  waiting for transfers between devices  14.7 us (26%)
  Pallas kernels  9.71 us (17%)
  matrix products  5.28 us (9%)
  between operations  0.76 us (1%)
    ppermute x25, starting transfers between devices, swap(): return lax.ppermute(value, axis, [(i, i ^ mask) for i in range(size)])  26.6 us
    ppermute x25, waiting for transfers between devices, swap(): return lax.ppermute(value, axis, [(i, i ^ mask) for i in range(size)])  14.7 us
    pallas_call x2, Pallas kernels, expert_step(): pl.pallas_call(functools.partial(expert_body, experts, count, load, len(p...  7.46 us
    dot_general x3, matrix products, contract_first(): lax.dot_general(left, right, (((0,), (0,)), ((), ())), preferred_element_...  5.28 us
  transfers between devices with their start and end apart: 25, of which 11 were waited for; matrix products, arithmetic and copies ran while one was open for 9% of the time, Pallas kernels for 13%

profile of v4, /device:TPU:0, one launch (start us, length us, event | category | flops | bytes accessed | tf_op | source)
XLA Modules:
  0.0 57.2 jit_solution(1988447044227689668)
XLA Ops:
  0.6 0.0 copy-start
  0.6 1.1 %pack.1 = bf16[16,3200]{1,0:T(8,128)(2,1)S(1)} custom-call(bf16[8,3072]{1,0:T(8,128)(2,1)} %x_hbm.1, bf16[8,3072]{1,0:T(8,128)(2,1)} %dy_hbm.1, s32[2,8]{1,0:T(2,128)} %bitcast.11, bf16[2,8]{1,0:T(2,128)(2,1)} %bitcast.13), custom_call_target="tpu_custom_call" | custom-call | tf_op jit(solution)/shard_map/pack/pallas_call | solution.py:313
  1.7 5.1 %collective-permute-start.1 = (bf16[16,3200]{1,0:T(8,128)(2,1)S(1)}, bf16[16,3200]{1,0:T(8,128)(2,1)S(1)}, u32[]{:S(2)}, u32[]{:S(2)}) collective-permute-start(bf16[16,3200]{1,0:T(8,128)(2,1)S(1)} %pack.1), channel_id=1, source_target_pairs={{0,24},{4,28},{8,16},{12,20},{16,8},{20,12},{24,0},{28,4},{1,25},{... | collective-permute-start | bytes 307208 | tf_op jit(solution)/shard_map/ppermute | solution.py:32
  6.9 0.0 collective-permute-start
  6.9 1.5 %collective-permute-start.4 = (bf16[16,3200]{1,0:T(8,128)(2,1)S(1)}, bf16[16,3200]{1,0:T(8,128)(2,1)S(1)}, u32[]{:S(2)}, u32[]{:S(2)}) collective-permute-start(bf16[16,3200]{1,0:T(8,128)(2,1)S(1)} %pack.1), channel_id=1, source_target_pairs={{0,2},{1,3},{2,0},{3,1},{4,6},{5,7},{6,4},{7,5},{8,10},{9,11},{10,... | collective-permute-start | bytes 307208 | tf_op jit(solution)/shard_map/ppermute | solution.py:32
  8.4 1.5 %collective-permute-start.3 = (bf16[16,3200]{1,0:T(8,128)(2,1)S(1)}, bf16[16,3200]{1,0:T(8,128)(2,1)S(1)}, u32[]{:S(2)}, u32[]{:S(2)}) collective-permute-start(bf16[16,3200]{1,0:T(8,128)(2,1)S(1)} %pack.1), channel_id=1, source_target_pairs={{0,1},{1,0},{2,3},{3,2},{4,5},{5,4},{6,7},{7,6},{8,9},{9,8},{10,11... | collective-permute-start | bytes 307208 | tf_op jit(solution)/shard_map/ppermute | solution.py:32
  9.9 0.5 collective-permute-start.2
  10.4 0.3 collective-permute-done.1
  10.7 4.8 %collective-permute-done = bf16[16,3200]{1,0:T(8,128)(2,1)S(1)} collective-permute-done((bf16[16,3200]{1,0:T(8,128)(2,1)S(1)}, bf16[16,3200]{1,0:T(8,128)(2,1)S(1)}, u32[]{:S(2)}, u32[]{:S(2)}) %collective-permute-start) | collective-permute-done | bytes 102432 | tf_op jit(solution)/shard_map/ppermute | solution.py:32
  15.5 0.0 collective-permute-done.4
  15.5 0.0 collective-permute-done.3
  15.5 0.0 collective-permute-done.2
  15.6 0.1 collective-permute-start.5
  15.7 0.8 %collective-permute-start.8 = (bf16[64,3200]{1,0:T(8,128)(2,1)S(1)}, bf16[64,3200]{1,0:T(8,128)(2,1)S(1)}, u32[]{:S(2)}, u32[]{:S(2)}) collective-permute-start(bf16[64,3200]{1,0:T(8,128)(2,1)S(1)} %pad_maximum_fusion), channel_id=1, source_target_pairs={{0,8},{4,12},{8,0},{12,4},{16,24},{20,28},{24,16},{28,20},{1,9},{5... | collective-permute-start | bytes 1228808 | tf_op jit(solution)/shard_map/ppermute | solution.py:32
  16.5 1.8 %collective-permute-start.9 = (bf16[32,3200]{1,0:T(8,128)(2,1)S(1)}, bf16[32,3200]{1,0:T(8,128)(2,1)S(1)}, u32[]{:S(2)}, u32[]{:S(2)}) collective-permute-start(bf16[32,3200]{1,0:T(8,128)(2,1)S(1)} %pad_maximum_fusion.1), channel_id=1, source_target_pairs={{0,3},{1,2},{2,1},{3,0},{4,7},{5,6},{6,5},{7,4},{8,11},{9,10},{10,... | collective-permute-start | bytes 614408 | tf_op jit(solution)/shard_map/ppermute | solution.py:32
  18.3 0.5 collective-permute-start.7
  18.8 1.1 %collective-permute-start.6 = (bf16[32,3200]{1,0:T(8,128)(2,1)S(1)}, bf16[32,3200]{1,0:T(8,128)(2,1)S(1)}, u32[]{:S(2)}, u32[]{:S(2)}) collective-permute-start(bf16[32,3200]{1,0:T(8,128)(2,1)S(1)} %pad_maximum_fusion.1), channel_id=1, source_target_pairs={{0,1},{1,0},{2,3},{3,2},{4,5},{5,4},{6,7},{7,6},{8,9},{9,8},{10,11... | collective-permute-start | bytes 614408 | tf_op jit(solution)/shard_map/ppermute | solution.py:32
  20.0 0.0 collective-permute-done.5.refs_1_
  20.0 0.0 copy-done
  20.0 4.4 %expert.2 = (bf16[96,3072]{1,0:T(8,128)(2,1)S(1)}, bf16[96,3072]{1,0:T(8,128)(2,1)S(1)}, bf16[96,256]{1,0:T(8,128)(2,1)S(1)}, bf16[96,256]{1,0:T(8,128)(2,1)S(1)...) custom-call(bf16[96,3200]{1,0:T(8,128)(2,1)S(1)} %constant_dynamic-u, ...), custom_call_target="tpu_custom_call" | custom-call | bytes 1024 | tf_op jit(solution)/shard_map/expert/pallas_call | solution.py:289
  24.4 1.0 %collective-permute-done.9.refs_3_ = bf16[32,3200]{1,0:T(8,128)(2,1)S(1)} collective-permute-done((bf16[32,3200]{1,0:T(8,128)(2,1)S(1)}, bf16[32,3200]{1,0:T(8,128)(2,1)S(1)}, u32[]{:S(2)}, u32[]{:S(2)}) %collective-permute-start.9) | collective-permute-done | bytes 204832 | tf_op jit(solution)/shard_map/ppermute | solution.py:32
  25.3 3.6 %collective-permute-done.7.refs_1_ = bf16[32,3200]{1,0:T(8,128)(2,1)S(1)} collective-permute-done((bf16[32,3200]{1,0:T(8,128)(2,1)S(1)}, bf16[32,3200]{1,0:T(8,128)(2,1)S(1)}, u32[]{:S(2)}, u32[]{:S(2)}) %collective-permute-start.7) | collective-permute-done | bytes 204832 | tf_op jit(solution)/shard_map/ppermute | solution.py:32
  28.9 0.0 collective-permute-done.6.refs_0_
  28.9 0.0 collective-permute-done.8.refs_2_
  28.9 0.0 collective-permute-start.12
  28.9 0.5 collective-permute-start.10
  29.4 0.1 collective-permute-start.11
  29.5 0.4 collective-permute-start.13
  29.9 0.1 collective-permute-start.14
  30.0 0.9 %collective-permute-done.10.refs_4_ = bf16[32,3200]{1,0:T(8,128)(2,1)S(1)} collective-permute-done((bf16[32,3200]{1,0:T(8,128)(2,1)S(1)}, bf16[32,3200]{1,0:T(8,128)(2,1)S(1)}, u32[]{:S(2)}, u32[]{:S(2)}) %collective-permute-start.10) | collective-permute-done | bytes 204832 | tf_op jit(solution)/shard_map/ppermute | solution.py:32
  30.9 0.3 collective-permute-done.11.refs_5_
  31.2 0.3 collective-permute-done.13.refs_7_
  31.5 0.0 collective-permute-done.12.refs_6_
  31.5 3.1 %expert.3 = (bf16[160,3072]{1,0:T(8,128)(2,1)S(1)}, bf16[160,3072]{1,0:T(8,128)(2,1)S(1)}, bf16[160,256]{1,0:T(8,128)(2,1)S(1)}, bf16[160,256]{1,0:T(8,128)(2,1)...) custom-call(bf16[32,3200]{1,0:T(8,128)(2,1)S(1)} %collective-permute-done.6.refs_0_, ...), custom_call_target="tpu_custom_call" | custom-call | bytes 1024 | tf_op jit(solution)/shard_map/expert/pallas_call | solution.py:289
  34.6 0.2 collective-permute-start.15
  34.8 0.1 constant_dynamic-update-slice_fusion.2
  34.9 1.8 %fusion.1 = bf16[1,3072,256]{2,1,0:T(8,128)(2,1)} fusion(bf16[256,3072]{1,0:T(8,128)(2,1)S(1)} %constant_dynamic-update-slice_fusion.2, bf16[160,256]{1,0:T(8,128)(2,1)S(1)} %get-tuple-element.76, bf16[96,256]{1,0:T(8,128)(2,1)S(1)} %get-tuple-element.75), kind=kOutput, calls=%fused_computation.4 | convolution fusion | flops 403701760 | bytes 3276800 | tf_op jit(solution)/shard_map/dot_general | solution.py:25
  36.7 0.0 collective-permute-done.14.send_a
  36.7 0.0 collective-permute-done.15.send_b
  36.7 0.3 sum_cores.1
  36.9 1.8 %collective-permute-start.20 = (bf16[16,3200]{1,0:T(8,128)(2,1)S(1)}, bf16[16,3200]{1,0:T(8,128)(2,1)S(1)}, u32[]{:S(2)}, u32[]{:S(2)}) collective-permute-start(bf16[16,3200]{1,0:T(8,128)(2,1)S(1)} %get-tuple-element.64), channel_id=1, source_target_pairs={{0,3},{1,2},{2,1},{3,0},{4,7},{5,6},{6,5},{7,4},{8,11},{9,10},{10,... | collective-permute-start | bytes 307208 | tf_op jit(solution)/shard_map/ppermute | solution.py:32
  38.7 0.8 %collective-permute-start.21 = (bf16[16,3200]{1,0:T(8,128)(2,1)S(1)}, bf16[16,3200]{1,0:T(8,128)(2,1)S(1)}, u32[]{:S(2)}, u32[]{:S(2)}) collective-permute-start(bf16[16,3200]{1,0:T(8,128)(2,1)S(1)} %get-tuple-element.65), channel_id=1, source_target_pairs={{0,1},{1,0},{2,3},{3,2},{4,5},{5,4},{6,7},{7,6},{8,9},{9,8},{10,11... | collective-permute-start | bytes 307208 | tf_op jit(solution)/shard_map/ppermute | solution.py:32
  39.6 0.9 %collective-permute-start.22 = (bf16[16,3200]{1,0:T(8,128)(2,1)S(1)}, bf16[16,3200]{1,0:T(8,128)(2,1)S(1)}, u32[]{:S(2)}, u32[]{:S(2)}) collective-permute-start(bf16[16,3200]{1,0:T(8,128)(2,1)S(1)} %get-tuple-element.66), channel_id=1, source_target_pairs={{0,2},{1,3},{2,0},{3,1},{4,6},{5,7},{6,4},{7,5},{8,10},{9,11},{10,... | collective-permute-start | bytes 307208 | tf_op jit(solution)/shard_map/ppermute | solution.py:32
  40.5 1.4 %collective-permute-start.16 = (bf16[32,3200]{1,0:T(8,128)(2,1)S(1)}, bf16[32,3200]{1,0:T(8,128)(2,1)S(1)}, u32[]{:S(2)}, u32[]{:S(2)}) collective-permute-start(bf16[32,3200]{1,0:T(8,128)(2,1)S(1)} %get-tuple-element.58), channel_id=1, source_target_pairs={{0,8},{4,12},{8,0},{12,4},{16,24},{20,28},{24,16},{28,20},{1,9},{5... | collective-permute-start | bytes 614408 | tf_op jit(solution)/shard_map/ppermute | solution.py:32
  41.9 1.8 %fusion = bf16[1,3072,256]{2,1,0:T(8,128)(2,1)} fusion(bf16[256,3072]{1,0:T(8,128)(2,1)S(1)} %constant_dynamic-update-slice_fusion.2, bf16[160,256]{1,0:T(8,128)(2,1)S(1)} %get-tuple-element.74, bf16[96,256]{1,0:T(8,128)(2,1)S(1)} %get-tuple-element.73), kind=kOutput, calls=%fused_computation.3 | convolution fusion | flops 403701760 | bytes 3276800 | tf_op jit(solution)/shard_map/dot_general | solution.py:25
  43.7 0.0 collective-permute-done.20.refs_1_
  43.7 1.2 %collective-permute-done.21.refs_2_ = bf16[16,3200]{1,0:T(8,128)(2,1)S(1)} collective-permute-done((bf16[16,3200]{1,0:T(8,128)(2,1)S(1)}, bf16[16,3200]{1,0:T(8,128)(2,1)S(1)}, u32[]{:S(2)}, u32[]{:S(2)}) %collective-permute-start.21) | collective-permute-done | bytes 102432 | tf_op jit(solution)/shard_map/ppermute | solution.py:32
  44.9 0.4 collective-permute-done.22.refs_3_
  45.2 0.1 sum_far.1
  45.3 2.5 %collective-permute-start.23 = (bf16[8,3200]{1,0:T(8,128)(2,1)S(1)}, bf16[8,3200]{1,0:T(8,128)(2,1)S(1)}, u32[]{:S(2)}, u32[]{:S(2)}) collective-permute-start(bf16[8,3200]{1,0:T(8,128)(2,1)S(1)} %get-tuple-element.67), channel_id=1, source_target_pairs={{0,16},{4,20},{8,24},{12,28},{16,0},{20,4},{24,8},{28,12},{1,17},{... | collective-permute-start | bytes 153608 | tf_op jit(solution)/shard_map/ppermute | solution.py:32
  47.8 1.4 %collective-permute-start.24 = (bf16[8,3200]{1,0:T(8,128)(2,1)S(1)}, bf16[8,3200]{1,0:T(8,128)(2,1)S(1)}, u32[]{:S(2)}, u32[]{:S(2)}) collective-permute-start(bf16[8,3200]{1,0:T(8,128)(2,1)S(1)} %get-tuple-element.68), channel_id=1, source_target_pairs={{0,24},{4,28},{8,16},{12,20},{16,8},{20,12},{24,0},{28,4},{1,25},{... | collective-permute-start | bytes 153608 | tf_op jit(solution)/shard_map/ppermute | solution.py:32
  49.2 0.0 collective-permute-done.16.refs_1_
  49.2 0.1 sum_near.1
  49.2 1.5 %collective-permute-start.17 = (bf16[8,3200]{1,0:T(8,128)(2,1)S(1)}, bf16[8,3200]{1,0:T(8,128)(2,1)S(1)}, u32[]{:S(2)}, u32[]{:S(2)}) collective-permute-start(bf16[8,3200]{1,0:T(8,128)(2,1)S(1)} %get-tuple-element.60), channel_id=1, source_target_pairs={{0,1},{1,0},{2,3},{3,2},{4,5},{5,4},{6,7},{7,6},{8,9},{9,8},{10,11... | collective-permute-start | bytes 153608 | tf_op jit(solution)/shard_map/ppermute | solution.py:32
  50.8 0.7 %collective-permute-start.18 = (bf16[8,3200]{1,0:T(8,128)(2,1)S(1)}, bf16[8,3200]{1,0:T(8,128)(2,1)S(1)}, u32[]{:S(2)}, u32[]{:S(2)}) collective-permute-start(bf16[8,3200]{1,0:T(8,128)(2,1)S(1)} %get-tuple-element.61), channel_id=1, source_target_pairs={{0,2},{1,3},{2,0},{3,1},{4,6},{5,7},{6,4},{7,5},{8,10},{9,11},{10,... | collective-permute-start | bytes 153608 | tf_op jit(solution)/shard_map/ppermute | solution.py:32
  51.5 1.3 %collective-permute-start.19 = (bf16[8,3200]{1,0:T(8,128)(2,1)S(1)}, bf16[8,3200]{1,0:T(8,128)(2,1)S(1)}, u32[]{:S(2)}, u32[]{:S(2)}) collective-permute-start(bf16[8,3200]{1,0:T(8,128)(2,1)S(1)} %get-tuple-element.62), channel_id=1, source_target_pairs={{0,3},{1,2},{2,1},{3,0},{4,7},{5,6},{6,5},{7,4},{8,11},{9,10},{10,... | collective-permute-start | bytes 153608 | tf_op jit(solution)/shard_map/ppermute | solution.py:32
  52.8 1.7 %fusion.2 = bf16[1,256,3072]{2,1,0:T(8,128)(2,1)} fusion(bf16[160,3072]{1,0:T(8,128)(2,1)S(1)} %get-tuple-element.80, bf16[96,3072]{1,0:T(8,128)(2,1)S(1)} %get-tuple-element.79, bf16[160,256]{1,0:T(8,128)(2,1)S(1)} %get-tuple-element.78, bf16[96,256]{1,0:T(8,128)(2,1)S(1)} %get-tuple-element.77), kind=kOutput, calls=%fused_computation.5 | convolution fusion | flops 406847488 | bytes 3276800 | tf_op jit(solution)/shard_map/dot_general | solution.py:25
  54.5 0.0 collective-permute-done.23.refs_4_
  54.5 0.0 collective-permute-done.24.refs_5_
  54.5 0.0 collective-permute-done.17.refs_1_
  54.5 0.6 %collective-permute-done.18.refs_2_ = bf16[8,3200]{1,0:T(8,128)(2,1)S(1)} collective-permute-done((bf16[8,3200]{1,0:T(8,128)(2,1)S(1)}, bf16[8,3200]{1,0:T(8,128)(2,1)S(1)}, u32[]{:S(2)}, u32[]{:S(2)}) %collective-permute-start.18) | collective-permute-done | bytes 51232 | tf_op jit(solution)/shard_map/ppermute | solution.py:32
  55.1 1.4 %collective-permute-done.19.refs_3_ = bf16[8,3200]{1,0:T(8,128)(2,1)S(1)} collective-permute-done((bf16[8,3200]{1,0:T(8,128)(2,1)S(1)}, bf16[8,3200]{1,0:T(8,128)(2,1)S(1)}, u32[]{:S(2)}, u32[]{:S(2)}) %collective-permute-start.19) | collective-permute-done | bytes 51232 | tf_op jit(solution)/shard_map/ppermute | solution.py:32
  56.5 0.0 copy-done.1
  56.5 0.7 %final.1 = (bf16[8,3072]{1,0:T(8,128)(2,1)}, f32[2,8]{1,0:T(2,128)}) custom-call(f32[8,3200]{1,0:T(8,128)S(1)} %get-tuple-element.59.refs_0_, bf16[8,3200]{1,0:T(8,128)(2,1)S(1)} %collective-permute-done.17.refs_1_, bf16[8,3200]{1,0:T(8,128)(2,1)S(1)} %collective-permute-done.18.refs_2_, bf16[8,3200]{1,0:T(8,128)(2,1)S(1)} %collective-permute-done.19.refs_3_, ...), custom_call_target="tpu_custom_call" | custom-call | bytes 204800 | tf_op jit(solution)/shard_map/final/pallas_call | solution.py:396
  (6 shorter events, 0.1 us)
Async XLA Ops:
  0.6 19.3 %copy-start = (bf16[1,3072,256]{2,1,0:T(8,128)(2,1)S(1)}, bf16[1,3072,256]{2,1,0:T(8,128)(2,1)}, u32[]{:S(2)}) copy-start(bf16[1,3072,256]{2,1,0:T(8,128)(2,1)} %refs_2_.1) | copy-start | bytes 4718596
  1.7 8.9 %collective-permute-start.1 = (bf16[16,3200]{1,0:T(8,128)(2,1)S(1)}, bf16[16,3200]{1,0:T(8,128)(2,1)S(1)}, u32[]{:S(2)}, u32[]{:S(2)}) collective-permute-start(bf16[16,3200]{1,0:T(8,128)(2,1)S(1)} %pack.1), channel_id=1, source_target_pairs={{0,24},{4,28},{8,16},{12,20},{16,8},{20,12},{24,0},{28,4},{1,25},{... | collective-permute-start | bytes 307208 | tf_op jit(solution)/shard_map/ppermute | solution.py:32
  6.9 8.6 %collective-permute-start = (bf16[16,3200]{1,0:T(8,128)(2,1)S(1)}, bf16[16,3200]{1,0:T(8,128)(2,1)S(1)}, u32[]{:S(2)}, u32[]{:S(2)}) collective-permute-start(bf16[16,3200]{1,0:T(8,128)(2,1)S(1)} %pack.1), channel_id=1, source_target_pairs={{0,16},{4,20},{8,24},{12,28},{16,0},{20,4},{24,8},{28,12},{1,17},{... | collective-permute-start | bytes 307208 | tf_op jit(solution)/shard_map/ppermute | solution.py:32
  6.9 8.6 %collective-permute-start.4 = (bf16[16,3200]{1,0:T(8,128)(2,1)S(1)}, bf16[16,3200]{1,0:T(8,128)(2,1)S(1)}, u32[]{:S(2)}, u32[]{:S(2)}) collective-permute-start(bf16[16,3200]{1,0:T(8,128)(2,1)S(1)} %pack.1), channel_id=1, source_target_pairs={{0,2},{1,3},{2,0},{3,1},{4,6},{5,7},{6,4},{7,5},{8,10},{9,11},{10,... | collective-permute-start | bytes 307208 | tf_op jit(solution)/shard_map/ppermute | solution.py:32
  8.4 7.1 %collective-permute-start.3 = (bf16[16,3200]{1,0:T(8,128)(2,1)S(1)}, bf16[16,3200]{1,0:T(8,128)(2,1)S(1)}, u32[]{:S(2)}, u32[]{:S(2)}) collective-permute-start(bf16[16,3200]{1,0:T(8,128)(2,1)S(1)} %pack.1), channel_id=1, source_target_pairs={{0,1},{1,0},{2,3},{3,2},{4,5},{5,4},{6,7},{7,6},{8,9},{9,8},{10,11... | collective-permute-start | bytes 307208 | tf_op jit(solution)/shard_map/ppermute | solution.py:32
  9.9 5.6 %collective-permute-start.2 = (bf16[16,3200]{1,0:T(8,128)(2,1)S(1)}, bf16[16,3200]{1,0:T(8,128)(2,1)S(1)}, u32[]{:S(2)}, u32[]{:S(2)}) collective-permute-start(bf16[16,3200]{1,0:T(8,128)(2,1)S(1)} %pack.1), channel_id=1, source_target_pairs={{0,3},{1,2},{2,1},{3,0},{4,7},{5,6},{6,5},{7,4},{8,11},{9,10},{10,... | collective-permute-start | bytes 307208 | tf_op jit(solution)/shard_map/ppermute | solution.py:32
  15.6 4.3 %collective-permute-start.5 = (bf16[96,3200]{1,0:T(8,128)(2,1)S(1)}, bf16[96,3200]{1,0:T(8,128)(2,1)S(1)}, u32[]{:S(2)}, u32[]{:S(2)}) collective-permute-start(bf16[96,3200]{1,0:T(8,128)(2,1)S(1)} %constant_dynamic-update-slice_fusion.refs_0_), channel_id=1, source_target_pairs={{0,4},{4,0},{8,12},{12,8},{16,20},{20,16},{24,28},{28,24},{1,5},{5... | collective-permute-start | bytes 1843208 | tf_op jit(solution)/shard_map/ppermute | solution.py:32
  15.7 13.2 %collective-permute-start.8 = (bf16[64,3200]{1,0:T(8,128)(2,1)S(1)}, bf16[64,3200]{1,0:T(8,128)(2,1)S(1)}, u32[]{:S(2)}, u32[]{:S(2)}) collective-permute-start(bf16[64,3200]{1,0:T(8,128)(2,1)S(1)} %pad_maximum_fusion), channel_id=1, source_target_pairs={{0,8},{4,12},{8,0},{12,4},{16,24},{20,28},{24,16},{28,20},{1,9},{5... | collective-permute-start | bytes 1228808 | tf_op jit(solution)/shard_map/ppermute | solution.py:32
  16.5 8.9 %collective-permute-start.9 = (bf16[32,3200]{1,0:T(8,128)(2,1)S(1)}, bf16[32,3200]{1,0:T(8,128)(2,1)S(1)}, u32[]{:S(2)}, u32[]{:S(2)}) collective-permute-start(bf16[32,3200]{1,0:T(8,128)(2,1)S(1)} %pad_maximum_fusion.1), channel_id=1, source_target_pairs={{0,3},{1,2},{2,1},{3,0},{4,7},{5,6},{6,5},{7,4},{8,11},{9,10},{10,... | collective-permute-start | bytes 614408 | tf_op jit(solution)/shard_map/ppermute | solution.py:32
  18.3 10.6 %collective-permute-start.7 = (bf16[32,3200]{1,0:T(8,128)(2,1)S(1)}, bf16[32,3200]{1,0:T(8,128)(2,1)S(1)}, u32[]{:S(2)}, u32[]{:S(2)}) collective-permute-start(bf16[32,3200]{1,0:T(8,128)(2,1)S(1)} %pad_maximum_fusion.1), channel_id=1, source_target_pairs={{0,2},{1,3},{2,0},{3,1},{4,6},{5,7},{6,4},{7,5},{8,10},{9,11},{10,... | collective-permute-start | bytes 614408 | tf_op jit(solution)/shard_map/ppermute | solution.py:32
  18.8 10.1 %collective-permute-start.6 = (bf16[32,3200]{1,0:T(8,128)(2,1)S(1)}, bf16[32,3200]{1,0:T(8,128)(2,1)S(1)}, u32[]{:S(2)}, u32[]{:S(2)}) collective-permute-start(bf16[32,3200]{1,0:T(8,128)(2,1)S(1)} %pad_maximum_fusion.1), channel_id=1, source_target_pairs={{0,1},{1,0},{2,3},{3,2},{4,5},{5,4},{6,7},{7,6},{8,9},{9,8},{10,11... | collective-permute-start | bytes 614408 | tf_op jit(solution)/shard_map/ppermute | solution.py:32
  28.9 2.6 %collective-permute-start.12 = (bf16[64,3200]{1,0:T(8,128)(2,1)S(1)}, bf16[64,3200]{1,0:T(8,128)(2,1)S(1)}, u32[]{:S(2)}, u32[]{:S(2)}) collective-permute-start(bf16[64,3200]{1,0:T(8,128)(2,1)S(1)} %collective-permute-done.8.refs_2_), channel_id=1, source_target_pairs={{0,4},{4,0},{8,12},{12,8},{16,20},{20,16},{24,28},{28,24},{1,5},{5... | collective-permute-start | bytes 1228808 | tf_op jit(solution)/shard_map/ppermute | solution.py:32
  28.9 2.0 %collective-permute-start.10 = (bf16[32,3200]{1,0:T(8,128)(2,1)S(1)}, bf16[32,3200]{1,0:T(8,128)(2,1)S(1)}, u32[]{:S(2)}, u32[]{:S(2)}) collective-permute-start(bf16[32,3200]{1,0:T(8,128)(2,1)S(1)} %collective-permute-done.6.refs_0_), channel_id=1, source_target_pairs={{0,4},{4,0},{8,12},{12,8},{16,20},{20,16},{24,28},{28,24},{1,5},{5... | collective-permute-start | bytes 614408 | tf_op jit(solution)/shard_map/ppermute | solution.py:32
  29.4 1.8 %collective-permute-start.11 = (bf16[32,3200]{1,0:T(8,128)(2,1)S(1)}, bf16[32,3200]{1,0:T(8,128)(2,1)S(1)}, u32[]{:S(2)}, u32[]{:S(2)}) collective-permute-start(bf16[32,3200]{1,0:T(8,128)(2,1)S(1)} %collective-permute-done.7.refs_1_), channel_id=1, source_target_pairs={{0,4},{4,0},{8,12},{12,8},{16,20},{20,16},{24,28},{28,24},{1,5},{5... | collective-permute-start | bytes 614408 | tf_op jit(solution)/shard_map/ppermute | solution.py:32
  29.5 2.0 %collective-permute-start.13 = (bf16[32,3200]{1,0:T(8,128)(2,1)S(1)}, bf16[32,3200]{1,0:T(8,128)(2,1)S(1)}, u32[]{:S(2)}, u32[]{:S(2)}) collective-permute-start(bf16[32,3200]{1,0:T(8,128)(2,1)S(1)} %collective-permute-done.9.refs_3_), channel_id=1, source_target_pairs={{0,4},{4,0},{8,12},{12,8},{16,20},{20,16},{24,28},{28,24},{1,5},{5... | collective-permute-start | bytes 614408 | tf_op jit(solution)/shard_map/ppermute | solution.py:32
  29.9 6.7 %collective-permute-start.14 = (bf16[48,3200]{1,0:T(8,128)(2,1)S(1)}, bf16[48,3200]{1,0:T(8,128)(2,1)S(1)}, u32[]{:S(2)}, u32[]{:S(2)}) collective-permute-start(bf16[48,3200]{1,0:T(8,128)(2,1)S(1)} %get-tuple-element.55), channel_id=1, source_target_pairs={{0,4},{4,0},{8,12},{12,8},{16,20},{20,16},{24,28},{28,24},{1,5},{5... | collective-permute-start | bytes 921608 | tf_op jit(solution)/shard_map/ppermute | solution.py:32
  34.6 2.1 %collective-permute-start.15 = (bf16[80,3200]{1,0:T(8,128)(2,1)S(1)}, bf16[80,3200]{1,0:T(8,128)(2,1)S(1)}, u32[]{:S(2)}, u32[]{:S(2)}) collective-permute-start(bf16[80,3200]{1,0:T(8,128)(2,1)S(1)} %get-tuple-element.56), channel_id=1, source_target_pairs={{0,4},{4,0},{8,12},{12,8},{16,20},{20,16},{24,28},{28,24},{1,5},{5... | collective-permute-start | bytes 1536008 | tf_op jit(solution)/shard_map/ppermute | solution.py:32
  36.9 6.8 %collective-permute-start.20 = (bf16[16,3200]{1,0:T(8,128)(2,1)S(1)}, bf16[16,3200]{1,0:T(8,128)(2,1)S(1)}, u32[]{:S(2)}, u32[]{:S(2)}) collective-permute-start(bf16[16,3200]{1,0:T(8,128)(2,1)S(1)} %get-tuple-element.64), channel_id=1, source_target_pairs={{0,3},{1,2},{2,1},{3,0},{4,7},{5,6},{6,5},{7,4},{8,11},{9,10},{10,... | collective-permute-start | bytes 307208 | tf_op jit(solution)/shard_map/ppermute | solution.py:32
  38.7 6.1 %collective-permute-start.21 = (bf16[16,3200]{1,0:T(8,128)(2,1)S(1)}, bf16[16,3200]{1,0:T(8,128)(2,1)S(1)}, u32[]{:S(2)}, u32[]{:S(2)}) collective-permute-start(bf16[16,3200]{1,0:T(8,128)(2,1)S(1)} %get-tuple-element.65), channel_id=1, source_target_pairs={{0,1},{1,0},{2,3},{3,2},{4,5},{5,4},{6,7},{7,6},{8,9},{9,8},{10,11... | collective-permute-start | bytes 307208 | tf_op jit(solution)/shard_map/ppermute | solution.py:32
  39.6 5.7 %collective-permute-start.22 = (bf16[16,3200]{1,0:T(8,128)(2,1)S(1)}, bf16[16,3200]{1,0:T(8,128)(2,1)S(1)}, u32[]{:S(2)}, u32[]{:S(2)}) collective-permute-start(bf16[16,3200]{1,0:T(8,128)(2,1)S(1)} %get-tuple-element.66), channel_id=1, source_target_pairs={{0,2},{1,3},{2,0},{3,1},{4,6},{5,7},{6,4},{7,5},{8,10},{9,11},{10,... | collective-permute-start | bytes 307208 | tf_op jit(solution)/shard_map/ppermute | solution.py:32
  40.5 8.7 %collective-permute-start.16 = (bf16[32,3200]{1,0:T(8,128)(2,1)S(1)}, bf16[32,3200]{1,0:T(8,128)(2,1)S(1)}, u32[]{:S(2)}, u32[]{:S(2)}) collective-permute-start(bf16[32,3200]{1,0:T(8,128)(2,1)S(1)} %get-tuple-element.58), channel_id=1, source_target_pairs={{0,8},{4,12},{8,0},{12,4},{16,24},{20,28},{24,16},{28,20},{1,9},{5... | collective-permute-start | bytes 614408 | tf_op jit(solution)/shard_map/ppermute | solution.py:32
  45.3 9.2 %collective-permute-start.23 = (bf16[8,3200]{1,0:T(8,128)(2,1)S(1)}, bf16[8,3200]{1,0:T(8,128)(2,1)S(1)}, u32[]{:S(2)}, u32[]{:S(2)}) collective-permute-start(bf16[8,3200]{1,0:T(8,128)(2,1)S(1)} %get-tuple-element.67), channel_id=1, source_target_pairs={{0,16},{4,20},{8,24},{12,28},{16,0},{20,4},{24,8},{28,12},{1,17},{... | collective-permute-start | bytes 153608 | tf_op jit(solution)/shard_map/ppermute | solution.py:32
  47.8 6.7 %collective-permute-start.24 = (bf16[8,3200]{1,0:T(8,128)(2,1)S(1)}, bf16[8,3200]{1,0:T(8,128)(2,1)S(1)}, u32[]{:S(2)}, u32[]{:S(2)}) collective-permute-start(bf16[8,3200]{1,0:T(8,128)(2,1)S(1)} %get-tuple-element.68), channel_id=1, source_target_pairs={{0,24},{4,28},{8,16},{12,20},{16,8},{20,12},{24,0},{28,4},{1,25},{... | collective-permute-start | bytes 153608 | tf_op jit(solution)/shard_map/ppermute | solution.py:32
  49.2 5.3 %collective-permute-start.17 = (bf16[8,3200]{1,0:T(8,128)(2,1)S(1)}, bf16[8,3200]{1,0:T(8,128)(2,1)S(1)}, u32[]{:S(2)}, u32[]{:S(2)}) collective-permute-start(bf16[8,3200]{1,0:T(8,128)(2,1)S(1)} %get-tuple-element.60), channel_id=1, source_target_pairs={{0,1},{1,0},{2,3},{3,2},{4,5},{5,4},{6,7},{7,6},{8,9},{9,8},{10,11... | collective-permute-start | bytes 153608 | tf_op jit(solution)/shard_map/ppermute | solution.py:32
  50.8 4.4 %collective-permute-start.18 = (bf16[8,3200]{1,0:T(8,128)(2,1)S(1)}, bf16[8,3200]{1,0:T(8,128)(2,1)S(1)}, u32[]{:S(2)}, u32[]{:S(2)}) collective-permute-start(bf16[8,3200]{1,0:T(8,128)(2,1)S(1)} %get-tuple-element.61), channel_id=1, source_target_pairs={{0,2},{1,3},{2,0},{3,1},{4,6},{5,7},{6,4},{7,5},{8,10},{9,11},{10,... | collective-permute-start | bytes 153608 | tf_op jit(solution)/shard_map/ppermute | solution.py:32
  51.5 5.0 %collective-permute-start.19 = (bf16[8,3200]{1,0:T(8,128)(2,1)S(1)}, bf16[8,3200]{1,0:T(8,128)(2,1)S(1)}, u32[]{:S(2)}, u32[]{:S(2)}) collective-permute-start(bf16[8,3200]{1,0:T(8,128)(2,1)S(1)} %get-tuple-element.62), channel_id=1, source_target_pairs={{0,3},{1,2},{2,1},{3,0},{4,7},{5,6},{6,5},{7,4},{8,11},{9,10},{10,... | collective-permute-start | bytes 153608 | tf_op jit(solution)/shard_map/ppermute | solution.py:32
  52.8 3.7 %copy-start.1 = (s32[8,2]{0,1:T(2,128)S(1)}, s32[8,2]{0,1:T(2,128)}, u32[]{:S(2)}) copy-start(s32[8,2]{0,1:T(2,128)} %param.9) | copy-start | bytes 196

commit v5 on v4

v5 whole, which is shorter than its diff:
```python
import functools

import jax
import jax.numpy as jnp
from jax import lax
from jax.experimental import pallas as pl
from jax.experimental.pallas import tpu as pltpu
from jax.sharding import PartitionSpec as P

PAD = 128
MIB = 1024 * 1024
VMEM = 28 * MIB
LARGEST = 256
PARTS = 4
BF = jnp.bfloat16
F32 = jnp.float32


def contract_last(left, right):
    return lax.dot_general(
        left, right, (((1,), (1,)), ((), ())), preferred_element_type=jnp.float32
    )


def contract_first(left, right):
    return lax.dot_general(
        left, right, (((0,), (0,)), ((), ())), preferred_element_type=jnp.float32
    )


def swap(value, axis, mask):
    size = lax.axis_size(axis)
    return lax.ppermute(value, axis, [(i, i ^ mask) for i in range(size)])


def call(body, outs, name, flops=0, moved=0):
    return pl.pallas_call(
        body,
        out_shape=outs,
        name=name,
        compiler_params=pltpu.CompilerParams(vmem_limit_bytes=VMEM),
        cost_estimate=pl.CostEstimate(flops=flops, bytes_accessed=moved, transcendentals=0),
    )


def shape(dims, dtype):
    return jax.ShapeDtypeStruct(dims, dtype)


def lanes(rows):
    return lax.broadcasted_iota(jnp.int32, (rows, PAD), 1)


def wire_pad(total, experts):
    lane = lanes(total.shape[0])
    rest = total - total.astype(BF).astype(F32)
    low = (lane >= experts) & (lane < 2 * experts)
    return jnp.where(low, total + pltpu.roll(rest, experts, 1), total).astype(BF)


def column(row):
    count = row.shape[1]
    here = lax.broadcasted_iota(jnp.int32, (count, count), 0)
    there = lax.broadcasted_iota(jnp.int32, (count, count), 1)
    return jnp.sum(jnp.where(here == there, row, 0.0), axis=1, keepdims=True)


def as_row(col):
    count = col.shape[0]
    here = lax.broadcasted_iota(jnp.int32, (count, count), 0)
    there = lax.broadcasted_iota(jnp.int32, (count, count), 1)
    return jnp.sum(jnp.where(here == there, col, 0.0), axis=0, keepdims=True)


def pack_body(x_hbm, dy_hbm, ids_hbm, gates_hbm, out_ref, x_ref, dy_ref, ids_ref, gates_ref, sems):
    pairs = ((ids_hbm, ids_ref), (gates_hbm, gates_ref), (x_hbm, x_ref), (dy_hbm, dy_ref))
    copies = [pltpu.make_async_copy(src, dst, sems.at[i]) for i, (src, dst) in enumerate(pairs)]
    for copy in copies:
        copy.start()
    for copy in copies:
        copy.wait()
    count, features = x_ref.shape
    lane = lanes(count).astype(F32)
    gates = gates_ref[...].astype(F32)
    ids = ids_ref[...].astype(F32)
    dense = jnp.zeros((count, PAD), F32)
    for k in range(ids.shape[0]):
        dense = jnp.where(lane == column(ids[k : k + 1]), column(gates[k : k + 1]), dense)
    out_ref[:, :features] = jnp.concatenate(
        [x_ref[...].astype(F32), dy_ref[...].astype(F32)], axis=0
    ).astype(BF)
    out_ref[:, features:] = jnp.concatenate([dense, dense], axis=0).astype(BF)


def weights_body(gate_hbm, up_hbm, down_hbm, out_ref, stage_ref, sems):
    units = stage_ref.shape[0]
    places = (stage_ref, out_ref.at[:, :units], out_ref.at[:, units : 2 * units])
    copies = []
    for i, (src, dst) in enumerate(zip((down_hbm, gate_hbm, up_hbm), places)):
        copies.append(pltpu.make_async_copy(src.at[0], dst, sems.at[i]))
        copies[i].start()
    for copy in copies:
        copy.wait()
    out_ref[:, 2 * units :] = stage_ref[...].T


def back_body(own_ref, other_ref, out_ref):
    both = own_ref.shape[1] // 3 * 2
    out_ref[:both, :] = own_ref[:, :both].T
    out_ref[both:, :] = other_ref[:, :both].T


def expert_body(experts, count, pieces_count, *refs):
    pieces, (own_ref, other_ref, back_ref) = refs[:pieces_count], refs[pieces_count : pieces_count + 3]
    *sums, pass_ref, acts_ref, x_ref, dy_ref, weight_ref = refs[pieces_count + 3 :]
    features = x_ref.shape[1]
    units = own_ref.shape[1] // 3
    own = lax.axis_index("expert")

    blocks = [(piece, at) for piece in pieces for at in range(0, piece.shape[0], 2 * count)]
    lane = lanes(2 * count)
    for i in range(0, len(blocks), 2):
        halves = [ref[at : at + 2 * count, :].astype(F32) for ref, at in blocks[i : i + 2]]
        rows = pl.ds(i * count, 2 * count)
        x = jnp.concatenate([h[:count, :features] for h in halves], axis=0).astype(BF)
        dy = jnp.concatenate([h[count:, :features] for h in halves], axis=0)
        dense = jnp.concatenate([h[:count, features:] for h in halves], axis=0)
        weight = jnp.sum(jnp.where(lane == own, dense, 0.0), axis=1, keepdims=True)
        weight_ref[rows, :] = jnp.broadcast_to(weight, (2 * count, PAD))
        x_ref[rows, :] = x
        dy_ref[rows, :] = dy.astype(BF)
        pass_ref[rows, :features] = x
        pass_ref[rows, features : 2 * features] = (weight * dy).astype(BF)

    grads = []
    product = 0.0
    for ref in (own_ref, other_ref):
        both = jnp.dot(x_ref[...], ref[:, : 2 * units], preferred_element_type=F32)
        pre_gate, pre_up = both[:, :units], both[:, units:]
        back = jnp.dot(dy_ref[...], ref[:, 2 * units :], preferred_element_type=F32)
        sig = jax.nn.sigmoid(pre_gate)
        active = pre_gate * sig
        hidden = (active * pre_up).astype(BF)
        d_hidden = weight_ref[:, :1] * back
        d_gate = (d_hidden * pre_up * (sig * (1.0 + pre_gate * (1.0 - sig)))).astype(BF)
        d_up = (d_hidden * active).astype(BF)
        product = product + jnp.sum(hidden.astype(F32) * back, axis=1, keepdims=True)
        grads += [d_gate, d_up]
        if ref is own_ref:
            acts_ref[...] = jnp.concatenate([hidden, d_gate, d_up], axis=1)
        else:
            pass_ref[:, 2 * features :] = jnp.concatenate([hidden, d_gate, d_up], axis=1)
    part = jnp.dot(jnp.concatenate(grads, axis=1), back_ref[...], preferred_element_type=F32)
    spread = jnp.where(lanes(part.shape[0]) == own, product, 0.0)
    at = 0
    for out in sums:
        rows = slice(at, at + out.shape[0])
        at += out.shape[0]
        out[:, :features] = part[rows].astype(out.dtype)
        if out.dtype == F32:
            out[:, features:] = spread[rows]
        else:
            out[:, features:] = wire_pad(spread[rows], experts)


def grads_body(parts, pass_ref, got_ref, acts_ref, *refs):
    gate_hbm, up_hbm, down_hbm, x_ref, scaled_ref, all_ref, gate_ref, up_ref, down_ref, sems = refs
    half, features = pass_ref.shape[0], x_ref.shape[1]
    units = acts_ref.shape[1] // 3
    for i, ref in enumerate((pass_ref, got_ref)):
        rows = pl.ds(i * half, half)
        x_ref[rows, :] = ref[:, :features]
        scaled_ref[rows, :] = ref[:, features : 2 * features]
    all_ref[:half, :] = acts_ref[...]
    all_ref[half:, :] = got_ref[:, 2 * features :]
    step = features // parts
    copies = []
    for i in range(parts):
        at = pl.ds(i * step, step)
        both = contract_first(x_ref[:, at], all_ref[:, units:])
        gate_ref[at, :] = both[:, :units].astype(BF)
        up_ref[at, :] = both[:, units:].astype(BF)
        down_ref[:, at] = contract_first(all_ref[:, :units], scaled_ref[:, at]).astype(BF)
        for j, (src, dst) in enumerate(
            (
                (gate_ref.at[at, :], gate_hbm.at[0, at, :]),
                (up_ref.at[at, :], up_hbm.at[0, at, :]),
                (down_ref.at[:, at], down_hbm.at[0, :, at]),
            )
        ):
            copies.append(pltpu.make_async_copy(src, dst, sems.at[i, j]))
            copies[-1].start()
    for copy in copies:
        copy.wait()


def sum_body(experts, added, stays, *refs):
    keep_ref, parts, outs = refs[0], refs[1 : 1 + added], refs[1 + added :]
    rows, width = outs[0].shape
    for i, out in enumerate(outs):
        at = pl.ds(i * rows, rows)
        total = keep_ref[at, :]
        for part in parts:
            total = total + part[at, :].astype(F32)
        if i == 0 and stays:
            out[...] = total
        else:
            out[:, : width - PAD] = total[:, : width - PAD].astype(BF)
            out[:, width - PAD :] = wire_pad(total[:, width - PAD :], experts)


def sum_parts(keep, parts, pieces, stays, experts, name):
    rows = keep.shape[0] // pieces
    dims = (rows, keep.shape[1])
    outs = [shape(dims, F32 if stays and i == 0 else BF) for i in range(pieces)]
    moved = 2 * keep.size * (2 + len(parts))
    return call(
        functools.partial(sum_body, experts, len(parts), stays),
        outs,
        name,
        keep.size * len(parts),
        moved,
    )(keep, *parts)


def final_body(experts, added, *refs):
    keep_ref, parts, (ids_ref, tokens_ref, gates_ref) = refs[0], refs[1 : 1 + added], refs[1 + added :]
    count, features = tokens_ref.shape
    total = keep_ref[...]
    for part in parts:
        total = total + part[...].astype(F32)
    tokens_ref[...] = total[:, :features].astype(BF)
    product = total[:, features:]
    lane = lanes(count).astype(F32)
    ids = ids_ref[...].astype(F32)
    for k in range(ids.shape[0]):
        id_k = column(ids[k : k + 1])
        picked = (lane == id_k) | (lane == id_k + experts)
        gates_ref[k : k + 1, :] = as_row(
            jnp.sum(jnp.where(picked, product, 0.0), axis=1, keepdims=True)
        )


def to_wire(total, experts):
    pad = total[:, -PAD:]
    rest = jnp.roll(pad - lax.reduce_precision(pad, 8, 7), experts, 1)
    lane = jnp.arange(PAD)[None, :]
    pad = jnp.where((lane >= experts) & (lane < 2 * experts), pad + rest, pad)
    return jnp.concatenate([total[:, :-PAD], pad], axis=1).astype(BF)


def sum_plain(keep, parts, pieces, stays, experts):
    for part in parts:
        keep = keep + part.astype(F32)
    split = jnp.split(keep, pieces, axis=0)
    return [
        piece if stays and i == 0 else to_wire(piece, experts) for i, piece in enumerate(split)
    ]


def expert_plain(pieces, own_slabs, other_slabs, experts, count, sizes):
    features = own_slabs.shape[0]
    units = own_slabs.shape[1] // 3
    rows = jnp.concatenate(pieces, axis=0).reshape(-1, 2, count, features + PAD)
    rows_x = rows[:, 0].reshape(-1, features + PAD)
    rows_dy = rows[:, 1, :, :features].reshape(-1, features)
    is_own = jnp.arange(PAD, dtype=jnp.int32)[None, :] == lax.axis_index("expert")
    weight = jnp.sum(
        jnp.where(is_own, rows_x[:, features:].astype(F32), 0.0), axis=1, keepdims=True
    )
    rows_x = rows_x[:, :features]
    scaled = (weight * rows_dy.astype(F32)).astype(BF)
    part = product = 0.0
    acts = []
    for slabs in (own_slabs, other_slabs):
        both = jnp.dot(rows_x, slabs[:, : 2 * units], preferred_element_type=F32)
        pre_gate, pre_up = both[:, :units], both[:, units:]
        back = jnp.dot(rows_dy, slabs[:, 2 * units :], preferred_element_type=F32)
        sig = jax.nn.sigmoid(pre_gate)
        active = pre_gate * sig
        hidden = (active * pre_up).astype(BF)
        d_hidden = weight * back
        d_gate = (d_hidden * pre_up * (sig * (1.0 + pre_gate * (1.0 - sig)))).astype(BF)
        d_up = (d_hidden * active).astype(BF)
        product = product + jnp.sum(hidden.astype(F32) * back, axis=1, keepdims=True)
        part = part + contract_last(jnp.concatenate([d_gate, d_up], axis=1), slabs[:, : 2 * units])
        acts.append(jnp.concatenate([hidden, d_gate, d_up], axis=1))
    wide = jnp.concatenate([part, jnp.where(is_own, product, 0.0)], axis=1)
    sums = []
    at = 0
    for rows, dtype in sizes:
        piece = wide[at : at + rows]
        at += rows
        sums.append(piece if dtype == F32 else to_wire(piece, experts))
    return *sums, jnp.concatenate([rows_x, scaled, acts[1]], axis=1), acts[0]


def local(tokens, upstream, route_ids, route_gates, w_gate, w_up, w_down):
    experts = lax.axis_size("expert")
    groups = lax.axis_size("section") // 2
    count, features = tokens.shape
    units = w_gate.shape[2]
    width = features + PAD
    rows = experts * groups * count
    fits = 2 * rows <= LARGEST
    ids, gates = route_ids.T, route_gates.T

    def in_hbm(*values):
        return [pltpu.with_memory_space_constraint(v, pltpu.HBM) for v in values]

    block = pl.pallas_call(
        pack_body,
        out_shape=shape((2 * count, width), BF),
        in_specs=[pl.BlockSpec(memory_space=pltpu.HBM)] * 4,
        scratch_shapes=[
            pltpu.VMEM(tokens.shape, BF),
            pltpu.VMEM(tokens.shape, BF),
            pltpu.VMEM(ids.shape, jnp.int32),
            pltpu.VMEM(ids.shape, BF),
            pltpu.SemaphoreType.DMA((4,)),
        ],
        name="pack",
        compiler_params=pltpu.CompilerParams(vmem_limit_bytes=VMEM),
    )(*in_hbm(tokens, upstream, ids, gates))

    def added(total, parts, pieces, stays, name):
        if fits:
            return sum_parts(total, parts, pieces, stays, experts, name)
        return sum_plain(total, parts, pieces, stays, experts)

    others = sorted(range(1, experts), key=lambda d: -d.bit_count())
    along = [swap(block, "section", 2 * k) for k in range(groups - 1, 1, -1)][::-1]
    near = [swap(block, "expert", d) for d in others]
    far_block = jnp.concatenate(along, axis=0)
    near_block = jnp.concatenate([block] + near, axis=0)

    if fits:
        slabs = pl.pallas_call(
            weights_body,
            out_shape=shape((features, 3 * units), BF),
            in_specs=[pl.BlockSpec(memory_space=pltpu.HBM)] * 3,
            scratch_shapes=[pltpu.VMEM((units, features), BF), pltpu.SemaphoreType.DMA((3,))],
            name="weights",
            compiler_params=pltpu.CompilerParams(vmem_limit_bytes=VMEM),
            cost_estimate=pl.CostEstimate(flops=0, bytes_accessed=1024, transcendentals=0),
        )(*in_hbm(w_gate, w_up, w_down))
    else:
        slabs = jnp.concatenate([w_gate[0], w_up[0], w_down[0].T], axis=1)
    far_block, near_block, slabs = lax.optimization_barrier((far_block, near_block, slabs))
    other_slabs = swap(slabs, "section", 1)

    far = [swap(far_block, "expert", d) for d in others[1:]]
    far += [swap(near_block, "section", 2), swap(far_block, "expert", others[0])]
    *direct, beside, diagonal = far
    pieces = [near_block, far_block, beside, diagonal, *direct]
    sizes = [(experts * count, F32), ((groups - 2) * count, F32), (experts * count, BF)]
    sizes += [((groups - 2) * count, BF)] * len(others)
    if fits:
        back_slabs = call(back_body, shape((4 * units, features), BF), "back")(slabs, other_slabs)
        *split, passed, acts = pl.pallas_call(
            functools.partial(expert_body, experts, count, len(pieces)),
            out_shape=[shape((size, width), dtype) for size, dtype in sizes]
            + [shape((rows, 2 * features + 3 * units), BF), shape((rows, 3 * units), BF)],
            scratch_shapes=[
                pltpu.VMEM((rows, features), BF),
                pltpu.VMEM((rows, features), BF),
                pltpu.VMEM((rows, PAD), F32),
            ],
            name="expert",
            compiler_params=pltpu.CompilerParams(vmem_limit_bytes=VMEM),
            cost_estimate=pl.CostEstimate(flops=0, bytes_accessed=1024, transcendentals=0),
        )(*pieces, slabs, other_slabs, back_slabs)
    else:
        *split, passed, acts = expert_plain(pieces, slabs, other_slabs, experts, count, sizes)

    got = swap(passed, "section", 1)
    if fits:
        grad_gate, grad_up, grad_down = pl.pallas_call(
            functools.partial(grads_body, PARTS),
            out_shape=[shape(w.shape, BF) for w in (w_gate, w_up, w_down)],
            out_specs=[pl.BlockSpec(memory_space=pltpu.HBM)] * 3,
            scratch_shapes=[
                pltpu.VMEM((2 * rows, features), BF),
                pltpu.VMEM((2 * rows, features), BF),
                pltpu.VMEM((2 * rows, 3 * units), BF),
                pltpu.VMEM((features, units), BF),
                pltpu.VMEM((features, units), BF),
                pltpu.VMEM((units, features), BF),
                pltpu.SemaphoreType.DMA((PARTS, 3)),
            ],
            name="grads",
            compiler_params=pltpu.CompilerParams(vmem_limit_bytes=VMEM),
            cost_estimate=pl.CostEstimate(flops=0, bytes_accessed=1024, transcendentals=0),
        )(passed, got, acts)
    else:
        every = jnp.concatenate([passed, got], axis=0)
        acts = jnp.concatenate([acts, got[:, 2 * features :]], axis=0)
        hidden, d_gate, d_up = jnp.split(acts, 3, axis=1)
        rows_x, scaled = every[:, :features], every[:, features : 2 * features]
        grad_gate = contract_first(rows_x, d_gate).astype(BF)[None]
        grad_up = contract_first(rows_x, d_up).astype(BF)[None]
        grad_down = contract_first(hidden, scaled).astype(BF)[None]

    crossed = [swap(part, "expert", d) for d, part in zip(others, split[3:])]
    beside = swap(split[2], "section", 2)
    crossed, beside, grad_gate = lax.optimization_barrier((crossed, beside, grad_gate))
    own, *sideways = added(split[0], [beside], experts, True, "sum_near")
    onward = added(split[1], crossed, groups - 2, False, "sum_far")
    parts = [swap(part, "expert", d) for d, part in zip(others, sideways)]
    parts += [swap(part, "section", 2 * k) for k, part in enumerate(onward, 2)]
    grad_tokens, grad_gates = call(
        functools.partial(final_body, experts, len(parts)),
        [shape((count, features), BF), shape(ids.shape, F32)],
        "final",
        0,
        4 * count * width * 2,
    )(own, *parts, ids)

    return (
        grad_tokens,
        grad_gates.T,
        grad_gate,
        grad_up,
        grad_down,
    )


def solution(mesh):
    placed = (
        P(("section", "expert"), None),
        P(("section", "expert"), None),
        P(("section", "expert"), None),
        P(("section", "expert"), None),
        P("expert", None, "section"),
        P("expert", None, "section"),
        P("expert", "section", None),
    )
    return jax.shard_map(
        local,
        mesh=mesh,
        in_specs=placed,
        out_specs=(
            P(("section", "expert"), None),
            P(("section", "expert"), None),
            P("expert", None, "section"),
            P("expert", None, "section"),
            P("expert", "section", None),
        ),
        check_vma=False,
    )
```

time: 57.4 us -> 51.9 us (0.904)
  matrix products: 5.28 us -> 0 us
  starting transfers between devices: 26.6 us -> 24.4 us
  Pallas kernels: 9.71 us -> 11.6 us
    dot_general x3 -> x0, matrix products: 5.28 us -> none  [contract_first(): lax.dot_general(left, right, (((0,), (0,)), ((), ())), preferred_element_...]
    ppermute x25 -> x20, starting transfers between devices: 26.6 us -> 24.4 us  [swap(): return lax.ppermute(value, axis, [(i, i ^ mask) for i in range(size)])]
    pallas_call x3 -> x4, Pallas kernels: 7.72 us -> 9.77 us  [the longest x1 2.84 us: local(): pl.pallas_call(weights_body, out_shape=shape((features, 3 * units), BF),...]
    ppermute x25 -> x20, waiting for transfers between devices: 14.7 us -> 14.8 us  [swap(): return lax.ppermute(value, axis, [(i, i ^ mask) for i in range(size)])]
  transfers between devices with their start and end apart: 25 -> 20, of which waited for: 11 -> 8; matrix products, arithmetic and copies ran while one was open for 9% -> 0% of each run, Pallas kernels for 13% -> 14%
where the time goes in v5:
time: 51.9 us; the launch traced here: 51.7 us
  starting transfers between devices  24.4 us (47%)
  waiting for transfers between devices  14.8 us (29%)
  Pallas kernels  11.6 us (22%)
  between operations  0.76 us (1%)
    ppermute x20, starting transfers between devices, swap(): return lax.ppermute(value, axis, [(i, i ^ mask) for i in range(size)])  24.4 us
    ppermute x20, waiting for transfers between devices, swap(): return lax.ppermute(value, axis, [(i, i ^ mask) for i in range(size)])  14.8 us
    pallas_call x1, Pallas kernels, local(): pl.pallas_call(weights_body, out_shape=shape((features, 3 * units), BF),...  2.84 us
    pallas_call x1, Pallas kernels, local(): pl.pallas_call(functools.partial(grads_body, PARTS), out_shape=[shape(w.s...  2.68 us
    pallas_call x1, Pallas kernels, local(): pl.pallas_call(functools.partial(expert_body, experts, count, len(pieces)...  2.45 us
    pallas_call x1, Pallas kernels, local(): call(back_body, shape((4 * units, features), BF), 'back')  1.8 us
  transfers between devices with their start and end apart: 20, of which 8 were waited for; matrix products, arithmetic and copies ran while one was open for 0% of the time, Pallas kernels for 14%

profile of v5, /device:TPU:0, one launch (start us, length us, event | category | flops | bytes accessed | tf_op | source)
XLA Modules:
  0.0 51.7 jit_solution(8919033853870744830)
XLA Ops:
  0.6 1.0 %pack.1 = bf16[16,3200]{1,0:T(8,128)(2,1)S(1)} custom-call(bf16[8,3072]{1,0:T(8,128)(2,1)} %x_hbm.1, bf16[8,3072]{1,0:T(8,128)(2,1)} %dy_hbm.1, s32[2,8]{1,0:T(2,128)} %bitcast.3, bf16[2,8]{1,0:T(2,128)(2,1)} %bitcast.5), custom_call_target="tpu_custom_call" | custom-call | tf_op jit(solution)/shard_map/pack/pallas_call | solution.py:311
  1.6 5.1 %collective-permute-start.1 = (bf16[16,3200]{1,0:T(8,128)(2,1)S(1)}, bf16[16,3200]{1,0:T(8,128)(2,1)S(1)}, u32[]{:S(2)}, u32[]{:S(2)}) collective-permute-start(bf16[16,3200]{1,0:T(8,128)(2,1)S(1)} %pack.1), channel_id=1, source_target_pairs={{0,24},{4,28},{8,16},{12,20},{16,8},{20,12},{24,0},{28,4},{1,25},{... | collective-permute-start | bytes 307208 | tf_op jit(solution)/shard_map/ppermute | solution.py:33
  6.7 0.0 collective-permute-start
  6.7 1.5 %collective-permute-start.4 = (bf16[16,3200]{1,0:T(8,128)(2,1)S(1)}, bf16[16,3200]{1,0:T(8,128)(2,1)S(1)}, u32[]{:S(2)}, u32[]{:S(2)}) collective-permute-start(bf16[16,3200]{1,0:T(8,128)(2,1)S(1)} %pack.1), channel_id=1, source_target_pairs={{0,2},{1,3},{2,0},{3,1},{4,6},{5,7},{6,4},{7,5},{8,10},{9,11},{10,... | collective-permute-start | bytes 307208 | tf_op jit(solution)/shard_map/ppermute | solution.py:33
  8.3 1.5 %collective-permute-start.3 = (bf16[16,3200]{1,0:T(8,128)(2,1)S(1)}, bf16[16,3200]{1,0:T(8,128)(2,1)S(1)}, u32[]{:S(2)}, u32[]{:S(2)}) collective-permute-start(bf16[16,3200]{1,0:T(8,128)(2,1)S(1)} %pack.1), channel_id=1, source_target_pairs={{0,1},{1,0},{2,3},{3,2},{4,5},{5,4},{6,7},{7,6},{8,9},{9,8},{10,11... | collective-permute-start | bytes 307208 | tf_op jit(solution)/shard_map/ppermute | solution.py:33
  9.7 0.5 collective-permute-start.2
  10.2 2.8 %weights.1.own_ref.refs_6_ = bf16[3072,768]{1,0:T(8,128)(2,1)S(1)} custom-call(bf16[1,3072,256]{2,1,0:T(8,128)(2,1)} %gate_hbm.1, bf16[1,3072,256]{2,1,0:T(8,128)(2,1)} %up_hbm.1, bf16[1,256,3072]{2,1,0:T(8,128)(2,1)} %down_hbm.1), custom_call_target="tpu_custom_call" | custom-call | bytes 1024 | tf_op jit(solution)/shard_map/weights/pallas_call | solution.py:338
  13.1 0.0 collective-permute-done.1
  13.1 2.3 %collective-permute-done = bf16[16,3200]{1,0:T(8,128)(2,1)S(1)} collective-permute-done((bf16[16,3200]{1,0:T(8,128)(2,1)S(1)}, bf16[16,3200]{1,0:T(8,128)(2,1)S(1)}, u32[]{:S(2)}, u32[]{:S(2)}) %collective-permute-start) | collective-permute-done | bytes 102432 | tf_op jit(solution)/shard_map/ppermute | solution.py:33
  15.4 0.0 collective-permute-done.4
  15.4 0.0 collective-permute-done.3
  15.4 0.0 collective-permute-done.2
  15.4 0.1 collective-permute-start.9
  15.5 0.8 %collective-permute-start.5 = (bf16[64,3200]{1,0:T(8,128)(2,1)S(1)}, bf16[64,3200]{1,0:T(8,128)(2,1)S(1)}, u32[]{:S(2)}, u32[]{:S(2)}) collective-permute-start(bf16[64,3200]{1,0:T(8,128)(2,1)S(1)} %pad_maximum_fusion.refs_0_), channel_id=1, source_target_pairs={{0,8},{4,12},{8,0},{12,4},{16,24},{20,28},{24,16},{28,20},{1,9},{5... | collective-permute-start | bytes 1228808 | tf_op jit(solution)/shard_map/ppermute | solution.py:33
  16.3 0.9 %collective-permute-start.8 = (bf16[32,3200]{1,0:T(8,128)(2,1)S(1)}, bf16[32,3200]{1,0:T(8,128)(2,1)S(1)}, u32[]{:S(2)}, u32[]{:S(2)}) collective-permute-start(bf16[32,3200]{1,0:T(8,128)(2,1)S(1)} %pad_maximum_fusion.1.refs_1_), channel_id=1, source_target_pairs={{0,2},{1,3},{2,0},{3,1},{4,6},{5,7},{6,4},{7,5},{8,10},{9,11},{10,... | collective-permute-start | bytes 614408 | tf_op jit(solution)/shard_map/ppermute | solution.py:33
  17.2 1.5 %collective-permute-start.7 = (bf16[32,3200]{1,0:T(8,128)(2,1)S(1)}, bf16[32,3200]{1,0:T(8,128)(2,1)S(1)}, u32[]{:S(2)}, u32[]{:S(2)}) collective-permute-start(bf16[32,3200]{1,0:T(8,128)(2,1)S(1)} %pad_maximum_fusion.1.refs_1_), channel_id=1, source_target_pairs={{0,1},{1,0},{2,3},{3,2},{4,5},{5,4},{6,7},{7,6},{8,9},{9,8},{10,11... | collective-permute-start | bytes 614408 | tf_op jit(solution)/shard_map/ppermute | solution.py:33
  18.7 1.1 %collective-permute-start.6 = (bf16[32,3200]{1,0:T(8,128)(2,1)S(1)}, bf16[32,3200]{1,0:T(8,128)(2,1)S(1)}, u32[]{:S(2)}, u32[]{:S(2)}) collective-permute-start(bf16[32,3200]{1,0:T(8,128)(2,1)S(1)} %pad_maximum_fusion.1.refs_1_), channel_id=1, source_target_pairs={{0,3},{1,2},{2,1},{3,0},{4,7},{5,6},{6,5},{7,4},{8,11},{9,10},{10,... | collective-permute-start | bytes 614408 | tf_op jit(solution)/shard_map/ppermute | solution.py:33
  19.8 3.7 %collective-permute-done.9.other_ref.refs_7_ = bf16[3072,768]{1,0:T(8,128)(2,1)S(1)} collective-permute-done((bf16[3072,768]{1,0:T(8,128)(2,1)S(1)}, bf16[3072,768]{1,0:T(8,128)(2,1)S(1)}, u32[]{:S(2)}, u32[]{:S(2)}) %collective-permute-start.9) | collective-permute-done | bytes 4718624 | tf_op jit(solution)/shard_map/ppermute | solution.py:33
  23.4 1.8 %back.1.refs_8_ = bf16[1024,3072]{1,0:T(8,128)(2,1)S(1)} custom-call(bf16[3072,768]{1,0:T(8,128)(2,1)S(1)} %weights.1.own_ref.refs_6_, bf16[3072,768]{1,0:T(8,128)(2,1)S(1)} %collective-permute-done.9.other_ref.refs_7_), custom_call_target="tpu_custom_call" | custom-call | tf_op jit(solution)/shard_map/back/pallas_call | solution.py:359
  25.2 0.0 collective-permute-done.8.refs_5_
  25.2 0.0 collective-permute-done.7.refs_4_
  25.2 3.7 %collective-permute-done.6.refs_3_ = bf16[32,3200]{1,0:T(8,128)(2,1)S(1)} collective-permute-done((bf16[32,3200]{1,0:T(8,128)(2,1)S(1)}, bf16[32,3200]{1,0:T(8,128)(2,1)S(1)}, u32[]{:S(2)}, u32[]{:S(2)}) %collective-permute-start.6) | collective-permute-done | bytes 204832 | tf_op jit(solution)/shard_map/ppermute | solution.py:33
  29.0 0.0 collective-permute-done.5.refs_2_
  29.0 2.5 %expert.1 = (f32[32,3200]{1,0:T(8,128)S(1)}, f32[16,3200]{1,0:T(8,128)S(1)}, bf16[32,3200]{1,0:T(8,128)(2,1)S(1)}, bf16[16,3200]{1,0:T(8,128)(2,1)S(1)}, bf16[16...) custom-call(bf16[64,3200]{1,0:T(8,128)(2,1)S(1)} %pad_maximum_fusion, ...), custom_call_target="tpu_custom_call" | custom-call | bytes 1024 | tf_op jit(solution)/shard_map/expert/pallas_call | solution.py:360
  31.5 0.1 collective-permute-start.14
  31.5 1.4 %collective-permute-start.13 = (bf16[32,3200]{1,0:T(8,128)(2,1)S(1)}, bf16[32,3200]{1,0:T(8,128)(2,1)S(1)}, u32[]{:S(2)}, u32[]{:S(2)}) collective-permute-start(bf16[32,3200]{1,0:T(8,128)(2,1)S(1)} %get-tuple-element.39), channel_id=1, source_target_pairs={{0,8},{4,12},{8,0},{12,4},{16,24},{20,28},{24,16},{28,20},{1,9},{5... | collective-permute-start | bytes 614408 | tf_op jit(solution)/shard_map/ppermute | solution.py:33
  32.9 2.4 %collective-permute-start.10 = (bf16[16,3200]{1,0:T(8,128)(2,1)S(1)}, bf16[16,3200]{1,0:T(8,128)(2,1)S(1)}, u32[]{:S(2)}, u32[]{:S(2)}) collective-permute-start(bf16[16,3200]{1,0:T(8,128)(2,1)S(1)} %get-tuple-element.36), channel_id=1, source_target_pairs={{0,3},{1,2},{2,1},{3,0},{4,7},{5,6},{6,5},{7,4},{8,11},{9,10},{10,... | collective-permute-start | bytes 307208 | tf_op jit(solution)/shard_map/ppermute | solution.py:33
  35.4 0.5 %collective-permute-start.11 = (bf16[16,3200]{1,0:T(8,128)(2,1)S(1)}, bf16[16,3200]{1,0:T(8,128)(2,1)S(1)}, u32[]{:S(2)}, u32[]{:S(2)}) collective-permute-start(bf16[16,3200]{1,0:T(8,128)(2,1)S(1)} %get-tuple-element.37), channel_id=1, source_target_pairs={{0,1},{1,0},{2,3},{3,2},{4,5},{5,4},{6,7},{7,6},{8,9},{9,8},{10,11... | collective-permute-start | bytes 307208 | tf_op jit(solution)/shard_map/ppermute | solution.py:33
  35.9 0.5 collective-permute-start.12
  36.4 0.0 collective-permute-done.14.got_ref
  36.4 0.0 copy-start
  36.4 2.7 %grads.1 = (bf16[1,3072,256]{2,1,0:T(8,128)(2,1)}, bf16[1,3072,256]{2,1,0:T(8,128)(2,1)}, bf16[1,256,3072]{2,1,0:T(8,128)(2,1)}) custom-call(bf16[128,6912]{1,0:T(8,128)(2,1)S(1)} %get-tuple-element.40.pass_ref, bf16[128,6912]{1,0:T(8,128)(2,1)S(1)} %collective-permute-done.14.got_ref, bf16[128,768]{1,0:T(8,128)(2,1)S(1)} %get-tuple-element.41.acts_ref), custom_call_target="tpu_custom_call" | custom-call | bytes 1024 | tf_op jit(solution)/shard_map/grads/pallas_call | solution.py:378
  39.1 0.5 collective-permute-done.10.refs_1_
  39.6 1.5 %collective-permute-done.11.refs_2_ = bf16[16,3200]{1,0:T(8,128)(2,1)S(1)} collective-permute-done((bf16[16,3200]{1,0:T(8,128)(2,1)S(1)}, bf16[16,3200]{1,0:T(8,128)(2,1)S(1)}, u32[]{:S(2)}, u32[]{:S(2)}) %collective-permute-start.11) | collective-permute-done | bytes 102432 | tf_op jit(solution)/shard_map/ppermute | solution.py:33
  41.0 0.0 collective-permute-done.12.refs_3_
  41.0 0.0 collective-permute-done.13.refs_1_
  41.0 0.1 sum_far.1
  41.1 2.8 %collective-permute-start.18 = (bf16[8,3200]{1,0:T(8,128)(2,1)S(1)}, bf16[8,3200]{1,0:T(8,128)(2,1)S(1)}, u32[]{:S(2)}, u32[]{:S(2)}) collective-permute-start(bf16[8,3200]{1,0:T(8,128)(2,1)S(1)} %get-tuple-element.52), channel_id=1, source_target_pairs={{0,16},{4,20},{8,24},{12,28},{16,0},{20,4},{24,8},{28,12},{1,17},{... | collective-permute-start | bytes 153608 | tf_op jit(solution)/shard_map/ppermute | solution.py:33
  43.9 0.2 collective-permute-start.19
  44.2 0.1 sum_near.1
  44.2 2.1 %collective-permute-start.15 = (bf16[8,3200]{1,0:T(8,128)(2,1)S(1)}, bf16[8,3200]{1,0:T(8,128)(2,1)S(1)}, u32[]{:S(2)}, u32[]{:S(2)}) collective-permute-start(bf16[8,3200]{1,0:T(8,128)(2,1)S(1)} %get-tuple-element.45), channel_id=1, source_target_pairs={{0,3},{1,2},{2,1},{3,0},{4,7},{5,6},{6,5},{7,4},{8,11},{9,10},{10,... | collective-permute-start | bytes 153608 | tf_op jit(solution)/shard_map/ppermute | solution.py:33
  46.3 0.5 %collective-permute-start.16 = (bf16[8,3200]{1,0:T(8,128)(2,1)S(1)}, bf16[8,3200]{1,0:T(8,128)(2,1)S(1)}, u32[]{:S(2)}, u32[]{:S(2)}) collective-permute-start(bf16[8,3200]{1,0:T(8,128)(2,1)S(1)} %get-tuple-element.46), channel_id=1, source_target_pairs={{0,1},{1,0},{2,3},{3,2},{4,5},{5,4},{6,7},{7,6},{8,9},{9,8},{10,11... | collective-permute-start | bytes 153608 | tf_op jit(solution)/shard_map/ppermute | solution.py:33
  46.9 0.9 %collective-permute-start.17 = (bf16[8,3200]{1,0:T(8,128)(2,1)S(1)}, bf16[8,3200]{1,0:T(8,128)(2,1)S(1)}, u32[]{:S(2)}, u32[]{:S(2)}) collective-permute-start(bf16[8,3200]{1,0:T(8,128)(2,1)S(1)} %get-tuple-element.47), channel_id=1, source_target_pairs={{0,2},{1,3},{2,0},{3,1},{4,6},{5,7},{6,4},{7,5},{8,10},{9,11},{10,... | collective-permute-start | bytes 153608 | tf_op jit(solution)/shard_map/ppermute | solution.py:33
  47.8 0.0 collective-permute-done.18.refs_4_
  47.8 2.1 %collective-permute-done.19.refs_5_ = bf16[8,3200]{1,0:T(8,128)(2,1)S(1)} collective-permute-done((bf16[8,3200]{1,0:T(8,128)(2,1)S(1)}, bf16[8,3200]{1,0:T(8,128)(2,1)S(1)}, u32[]{:S(2)}, u32[]{:S(2)}) %collective-permute-start.19) | collective-permute-done | bytes 51232 | tf_op jit(solution)/shard_map/ppermute | solution.py:33
  49.9 0.0 collective-permute-done.15.refs_1_
  49.9 0.6 %collective-permute-done.16.refs_2_ = bf16[8,3200]{1,0:T(8,128)(2,1)S(1)} collective-permute-done((bf16[8,3200]{1,0:T(8,128)(2,1)S(1)}, bf16[8,3200]{1,0:T(8,128)(2,1)S(1)}, u32[]{:S(2)}, u32[]{:S(2)}) %collective-permute-start.16) | collective-permute-done | bytes 51232 | tf_op jit(solution)/shard_map/ppermute | solution.py:33
  50.4 0.5 %collective-permute-done.17.refs_3_ = bf16[8,3200]{1,0:T(8,128)(2,1)S(1)} collective-permute-done((bf16[8,3200]{1,0:T(8,128)(2,1)S(1)}, bf16[8,3200]{1,0:T(8,128)(2,1)S(1)}, u32[]{:S(2)}, u32[]{:S(2)}) %collective-permute-start.17) | collective-permute-done | bytes 51232 | tf_op jit(solution)/shard_map/ppermute | solution.py:33
  51.0 0.0 copy-done
  51.0 0.7 %final.1 = (bf16[8,3072]{1,0:T(8,128)(2,1)}, f32[2,8]{1,0:T(2,128)}) custom-call(f32[8,3200]{1,0:T(8,128)S(1)} %get-tuple-element.44.refs_0_, bf16[8,3200]{1,0:T(8,128)(2,1)S(1)} %collective-permute-done.15.refs_1_, bf16[8,3200]{1,0:T(8,128)(2,1)S(1)} %collective-permute-done.16.refs_2_, bf16[8,3200]{1,0:T(8,128)(2,1)S(1)} %collective-permute-done.17.refs_3_, ...), custom_call_target="tpu_custom_call" | custom-call | bytes 204800 | tf_op jit(solution)/shard_map/final/pallas_call | solution.py:411
  (2 shorter events, 0.0 us)
Async XLA Ops:
  1.6 11.5 %collective-permute-start.1 = (bf16[16,3200]{1,0:T(8,128)(2,1)S(1)}, bf16[16,3200]{1,0:T(8,128)(2,1)S(1)}, u32[]{:S(2)}, u32[]{:S(2)}) collective-permute-start(bf16[16,3200]{1,0:T(8,128)(2,1)S(1)} %pack.1), channel_id=1, source_target_pairs={{0,24},{4,28},{8,16},{12,20},{16,8},{20,12},{24,0},{28,4},{1,25},{... | collective-permute-start | bytes 307208 | tf_op jit(solution)/shard_map/ppermute | solution.py:33
  6.7 8.6 %collective-permute-start = (bf16[16,3200]{1,0:T(8,128)(2,1)S(1)}, bf16[16,3200]{1,0:T(8,128)(2,1)S(1)}, u32[]{:S(2)}, u32[]{:S(2)}) collective-permute-start(bf16[16,3200]{1,0:T(8,128)(2,1)S(1)} %pack.1), channel_id=1, source_target_pairs={{0,16},{4,20},{8,24},{12,28},{16,0},{20,4},{24,8},{28,12},{1,17},{... | collective-permute-start | bytes 307208 | tf_op jit(solution)/shard_map/ppermute | solution.py:33
  6.7 8.6 %collective-permute-start.4 = (bf16[16,3200]{1,0:T(8,128)(2,1)S(1)}, bf16[16,3200]{1,0:T(8,128)(2,1)S(1)}, u32[]{:S(2)}, u32[]{:S(2)}) collective-permute-start(bf16[16,3200]{1,0:T(8,128)(2,1)S(1)} %pack.1), channel_id=1, source_target_pairs={{0,2},{1,3},{2,0},{3,1},{4,6},{5,7},{6,4},{7,5},{8,10},{9,11},{10,... | collective-permute-start | bytes 307208 | tf_op jit(solution)/shard_map/ppermute | solution.py:33
  8.3 7.1 %collective-permute-start.3 = (bf16[16,3200]{1,0:T(8,128)(2,1)S(1)}, bf16[16,3200]{1,0:T(8,128)(2,1)S(1)}, u32[]{:S(2)}, u32[]{:S(2)}) collective-permute-start(bf16[16,3200]{1,0:T(8,128)(2,1)S(1)} %pack.1), channel_id=1, source_target_pairs={{0,1},{1,0},{2,3},{3,2},{4,5},{5,4},{6,7},{7,6},{8,9},{9,8},{10,11... | collective-permute-start | bytes 307208 | tf_op jit(solution)/shard_map/ppermute | solution.py:33
  9.7 5.6 %collective-permute-start.2 = (bf16[16,3200]{1,0:T(8,128)(2,1)S(1)}, bf16[16,3200]{1,0:T(8,128)(2,1)S(1)}, u32[]{:S(2)}, u32[]{:S(2)}) collective-permute-start(bf16[16,3200]{1,0:T(8,128)(2,1)S(1)} %pack.1), channel_id=1, source_target_pairs={{0,3},{1,2},{2,1},{3,0},{4,7},{5,6},{6,5},{7,4},{8,11},{9,10},{10,... | collective-permute-start | bytes 307208 | tf_op jit(solution)/shard_map/ppermute | solution.py:33
  15.4 8.0 %collective-permute-start.9 = (bf16[3072,768]{1,0:T(8,128)(2,1)S(1)}, bf16[3072,768]{1,0:T(8,128)(2,1)S(1)}, u32[]{:S(2)}, u32[]{:S(2)}) collective-permute-start(bf16[3072,768]{1,0:T(8,128)(2,1)S(1)} %weights.1.own_ref.refs_6_), channel_id=1, source_target_pairs={{0,4},{4,0},{8,12},{12,8},{16,20},{20,16},{24,28},{28,24},{1,5},{5... | collective-permute-start | bytes 14155784 | tf_op jit(solution)/shard_map/ppermute | solution.py:33
  15.5 13.5 %collective-permute-start.5 = (bf16[64,3200]{1,0:T(8,128)(2,1)S(1)}, bf16[64,3200]{1,0:T(8,128)(2,1)S(1)}, u32[]{:S(2)}, u32[]{:S(2)}) collective-permute-start(bf16[64,3200]{1,0:T(8,128)(2,1)S(1)} %pad_maximum_fusion.refs_0_), channel_id=1, source_target_pairs={{0,8},{4,12},{8,0},{12,4},{16,24},{20,28},{24,16},{28,20},{1,9},{5... | collective-permute-start | bytes 1228808 | tf_op jit(solution)/shard_map/ppermute | solution.py:33
  16.3 9.0 %collective-permute-start.8 = (bf16[32,3200]{1,0:T(8,128)(2,1)S(1)}, bf16[32,3200]{1,0:T(8,128)(2,1)S(1)}, u32[]{:S(2)}, u32[]{:S(2)}) collective-permute-start(bf16[32,3200]{1,0:T(8,128)(2,1)S(1)} %pad_maximum_fusion.1.refs_1_), channel_id=1, source_target_pairs={{0,2},{1,3},{2,0},{3,1},{4,6},{5,7},{6,4},{7,5},{8,10},{9,11},{10,... | collective-permute-start | bytes 614408 | tf_op jit(solution)/shard_map/ppermute | solution.py:33
  17.2 8.1 %collective-permute-start.7 = (bf16[32,3200]{1,0:T(8,128)(2,1)S(1)}, bf16[32,3200]{1,0:T(8,128)(2,1)S(1)}, u32[]{:S(2)}, u32[]{:S(2)}) collective-permute-start(bf16[32,3200]{1,0:T(8,128)(2,1)S(1)} %pad_maximum_fusion.1.refs_1_), channel_id=1, source_target_pairs={{0,1},{1,0},{2,3},{3,2},{4,5},{5,4},{6,7},{7,6},{8,9},{9,8},{10,11... | collective-permute-start | bytes 614408 | tf_op jit(solution)/shard_map/ppermute | solution.py:33
  18.7 10.3 %collective-permute-start.6 = (bf16[32,3200]{1,0:T(8,128)(2,1)S(1)}, bf16[32,3200]{1,0:T(8,128)(2,1)S(1)}, u32[]{:S(2)}, u32[]{:S(2)}) collective-permute-start(bf16[32,3200]{1,0:T(8,128)(2,1)S(1)} %pad_maximum_fusion.1.refs_1_), channel_id=1, source_target_pairs={{0,3},{1,2},{2,1},{3,0},{4,7},{5,6},{6,5},{7,4},{8,11},{9,10},{10,... | collective-permute-start | bytes 614408 | tf_op jit(solution)/shard_map/ppermute | solution.py:33
  31.5 5.0 %collective-permute-start.14 = (bf16[128,6912]{1,0:T(8,128)(2,1)S(1)}, bf16[128,6912]{1,0:T(8,128)(2,1)S(1)}, u32[]{:S(2)}, u32[]{:S(2)}) collective-permute-start(bf16[128,6912]{1,0:T(8,128)(2,1)S(1)} %get-tuple-element.40.pass_ref), channel_id=1, source_target_pairs={{0,4},{4,0},{8,12},{12,8},{16,20},{20,16},{24,28},{28,24},{1,5},{5... | collective-permute-start | bytes 5308424 | tf_op jit(solution)/shard_map/ppermute | solution.py:33
  31.5 9.5 %collective-permute-start.13 = (bf16[32,3200]{1,0:T(8,128)(2,1)S(1)}, bf16[32,3200]{1,0:T(8,128)(2,1)S(1)}, u32[]{:S(2)}, u32[]{:S(2)}) collective-permute-start(bf16[32,3200]{1,0:T(8,128)(2,1)S(1)} %get-tuple-element.39), channel_id=1, source_target_pairs={{0,8},{4,12},{8,0},{12,4},{16,24},{20,28},{24,16},{28,20},{1,9},{5... | collective-permute-start | bytes 614408 | tf_op jit(solution)/shard_map/ppermute | solution.py:33
  32.9 6.6 %collective-permute-start.10 = (bf16[16,3200]{1,0:T(8,128)(2,1)S(1)}, bf16[16,3200]{1,0:T(8,128)(2,1)S(1)}, u32[]{:S(2)}, u32[]{:S(2)}) collective-permute-start(bf16[16,3200]{1,0:T(8,128)(2,1)S(1)} %get-tuple-element.36), channel_id=1, source_target_pairs={{0,3},{1,2},{2,1},{3,0},{4,7},{5,6},{6,5},{7,4},{8,11},{9,10},{10,... | collective-permute-start | bytes 307208 | tf_op jit(solution)/shard_map/ppermute | solution.py:33
  35.4 5.7 %collective-permute-start.11 = (bf16[16,3200]{1,0:T(8,128)(2,1)S(1)}, bf16[16,3200]{1,0:T(8,128)(2,1)S(1)}, u32[]{:S(2)}, u32[]{:S(2)}) collective-permute-start(bf16[16,3200]{1,0:T(8,128)(2,1)S(1)} %get-tuple-element.37), channel_id=1, source_target_pairs={{0,1},{1,0},{2,3},{3,2},{4,5},{5,4},{6,7},{7,6},{8,9},{9,8},{10,11... | collective-permute-start | bytes 307208 | tf_op jit(solution)/shard_map/ppermute | solution.py:33
  35.9 5.1 %collective-permute-start.12 = (bf16[16,3200]{1,0:T(8,128)(2,1)S(1)}, bf16[16,3200]{1,0:T(8,128)(2,1)S(1)}, u32[]{:S(2)}, u32[]{:S(2)}) collective-permute-start(bf16[16,3200]{1,0:T(8,128)(2,1)S(1)} %get-tuple-element.38), channel_id=1, source_target_pairs={{0,2},{1,3},{2,0},{3,1},{4,6},{5,7},{6,4},{7,5},{8,10},{9,11},{10,... | collective-permute-start | bytes 307208 | tf_op jit(solution)/shard_map/ppermute | solution.py:33
  36.4 14.5 %copy-start = (s32[8,2]{0,1:T(2,128)S(1)}, s32[8,2]{0,1:T(2,128)}, u32[]{:S(2)}) copy-start(s32[8,2]{0,1:T(2,128)} %param.9) | copy-start | bytes 196
  41.1 6.6 %collective-permute-start.18 = (bf16[8,3200]{1,0:T(8,128)(2,1)S(1)}, bf16[8,3200]{1,0:T(8,128)(2,1)S(1)}, u32[]{:S(2)}, u32[]{:S(2)}) collective-permute-start(bf16[8,3200]{1,0:T(8,128)(2,1)S(1)} %get-tuple-element.52), channel_id=1, source_target_pairs={{0,16},{4,20},{8,24},{12,28},{16,0},{20,4},{24,8},{28,12},{1,17},{... | collective-permute-start | bytes 153608 | tf_op jit(solution)/shard_map/ppermute | solution.py:33
  43.9 5.9 %collective-permute-start.19 = (bf16[8,3200]{1,0:T(8,128)(2,1)S(1)}, bf16[8,3200]{1,0:T(8,128)(2,1)S(1)}, u32[]{:S(2)}, u32[]{:S(2)}) collective-permute-start(bf16[8,3200]{1,0:T(8,128)(2,1)S(1)} %get-tuple-element.53), channel_id=1, source_target_pairs={{0,24},{4,28},{8,16},{12,20},{16,8},{20,12},{24,0},{28,4},{1,25},{... | collective-permute-start | bytes 153608 | tf_op jit(solution)/shard_map/ppermute | solution.py:33
  44.2 5.6 %collective-permute-start.15 = (bf16[8,3200]{1,0:T(8,128)(2,1)S(1)}, bf16[8,3200]{1,0:T(8,128)(2,1)S(1)}, u32[]{:S(2)}, u32[]{:S(2)}) collective-permute-start(bf16[8,3200]{1,0:T(8,128)(2,1)S(1)} %get-tuple-element.45), channel_id=1, source_target_pairs={{0,3},{1,2},{2,1},{3,0},{4,7},{5,6},{6,5},{7,4},{8,11},{9,10},{10,... | collective-permute-start | bytes 153608 | tf_op jit(solution)/shard_map/ppermute | solution.py:33
  46.3 4.1 %collective-permute-start.16 = (bf16[8,3200]{1,0:T(8,128)(2,1)S(1)}, bf16[8,3200]{1,0:T(8,128)(2,1)S(1)}, u32[]{:S(2)}, u32[]{:S(2)}) collective-permute-start(bf16[8,3200]{1,0:T(8,128)(2,1)S(1)} %get-tuple-element.46), channel_id=1, source_target_pairs={{0,1},{1,0},{2,3},{3,2},{4,5},{5,4},{6,7},{7,6},{8,9},{9,8},{10,11... | collective-permute-start | bytes 153608 | tf_op jit(solution)/shard_map/ppermute | solution.py:33
  46.9 4.1 %collective-permute-start.17 = (bf16[8,3200]{1,0:T(8,128)(2,1)S(1)}, bf16[8,3200]{1,0:T(8,128)(2,1)S(1)}, u32[]{:S(2)}, u32[]{:S(2)}) collective-permute-start(bf16[8,3200]{1,0:T(8,128)(2,1)S(1)} %get-tuple-element.47), channel_id=1, source_target_pairs={{0,2},{1,3},{2,0},{3,1},{4,6},{5,7},{6,4},{7,5},{8,10},{9,11},{10,... | collective-permute-start | bytes 153608 | tf_op jit(solution)/shard_map/ppermute | solution.py:33

commit v6 on v5

--- a/solution.py
+++ b/solution.py
@@ -72,24 +72,24 @@
     return jnp.sum(jnp.where(here == there, col, 0.0), axis=0, keepdims=True)
 
 
-def pack_body(x_hbm, dy_hbm, ids_hbm, gates_hbm, out_ref, x_ref, dy_ref, ids_ref, gates_ref, sems):
-    pairs = ((ids_hbm, ids_ref), (gates_hbm, gates_ref), (x_hbm, x_ref), (dy_hbm, dy_ref))
-    copies = [pltpu.make_async_copy(src, dst, sems.at[i]) for i, (src, dst) in enumerate(pairs)]
-    for copy in copies:
-        copy.start()
-    for copy in copies:
-        copy.wait()
-    count, features = x_ref.shape
+def pack_body(x_hbm, dy_hbm, ids_hbm, gates_hbm, out_ref, ids_ref, gates_ref, sems):
+    count, features = x_hbm.shape
+    places = (ids_ref, gates_ref, out_ref.at[:, :features], out_ref.at[:, features : 2 * features])
+    copies = []
+    for i, (src, dst) in enumerate(zip((ids_hbm, gates_hbm, x_hbm, dy_hbm), places)):
+        copies.append(pltpu.make_async_copy(src, dst, sems.at[i]))
+        copies[i].start()
+    copies[0].wait()
+    copies[1].wait()
     lane = lanes(count).astype(F32)
     gates = gates_ref[...].astype(F32)
     ids = ids_ref[...].astype(F32)
     dense = jnp.zeros((count, PAD), F32)
     for k in range(ids.shape[0]):
         dense = jnp.where(lane == column(ids[k : k + 1]), column(gates[k : k + 1]), dense)
-    out_ref[:, :features] = jnp.concatenate(
-        [x_ref[...].astype(F32), dy_ref[...].astype(F32)], axis=0
-    ).astype(BF)
-    out_ref[:, features:] = jnp.concatenate([dense, dense], axis=0).astype(BF)
+    out_ref[:, 2 * features :] = dense.astype(BF)
+    copies[2].wait()
+    copies[3].wait()
 
 
 def weights_body(gate_hbm, up_hbm, down_hbm, out_ref, stage_ref, sems):
@@ -110,32 +110,31 @@
     out_ref[both:, :] = other_ref[:, :both].T
 
 
-def expert_body(experts, count, pieces_count, *refs):
+def expert_body(experts, pieces_count, *refs):
     pieces, (own_ref, other_ref, back_ref) = refs[:pieces_count], refs[pieces_count : pieces_count + 3]
-    *sums, pass_ref, acts_ref, x_ref, dy_ref, weight_ref = refs[pieces_count + 3 :]
-    features = x_ref.shape[1]
+    *sums, pass_ref, acts_ref, dy_ref, weight_ref = refs[pieces_count + 3 :]
+    features = dy_ref.shape[1]
     units = own_ref.shape[1] // 3
     own = lax.axis_index("expert")
 
-    blocks = [(piece, at) for piece in pieces for at in range(0, piece.shape[0], 2 * count)]
-    lane = lanes(2 * count)
-    for i in range(0, len(blocks), 2):
-        halves = [ref[at : at + 2 * count, :].astype(F32) for ref, at in blocks[i : i + 2]]
-        rows = pl.ds(i * count, 2 * count)
-        x = jnp.concatenate([h[:count, :features] for h in halves], axis=0).astype(BF)
-        dy = jnp.concatenate([h[count:, :features] for h in halves], axis=0)
-        dense = jnp.concatenate([h[:count, features:] for h in halves], axis=0)
-        weight = jnp.sum(jnp.where(lane == own, dense, 0.0), axis=1, keepdims=True)
-        weight_ref[rows, :] = jnp.broadcast_to(weight, (2 * count, PAD))
-        x_ref[rows, :] = x
-        dy_ref[rows, :] = dy.astype(BF)
-        pass_ref[rows, :features] = x
-        pass_ref[rows, features : 2 * features] = (weight * dy).astype(BF)
+    at = 0
+    for piece in pieces:
+        rows = pl.ds(at, piece.shape[0])
+        at += piece.shape[0]
+        dense = piece[:, 2 * features :].astype(F32)
+        weight = jnp.sum(jnp.where(lanes(piece.shape[0]) == own, dense, 0.0), axis=1, keepdims=True)
+        weight_ref[rows, :] = jnp.broadcast_to(weight, dense.shape)
+        dy = piece[:, features : 2 * features]
+        dy_ref[rows, :] = dy
+        pass_ref[rows, :features] = piece[:, :features]
+        pass_ref[rows, features : 2 * features] = (weight * dy.astype(F32)).astype(BF)
 
     grads = []
     product = 0.0
     for ref in (own_ref, other_ref):
-        both = jnp.dot(x_ref[...], ref[:, : 2 * units], preferred_element_type=F32)
+        both = jnp.dot(
+            pass_ref[:, :features], ref[:, : 2 * units], preferred_element_type=F32
+        )
         pre_gate, pre_up = both[:, :units], both[:, units:]
         back = jnp.dot(dy_ref[...], ref[:, 2 * units :], preferred_element_type=F32)
         sig = jax.nn.sigmoid(pre_gate)
@@ -258,17 +257,15 @@
     ]
 
 
-def expert_plain(pieces, own_slabs, other_slabs, experts, count, sizes):
+def expert_plain(pieces, own_slabs, other_slabs, experts, sizes):
     features = own_slabs.shape[0]
     units = own_slabs.shape[1] // 3
-    rows = jnp.concatenate(pieces, axis=0).reshape(-1, 2, count, features + PAD)
-    rows_x = rows[:, 0].reshape(-1, features + PAD)
-    rows_dy = rows[:, 1, :, :features].reshape(-1, features)
+    rows = jnp.concatenate(pieces, axis=0)
+    rows_x, rows_dy = rows[:, :features], rows[:, features : 2 * features]
     is_own = jnp.arange(PAD, dtype=jnp.int32)[None, :] == lax.axis_index("expert")
     weight = jnp.sum(
-        jnp.where(is_own, rows_x[:, features:].astype(F32), 0.0), axis=1, keepdims=True
-    )
-    rows_x = rows_x[:, :features]
+        jnp.where(is_own, rows[:, 2 * features :].astype(F32), 0.0), axis=1, keepdims=True
+    )
     scaled = (weight * rows_dy.astype(F32)).astype(BF)
     part = product = 0.0
     acts = []
@@ -310,11 +307,9 @@
 
     block = pl.pallas_call(
         pack_body,
-        out_shape=shape((2 * count, width), BF),
+        out_shape=shape((count, 2 * features + PAD), BF),
         in_specs=[pl.BlockSpec(memory_space=pltpu.HBM)] * 4,
         scratch_shapes=[
-            pltpu.VMEM(tokens.shape, BF),
-            pltpu.VMEM(tokens.shape, BF),
             pltpu.VMEM(ids.shape, jnp.int32),
             pltpu.VMEM(ids.shape, BF),
             pltpu.SemaphoreType.DMA((4,)),
@@ -352,17 +347,16 @@
     far = [swap(far_block, "expert", d) for d in others[1:]]
     far += [swap(near_block, "section", 2), swap(far_block, "expert", others[0])]
     *direct, beside, diagonal = far
-    pieces = [near_block, far_block, beside, diagonal, *direct]
+    pieces = [near_block, far_block, beside, *direct, diagonal]
     sizes = [(experts * count, F32), ((groups - 2) * count, F32), (experts * count, BF)]
     sizes += [((groups - 2) * count, BF)] * len(others)
     if fits:
         back_slabs = call(back_body, shape((4 * units, features), BF), "back")(slabs, other_slabs)
         *split, passed, acts = pl.pallas_call(
-            functools.partial(expert_body, experts, count, len(pieces)),
+            functools.partial(expert_body, experts, len(pieces)),
             out_shape=[shape((size, width), dtype) for size, dtype in sizes]
             + [shape((rows, 2 * features + 3 * units), BF), shape((rows, 3 * units), BF)],
             scratch_shapes=[
-                pltpu.VMEM((rows, features), BF),
                 pltpu.VMEM((rows, features), BF),
                 pltpu.VMEM((rows, PAD), F32),
             ],
@@ -371,7 +365,7 @@
             cost_estimate=pl.CostEstimate(flops=0, bytes_accessed=1024, transcendentals=0),
         )(*pieces, slabs, other_slabs, back_slabs)
     else:
-        *split, passed, acts = expert_plain(pieces, slabs, other_slabs, experts, count, sizes)
+        *split, passed, acts = expert_plain(pieces, slabs, other_slabs, experts, sizes)
 
     got = swap(passed, "section", 1)
     if fits:
@@ -401,7 +395,9 @@
         grad_up = contract_first(rows_x, d_up).astype(BF)[None]
         grad_down = contract_first(hidden, scaled).astype(BF)[None]
 
-    crossed = [swap(part, "expert", d) for d, part in zip(others, split[3:])]
+    crossed = [
+        swap(part, "expert", d) for d, part in zip(others, [split[-1], *split[3:-1]])
+    ]
     beside = swap(split[2], "section", 2)
     crossed, beside, grad_gate = lax.optimization_barrier((crossed, beside, grad_gate))
     own, *sideways = added(split[0], [beside], experts, True, "sum_near")

time: 51.9 us -> 51.2 us (0.987)
  waiting for transfers between devices: 14.8 us -> 14 us
    ppermute x20, waiting for transfers between devices: 14.8 us -> 14 us  [swap(): return lax.ppermute(value, axis, [(i, i ^ mask) for i in range(size)])]
  transfers between devices with their start and end apart: 20 -> 20, of which waited for: 8 -> 9; matrix products, arithmetic and copies ran while one was open for 0% -> 0% of each run, Pallas kernels for 14% -> 15%
where the time goes in v6:
time: 51.2 us; the launch traced here: 51 us
  starting transfers between devices  24.6 us (48%)
  waiting for transfers between devices  14 us (27%)
  Pallas kernels  11.6 us (23%)
  between operations  0.74 us (1%)
    ppermute x20, starting transfers between devices, swap(): return lax.ppermute(value, axis, [(i, i ^ mask) for i in range(size)])  24.6 us
    ppermute x20, waiting for transfers between devices, swap(): return lax.ppermute(value, axis, [(i, i ^ mask) for i in range(size)])  14 us
    pallas_call x1, Pallas kernels, local(): pl.pallas_call(weights_body, out_shape=shape((features, 3 * units), BF),...  2.84 us
    pallas_call x1, Pallas kernels, local(): pl.pallas_call(functools.partial(grads_body, PARTS), out_shape=[shape(w.s...  2.68 us
    pallas_call x1, Pallas kernels, local(): pl.pallas_call(functools.partial(expert_body, experts, len(pieces)), out_...  2.46 us
    pallas_call x1, Pallas kernels, local(): call(back_body, shape((4 * units, features), BF), 'back')  1.8 us
  transfers between devices with their start and end apart: 20, of which 9 were waited for; matrix products, arithmetic and copies ran while one was open for 0% of the time, Pallas kernels for 15%

profile of v6, /device:TPU:0, one launch (start us, length us, event | category | flops | bytes accessed | tf_op | source)
XLA Modules:
  0.0 51.0 jit_solution(4354987835027453404)
XLA Ops:
  0.6 0.9 %pack.1 = bf16[8,6272]{1,0:T(8,128)(2,1)S(1)} custom-call(bf16[8,3072]{1,0:T(8,128)(2,1)} %x_hbm.1, bf16[8,3072]{1,0:T(8,128)(2,1)} %dy_hbm.1, s32[2,8]{1,0:T(2,128)} %bitcast.3, bf16[2,8]{1,0:T(2,128)(2,1)} %bitcast.5), custom_call_target="tpu_custom_call" | custom-call | tf_op jit(solution)/shard_map/pack/pallas_call | solution.py:308
  1.5 5.1 %collective-permute-start.1 = (bf16[8,6272]{1,0:T(8,128)(2,1)S(1)}, bf16[8,6272]{1,0:T(8,128)(2,1)S(1)}, u32[]{:S(2)}, u32[]{:S(2)}) collective-permute-start(bf16[8,6272]{1,0:T(8,128)(2,1)S(1)} %pack.1), channel_id=1, source_target_pairs={{0,24},{4,28},{8,16},{12,20},{16,8},{20,12},{24,0},{28,4},{1,25},{... | collective-permute-start | bytes 301064 | tf_op jit(solution)/shard_map/ppermute | solution.py:33
  6.6 0.0 collective-permute-start
  6.6 1.5 %collective-permute-start.4 = (bf16[8,6272]{1,0:T(8,128)(2,1)S(1)}, bf16[8,6272]{1,0:T(8,128)(2,1)S(1)}, u32[]{:S(2)}, u32[]{:S(2)}) collective-permute-start(bf16[8,6272]{1,0:T(8,128)(2,1)S(1)} %pack.1), channel_id=1, source_target_pairs={{0,2},{1,3},{2,0},{3,1},{4,6},{5,7},{6,4},{7,5},{8,10},{9,11},{10,... | collective-permute-start | bytes 301064 | tf_op jit(solution)/shard_map/ppermute | solution.py:33
  8.2 1.5 %collective-permute-start.3 = (bf16[8,6272]{1,0:T(8,128)(2,1)S(1)}, bf16[8,6272]{1,0:T(8,128)(2,1)S(1)}, u32[]{:S(2)}, u32[]{:S(2)}) collective-permute-start(bf16[8,6272]{1,0:T(8,128)(2,1)S(1)} %pack.1), channel_id=1, source_target_pairs={{0,1},{1,0},{2,3},{3,2},{4,5},{5,4},{6,7},{7,6},{8,9},{9,8},{10,11... | collective-permute-start | bytes 301064 | tf_op jit(solution)/shard_map/ppermute | solution.py:33
  9.7 0.5 collective-permute-start.2
  10.1 2.8 %weights.1.own_ref.refs_6_ = bf16[3072,768]{1,0:T(8,128)(2,1)S(1)} custom-call(bf16[1,3072,256]{2,1,0:T(8,128)(2,1)} %gate_hbm.1, bf16[1,3072,256]{2,1,0:T(8,128)(2,1)} %up_hbm.1, bf16[1,256,3072]{2,1,0:T(8,128)(2,1)} %down_hbm.1), custom_call_target="tpu_custom_call" | custom-call | bytes 1024 | tf_op jit(solution)/shard_map/weights/pallas_call | solution.py:333
  13.0 0.0 collective-permute-done.1
  13.0 2.1 %collective-permute-done = bf16[8,6272]{1,0:T(8,128)(2,1)S(1)} collective-permute-done((bf16[8,6272]{1,0:T(8,128)(2,1)S(1)}, bf16[8,6272]{1,0:T(8,128)(2,1)S(1)}, u32[]{:S(2)}, u32[]{:S(2)}) %collective-permute-start) | collective-permute-done | bytes 100384 | tf_op jit(solution)/shard_map/ppermute | solution.py:33
  15.1 0.0 collective-permute-done.4
  15.1 0.0 collective-permute-done.3
  15.1 0.1 collective-permute-done.2
  15.2 0.1 collective-permute-start.9
  15.3 0.8 %collective-permute-start.5 = (bf16[32,6272]{1,0:T(8,128)(2,1)S(1)}, bf16[32,6272]{1,0:T(8,128)(2,1)S(1)}, u32[]{:S(2)}, u32[]{:S(2)}) collective-permute-start(bf16[32,6272]{1,0:T(8,128)(2,1)S(1)} %pad_maximum_fusion.refs_0_), channel_id=1, source_target_pairs={{0,8},{4,12},{8,0},{12,4},{16,24},{20,28},{24,16},{28,20},{1,9},{5... | collective-permute-start | bytes 1204232 | tf_op jit(solution)/shard_map/ppermute | solution.py:33
  16.2 1.7 %collective-permute-start.8 = (bf16[16,6272]{1,0:T(8,128)(2,1)S(1)}, bf16[16,6272]{1,0:T(8,128)(2,1)S(1)}, u32[]{:S(2)}, u32[]{:S(2)}) collective-permute-start(bf16[16,6272]{1,0:T(8,128)(2,1)S(1)} %pad_maximum_fusion.1.refs_1_), channel_id=1, source_target_pairs={{0,3},{1,2},{2,1},{3,0},{4,7},{5,6},{6,5},{7,4},{8,11},{9,10},{10,... | collective-permute-start | bytes 602120 | tf_op jit(solution)/shard_map/ppermute | solution.py:33
  17.8 0.5 collective-permute-start.7
  18.4 1.3 %collective-permute-start.6 = (bf16[16,6272]{1,0:T(8,128)(2,1)S(1)}, bf16[16,6272]{1,0:T(8,128)(2,1)S(1)}, u32[]{:S(2)}, u32[]{:S(2)}) collective-permute-start(bf16[16,6272]{1,0:T(8,128)(2,1)S(1)} %pad_maximum_fusion.1.refs_1_), channel_id=1, source_target_pairs={{0,1},{1,0},{2,3},{3,2},{4,5},{5,4},{6,7},{7,6},{8,9},{9,8},{10,11... | collective-permute-start | bytes 602120 | tf_op jit(solution)/shard_map/ppermute | solution.py:33
  19.7 3.6 %collective-permute-done.9.other_ref.refs_7_ = bf16[3072,768]{1,0:T(8,128)(2,1)S(1)} collective-permute-done((bf16[3072,768]{1,0:T(8,128)(2,1)S(1)}, bf16[3072,768]{1,0:T(8,128)(2,1)S(1)}, u32[]{:S(2)}, u32[]{:S(2)}) %collective-permute-start.9) | collective-permute-done | bytes 4718624 | tf_op jit(solution)/shard_map/ppermute | solution.py:33
  23.2 1.8 %back.1.refs_8_ = bf16[1024,3072]{1,0:T(8,128)(2,1)S(1)} custom-call(bf16[3072,768]{1,0:T(8,128)(2,1)S(1)} %weights.1.own_ref.refs_6_, bf16[3072,768]{1,0:T(8,128)(2,1)S(1)} %collective-permute-done.9.other_ref.refs_7_), custom_call_target="tpu_custom_call" | custom-call | tf_op jit(solution)/shard_map/back/pallas_call | solution.py:354
  25.0 0.0 collective-permute-done.8.refs_5_
  25.0 3.4 %collective-permute-done.7.refs_4_ = bf16[16,6272]{1,0:T(8,128)(2,1)S(1)} collective-permute-done((bf16[16,6272]{1,0:T(8,128)(2,1)S(1)}, bf16[16,6272]{1,0:T(8,128)(2,1)S(1)}, u32[]{:S(2)}, u32[]{:S(2)}) %collective-permute-start.7) | collective-permute-done | bytes 200736 | tf_op jit(solution)/shard_map/ppermute | solution.py:33
  28.4 0.0 collective-permute-done.6.refs_3_
  28.4 0.0 collective-permute-done.5.refs_2_
  28.4 2.5 %expert.1 = (f32[32,3200]{1,0:T(8,128)S(1)}, f32[16,3200]{1,0:T(8,128)S(1)}, bf16[32,3200]{1,0:T(8,128)(2,1)S(1)}, bf16[16,3200]{1,0:T(8,128)(2,1)S(1)}, bf16[16...) custom-call(bf16[32,6272]{1,0:T(8,128)(2,1)S(1)} %pad_maximum_fusion, ...), custom_call_target="tpu_custom_call" | custom-call | bytes 1024 | tf_op jit(solution)/shard_map/expert/pallas_call | solution.py:355
  30.9 0.1 collective-permute-start.14
  31.0 1.3 %collective-permute-start.13 = (bf16[32,3200]{1,0:T(8,128)(2,1)S(1)}, bf16[32,3200]{1,0:T(8,128)(2,1)S(1)}, u32[]{:S(2)}, u32[]{:S(2)}) collective-permute-start(bf16[32,3200]{1,0:T(8,128)(2,1)S(1)} %get-tuple-element.39), channel_id=1, source_target_pairs={{0,8},{4,12},{8,0},{12,4},{16,24},{20,28},{24,16},{28,20},{1,9},{5... | collective-permute-start | bytes 614408 | tf_op jit(solution)/shard_map/ppermute | solution.py:33
  32.3 1.7 %collective-permute-start.10 = (bf16[16,3200]{1,0:T(8,128)(2,1)S(1)}, bf16[16,3200]{1,0:T(8,128)(2,1)S(1)}, u32[]{:S(2)}, u32[]{:S(2)}) collective-permute-start(bf16[16,3200]{1,0:T(8,128)(2,1)S(1)} %get-tuple-element.36), channel_id=1, source_target_pairs={{0,3},{1,2},{2,1},{3,0},{4,7},{5,6},{6,5},{7,4},{8,11},{9,10},{10,... | collective-permute-start | bytes 307208 | tf_op jit(solution)/shard_map/ppermute | solution.py:33
  34.0 1.2 %collective-permute-start.11 = (bf16[16,3200]{1,0:T(8,128)(2,1)S(1)}, bf16[16,3200]{1,0:T(8,128)(2,1)S(1)}, u32[]{:S(2)}, u32[]{:S(2)}) collective-permute-start(bf16[16,3200]{1,0:T(8,128)(2,1)S(1)} %get-tuple-element.37), channel_id=1, source_target_pairs={{0,1},{1,0},{2,3},{3,2},{4,5},{5,4},{6,7},{7,6},{8,9},{9,8},{10,11... | collective-permute-start | bytes 307208 | tf_op jit(solution)/shard_map/ppermute | solution.py:33
  35.2 0.6 %collective-permute-start.12 = (bf16[16,3200]{1,0:T(8,128)(2,1)S(1)}, bf16[16,3200]{1,0:T(8,128)(2,1)S(1)}, u32[]{:S(2)}, u32[]{:S(2)}) collective-permute-start(bf16[16,3200]{1,0:T(8,128)(2,1)S(1)} %get-tuple-element.38), channel_id=1, source_target_pairs={{0,2},{1,3},{2,0},{3,1},{4,6},{5,7},{6,4},{7,5},{8,10},{9,11},{10,... | collective-permute-start | bytes 307208 | tf_op jit(solution)/shard_map/ppermute | solution.py:33
  35.8 0.0 collective-permute-done.14.got_ref
  35.8 0.0 copy-start
  35.8 2.7 %grads.1 = (bf16[1,3072,256]{2,1,0:T(8,128)(2,1)}, bf16[1,3072,256]{2,1,0:T(8,128)(2,1)}, bf16[1,256,3072]{2,1,0:T(8,128)(2,1)}) custom-call(bf16[128,6912]{1,0:T(8,128)(2,1)S(1)} %get-tuple-element.40.pass_ref, bf16[128,6912]{1,0:T(8,128)(2,1)S(1)} %collective-permute-done.14.got_ref, bf16[128,768]{1,0:T(8,128)(2,1)S(1)} %get-tuple-element.41.acts_ref), custom_call_target="tpu_custom_call" | custom-call | bytes 1024 | tf_op jit(solution)/shard_map/grads/pallas_call | solution.py:372
  38.5 0.5 collective-permute-done.10.refs_1_
  38.9 1.4 %collective-permute-done.11.refs_2_ = bf16[16,3200]{1,0:T(8,128)(2,1)S(1)} collective-permute-done((bf16[16,3200]{1,0:T(8,128)(2,1)S(1)}, bf16[16,3200]{1,0:T(8,128)(2,1)S(1)}, u32[]{:S(2)}, u32[]{:S(2)}) %collective-permute-start.11) | collective-permute-done | bytes 102432 | tf_op jit(solution)/shard_map/ppermute | solution.py:33
  40.3 0.0 collective-permute-done.12.refs_3_
  40.4 0.0 collective-permute-done.13.refs_1_
  40.4 0.1 sum_far.1
  40.5 2.9 %collective-permute-start.18 = (bf16[8,3200]{1,0:T(8,128)(2,1)S(1)}, bf16[8,3200]{1,0:T(8,128)(2,1)S(1)}, u32[]{:S(2)}, u32[]{:S(2)}) collective-permute-start(bf16[8,3200]{1,0:T(8,128)(2,1)S(1)} %get-tuple-element.52), channel_id=1, source_target_pairs={{0,16},{4,20},{8,24},{12,28},{16,0},{20,4},{24,8},{28,12},{1,17},{... | collective-permute-start | bytes 153608 | tf_op jit(solution)/shard_map/ppermute | solution.py:33
  43.4 0.2 collective-permute-start.19
  43.6 0.1 sum_near.1
  43.7 1.8 %collective-permute-start.15 = (bf16[8,3200]{1,0:T(8,128)(2,1)S(1)}, bf16[8,3200]{1,0:T(8,128)(2,1)S(1)}, u32[]{:S(2)}, u32[]{:S(2)}) collective-permute-start(bf16[8,3200]{1,0:T(8,128)(2,1)S(1)} %get-tuple-element.45), channel_id=1, source_target_pairs={{0,3},{1,2},{2,1},{3,0},{4,7},{5,6},{6,5},{7,4},{8,11},{9,10},{10,... | collective-permute-start | bytes 153608 | tf_op jit(solution)/shard_map/ppermute | solution.py:33
  45.5 0.7 %collective-permute-start.16 = (bf16[8,3200]{1,0:T(8,128)(2,1)S(1)}, bf16[8,3200]{1,0:T(8,128)(2,1)S(1)}, u32[]{:S(2)}, u32[]{:S(2)}) collective-permute-start(bf16[8,3200]{1,0:T(8,128)(2,1)S(1)} %get-tuple-element.46), channel_id=1, source_target_pairs={{0,1},{1,0},{2,3},{3,2},{4,5},{5,4},{6,7},{7,6},{8,9},{9,8},{10,11... | collective-permute-start | bytes 153608 | tf_op jit(solution)/shard_map/ppermute | solution.py:33
  46.1 1.1 %collective-permute-start.17 = (bf16[8,3200]{1,0:T(8,128)(2,1)S(1)}, bf16[8,3200]{1,0:T(8,128)(2,1)S(1)}, u32[]{:S(2)}, u32[]{:S(2)}) collective-permute-start(bf16[8,3200]{1,0:T(8,128)(2,1)S(1)} %get-tuple-element.47), channel_id=1, source_target_pairs={{0,2},{1,3},{2,0},{3,1},{4,6},{5,7},{6,4},{7,5},{8,10},{9,11},{10,... | collective-permute-start | bytes 153608 | tf_op jit(solution)/shard_map/ppermute | solution.py:33
  47.2 0.0 collective-permute-done.18.refs_4_
  47.2 2.1 %collective-permute-done.19.refs_5_ = bf16[8,3200]{1,0:T(8,128)(2,1)S(1)} collective-permute-done((bf16[8,3200]{1,0:T(8,128)(2,1)S(1)}, bf16[8,3200]{1,0:T(8,128)(2,1)S(1)}, u32[]{:S(2)}, u32[]{:S(2)}) %collective-permute-start.19) | collective-permute-done | bytes 51232 | tf_op jit(solution)/shard_map/ppermute | solution.py:33
  49.3 0.0 collective-permute-done.15.refs_1_
  49.3 0.3 collective-permute-done.16.refs_2_
  49.6 0.7 %collective-permute-done.17.refs_3_ = bf16[8,3200]{1,0:T(8,128)(2,1)S(1)} collective-permute-done((bf16[8,3200]{1,0:T(8,128)(2,1)S(1)}, bf16[8,3200]{1,0:T(8,128)(2,1)S(1)}, u32[]{:S(2)}, u32[]{:S(2)}) %collective-permute-start.17) | collective-permute-done | bytes 51232 | tf_op jit(solution)/shard_map/ppermute | solution.py:33
  50.2 0.0 copy-done
  50.2 0.7 %final.1 = (bf16[8,3072]{1,0:T(8,128)(2,1)}, f32[2,8]{1,0:T(2,128)}) custom-call(f32[8,3200]{1,0:T(8,128)S(1)} %get-tuple-element.44.refs_0_, bf16[8,3200]{1,0:T(8,128)(2,1)S(1)} %collective-permute-done.15.refs_1_, bf16[8,3200]{1,0:T(8,128)(2,1)S(1)} %collective-permute-done.16.refs_2_, bf16[8,3200]{1,0:T(8,128)(2,1)S(1)} %collective-permute-done.17.refs_3_, ...), custom_call_target="tpu_custom_call" | custom-call | bytes 204800 | tf_op jit(solution)/shard_map/final/pallas_call | solution.py:407
  (2 shorter events, 0.0 us)
Async XLA Ops:
  1.5 11.5 %collective-permute-start.1 = (bf16[8,6272]{1,0:T(8,128)(2,1)S(1)}, bf16[8,6272]{1,0:T(8,128)(2,1)S(1)}, u32[]{:S(2)}, u32[]{:S(2)}) collective-permute-start(bf16[8,6272]{1,0:T(8,128)(2,1)S(1)} %pack.1), channel_id=1, source_target_pairs={{0,24},{4,28},{8,16},{12,20},{16,8},{20,12},{24,0},{28,4},{1,25},{... | collective-permute-start | bytes 301064 | tf_op jit(solution)/shard_map/ppermute | solution.py:33
  6.6 8.4 %collective-permute-start = (bf16[8,6272]{1,0:T(8,128)(2,1)S(1)}, bf16[8,6272]{1,0:T(8,128)(2,1)S(1)}, u32[]{:S(2)}, u32[]{:S(2)}) collective-permute-start(bf16[8,6272]{1,0:T(8,128)(2,1)S(1)} %pack.1), channel_id=1, source_target_pairs={{0,16},{4,20},{8,24},{12,28},{16,0},{20,4},{24,8},{28,12},{1,17},{... | collective-permute-start | bytes 301064 | tf_op jit(solution)/shard_map/ppermute | solution.py:33
  6.6 8.5 %collective-permute-start.4 = (bf16[8,6272]{1,0:T(8,128)(2,1)S(1)}, bf16[8,6272]{1,0:T(8,128)(2,1)S(1)}, u32[]{:S(2)}, u32[]{:S(2)}) collective-permute-start(bf16[8,6272]{1,0:T(8,128)(2,1)S(1)} %pack.1), channel_id=1, source_target_pairs={{0,2},{1,3},{2,0},{3,1},{4,6},{5,7},{6,4},{7,5},{8,10},{9,11},{10,... | collective-permute-start | bytes 301064 | tf_op jit(solution)/shard_map/ppermute | solution.py:33
  8.2 6.9 %collective-permute-start.3 = (bf16[8,6272]{1,0:T(8,128)(2,1)S(1)}, bf16[8,6272]{1,0:T(8,128)(2,1)S(1)}, u32[]{:S(2)}, u32[]{:S(2)}) collective-permute-start(bf16[8,6272]{1,0:T(8,128)(2,1)S(1)} %pack.1), channel_id=1, source_target_pairs={{0,1},{1,0},{2,3},{3,2},{4,5},{5,4},{6,7},{7,6},{8,9},{9,8},{10,11... | collective-permute-start | bytes 301064 | tf_op jit(solution)/shard_map/ppermute | solution.py:33
  9.7 5.5 %collective-permute-start.2 = (bf16[8,6272]{1,0:T(8,128)(2,1)S(1)}, bf16[8,6272]{1,0:T(8,128)(2,1)S(1)}, u32[]{:S(2)}, u32[]{:S(2)}) collective-permute-start(bf16[8,6272]{1,0:T(8,128)(2,1)S(1)} %pack.1), channel_id=1, source_target_pairs={{0,3},{1,2},{2,1},{3,0},{4,7},{5,6},{6,5},{7,4},{8,11},{9,10},{10,... | collective-permute-start | bytes 301064 | tf_op jit(solution)/shard_map/ppermute | solution.py:33
  15.2 8.0 %collective-permute-start.9 = (bf16[3072,768]{1,0:T(8,128)(2,1)S(1)}, bf16[3072,768]{1,0:T(8,128)(2,1)S(1)}, u32[]{:S(2)}, u32[]{:S(2)}) collective-permute-start(bf16[3072,768]{1,0:T(8,128)(2,1)S(1)} %weights.1.own_ref.refs_6_), channel_id=1, source_target_pairs={{0,4},{4,0},{8,12},{12,8},{16,20},{20,16},{24,28},{28,24},{1,5},{5... | collective-permute-start | bytes 14155784 | tf_op jit(solution)/shard_map/ppermute | solution.py:33
  15.3 13.1 %collective-permute-start.5 = (bf16[32,6272]{1,0:T(8,128)(2,1)S(1)}, bf16[32,6272]{1,0:T(8,128)(2,1)S(1)}, u32[]{:S(2)}, u32[]{:S(2)}) collective-permute-start(bf16[32,6272]{1,0:T(8,128)(2,1)S(1)} %pad_maximum_fusion.refs_0_), channel_id=1, source_target_pairs={{0,8},{4,12},{8,0},{12,4},{16,24},{20,28},{24,16},{28,20},{1,9},{5... | collective-permute-start | bytes 1204232 | tf_op jit(solution)/shard_map/ppermute | solution.py:33
  16.2 8.9 %collective-permute-start.8 = (bf16[16,6272]{1,0:T(8,128)(2,1)S(1)}, bf16[16,6272]{1,0:T(8,128)(2,1)S(1)}, u32[]{:S(2)}, u32[]{:S(2)}) collective-permute-start(bf16[16,6272]{1,0:T(8,128)(2,1)S(1)} %pad_maximum_fusion.1.refs_1_), channel_id=1, source_target_pairs={{0,3},{1,2},{2,1},{3,0},{4,7},{5,6},{6,5},{7,4},{8,11},{9,10},{10,... | collective-permute-start | bytes 602120 | tf_op jit(solution)/shard_map/ppermute | solution.py:33
  17.8 10.6 %collective-permute-start.7 = (bf16[16,6272]{1,0:T(8,128)(2,1)S(1)}, bf16[16,6272]{1,0:T(8,128)(2,1)S(1)}, u32[]{:S(2)}, u32[]{:S(2)}) collective-permute-start(bf16[16,6272]{1,0:T(8,128)(2,1)S(1)} %pad_maximum_fusion.1.refs_1_), channel_id=1, source_target_pairs={{0,2},{1,3},{2,0},{3,1},{4,6},{5,7},{6,4},{7,5},{8,10},{9,11},{10,... | collective-permute-start | bytes 602120 | tf_op jit(solution)/shard_map/ppermute | solution.py:33
  18.4 10.1 %collective-permute-start.6 = (bf16[16,6272]{1,0:T(8,128)(2,1)S(1)}, bf16[16,6272]{1,0:T(8,128)(2,1)S(1)}, u32[]{:S(2)}, u32[]{:S(2)}) collective-permute-start(bf16[16,6272]{1,0:T(8,128)(2,1)S(1)} %pad_maximum_fusion.1.refs_1_), channel_id=1, source_target_pairs={{0,1},{1,0},{2,3},{3,2},{4,5},{5,4},{6,7},{7,6},{8,9},{9,8},{10,11... | collective-permute-start | bytes 602120 | tf_op jit(solution)/shard_map/ppermute | solution.py:33
  30.9 4.9 %collective-permute-start.14 = (bf16[128,6912]{1,0:T(8,128)(2,1)S(1)}, bf16[128,6912]{1,0:T(8,128)(2,1)S(1)}, u32[]{:S(2)}, u32[]{:S(2)}) collective-permute-start(bf16[128,6912]{1,0:T(8,128)(2,1)S(1)} %get-tuple-element.40.pass_ref), channel_id=1, source_target_pairs={{0,4},{4,0},{8,12},{12,8},{16,20},{20,16},{24,28},{28,24},{1,5},{5... | collective-permute-start | bytes 5308424 | tf_op jit(solution)/shard_map/ppermute | solution.py:33
  31.0 9.4 %collective-permute-start.13 = (bf16[32,3200]{1,0:T(8,128)(2,1)S(1)}, bf16[32,3200]{1,0:T(8,128)(2,1)S(1)}, u32[]{:S(2)}, u32[]{:S(2)}) collective-permute-start(bf16[32,3200]{1,0:T(8,128)(2,1)S(1)} %get-tuple-element.39), channel_id=1, source_target_pairs={{0,8},{4,12},{8,0},{12,4},{16,24},{20,28},{24,16},{28,20},{1,9},{5... | collective-permute-start | bytes 614408 | tf_op jit(solution)/shard_map/ppermute | solution.py:33
  32.3 6.6 %collective-permute-start.10 = (bf16[16,3200]{1,0:T(8,128)(2,1)S(1)}, bf16[16,3200]{1,0:T(8,128)(2,1)S(1)}, u32[]{:S(2)}, u32[]{:S(2)}) collective-permute-start(bf16[16,3200]{1,0:T(8,128)(2,1)S(1)} %get-tuple-element.36), channel_id=1, source_target_pairs={{0,3},{1,2},{2,1},{3,0},{4,7},{5,6},{6,5},{7,4},{8,11},{9,10},{10,... | collective-permute-start | bytes 307208 | tf_op jit(solution)/shard_map/ppermute | solution.py:33
  34.0 6.3 %collective-permute-start.11 = (bf16[16,3200]{1,0:T(8,128)(2,1)S(1)}, bf16[16,3200]{1,0:T(8,128)(2,1)S(1)}, u32[]{:S(2)}, u32[]{:S(2)}) collective-permute-start(bf16[16,3200]{1,0:T(8,128)(2,1)S(1)} %get-tuple-element.37), channel_id=1, source_target_pairs={{0,1},{1,0},{2,3},{3,2},{4,5},{5,4},{6,7},{7,6},{8,9},{9,8},{10,11... | collective-permute-start | bytes 307208 | tf_op jit(solution)/shard_map/ppermute | solution.py:33
  35.2 5.2 %collective-permute-start.12 = (bf16[16,3200]{1,0:T(8,128)(2,1)S(1)}, bf16[16,3200]{1,0:T(8,128)(2,1)S(1)}, u32[]{:S(2)}, u32[]{:S(2)}) collective-permute-start(bf16[16,3200]{1,0:T(8,128)(2,1)S(1)} %get-tuple-element.38), channel_id=1, source_target_pairs={{0,2},{1,3},{2,0},{3,1},{4,6},{5,7},{6,4},{7,5},{8,10},{9,11},{10,... | collective-permute-start | bytes 307208 | tf_op jit(solution)/shard_map/ppermute | solution.py:33
  35.8 14.4 %copy-start = (s32[8,2]{0,1:T(2,128)S(1)}, s32[8,2]{0,1:T(2,128)}, u32[]{:S(2)}) copy-start(s32[8,2]{0,1:T(2,128)} %param.9) | copy-start | bytes 196
  40.5 6.7 %collective-permute-start.18 = (bf16[8,3200]{1,0:T(8,128)(2,1)S(1)}, bf16[8,3200]{1,0:T(8,128)(2,1)S(1)}, u32[]{:S(2)}, u32[]{:S(2)}) collective-permute-start(bf16[8,3200]{1,0:T(8,128)(2,1)S(1)} %get-tuple-element.52), channel_id=1, source_target_pairs={{0,16},{4,20},{8,24},{12,28},{16,0},{20,4},{24,8},{28,12},{1,17},{... | collective-permute-start | bytes 153608 | tf_op jit(solution)/shard_map/ppermute | solution.py:33
  43.4 5.9 %collective-permute-start.19 = (bf16[8,3200]{1,0:T(8,128)(2,1)S(1)}, bf16[8,3200]{1,0:T(8,128)(2,1)S(1)}, u32[]{:S(2)}, u32[]{:S(2)}) collective-permute-start(bf16[8,3200]{1,0:T(8,128)(2,1)S(1)} %get-tuple-element.53), channel_id=1, source_target_pairs={{0,24},{4,28},{8,16},{12,20},{16,8},{20,12},{24,0},{28,4},{1,25},{... | collective-permute-start | bytes 153608 | tf_op jit(solution)/shard_map/ppermute | solution.py:33
  43.7 5.6 %collective-permute-start.15 = (bf16[8,3200]{1,0:T(8,128)(2,1)S(1)}, bf16[8,3200]{1,0:T(8,128)(2,1)S(1)}, u32[]{:S(2)}, u32[]{:S(2)}) collective-permute-start(bf16[8,3200]{1,0:T(8,128)(2,1)S(1)} %get-tuple-element.45), channel_id=1, source_target_pairs={{0,3},{1,2},{2,1},{3,0},{4,7},{5,6},{6,5},{7,4},{8,11},{9,10},{10,... | collective-permute-start | bytes 153608 | tf_op jit(solution)/shard_map/ppermute | solution.py:33
  45.5 4.1 %collective-permute-start.16 = (bf16[8,3200]{1,0:T(8,128)(2,1)S(1)}, bf16[8,3200]{1,0:T(8,128)(2,1)S(1)}, u32[]{:S(2)}, u32[]{:S(2)}) collective-permute-start(bf16[8,3200]{1,0:T(8,128)(2,1)S(1)} %get-tuple-element.46), channel_id=1, source_target_pairs={{0,1},{1,0},{2,3},{3,2},{4,5},{5,4},{6,7},{7,6},{8,9},{9,8},{10,11... | collective-permute-start | bytes 153608 | tf_op jit(solution)/shard_map/ppermute | solution.py:33
  46.1 4.1 %collective-permute-start.17 = (bf16[8,3200]{1,0:T(8,128)(2,1)S(1)}, bf16[8,3200]{1,0:T(8,128)(2,1)S(1)}, u32[]{:S(2)}, u32[]{:S(2)}) collective-permute-start(bf16[8,3200]{1,0:T(8,128)(2,1)S(1)} %get-tuple-element.47), channel_id=1, source_target_pairs={{0,2},{1,3},{2,0},{3,1},{4,6},{5,7},{6,4},{7,5},{8,10},{9,11},{10,... | collective-permute-start | bytes 153608 | tf_op jit(solution)/shard_map/ppermute | solution.py:33

commit v7 on v6

--- a/solution.py
+++ b/solution.py
@@ -11,6 +11,8 @@
 MIB = 1024 * 1024
 VMEM = 28 * MIB
 LARGEST = 256
+COST = 4 * 10**9
+LONG = ("sum_far", "sum_along")
 PARTS = 4
 BF = jnp.bfloat16
 F32 = jnp.float32
@@ -212,13 +214,12 @@
     rows = keep.shape[0] // pieces
     dims = (rows, keep.shape[1])
     outs = [shape(dims, F32 if stays and i == 0 else BF) for i in range(pieces)]
-    moved = 2 * keep.size * (2 + len(parts))
     return call(
         functools.partial(sum_body, experts, len(parts), stays),
         outs,
         name,
-        keep.size * len(parts),
-        moved,
+        COST if name in LONG else 0,
+        1024,
     )(keep, *parts)
 
 
@@ -324,8 +325,9 @@
         return sum_plain(total, parts, pieces, stays, experts)
 
     others = sorted(range(1, experts), key=lambda d: -d.bit_count())
-    along = [swap(block, "section", 2 * k) for k in range(groups - 1, 1, -1)][::-1]
-    near = [swap(block, "expert", d) for d in others]
+    along = [swap(block, "section", 2 * k) for k in range(groups - 1, 1, -1)]
+    close = others[::-1]
+    near = [swap(block, "expert", d) for d in close]
     far_block = jnp.concatenate(along, axis=0)
     near_block = jnp.concatenate([block] + near, axis=0)
 
@@ -399,11 +401,14 @@
         swap(part, "expert", d) for d, part in zip(others, [split[-1], *split[3:-1]])
     ]
     beside = swap(split[2], "section", 2)
-    crossed, beside, grad_gate = lax.optimization_barrier((crossed, beside, grad_gate))
+    crossed, grad_gate = lax.optimization_barrier((crossed, grad_gate))
+    onward = added(split[1], crossed, groups - 2, False, "sum_far")
     own, *sideways = added(split[0], [beside], experts, True, "sum_near")
-    onward = added(split[1], crossed, groups - 2, False, "sum_far")
-    parts = [swap(part, "expert", d) for d, part in zip(others, sideways)]
-    parts += [swap(part, "section", 2 * k) for k, part in enumerate(onward, 2)]
+    ahead = dict(zip(range(groups - 1, 1, -1), onward))
+    along = [swap(ahead[k], "section", 2 * k) for k in range(2, groups)]
+    (own,) = added(own, along, 1, True, "sum_along")
+    around = dict(zip(close, sideways))
+    parts = [swap(around[d], "expert", d) for d in others]
     grad_tokens, grad_gates = call(
         functools.partial(final_body, experts, len(parts)),
         [shape((count, features), BF), shape(ids.shape, F32)],

time: 51.2 us -> 50.8 us (level)
  waiting for transfers between devices: 14 us -> 13.1 us
    ppermute x20, waiting for transfers between devices: 14 us -> 13.1 us  [swap(): return lax.ppermute(value, axis, [(i, i ^ mask) for i in range(size)])]
    ppermute x20, starting transfers between devices: 24.6 us -> 25.1 us  [swap(): return lax.ppermute(value, axis, [(i, i ^ mask) for i in range(size)])]
  transfers between devices with their start and end apart: 20 -> 20, of which waited for: 9 -> 12; matrix products, arithmetic and copies ran while one was open for 0% -> 0% of each run, Pallas kernels for 15% -> 15%
where the time goes in v7:
time: 50.8 us; the launch traced here: 50.6 us
  starting transfers between devices  25.1 us (49%)
  waiting for transfers between devices  13.1 us (26%)
  Pallas kernels  11.6 us (23%)
  between operations  0.73 us (1%)
    ppermute x20, starting transfers between devices, swap(): return lax.ppermute(value, axis, [(i, i ^ mask) for i in range(size)])  25.1 us
    ppermute x20, waiting for transfers between devices, swap(): return lax.ppermute(value, axis, [(i, i ^ mask) for i in range(size)])  13.1 us
    pallas_call x1, Pallas kernels, local(): pl.pallas_call(weights_body, out_shape=shape((features, 3 * units), BF),...  2.84 us
    pallas_call x1, Pallas kernels, local(): pl.pallas_call(functools.partial(grads_body, PARTS), out_shape=[shape(w.s...  2.68 us
    pallas_call x1, Pallas kernels, local(): pl.pallas_call(functools.partial(expert_body, experts, len(pieces)), out_...  2.46 us
    pallas_call x1, Pallas kernels, local(): call(back_body, shape((4 * units, features), BF), 'back')  1.8 us
  transfers between devices with their start and end apart: 20, of which 12 were waited for; matrix products, arithmetic and copies ran while one was open for 0% of the time, Pallas kernels for 15%

profile of v7, /device:TPU:0, one launch (start us, length us, event | category | flops | bytes accessed | tf_op | source)
XLA Modules:
  0.0 50.6 jit_solution(9426701224079313221)
XLA Ops:
  0.6 0.9 %pack.1 = bf16[8,6272]{1,0:T(8,128)(2,1)S(1)} custom-call(bf16[8,3072]{1,0:T(8,128)(2,1)} %x_hbm.1, bf16[8,3072]{1,0:T(8,128)(2,1)} %dy_hbm.1, s32[2,8]{1,0:T(2,128)} %bitcast.3, bf16[2,8]{1,0:T(2,128)(2,1)} %bitcast.5), custom_call_target="tpu_custom_call" | custom-call | tf_op jit(solution)/shard_map/pack/pallas_call | solution.py:309
  1.5 4.1 %collective-permute-start.1 = (bf16[8,6272]{1,0:T(8,128)(2,1)S(1)}, bf16[8,6272]{1,0:T(8,128)(2,1)S(1)}, u32[]{:S(2)}, u32[]{:S(2)}) collective-permute-start(bf16[8,6272]{1,0:T(8,128)(2,1)S(1)} %pack.1), channel_id=1, source_target_pairs={{0,16},{4,20},{8,24},{12,28},{16,0},{20,4},{24,8},{28,12},{1,17},{... | collective-permute-start | bytes 301064 | tf_op jit(solution)/shard_map/ppermute | solution.py:35
  5.6 1.3 %collective-permute-start = (bf16[8,6272]{1,0:T(8,128)(2,1)S(1)}, bf16[8,6272]{1,0:T(8,128)(2,1)S(1)}, u32[]{:S(2)}, u32[]{:S(2)}) collective-permute-start(bf16[8,6272]{1,0:T(8,128)(2,1)S(1)} %pack.1), channel_id=1, source_target_pairs={{0,24},{4,28},{8,16},{12,20},{16,8},{20,12},{24,0},{28,4},{1,25},{... | collective-permute-start | bytes 301064 | tf_op jit(solution)/shard_map/ppermute | solution.py:35
  7.0 2.4 %collective-permute-start.4 = (bf16[8,6272]{1,0:T(8,128)(2,1)S(1)}, bf16[8,6272]{1,0:T(8,128)(2,1)S(1)}, u32[]{:S(2)}, u32[]{:S(2)}) collective-permute-start(bf16[8,6272]{1,0:T(8,128)(2,1)S(1)} %pack.1), channel_id=1, source_target_pairs={{0,3},{1,2},{2,1},{3,0},{4,7},{5,6},{6,5},{7,4},{8,11},{9,10},{10,... | collective-permute-start | bytes 301064 | tf_op jit(solution)/shard_map/ppermute | solution.py:35
  9.4 0.5 %collective-permute-start.3 = (bf16[8,6272]{1,0:T(8,128)(2,1)S(1)}, bf16[8,6272]{1,0:T(8,128)(2,1)S(1)}, u32[]{:S(2)}, u32[]{:S(2)}) collective-permute-start(bf16[8,6272]{1,0:T(8,128)(2,1)S(1)} %pack.1), channel_id=1, source_target_pairs={{0,1},{1,0},{2,3},{3,2},{4,5},{5,4},{6,7},{7,6},{8,9},{9,8},{10,11... | collective-permute-start | bytes 301064 | tf_op jit(solution)/shard_map/ppermute | solution.py:35
  10.0 0.5 %collective-permute-start.2 = (bf16[8,6272]{1,0:T(8,128)(2,1)S(1)}, bf16[8,6272]{1,0:T(8,128)(2,1)S(1)}, u32[]{:S(2)}, u32[]{:S(2)}) collective-permute-start(bf16[8,6272]{1,0:T(8,128)(2,1)S(1)} %pack.1), channel_id=1, source_target_pairs={{0,2},{1,3},{2,0},{3,1},{4,6},{5,7},{6,4},{7,5},{8,10},{9,11},{10,... | collective-permute-start | bytes 301064 | tf_op jit(solution)/shard_map/ppermute | solution.py:35
  10.5 2.8 %weights.1.own_ref.refs_6_ = bf16[3072,768]{1,0:T(8,128)(2,1)S(1)} custom-call(bf16[1,3072,256]{2,1,0:T(8,128)(2,1)} %gate_hbm.1, bf16[1,3072,256]{2,1,0:T(8,128)(2,1)} %up_hbm.1, bf16[1,256,3072]{2,1,0:T(8,128)(2,1)} %down_hbm.1), custom_call_target="tpu_custom_call" | custom-call | bytes 1024 | tf_op jit(solution)/shard_map/weights/pallas_call | solution.py:335
  13.3 0.3 collective-permute-done.1
  13.6 0.0 collective-permute-done
  13.6 0.0 collective-permute-done.4
  13.6 0.6 %collective-permute-done.3 = bf16[8,6272]{1,0:T(8,128)(2,1)S(1)} collective-permute-done((bf16[8,6272]{1,0:T(8,128)(2,1)S(1)}, bf16[8,6272]{1,0:T(8,128)(2,1)S(1)}, u32[]{:S(2)}, u32[]{:S(2)}) %collective-permute-start.3) | collective-permute-done | bytes 100384 | tf_op jit(solution)/shard_map/ppermute | solution.py:35
  14.3 0.3 collective-permute-done.2
  14.6 0.1 collective-permute-start.9
  14.7 1.2 %collective-permute-start.5 = (bf16[32,6272]{1,0:T(8,128)(2,1)S(1)}, bf16[32,6272]{1,0:T(8,128)(2,1)S(1)}, u32[]{:S(2)}, u32[]{:S(2)}) collective-permute-start(bf16[32,6272]{1,0:T(8,128)(2,1)S(1)} %pad_maximum_fusion.refs_0_), channel_id=1, source_target_pairs={{0,8},{4,12},{8,0},{12,4},{16,24},{20,28},{24,16},{28,20},{1,9},{5... | collective-permute-start | bytes 1204232 | tf_op jit(solution)/shard_map/ppermute | solution.py:35
  15.9 2.4 %collective-permute-start.8 = (bf16[16,6272]{1,0:T(8,128)(2,1)S(1)}, bf16[16,6272]{1,0:T(8,128)(2,1)S(1)}, u32[]{:S(2)}, u32[]{:S(2)}) collective-permute-start(bf16[16,6272]{1,0:T(8,128)(2,1)S(1)} %pad_maximum_fusion.1.refs_1_), channel_id=1, source_target_pairs={{0,3},{1,2},{2,1},{3,0},{4,7},{5,6},{6,5},{7,4},{8,11},{9,10},{10,... | collective-permute-start | bytes 602120 | tf_op jit(solution)/shard_map/ppermute | solution.py:35
  18.3 0.5 %collective-permute-start.7 = (bf16[16,6272]{1,0:T(8,128)(2,1)S(1)}, bf16[16,6272]{1,0:T(8,128)(2,1)S(1)}, u32[]{:S(2)}, u32[]{:S(2)}) collective-permute-start(bf16[16,6272]{1,0:T(8,128)(2,1)S(1)} %pad_maximum_fusion.1.refs_1_), channel_id=1, source_target_pairs={{0,2},{1,3},{2,0},{3,1},{4,6},{5,7},{6,4},{7,5},{8,10},{9,11},{10,... | collective-permute-start | bytes 602120 | tf_op jit(solution)/shard_map/ppermute | solution.py:35
  18.8 0.5 %collective-permute-start.6 = (bf16[16,6272]{1,0:T(8,128)(2,1)S(1)}, bf16[16,6272]{1,0:T(8,128)(2,1)S(1)}, u32[]{:S(2)}, u32[]{:S(2)}) collective-permute-start(bf16[16,6272]{1,0:T(8,128)(2,1)S(1)} %pad_maximum_fusion.1.refs_1_), channel_id=1, source_target_pairs={{0,1},{1,0},{2,3},{3,2},{4,5},{5,4},{6,7},{7,6},{8,9},{9,8},{10,11... | collective-permute-start | bytes 602120 | tf_op jit(solution)/shard_map/ppermute | solution.py:35
  19.4 3.2 %collective-permute-done.9.other_ref.refs_7_ = bf16[3072,768]{1,0:T(8,128)(2,1)S(1)} collective-permute-done((bf16[3072,768]{1,0:T(8,128)(2,1)S(1)}, bf16[3072,768]{1,0:T(8,128)(2,1)S(1)}, u32[]{:S(2)}, u32[]{:S(2)}) %collective-permute-start.9) | collective-permute-done | bytes 4718624 | tf_op jit(solution)/shard_map/ppermute | solution.py:35
  22.6 1.8 %back.1.refs_8_ = bf16[1024,3072]{1,0:T(8,128)(2,1)S(1)} custom-call(bf16[3072,768]{1,0:T(8,128)(2,1)S(1)} %weights.1.own_ref.refs_6_, bf16[3072,768]{1,0:T(8,128)(2,1)S(1)} %collective-permute-done.9.other_ref.refs_7_), custom_call_target="tpu_custom_call" | custom-call | tf_op jit(solution)/shard_map/back/pallas_call | solution.py:356
  24.4 0.2 collective-permute-done.8.refs_5_
  24.7 3.5 %collective-permute-done.7.refs_4_ = bf16[16,6272]{1,0:T(8,128)(2,1)S(1)} collective-permute-done((bf16[16,6272]{1,0:T(8,128)(2,1)S(1)}, bf16[16,6272]{1,0:T(8,128)(2,1)S(1)}, u32[]{:S(2)}, u32[]{:S(2)}) %collective-permute-start.7) | collective-permute-done | bytes 200736 | tf_op jit(solution)/shard_map/ppermute | solution.py:35
  28.1 0.1 collective-permute-done.6.refs_3_
  28.2 0.0 collective-permute-done.5.refs_2_
  28.2 2.5 %expert.1 = (f32[32,3200]{1,0:T(8,128)S(1)}, f32[16,3200]{1,0:T(8,128)S(1)}, bf16[32,3200]{1,0:T(8,128)(2,1)S(1)}, bf16[16,3200]{1,0:T(8,128)(2,1)S(1)}, bf16[16...) custom-call(bf16[32,6272]{1,0:T(8,128)(2,1)S(1)} %pad_maximum_fusion, ...), custom_call_target="tpu_custom_call" | custom-call | bytes 1024 | tf_op jit(solution)/shard_map/expert/pallas_call | solution.py:357
  30.7 0.1 collective-permute-start.14
  30.8 1.7 %collective-permute-start.11 = (bf16[16,3200]{1,0:T(8,128)(2,1)S(1)}, bf16[16,3200]{1,0:T(8,128)(2,1)S(1)}, u32[]{:S(2)}, u32[]{:S(2)}) collective-permute-start(bf16[16,3200]{1,0:T(8,128)(2,1)S(1)} %get-tuple-element.38), channel_id=1, source_target_pairs={{0,3},{1,2},{2,1},{3,0},{4,7},{5,6},{6,5},{7,4},{8,11},{9,10},{10,... | collective-permute-start | bytes 307208 | tf_op jit(solution)/shard_map/ppermute | solution.py:35
  32.5 1.2 %collective-permute-start.12 = (bf16[16,3200]{1,0:T(8,128)(2,1)S(1)}, bf16[16,3200]{1,0:T(8,128)(2,1)S(1)}, u32[]{:S(2)}, u32[]{:S(2)}) collective-permute-start(bf16[16,3200]{1,0:T(8,128)(2,1)S(1)} %get-tuple-element.39), channel_id=1, source_target_pairs={{0,1},{1,0},{2,3},{3,2},{4,5},{5,4},{6,7},{7,6},{8,9},{9,8},{10,11... | collective-permute-start | bytes 307208 | tf_op jit(solution)/shard_map/ppermute | solution.py:35
  33.7 0.6 %collective-permute-start.13 = (bf16[16,3200]{1,0:T(8,128)(2,1)S(1)}, bf16[16,3200]{1,0:T(8,128)(2,1)S(1)}, u32[]{:S(2)}, u32[]{:S(2)}) collective-permute-start(bf16[16,3200]{1,0:T(8,128)(2,1)S(1)} %get-tuple-element.40), channel_id=1, source_target_pairs={{0,2},{1,3},{2,0},{3,1},{4,6},{5,7},{6,4},{7,5},{8,10},{9,11},{10,... | collective-permute-start | bytes 307208 | tf_op jit(solution)/shard_map/ppermute | solution.py:35
  34.3 0.8 %collective-permute-start.10 = (bf16[32,3200]{1,0:T(8,128)(2,1)S(1)}, bf16[32,3200]{1,0:T(8,128)(2,1)S(1)}, u32[]{:S(2)}, u32[]{:S(2)}) collective-permute-start(bf16[32,3200]{1,0:T(8,128)(2,1)S(1)} %get-tuple-element.35), channel_id=1, source_target_pairs={{0,8},{4,12},{8,0},{12,4},{16,24},{20,28},{24,16},{28,20},{1,9},{5... | collective-permute-start | bytes 614408 | tf_op jit(solution)/shard_map/ppermute | solution.py:35
  35.2 0.0 collective-permute-done.14.got_ref
  35.2 2.7 %grads.1 = (bf16[1,3072,256]{2,1,0:T(8,128)(2,1)}, bf16[1,3072,256]{2,1,0:T(8,128)(2,1)}, bf16[1,256,3072]{2,1,0:T(8,128)(2,1)}) custom-call(bf16[128,6912]{1,0:T(8,128)(2,1)S(1)} %get-tuple-element.41.pass_ref, bf16[128,6912]{1,0:T(8,128)(2,1)S(1)} %collective-permute-done.14.got_ref, bf16[128,768]{1,0:T(8,128)(2,1)S(1)} %get-tuple-element.42.acts_ref), custom_call_target="tpu_custom_call" | custom-call | bytes 1024 | tf_op jit(solution)/shard_map/grads/pallas_call | solution.py:374
  37.9 0.0 collective-permute-done.11.refs_1_
  37.9 1.3 %collective-permute-done.12.refs_2_ = bf16[16,3200]{1,0:T(8,128)(2,1)S(1)} collective-permute-done((bf16[16,3200]{1,0:T(8,128)(2,1)S(1)}, bf16[16,3200]{1,0:T(8,128)(2,1)S(1)}, u32[]{:S(2)}, u32[]{:S(2)}) %collective-permute-start.12) | collective-permute-done | bytes 102432 | tf_op jit(solution)/shard_map/ppermute | solution.py:35
  39.1 0.0 collective-permute-done.13.refs_3_
  39.2 0.1 sum_far.1
  39.3 2.2 %collective-permute-start.15 = (bf16[8,3200]{1,0:T(8,128)(2,1)S(1)}, bf16[8,3200]{1,0:T(8,128)(2,1)S(1)}, u32[]{:S(2)}, u32[]{:S(2)}) collective-permute-start(bf16[8,3200]{1,0:T(8,128)(2,1)S(1)} %get-tuple-element.47), channel_id=1, source_target_pairs={{0,16},{4,20},{8,24},{12,28},{16,0},{20,4},{24,8},{28,12},{1,17},{... | collective-permute-start | bytes 153608 | tf_op jit(solution)/shard_map/ppermute | solution.py:35
  41.5 1.3 %collective-permute-start.16 = (bf16[8,3200]{1,0:T(8,128)(2,1)S(1)}, bf16[8,3200]{1,0:T(8,128)(2,1)S(1)}, u32[]{:S(2)}, u32[]{:S(2)}) collective-permute-start(bf16[8,3200]{1,0:T(8,128)(2,1)S(1)} %get-tuple-element.48), channel_id=1, source_target_pairs={{0,24},{4,28},{8,16},{12,20},{16,8},{20,12},{24,0},{28,4},{1,25},{... | collective-permute-start | bytes 153608 | tf_op jit(solution)/shard_map/ppermute | solution.py:35
  42.8 0.0 collective-permute-done.10.refs_1_
  42.8 0.1 sum_near.1
  42.9 1.7 %collective-permute-start.17 = (bf16[8,3200]{1,0:T(8,128)(2,1)S(1)}, bf16[8,3200]{1,0:T(8,128)(2,1)S(1)}, u32[]{:S(2)}, u32[]{:S(2)}) collective-permute-start(bf16[8,3200]{1,0:T(8,128)(2,1)S(1)} %get-tuple-element.49), channel_id=1, source_target_pairs={{0,3},{1,2},{2,1},{3,0},{4,7},{5,6},{6,5},{7,4},{8,11},{9,10},{10,... | collective-permute-start | bytes 153608 | tf_op jit(solution)/shard_map/ppermute | solution.py:35
  44.5 1.2 %collective-permute-start.18 = (bf16[8,3200]{1,0:T(8,128)(2,1)S(1)}, bf16[8,3200]{1,0:T(8,128)(2,1)S(1)}, u32[]{:S(2)}, u32[]{:S(2)}) collective-permute-start(bf16[8,3200]{1,0:T(8,128)(2,1)S(1)} %get-tuple-element.50), channel_id=1, source_target_pairs={{0,1},{1,0},{2,3},{3,2},{4,5},{5,4},{6,7},{7,6},{8,9},{9,8},{10,11... | collective-permute-start | bytes 153608 | tf_op jit(solution)/shard_map/ppermute | solution.py:35
  45.8 0.6 %collective-permute-start.19 = (bf16[8,3200]{1,0:T(8,128)(2,1)S(1)}, bf16[8,3200]{1,0:T(8,128)(2,1)S(1)}, u32[]{:S(2)}, u32[]{:S(2)}) collective-permute-start(bf16[8,3200]{1,0:T(8,128)(2,1)S(1)} %get-tuple-element.51), channel_id=1, source_target_pairs={{0,2},{1,3},{2,0},{3,1},{4,6},{5,7},{6,4},{7,5},{8,10},{9,11},{10,... | collective-permute-start | bytes 153608 | tf_op jit(solution)/shard_map/ppermute | solution.py:35
  46.4 0.0 collective-permute-done.15.refs_1_
  46.4 1.0 %collective-permute-done.16.refs_2_ = bf16[8,3200]{1,0:T(8,128)(2,1)S(1)} collective-permute-done((bf16[8,3200]{1,0:T(8,128)(2,1)S(1)}, bf16[8,3200]{1,0:T(8,128)(2,1)S(1)}, u32[]{:S(2)}, u32[]{:S(2)}) %collective-permute-start.16) | collective-permute-done | bytes 51232 | tf_op jit(solution)/shard_map/ppermute | solution.py:35
  47.4 0.0 copy-start
  47.4 1.1 %collective-permute-done.17.refs_1_ = bf16[8,3200]{1,0:T(8,128)(2,1)S(1)} collective-permute-done((bf16[8,3200]{1,0:T(8,128)(2,1)S(1)}, bf16[8,3200]{1,0:T(8,128)(2,1)S(1)}, u32[]{:S(2)}, u32[]{:S(2)}) %collective-permute-start.17) | collective-permute-done | bytes 51232 | tf_op jit(solution)/shard_map/ppermute | solution.py:35
  48.5 0.1 collective-permute-done.18.refs_2_
  48.6 1.2 %collective-permute-done.19.refs_3_ = bf16[8,3200]{1,0:T(8,128)(2,1)S(1)} collective-permute-done((bf16[8,3200]{1,0:T(8,128)(2,1)S(1)}, bf16[8,3200]{1,0:T(8,128)(2,1)S(1)}, u32[]{:S(2)}, u32[]{:S(2)}) %collective-permute-start.19) | collective-permute-done | bytes 51232 | tf_op jit(solution)/shard_map/ppermute | solution.py:35
  49.9 0.0 copy-done
  49.9 0.7 %final.1 = (bf16[8,3072]{1,0:T(8,128)(2,1)}, f32[2,8]{1,0:T(2,128)}) custom-call(f32[8,3200]{1,0:T(8,128)S(1)} %sum_along.1.refs_0_, bf16[8,3200]{1,0:T(8,128)(2,1)S(1)} %collective-permute-done.17.refs_1_, bf16[8,3200]{1,0:T(8,128)(2,1)S(1)} %collective-permute-done.18.refs_2_, bf16[8,3200]{1,0:T(8,128)(2,1)S(1)} %collective-permute-done.19.refs_3_, ...), custom_call_target="tpu_custom_call" | custom-call | bytes 204800 | tf_op jit(solution)/shard_map/final/pallas_call | solution.py:412
  (3 shorter events, 0.1 us)
Async XLA Ops:
  1.5 12.1 %collective-permute-start.1 = (bf16[8,6272]{1,0:T(8,128)(2,1)S(1)}, bf16[8,6272]{1,0:T(8,128)(2,1)S(1)}, u32[]{:S(2)}, u32[]{:S(2)}) collective-permute-start(bf16[8,6272]{1,0:T(8,128)(2,1)S(1)} %pack.1), channel_id=1, source_target_pairs={{0,16},{4,20},{8,24},{12,28},{16,0},{20,4},{24,8},{28,12},{1,17},{... | collective-permute-start | bytes 301064 | tf_op jit(solution)/shard_map/ppermute | solution.py:35
  5.6 8.0 %collective-permute-start = (bf16[8,6272]{1,0:T(8,128)(2,1)S(1)}, bf16[8,6272]{1,0:T(8,128)(2,1)S(1)}, u32[]{:S(2)}, u32[]{:S(2)}) collective-permute-start(bf16[8,6272]{1,0:T(8,128)(2,1)S(1)} %pack.1), channel_id=1, source_target_pairs={{0,24},{4,28},{8,16},{12,20},{16,8},{20,12},{24,0},{28,4},{1,25},{... | collective-permute-start | bytes 301064 | tf_op jit(solution)/shard_map/ppermute | solution.py:35
  7.0 6.6 %collective-permute-start.4 = (bf16[8,6272]{1,0:T(8,128)(2,1)S(1)}, bf16[8,6272]{1,0:T(8,128)(2,1)S(1)}, u32[]{:S(2)}, u32[]{:S(2)}) collective-permute-start(bf16[8,6272]{1,0:T(8,128)(2,1)S(1)} %pack.1), channel_id=1, source_target_pairs={{0,3},{1,2},{2,1},{3,0},{4,7},{5,6},{6,5},{7,4},{8,11},{9,10},{10,... | collective-permute-start | bytes 301064 | tf_op jit(solution)/shard_map/ppermute | solution.py:35
  9.4 4.8 %collective-permute-start.3 = (bf16[8,6272]{1,0:T(8,128)(2,1)S(1)}, bf16[8,6272]{1,0:T(8,128)(2,1)S(1)}, u32[]{:S(2)}, u32[]{:S(2)}) collective-permute-start(bf16[8,6272]{1,0:T(8,128)(2,1)S(1)} %pack.1), channel_id=1, source_target_pairs={{0,1},{1,0},{2,3},{3,2},{4,5},{5,4},{6,7},{7,6},{8,9},{9,8},{10,11... | collective-permute-start | bytes 301064 | tf_op jit(solution)/shard_map/ppermute | solution.py:35
  10.0 4.6 %collective-permute-start.2 = (bf16[8,6272]{1,0:T(8,128)(2,1)S(1)}, bf16[8,6272]{1,0:T(8,128)(2,1)S(1)}, u32[]{:S(2)}, u32[]{:S(2)}) collective-permute-start(bf16[8,6272]{1,0:T(8,128)(2,1)S(1)} %pack.1), channel_id=1, source_target_pairs={{0,2},{1,3},{2,0},{3,1},{4,6},{5,7},{6,4},{7,5},{8,10},{9,11},{10,... | collective-permute-start | bytes 301064 | tf_op jit(solution)/shard_map/ppermute | solution.py:35
  14.6 8.0 %collective-permute-start.9 = (bf16[3072,768]{1,0:T(8,128)(2,1)S(1)}, bf16[3072,768]{1,0:T(8,128)(2,1)S(1)}, u32[]{:S(2)}, u32[]{:S(2)}) collective-permute-start(bf16[3072,768]{1,0:T(8,128)(2,1)S(1)} %weights.1.own_ref.refs_6_), channel_id=1, source_target_pairs={{0,4},{4,0},{8,12},{12,8},{16,20},{20,16},{24,28},{28,24},{1,5},{5... | collective-permute-start | bytes 14155784 | tf_op jit(solution)/shard_map/ppermute | solution.py:35
  14.7 13.5 %collective-permute-start.5 = (bf16[32,6272]{1,0:T(8,128)(2,1)S(1)}, bf16[32,6272]{1,0:T(8,128)(2,1)S(1)}, u32[]{:S(2)}, u32[]{:S(2)}) collective-permute-start(bf16[32,6272]{1,0:T(8,128)(2,1)S(1)} %pad_maximum_fusion.refs_0_), channel_id=1, source_target_pairs={{0,8},{4,12},{8,0},{12,4},{16,24},{20,28},{24,16},{28,20},{1,9},{5... | collective-permute-start | bytes 1204232 | tf_op jit(solution)/shard_map/ppermute | solution.py:35
  15.9 8.8 %collective-permute-start.8 = (bf16[16,6272]{1,0:T(8,128)(2,1)S(1)}, bf16[16,6272]{1,0:T(8,128)(2,1)S(1)}, u32[]{:S(2)}, u32[]{:S(2)}) collective-permute-start(bf16[16,6272]{1,0:T(8,128)(2,1)S(1)} %pad_maximum_fusion.1.refs_1_), channel_id=1, source_target_pairs={{0,3},{1,2},{2,1},{3,0},{4,7},{5,6},{6,5},{7,4},{8,11},{9,10},{10,... | collective-permute-start | bytes 602120 | tf_op jit(solution)/shard_map/ppermute | solution.py:35
  18.3 9.8 %collective-permute-start.7 = (bf16[16,6272]{1,0:T(8,128)(2,1)S(1)}, bf16[16,6272]{1,0:T(8,128)(2,1)S(1)}, u32[]{:S(2)}, u32[]{:S(2)}) collective-permute-start(bf16[16,6272]{1,0:T(8,128)(2,1)S(1)} %pad_maximum_fusion.1.refs_1_), channel_id=1, source_target_pairs={{0,2},{1,3},{2,0},{3,1},{4,6},{5,7},{6,4},{7,5},{8,10},{9,11},{10,... | collective-permute-start | bytes 602120 | tf_op jit(solution)/shard_map/ppermute | solution.py:35
  18.8 9.4 %collective-permute-start.6 = (bf16[16,6272]{1,0:T(8,128)(2,1)S(1)}, bf16[16,6272]{1,0:T(8,128)(2,1)S(1)}, u32[]{:S(2)}, u32[]{:S(2)}) collective-permute-start(bf16[16,6272]{1,0:T(8,128)(2,1)S(1)} %pad_maximum_fusion.1.refs_1_), channel_id=1, source_target_pairs={{0,1},{1,0},{2,3},{3,2},{4,5},{5,4},{6,7},{7,6},{8,9},{9,8},{10,11... | collective-permute-start | bytes 602120 | tf_op jit(solution)/shard_map/ppermute | solution.py:35
  30.7 4.5 %collective-permute-start.14 = (bf16[128,6912]{1,0:T(8,128)(2,1)S(1)}, bf16[128,6912]{1,0:T(8,128)(2,1)S(1)}, u32[]{:S(2)}, u32[]{:S(2)}) collective-permute-start(bf16[128,6912]{1,0:T(8,128)(2,1)S(1)} %get-tuple-element.41.pass_ref), channel_id=1, source_target_pairs={{0,4},{4,0},{8,12},{12,8},{16,20},{20,16},{24,28},{28,24},{1,5},{5... | collective-permute-start | bytes 5308424 | tf_op jit(solution)/shard_map/ppermute | solution.py:35
  30.8 7.1 %collective-permute-start.11 = (bf16[16,3200]{1,0:T(8,128)(2,1)S(1)}, bf16[16,3200]{1,0:T(8,128)(2,1)S(1)}, u32[]{:S(2)}, u32[]{:S(2)}) collective-permute-start(bf16[16,3200]{1,0:T(8,128)(2,1)S(1)} %get-tuple-element.38), channel_id=1, source_target_pairs={{0,3},{1,2},{2,1},{3,0},{4,7},{5,6},{6,5},{7,4},{8,11},{9,10},{10,... | collective-permute-start | bytes 307208 | tf_op jit(solution)/shard_map/ppermute | solution.py:35
  32.5 6.6 %collective-permute-start.12 = (bf16[16,3200]{1,0:T(8,128)(2,1)S(1)}, bf16[16,3200]{1,0:T(8,128)(2,1)S(1)}, u32[]{:S(2)}, u32[]{:S(2)}) collective-permute-start(bf16[16,3200]{1,0:T(8,128)(2,1)S(1)} %get-tuple-element.39), channel_id=1, source_target_pairs={{0,1},{1,0},{2,3},{3,2},{4,5},{5,4},{6,7},{7,6},{8,9},{9,8},{10,11... | collective-permute-start | bytes 307208 | tf_op jit(solution)/shard_map/ppermute | solution.py:35
  33.7 5.4 %collective-permute-start.13 = (bf16[16,3200]{1,0:T(8,128)(2,1)S(1)}, bf16[16,3200]{1,0:T(8,128)(2,1)S(1)}, u32[]{:S(2)}, u32[]{:S(2)}) collective-permute-start(bf16[16,3200]{1,0:T(8,128)(2,1)S(1)} %get-tuple-element.40), channel_id=1, source_target_pairs={{0,2},{1,3},{2,0},{3,1},{4,6},{5,7},{6,4},{7,5},{8,10},{9,11},{10,... | collective-permute-start | bytes 307208 | tf_op jit(solution)/shard_map/ppermute | solution.py:35
  34.3 8.4 %collective-permute-start.10 = (bf16[32,3200]{1,0:T(8,128)(2,1)S(1)}, bf16[32,3200]{1,0:T(8,128)(2,1)S(1)}, u32[]{:S(2)}, u32[]{:S(2)}) collective-permute-start(bf16[32,3200]{1,0:T(8,128)(2,1)S(1)} %get-tuple-element.35), channel_id=1, source_target_pairs={{0,8},{4,12},{8,0},{12,4},{16,24},{20,28},{24,16},{28,20},{1,9},{5... | collective-permute-start | bytes 614408 | tf_op jit(solution)/shard_map/ppermute | solution.py:35
  39.3 7.1 %collective-permute-start.15 = (bf16[8,3200]{1,0:T(8,128)(2,1)S(1)}, bf16[8,3200]{1,0:T(8,128)(2,1)S(1)}, u32[]{:S(2)}, u32[]{:S(2)}) collective-permute-start(bf16[8,3200]{1,0:T(8,128)(2,1)S(1)} %get-tuple-element.47), channel_id=1, source_target_pairs={{0,16},{4,20},{8,24},{12,28},{16,0},{20,4},{24,8},{28,12},{1,17},{... | collective-permute-start | bytes 153608 | tf_op jit(solution)/shard_map/ppermute | solution.py:35
  41.5 5.9 %collective-permute-start.16 = (bf16[8,3200]{1,0:T(8,128)(2,1)S(1)}, bf16[8,3200]{1,0:T(8,128)(2,1)S(1)}, u32[]{:S(2)}, u32[]{:S(2)}) collective-permute-start(bf16[8,3200]{1,0:T(8,128)(2,1)S(1)} %get-tuple-element.48), channel_id=1, source_target_pairs={{0,24},{4,28},{8,16},{12,20},{16,8},{20,12},{24,0},{28,4},{1,25},{... | collective-permute-start | bytes 153608 | tf_op jit(solution)/shard_map/ppermute | solution.py:35
  42.9 5.7 %collective-permute-start.17 = (bf16[8,3200]{1,0:T(8,128)(2,1)S(1)}, bf16[8,3200]{1,0:T(8,128)(2,1)S(1)}, u32[]{:S(2)}, u32[]{:S(2)}) collective-permute-start(bf16[8,3200]{1,0:T(8,128)(2,1)S(1)} %get-tuple-element.49), channel_id=1, source_target_pairs={{0,3},{1,2},{2,1},{3,0},{4,7},{5,6},{6,5},{7,4},{8,11},{9,10},{10,... | collective-permute-start | bytes 153608 | tf_op jit(solution)/shard_map/ppermute | solution.py:35
  44.5 4.1 %collective-permute-start.18 = (bf16[8,3200]{1,0:T(8,128)(2,1)S(1)}, bf16[8,3200]{1,0:T(8,128)(2,1)S(1)}, u32[]{:S(2)}, u32[]{:S(2)}) collective-permute-start(bf16[8,3200]{1,0:T(8,128)(2,1)S(1)} %get-tuple-element.50), channel_id=1, source_target_pairs={{0,1},{1,0},{2,3},{3,2},{4,5},{5,4},{6,7},{7,6},{8,9},{9,8},{10,11... | collective-permute-start | bytes 153608 | tf_op jit(solution)/shard_map/ppermute | solution.py:35
  45.8 4.1 %collective-permute-start.19 = (bf16[8,3200]{1,0:T(8,128)(2,1)S(1)}, bf16[8,3200]{1,0:T(8,128)(2,1)S(1)}, u32[]{:S(2)}, u32[]{:S(2)}) collective-permute-start(bf16[8,3200]{1,0:T(8,128)(2,1)S(1)} %get-tuple-element.51), channel_id=1, source_target_pairs={{0,2},{1,3},{2,0},{3,1},{4,6},{5,7},{6,4},{7,5},{8,10},{9,11},{10,... | collective-permute-start | bytes 153608 | tf_op jit(solution)/shard_map/ppermute | solution.py:35
  47.4 2.5 %copy-start = (s32[8,2]{0,1:T(2,128)S(1)}, s32[8,2]{0,1:T(2,128)}, u32[]{:S(2)}) copy-start(s32[8,2]{0,1:T(2,128)} %param.9) | copy-start | bytes 196

commit v8 on v7

--- a/solution.py
+++ b/solution.py
@@ -114,8 +114,9 @@
 
 def expert_body(experts, pieces_count, *refs):
     pieces, (own_ref, other_ref, back_ref) = refs[:pieces_count], refs[pieces_count : pieces_count + 3]
-    *sums, pass_ref, acts_ref, dy_ref, weight_ref = refs[pieces_count + 3 :]
-    features = dy_ref.shape[1]
+    *sums, pass_ref, acts_ref, weight_ref = refs[pieces_count + 3 :]
+    features = own_ref.shape[0]
+    width = 2 * features + PAD
     units = own_ref.shape[1] // 3
     own = lax.axis_index("expert")
 
@@ -126,10 +127,7 @@
         dense = piece[:, 2 * features :].astype(F32)
         weight = jnp.sum(jnp.where(lanes(piece.shape[0]) == own, dense, 0.0), axis=1, keepdims=True)
         weight_ref[rows, :] = jnp.broadcast_to(weight, dense.shape)
-        dy = piece[:, features : 2 * features]
-        dy_ref[rows, :] = dy
-        pass_ref[rows, :features] = piece[:, :features]
-        pass_ref[rows, features : 2 * features] = (weight * dy.astype(F32)).astype(BF)
+        pass_ref[rows, :width] = piece[...]
 
     grads = []
     product = 0.0
@@ -138,7 +136,9 @@
             pass_ref[:, :features], ref[:, : 2 * units], preferred_element_type=F32
         )
         pre_gate, pre_up = both[:, :units], both[:, units:]
-        back = jnp.dot(dy_ref[...], ref[:, 2 * units :], preferred_element_type=F32)
+        back = jnp.dot(
+            pass_ref[:, features : 2 * features], ref[:, 2 * units :], preferred_element_type=F32
+        )
         sig = jax.nn.sigmoid(pre_gate)
         active = pre_gate * sig
         hidden = (active * pre_up).astype(BF)
@@ -150,7 +150,7 @@
         if ref is own_ref:
             acts_ref[...] = jnp.concatenate([hidden, d_gate, d_up], axis=1)
         else:
-            pass_ref[:, 2 * features :] = jnp.concatenate([hidden, d_gate, d_up], axis=1)
+            pass_ref[:, width:] = jnp.concatenate([hidden, d_gate, d_up], axis=1)
     part = jnp.dot(jnp.concatenate(grads, axis=1), back_ref[...], preferred_element_type=F32)
     spread = jnp.where(lanes(part.shape[0]) == own, product, 0.0)
     at = 0
@@ -168,12 +168,15 @@
     gate_hbm, up_hbm, down_hbm, x_ref, scaled_ref, all_ref, gate_ref, up_ref, down_ref, sems = refs
     half, features = pass_ref.shape[0], x_ref.shape[1]
     units = acts_ref.shape[1] // 3
+    own = lax.axis_index("expert")
     for i, ref in enumerate((pass_ref, got_ref)):
         rows = pl.ds(i * half, half)
         x_ref[rows, :] = ref[:, :features]
-        scaled_ref[rows, :] = ref[:, features : 2 * features]
+        dense = ref[:, 2 * features : 2 * features + PAD].astype(F32)
+        weight = jnp.sum(jnp.where(lanes(half) == own, dense, 0.0), axis=1, keepdims=True)
+        scaled_ref[rows, :] = (weight * ref[:, features : 2 * features].astype(F32)).astype(BF)
     all_ref[:half, :] = acts_ref[...]
-    all_ref[half:, :] = got_ref[:, 2 * features :]
+    all_ref[half:, :] = got_ref[:, 2 * features + PAD :]
     step = features // parts
     copies = []
     for i in range(parts):
@@ -261,13 +264,12 @@
 def expert_plain(pieces, own_slabs, other_slabs, experts, sizes):
     features = own_slabs.shape[0]
     units = own_slabs.shape[1] // 3
-    rows = jnp.concatenate(pieces, axis=0)
+    all_rows = rows = jnp.concatenate(pieces, axis=0)
     rows_x, rows_dy = rows[:, :features], rows[:, features : 2 * features]
     is_own = jnp.arange(PAD, dtype=jnp.int32)[None, :] == lax.axis_index("expert")
     weight = jnp.sum(
         jnp.where(is_own, rows[:, 2 * features :].astype(F32), 0.0), axis=1, keepdims=True
     )
-    scaled = (weight * rows_dy.astype(F32)).astype(BF)
     part = product = 0.0
     acts = []
     for slabs in (own_slabs, other_slabs):
@@ -290,7 +292,7 @@
         piece = wide[at : at + rows]
         at += rows
         sums.append(piece if dtype == F32 else to_wire(piece, experts))
-    return *sums, jnp.concatenate([rows_x, scaled, acts[1]], axis=1), acts[0]
+    return *sums, jnp.concatenate([all_rows, acts[1]], axis=1), acts[0]
 
 
 def local(tokens, upstream, route_ids, route_gates, w_gate, w_up, w_down):
@@ -357,9 +359,8 @@
         *split, passed, acts = pl.pallas_call(
             functools.partial(expert_body, experts, len(pieces)),
             out_shape=[shape((size, width), dtype) for size, dtype in sizes]
-            + [shape((rows, 2 * features + 3 * units), BF), shape((rows, 3 * units), BF)],
+            + [shape((rows, 2 * features + PAD + 3 * units), BF), shape((rows, 3 * units), BF)],
             scratch_shapes=[
-                pltpu.VMEM((rows, features), BF),
                 pltpu.VMEM((rows, PAD), F32),
             ],
             name="expert",
@@ -390,9 +391,13 @@
         )(passed, got, acts)
     else:
         every = jnp.concatenate([passed, got], axis=0)
-        acts = jnp.concatenate([acts, got[:, 2 * features :]], axis=0)
+        acts = jnp.concatenate([acts, got[:, 2 * features + PAD :]], axis=0)
         hidden, d_gate, d_up = jnp.split(acts, 3, axis=1)
-        rows_x, scaled = every[:, :features], every[:, features : 2 * features]
+        dense = every[:, 2 * features : 2 * features + PAD].astype(F32)
+        is_own = jnp.arange(PAD, dtype=jnp.int32)[None, :] == lax.axis_index("expert")
+        weight = jnp.sum(jnp.where(is_own, dense, 0.0), axis=1, keepdims=True)
+        rows_x = every[:, :features]
+        scaled = (weight * every[:, features : 2 * features].astype(F32)).astype(BF)
         grad_gate = contract_first(rows_x, d_gate).astype(BF)[None]
         grad_up = contract_first(rows_x, d_up).astype(BF)[None]
         grad_down = contract_first(hidden, scaled).astype(BF)[None]

time: 50.8 us -> 50.8 us (level)
  no operation moved by 1% of the time
where the time goes in v8:
time: 50.8 us; the launch traced here: 50.6 us
  starting transfers between devices  25.1 us (49%)
  waiting for transfers between devices  13.1 us (26%)
  Pallas kernels  11.6 us (23%)
  between operations  0.73 us (1%)
    ppermute x20, starting transfers between devices, swap(): return lax.ppermute(value, axis, [(i, i ^ mask) for i in range(size)])  25.1 us
    ppermute x20, waiting for transfers between devices, swap(): return lax.ppermute(value, axis, [(i, i ^ mask) for i in range(size)])  13.1 us
    pallas_call x1, Pallas kernels, local(): pl.pallas_call(weights_body, out_shape=shape((features, 3 * units), BF),...  2.84 us
    pallas_call x1, Pallas kernels, local(): pl.pallas_call(functools.partial(grads_body, PARTS), out_shape=[shape(w.s...  2.7 us
    pallas_call x1, Pallas kernels, local(): pl.pallas_call(functools.partial(expert_body, experts, len(pieces)), out_...  2.46 us
    pallas_call x1, Pallas kernels, local(): call(back_body, shape((4 * units, features), BF), 'back')  1.8 us
  transfers between devices with their start and end apart: 20, of which 12 were waited for; matrix products, arithmetic and copies ran while one was open for 0% of the time, Pallas kernels for 15%

profile of v8, /device:TPU:0, one launch (start us, length us, event | category | flops | bytes accessed | tf_op | source)
XLA Modules:
  0.0 50.6 jit_solution(5153650628853491976)
XLA Ops:
  0.6 0.9 %pack.1 = bf16[8,6272]{1,0:T(8,128)(2,1)S(1)} custom-call(bf16[8,3072]{1,0:T(8,128)(2,1)} %x_hbm.1, bf16[8,3072]{1,0:T(8,128)(2,1)} %dy_hbm.1, s32[2,8]{1,0:T(2,128)} %bitcast.3, bf16[2,8]{1,0:T(2,128)(2,1)} %bitcast.5), custom_call_target="tpu_custom_call" | custom-call | tf_op jit(solution)/shard_map/pack/pallas_call | solution.py:311
  1.5 4.1 %collective-permute-start.1 = (bf16[8,6272]{1,0:T(8,128)(2,1)S(1)}, bf16[8,6272]{1,0:T(8,128)(2,1)S(1)}, u32[]{:S(2)}, u32[]{:S(2)}) collective-permute-start(bf16[8,6272]{1,0:T(8,128)(2,1)S(1)} %pack.1), channel_id=1, source_target_pairs={{0,16},{4,20},{8,24},{12,28},{16,0},{20,4},{24,8},{28,12},{1,17},{... | collective-permute-start | bytes 301064 | tf_op jit(solution)/shard_map/ppermute | solution.py:35
  5.6 1.3 %collective-permute-start = (bf16[8,6272]{1,0:T(8,128)(2,1)S(1)}, bf16[8,6272]{1,0:T(8,128)(2,1)S(1)}, u32[]{:S(2)}, u32[]{:S(2)}) collective-permute-start(bf16[8,6272]{1,0:T(8,128)(2,1)S(1)} %pack.1), channel_id=1, source_target_pairs={{0,24},{4,28},{8,16},{12,20},{16,8},{20,12},{24,0},{28,4},{1,25},{... | collective-permute-start | bytes 301064 | tf_op jit(solution)/shard_map/ppermute | solution.py:35
  7.0 2.4 %collective-permute-start.4 = (bf16[8,6272]{1,0:T(8,128)(2,1)S(1)}, bf16[8,6272]{1,0:T(8,128)(2,1)S(1)}, u32[]{:S(2)}, u32[]{:S(2)}) collective-permute-start(bf16[8,6272]{1,0:T(8,128)(2,1)S(1)} %pack.1), channel_id=1, source_target_pairs={{0,3},{1,2},{2,1},{3,0},{4,7},{5,6},{6,5},{7,4},{8,11},{9,10},{10,... | collective-permute-start | bytes 301064 | tf_op jit(solution)/shard_map/ppermute | solution.py:35
  9.4 0.5 %collective-permute-start.3 = (bf16[8,6272]{1,0:T(8,128)(2,1)S(1)}, bf16[8,6272]{1,0:T(8,128)(2,1)S(1)}, u32[]{:S(2)}, u32[]{:S(2)}) collective-permute-start(bf16[8,6272]{1,0:T(8,128)(2,1)S(1)} %pack.1), channel_id=1, source_target_pairs={{0,1},{1,0},{2,3},{3,2},{4,5},{5,4},{6,7},{7,6},{8,9},{9,8},{10,11... | collective-permute-start | bytes 301064 | tf_op jit(solution)/shard_map/ppermute | solution.py:35
  10.0 0.5 %collective-permute-start.2 = (bf16[8,6272]{1,0:T(8,128)(2,1)S(1)}, bf16[8,6272]{1,0:T(8,128)(2,1)S(1)}, u32[]{:S(2)}, u32[]{:S(2)}) collective-permute-start(bf16[8,6272]{1,0:T(8,128)(2,1)S(1)} %pack.1), channel_id=1, source_target_pairs={{0,2},{1,3},{2,0},{3,1},{4,6},{5,7},{6,4},{7,5},{8,10},{9,11},{10,... | collective-permute-start | bytes 301064 | tf_op jit(solution)/shard_map/ppermute | solution.py:35
  10.5 2.8 %weights.1.own_ref.refs_6_ = bf16[3072,768]{1,0:T(8,128)(2,1)S(1)} custom-call(bf16[1,3072,256]{2,1,0:T(8,128)(2,1)} %gate_hbm.1, bf16[1,3072,256]{2,1,0:T(8,128)(2,1)} %up_hbm.1, bf16[1,256,3072]{2,1,0:T(8,128)(2,1)} %down_hbm.1), custom_call_target="tpu_custom_call" | custom-call | bytes 1024 | tf_op jit(solution)/shard_map/weights/pallas_call | solution.py:337
  13.3 0.3 collective-permute-done.1
  13.6 0.0 collective-permute-done
  13.6 0.0 collective-permute-done.4
  13.6 0.6 %collective-permute-done.3 = bf16[8,6272]{1,0:T(8,128)(2,1)S(1)} collective-permute-done((bf16[8,6272]{1,0:T(8,128)(2,1)S(1)}, bf16[8,6272]{1,0:T(8,128)(2,1)S(1)}, u32[]{:S(2)}, u32[]{:S(2)}) %collective-permute-start.3) | collective-permute-done | bytes 100384 | tf_op jit(solution)/shard_map/ppermute | solution.py:35
  14.3 0.3 collective-permute-done.2
  14.6 0.1 collective-permute-start.9
  14.7 1.2 %collective-permute-start.5 = (bf16[32,6272]{1,0:T(8,128)(2,1)S(1)}, bf16[32,6272]{1,0:T(8,128)(2,1)S(1)}, u32[]{:S(2)}, u32[]{:S(2)}) collective-permute-start(bf16[32,6272]{1,0:T(8,128)(2,1)S(1)} %pad_maximum_fusion.refs_0_), channel_id=1, source_target_pairs={{0,8},{4,12},{8,0},{12,4},{16,24},{20,28},{24,16},{28,20},{1,9},{5... | collective-permute-start | bytes 1204232 | tf_op jit(solution)/shard_map/ppermute | solution.py:35
  15.9 2.4 %collective-permute-start.8 = (bf16[16,6272]{1,0:T(8,128)(2,1)S(1)}, bf16[16,6272]{1,0:T(8,128)(2,1)S(1)}, u32[]{:S(2)}, u32[]{:S(2)}) collective-permute-start(bf16[16,6272]{1,0:T(8,128)(2,1)S(1)} %pad_maximum_fusion.1.refs_1_), channel_id=1, source_target_pairs={{0,3},{1,2},{2,1},{3,0},{4,7},{5,6},{6,5},{7,4},{8,11},{9,10},{10,... | collective-permute-start | bytes 602120 | tf_op jit(solution)/shard_map/ppermute | solution.py:35
  18.3 0.5 %collective-permute-start.7 = (bf16[16,6272]{1,0:T(8,128)(2,1)S(1)}, bf16[16,6272]{1,0:T(8,128)(2,1)S(1)}, u32[]{:S(2)}, u32[]{:S(2)}) collective-permute-start(bf16[16,6272]{1,0:T(8,128)(2,1)S(1)} %pad_maximum_fusion.1.refs_1_), channel_id=1, source_target_pairs={{0,2},{1,3},{2,0},{3,1},{4,6},{5,7},{6,4},{7,5},{8,10},{9,11},{10,... | collective-permute-start | bytes 602120 | tf_op jit(solution)/shard_map/ppermute | solution.py:35
  18.8 0.5 %collective-permute-start.6 = (bf16[16,6272]{1,0:T(8,128)(2,1)S(1)}, bf16[16,6272]{1,0:T(8,128)(2,1)S(1)}, u32[]{:S(2)}, u32[]{:S(2)}) collective-permute-start(bf16[16,6272]{1,0:T(8,128)(2,1)S(1)} %pad_maximum_fusion.1.refs_1_), channel_id=1, source_target_pairs={{0,1},{1,0},{2,3},{3,2},{4,5},{5,4},{6,7},{7,6},{8,9},{9,8},{10,11... | collective-permute-start | bytes 602120 | tf_op jit(solution)/shard_map/ppermute | solution.py:35
  19.4 3.2 %collective-permute-done.9.other_ref.refs_7_ = bf16[3072,768]{1,0:T(8,128)(2,1)S(1)} collective-permute-done((bf16[3072,768]{1,0:T(8,128)(2,1)S(1)}, bf16[3072,768]{1,0:T(8,128)(2,1)S(1)}, u32[]{:S(2)}, u32[]{:S(2)}) %collective-permute-start.9) | collective-permute-done | bytes 4718624 | tf_op jit(solution)/shard_map/ppermute | solution.py:35
  22.6 1.8 %back.1.refs_8_ = bf16[1024,3072]{1,0:T(8,128)(2,1)S(1)} custom-call(bf16[3072,768]{1,0:T(8,128)(2,1)S(1)} %weights.1.own_ref.refs_6_, bf16[3072,768]{1,0:T(8,128)(2,1)S(1)} %collective-permute-done.9.other_ref.refs_7_), custom_call_target="tpu_custom_call" | custom-call | tf_op jit(solution)/shard_map/back/pallas_call | solution.py:358
  24.4 0.2 collective-permute-done.8.refs_5_
  24.7 3.5 %collective-permute-done.7.refs_4_ = bf16[16,6272]{1,0:T(8,128)(2,1)S(1)} collective-permute-done((bf16[16,6272]{1,0:T(8,128)(2,1)S(1)}, bf16[16,6272]{1,0:T(8,128)(2,1)S(1)}, u32[]{:S(2)}, u32[]{:S(2)}) %collective-permute-start.7) | collective-permute-done | bytes 200736 | tf_op jit(solution)/shard_map/ppermute | solution.py:35
  28.1 0.1 collective-permute-done.6.refs_3_
  28.2 0.0 collective-permute-done.5.refs_2_
  28.2 2.5 %expert.1 = (f32[32,3200]{1,0:T(8,128)S(1)}, f32[16,3200]{1,0:T(8,128)S(1)}, bf16[32,3200]{1,0:T(8,128)(2,1)S(1)}, bf16[16,3200]{1,0:T(8,128)(2,1)S(1)}, bf16[16...) custom-call(bf16[32,6272]{1,0:T(8,128)(2,1)S(1)} %pad_maximum_fusion, ...), custom_call_target="tpu_custom_call" | custom-call | bytes 1024 | tf_op jit(solution)/shard_map/expert/pallas_call | solution.py:359
  30.7 0.1 collective-permute-start.14
  30.8 1.7 %collective-permute-start.11 = (bf16[16,3200]{1,0:T(8,128)(2,1)S(1)}, bf16[16,3200]{1,0:T(8,128)(2,1)S(1)}, u32[]{:S(2)}, u32[]{:S(2)}) collective-permute-start(bf16[16,3200]{1,0:T(8,128)(2,1)S(1)} %get-tuple-element.38), channel_id=1, source_target_pairs={{0,3},{1,2},{2,1},{3,0},{4,7},{5,6},{6,5},{7,4},{8,11},{9,10},{10,... | collective-permute-start | bytes 307208 | tf_op jit(solution)/shard_map/ppermute | solution.py:35
  32.5 1.2 %collective-permute-start.12 = (bf16[16,3200]{1,0:T(8,128)(2,1)S(1)}, bf16[16,3200]{1,0:T(8,128)(2,1)S(1)}, u32[]{:S(2)}, u32[]{:S(2)}) collective-permute-start(bf16[16,3200]{1,0:T(8,128)(2,1)S(1)} %get-tuple-element.39), channel_id=1, source_target_pairs={{0,1},{1,0},{2,3},{3,2},{4,5},{5,4},{6,7},{7,6},{8,9},{9,8},{10,11... | collective-permute-start | bytes 307208 | tf_op jit(solution)/shard_map/ppermute | solution.py:35
  33.7 0.6 %collective-permute-start.13 = (bf16[16,3200]{1,0:T(8,128)(2,1)S(1)}, bf16[16,3200]{1,0:T(8,128)(2,1)S(1)}, u32[]{:S(2)}, u32[]{:S(2)}) collective-permute-start(bf16[16,3200]{1,0:T(8,128)(2,1)S(1)} %get-tuple-element.40), channel_id=1, source_target_pairs={{0,2},{1,3},{2,0},{3,1},{4,6},{5,7},{6,4},{7,5},{8,10},{9,11},{10,... | collective-permute-start | bytes 307208 | tf_op jit(solution)/shard_map/ppermute | solution.py:35
  34.3 0.8 %collective-permute-start.10 = (bf16[32,3200]{1,0:T(8,128)(2,1)S(1)}, bf16[32,3200]{1,0:T(8,128)(2,1)S(1)}, u32[]{:S(2)}, u32[]{:S(2)}) collective-permute-start(bf16[32,3200]{1,0:T(8,128)(2,1)S(1)} %get-tuple-element.35), channel_id=1, source_target_pairs={{0,8},{4,12},{8,0},{12,4},{16,24},{20,28},{24,16},{28,20},{1,9},{5... | collective-permute-start | bytes 614408 | tf_op jit(solution)/shard_map/ppermute | solution.py:35
  35.2 0.0 collective-permute-done.14.got_ref
  35.2 2.7 %grads.1 = (bf16[1,3072,256]{2,1,0:T(8,128)(2,1)}, bf16[1,3072,256]{2,1,0:T(8,128)(2,1)}, bf16[1,256,3072]{2,1,0:T(8,128)(2,1)}) custom-call(bf16[128,7040]{1,0:T(8,128)(2,1)S(1)} %get-tuple-element.41.pass_ref, bf16[128,7040]{1,0:T(8,128)(2,1)S(1)} %collective-permute-done.14.got_ref, bf16[128,768]{1,0:T(8,128)(2,1)S(1)} %get-tuple-element.42.acts_ref), custom_call_target="tpu_custom_call" | custom-call | bytes 1024 | tf_op jit(solution)/shard_map/grads/pallas_call | solution.py:375
  37.9 0.0 collective-permute-done.11.refs_1_
  37.9 1.2 %collective-permute-done.12.refs_2_ = bf16[16,3200]{1,0:T(8,128)(2,1)S(1)} collective-permute-done((bf16[16,3200]{1,0:T(8,128)(2,1)S(1)}, bf16[16,3200]{1,0:T(8,128)(2,1)S(1)}, u32[]{:S(2)}, u32[]{:S(2)}) %collective-permute-start.12) | collective-permute-done | bytes 102432 | tf_op jit(solution)/shard_map/ppermute | solution.py:35
  39.1 0.0 collective-permute-done.13.refs_3_
  39.2 0.1 sum_far.1
  39.3 2.2 %collective-permute-start.15 = (bf16[8,3200]{1,0:T(8,128)(2,1)S(1)}, bf16[8,3200]{1,0:T(8,128)(2,1)S(1)}, u32[]{:S(2)}, u32[]{:S(2)}) collective-permute-start(bf16[8,3200]{1,0:T(8,128)(2,1)S(1)} %get-tuple-element.47), channel_id=1, source_target_pairs={{0,16},{4,20},{8,24},{12,28},{16,0},{20,4},{24,8},{28,12},{1,17},{... | collective-permute-start | bytes 153608 | tf_op jit(solution)/shard_map/ppermute | solution.py:35
  41.5 1.3 %collective-permute-start.16 = (bf16[8,3200]{1,0:T(8,128)(2,1)S(1)}, bf16[8,3200]{1,0:T(8,128)(2,1)S(1)}, u32[]{:S(2)}, u32[]{:S(2)}) collective-permute-start(bf16[8,3200]{1,0:T(8,128)(2,1)S(1)} %get-tuple-element.48), channel_id=1, source_target_pairs={{0,24},{4,28},{8,16},{12,20},{16,8},{20,12},{24,0},{28,4},{1,25},{... | collective-permute-start | bytes 153608 | tf_op jit(solution)/shard_map/ppermute | solution.py:35
  42.8 0.0 collective-permute-done.10.refs_1_
  42.8 0.1 sum_near.1
  42.8 1.7 %collective-permute-start.17 = (bf16[8,3200]{1,0:T(8,128)(2,1)S(1)}, bf16[8,3200]{1,0:T(8,128)(2,1)S(1)}, u32[]{:S(2)}, u32[]{:S(2)}) collective-permute-start(bf16[8,3200]{1,0:T(8,128)(2,1)S(1)} %get-tuple-element.49), channel_id=1, source_target_pairs={{0,3},{1,2},{2,1},{3,0},{4,7},{5,6},{6,5},{7,4},{8,11},{9,10},{10,... | collective-permute-start | bytes 153608 | tf_op jit(solution)/shard_map/ppermute | solution.py:35
  44.5 1.2 %collective-permute-start.18 = (bf16[8,3200]{1,0:T(8,128)(2,1)S(1)}, bf16[8,3200]{1,0:T(8,128)(2,1)S(1)}, u32[]{:S(2)}, u32[]{:S(2)}) collective-permute-start(bf16[8,3200]{1,0:T(8,128)(2,1)S(1)} %get-tuple-element.50), channel_id=1, source_target_pairs={{0,1},{1,0},{2,3},{3,2},{4,5},{5,4},{6,7},{7,6},{8,9},{9,8},{10,11... | collective-permute-start | bytes 153608 | tf_op jit(solution)/shard_map/ppermute | solution.py:35
  45.8 0.6 %collective-permute-start.19 = (bf16[8,3200]{1,0:T(8,128)(2,1)S(1)}, bf16[8,3200]{1,0:T(8,128)(2,1)S(1)}, u32[]{:S(2)}, u32[]{:S(2)}) collective-permute-start(bf16[8,3200]{1,0:T(8,128)(2,1)S(1)} %get-tuple-element.51), channel_id=1, source_target_pairs={{0,2},{1,3},{2,0},{3,1},{4,6},{5,7},{6,4},{7,5},{8,10},{9,11},{10,... | collective-permute-start | bytes 153608 | tf_op jit(solution)/shard_map/ppermute | solution.py:35
  46.4 0.0 collective-permute-done.15.refs_1_
  46.4 1.0 %collective-permute-done.16.refs_2_ = bf16[8,3200]{1,0:T(8,128)(2,1)S(1)} collective-permute-done((bf16[8,3200]{1,0:T(8,128)(2,1)S(1)}, bf16[8,3200]{1,0:T(8,128)(2,1)S(1)}, u32[]{:S(2)}, u32[]{:S(2)}) %collective-permute-start.16) | collective-permute-done | bytes 51232 | tf_op jit(solution)/shard_map/ppermute | solution.py:35
  47.4 0.0 copy-start
  47.4 1.1 %collective-permute-done.17.refs_1_ = bf16[8,3200]{1,0:T(8,128)(2,1)S(1)} collective-permute-done((bf16[8,3200]{1,0:T(8,128)(2,1)S(1)}, bf16[8,3200]{1,0:T(8,128)(2,1)S(1)}, u32[]{:S(2)}, u32[]{:S(2)}) %collective-permute-start.17) | collective-permute-done | bytes 51232 | tf_op jit(solution)/shard_map/ppermute | solution.py:35
  48.5 0.1 collective-permute-done.18.refs_2_
  48.6 1.2 %collective-permute-done.19.refs_3_ = bf16[8,3200]{1,0:T(8,128)(2,1)S(1)} collective-permute-done((bf16[8,3200]{1,0:T(8,128)(2,1)S(1)}, bf16[8,3200]{1,0:T(8,128)(2,1)S(1)}, u32[]{:S(2)}, u32[]{:S(2)}) %collective-permute-start.19) | collective-permute-done | bytes 51232 | tf_op jit(solution)/shard_map/ppermute | solution.py:35
  49.9 0.0 copy-done
  49.9 0.7 %final.1 = (bf16[8,3072]{1,0:T(8,128)(2,1)}, f32[2,8]{1,0:T(2,128)}) custom-call(f32[8,3200]{1,0:T(8,128)S(1)} %sum_along.1.refs_0_, bf16[8,3200]{1,0:T(8,128)(2,1)S(1)} %collective-permute-done.17.refs_1_, bf16[8,3200]{1,0:T(8,128)(2,1)S(1)} %collective-permute-done.18.refs_2_, bf16[8,3200]{1,0:T(8,128)(2,1)S(1)} %collective-permute-done.19.refs_3_, ...), custom_call_target="tpu_custom_call" | custom-call | bytes 204800 | tf_op jit(solution)/shard_map/final/pallas_call | solution.py:417
  (3 shorter events, 0.1 us)
Async XLA Ops:
  1.5 12.1 %collective-permute-start.1 = (bf16[8,6272]{1,0:T(8,128)(2,1)S(1)}, bf16[8,6272]{1,0:T(8,128)(2,1)S(1)}, u32[]{:S(2)}, u32[]{:S(2)}) collective-permute-start(bf16[8,6272]{1,0:T(8,128)(2,1)S(1)} %pack.1), channel_id=1, source_target_pairs={{0,16},{4,20},{8,24},{12,28},{16,0},{20,4},{24,8},{28,12},{1,17},{... | collective-permute-start | bytes 301064 | tf_op jit(solution)/shard_map/ppermute | solution.py:35
  5.6 8.0 %collective-permute-start = (bf16[8,6272]{1,0:T(8,128)(2,1)S(1)}, bf16[8,6272]{1,0:T(8,128)(2,1)S(1)}, u32[]{:S(2)}, u32[]{:S(2)}) collective-permute-start(bf16[8,6272]{1,0:T(8,128)(2,1)S(1)} %pack.1), channel_id=1, source_target_pairs={{0,24},{4,28},{8,16},{12,20},{16,8},{20,12},{24,0},{28,4},{1,25},{... | collective-permute-start | bytes 301064 | tf_op jit(solution)/shard_map/ppermute | solution.py:35
  7.0 6.6 %collective-permute-start.4 = (bf16[8,6272]{1,0:T(8,128)(2,1)S(1)}, bf16[8,6272]{1,0:T(8,128)(2,1)S(1)}, u32[]{:S(2)}, u32[]{:S(2)}) collective-permute-start(bf16[8,6272]{1,0:T(8,128)(2,1)S(1)} %pack.1), channel_id=1, source_target_pairs={{0,3},{1,2},{2,1},{3,0},{4,7},{5,6},{6,5},{7,4},{8,11},{9,10},{10,... | collective-permute-start | bytes 301064 | tf_op jit(solution)/shard_map/ppermute | solution.py:35
  9.4 4.8 %collective-permute-start.3 = (bf16[8,6272]{1,0:T(8,128)(2,1)S(1)}, bf16[8,6272]{1,0:T(8,128)(2,1)S(1)}, u32[]{:S(2)}, u32[]{:S(2)}) collective-permute-start(bf16[8,6272]{1,0:T(8,128)(2,1)S(1)} %pack.1), channel_id=1, source_target_pairs={{0,1},{1,0},{2,3},{3,2},{4,5},{5,4},{6,7},{7,6},{8,9},{9,8},{10,11... | collective-permute-start | bytes 301064 | tf_op jit(solution)/shard_map/ppermute | solution.py:35
  10.0 4.6 %collective-permute-start.2 = (bf16[8,6272]{1,0:T(8,128)(2,1)S(1)}, bf16[8,6272]{1,0:T(8,128)(2,1)S(1)}, u32[]{:S(2)}, u32[]{:S(2)}) collective-permute-start(bf16[8,6272]{1,0:T(8,128)(2,1)S(1)} %pack.1), channel_id=1, source_target_pairs={{0,2},{1,3},{2,0},{3,1},{4,6},{5,7},{6,4},{7,5},{8,10},{9,11},{10,... | collective-permute-start | bytes 301064 | tf_op jit(solution)/shard_map/ppermute | solution.py:35
  14.6 8.0 %collective-permute-start.9 = (bf16[3072,768]{1,0:T(8,128)(2,1)S(1)}, bf16[3072,768]{1,0:T(8,128)(2,1)S(1)}, u32[]{:S(2)}, u32[]{:S(2)}) collective-permute-start(bf16[3072,768]{1,0:T(8,128)(2,1)S(1)} %weights.1.own_ref.refs_6_), channel_id=1, source_target_pairs={{0,4},{4,0},{8,12},{12,8},{16,20},{20,16},{24,28},{28,24},{1,5},{5... | collective-permute-start | bytes 14155784 | tf_op jit(solution)/shard_map/ppermute | solution.py:35
  14.7 13.5 %collective-permute-start.5 = (bf16[32,6272]{1,0:T(8,128)(2,1)S(1)}, bf16[32,6272]{1,0:T(8,128)(2,1)S(1)}, u32[]{:S(2)}, u32[]{:S(2)}) collective-permute-start(bf16[32,6272]{1,0:T(8,128)(2,1)S(1)} %pad_maximum_fusion.refs_0_), channel_id=1, source_target_pairs={{0,8},{4,12},{8,0},{12,4},{16,24},{20,28},{24,16},{28,20},{1,9},{5... | collective-permute-start | bytes 1204232 | tf_op jit(solution)/shard_map/ppermute | solution.py:35
  15.9 8.8 %collective-permute-start.8 = (bf16[16,6272]{1,0:T(8,128)(2,1)S(1)}, bf16[16,6272]{1,0:T(8,128)(2,1)S(1)}, u32[]{:S(2)}, u32[]{:S(2)}) collective-permute-start(bf16[16,6272]{1,0:T(8,128)(2,1)S(1)} %pad_maximum_fusion.1.refs_1_), channel_id=1, source_target_pairs={{0,3},{1,2},{2,1},{3,0},{4,7},{5,6},{6,5},{7,4},{8,11},{9,10},{10,... | collective-permute-start | bytes 602120 | tf_op jit(solution)/shard_map/ppermute | solution.py:35
  18.3 9.8 %collective-permute-start.7 = (bf16[16,6272]{1,0:T(8,128)(2,1)S(1)}, bf16[16,6272]{1,0:T(8,128)(2,1)S(1)}, u32[]{:S(2)}, u32[]{:S(2)}) collective-permute-start(bf16[16,6272]{1,0:T(8,128)(2,1)S(1)} %pad_maximum_fusion.1.refs_1_), channel_id=1, source_target_pairs={{0,2},{1,3},{2,0},{3,1},{4,6},{5,7},{6,4},{7,5},{8,10},{9,11},{10,... | collective-permute-start | bytes 602120 | tf_op jit(solution)/shard_map/ppermute | solution.py:35
  18.8 9.4 %collective-permute-start.6 = (bf16[16,6272]{1,0:T(8,128)(2,1)S(1)}, bf16[16,6272]{1,0:T(8,128)(2,1)S(1)}, u32[]{:S(2)}, u32[]{:S(2)}) collective-permute-start(bf16[16,6272]{1,0:T(8,128)(2,1)S(1)} %pad_maximum_fusion.1.refs_1_), channel_id=1, source_target_pairs={{0,1},{1,0},{2,3},{3,2},{4,5},{5,4},{6,7},{7,6},{8,9},{9,8},{10,11... | collective-permute-start | bytes 602120 | tf_op jit(solution)/shard_map/ppermute | solution.py:35
  30.7 4.5 %collective-permute-start.14 = (bf16[128,7040]{1,0:T(8,128)(2,1)S(1)}, bf16[128,7040]{1,0:T(8,128)(2,1)S(1)}, u32[]{:S(2)}, u32[]{:S(2)}) collective-permute-start(bf16[128,7040]{1,0:T(8,128)(2,1)S(1)} %get-tuple-element.41.pass_ref), channel_id=1, source_target_pairs={{0,4},{4,0},{8,12},{12,8},{16,20},{20,16},{24,28},{28,24},{1,5},{5... | collective-permute-start | bytes 5406728 | tf_op jit(solution)/shard_map/ppermute | solution.py:35
  30.8 7.1 %collective-permute-start.11 = (bf16[16,3200]{1,0:T(8,128)(2,1)S(1)}, bf16[16,3200]{1,0:T(8,128)(2,1)S(1)}, u32[]{:S(2)}, u32[]{:S(2)}) collective-permute-start(bf16[16,3200]{1,0:T(8,128)(2,1)S(1)} %get-tuple-element.38), channel_id=1, source_target_pairs={{0,3},{1,2},{2,1},{3,0},{4,7},{5,6},{6,5},{7,4},{8,11},{9,10},{10,... | collective-permute-start | bytes 307208 | tf_op jit(solution)/shard_map/ppermute | solution.py:35
  32.5 6.6 %collective-permute-start.12 = (bf16[16,3200]{1,0:T(8,128)(2,1)S(1)}, bf16[16,3200]{1,0:T(8,128)(2,1)S(1)}, u32[]{:S(2)}, u32[]{:S(2)}) collective-permute-start(bf16[16,3200]{1,0:T(8,128)(2,1)S(1)} %get-tuple-element.39), channel_id=1, source_target_pairs={{0,1},{1,0},{2,3},{3,2},{4,5},{5,4},{6,7},{7,6},{8,9},{9,8},{10,11... | collective-permute-start | bytes 307208 | tf_op jit(solution)/shard_map/ppermute | solution.py:35
  33.7 5.4 %collective-permute-start.13 = (bf16[16,3200]{1,0:T(8,128)(2,1)S(1)}, bf16[16,3200]{1,0:T(8,128)(2,1)S(1)}, u32[]{:S(2)}, u32[]{:S(2)}) collective-permute-start(bf16[16,3200]{1,0:T(8,128)(2,1)S(1)} %get-tuple-element.40), channel_id=1, source_target_pairs={{0,2},{1,3},{2,0},{3,1},{4,6},{5,7},{6,4},{7,5},{8,10},{9,11},{10,... | collective-permute-start | bytes 307208 | tf_op jit(solution)/shard_map/ppermute | solution.py:35
  34.3 8.4 %collective-permute-start.10 = (bf16[32,3200]{1,0:T(8,128)(2,1)S(1)}, bf16[32,3200]{1,0:T(8,128)(2,1)S(1)}, u32[]{:S(2)}, u32[]{:S(2)}) collective-permute-start(bf16[32,3200]{1,0:T(8,128)(2,1)S(1)} %get-tuple-element.35), channel_id=1, source_target_pairs={{0,8},{4,12},{8,0},{12,4},{16,24},{20,28},{24,16},{28,20},{1,9},{5... | collective-permute-start | bytes 614408 | tf_op jit(solution)/shard_map/ppermute | solution.py:35
  39.3 7.1 %collective-permute-start.15 = (bf16[8,3200]{1,0:T(8,128)(2,1)S(1)}, bf16[8,3200]{1,0:T(8,128)(2,1)S(1)}, u32[]{:S(2)}, u32[]{:S(2)}) collective-permute-start(bf16[8,3200]{1,0:T(8,128)(2,1)S(1)} %get-tuple-element.47), channel_id=1, source_target_pairs={{0,16},{4,20},{8,24},{12,28},{16,0},{20,4},{24,8},{28,12},{1,17},{... | collective-permute-start | bytes 153608 | tf_op jit(solution)/shard_map/ppermute | solution.py:35
  41.5 5.9 %collective-permute-start.16 = (bf16[8,3200]{1,0:T(8,128)(2,1)S(1)}, bf16[8,3200]{1,0:T(8,128)(2,1)S(1)}, u32[]{:S(2)}, u32[]{:S(2)}) collective-permute-start(bf16[8,3200]{1,0:T(8,128)(2,1)S(1)} %get-tuple-element.48), channel_id=1, source_target_pairs={{0,24},{4,28},{8,16},{12,20},{16,8},{20,12},{24,0},{28,4},{1,25},{... | collective-permute-start | bytes 153608 | tf_op jit(solution)/shard_map/ppermute | solution.py:35
  42.8 5.7 %collective-permute-start.17 = (bf16[8,3200]{1,0:T(8,128)(2,1)S(1)}, bf16[8,3200]{1,0:T(8,128)(2,1)S(1)}, u32[]{:S(2)}, u32[]{:S(2)}) collective-permute-start(bf16[8,3200]{1,0:T(8,128)(2,1)S(1)} %get-tuple-element.49), channel_id=1, source_target_pairs={{0,3},{1,2},{2,1},{3,0},{4,7},{5,6},{6,5},{7,4},{8,11},{9,10},{10,... | collective-permute-start | bytes 153608 | tf_op jit(solution)/shard_map/ppermute | solution.py:35
  44.5 4.1 %collective-permute-start.18 = (bf16[8,3200]{1,0:T(8,128)(2,1)S(1)}, bf16[8,3200]{1,0:T(8,128)(2,1)S(1)}, u32[]{:S(2)}, u32[]{:S(2)}) collective-permute-start(bf16[8,3200]{1,0:T(8,128)(2,1)S(1)} %get-tuple-element.50), channel_id=1, source_target_pairs={{0,1},{1,0},{2,3},{3,2},{4,5},{5,4},{6,7},{7,6},{8,9},{9,8},{10,11... | collective-permute-start | bytes 153608 | tf_op jit(solution)/shard_map/ppermute | solution.py:35
  45.8 4.1 %collective-permute-start.19 = (bf16[8,3200]{1,0:T(8,128)(2,1)S(1)}, bf16[8,3200]{1,0:T(8,128)(2,1)S(1)}, u32[]{:S(2)}, u32[]{:S(2)}) collective-permute-start(bf16[8,3200]{1,0:T(8,128)(2,1)S(1)} %get-tuple-element.51), channel_id=1, source_target_pairs={{0,2},{1,3},{2,0},{3,1},{4,6},{5,7},{6,4},{7,5},{8,10},{9,11},{10,... | collective-permute-start | bytes 153608 | tf_op jit(solution)/shard_map/ppermute | solution.py:35
  47.4 2.5 %copy-start = (s32[8,2]{0,1:T(2,128)S(1)}, s32[8,2]{0,1:T(2,128)}, u32[]{:S(2)}) copy-start(s32[8,2]{0,1:T(2,128)} %param.9) | copy-start | bytes 196

commit v9 on v7

--- a/solution.py
+++ b/solution.py
@@ -13,7 +13,7 @@
 LARGEST = 256
 COST = 4 * 10**9
 LONG = ("sum_far", "sum_along")
-PARTS = 4
+PARTS = 6
 BF = jnp.bfloat16
 F32 = jnp.float32
 

time: 50.8 us -> 50.8 us (level)
  no operation moved by 1% of the time
where the time goes in v9:
time: 50.8 us; the launch traced here: 50.6 us
  starting transfers between devices  25.1 us (49%)
  waiting for transfers between devices  13.1 us (26%)
  Pallas kernels  11.6 us (23%)
  between operations  0.73 us (1%)
    ppermute x20, starting transfers between devices, swap(): return lax.ppermute(value, axis, [(i, i ^ mask) for i in range(size)])  25.1 us
    ppermute x20, waiting for transfers between devices, swap(): return lax.ppermute(value, axis, [(i, i ^ mask) for i in range(size)])  13.1 us
    pallas_call x1, Pallas kernels, local(): pl.pallas_call(weights_body, out_shape=shape((features, 3 * units), BF),...  2.84 us
    pallas_call x1, Pallas kernels, local(): pl.pallas_call(functools.partial(grads_body, PARTS), out_shape=[shape(w.s...  2.65 us
    pallas_call x1, Pallas kernels, local(): pl.pallas_call(functools.partial(expert_body, experts, len(pieces)), out_...  2.46 us
    pallas_call x1, Pallas kernels, local(): call(back_body, shape((4 * units, features), BF), 'back')  1.8 us
  transfers between devices with their start and end apart: 20, of which 12 were waited for; matrix products, arithmetic and copies ran while one was open for 0% of the time, Pallas kernels for 15%

profile of v9, /device:TPU:0, one launch (start us, length us, event | category | flops | bytes accessed | tf_op | source)
XLA Modules:
  0.0 50.6 jit_solution(7148659120189348108)
XLA Ops:
  0.6 0.9 %pack.1 = bf16[8,6272]{1,0:T(8,128)(2,1)S(1)} custom-call(bf16[8,3072]{1,0:T(8,128)(2,1)} %x_hbm.1, bf16[8,3072]{1,0:T(8,128)(2,1)} %dy_hbm.1, s32[2,8]{1,0:T(2,128)} %bitcast.3, bf16[2,8]{1,0:T(2,128)(2,1)} %bitcast.5), custom_call_target="tpu_custom_call" | custom-call | tf_op jit(solution)/shard_map/pack/pallas_call | solution.py:309
  1.5 4.1 %collective-permute-start.1 = (bf16[8,6272]{1,0:T(8,128)(2,1)S(1)}, bf16[8,6272]{1,0:T(8,128)(2,1)S(1)}, u32[]{:S(2)}, u32[]{:S(2)}) collective-permute-start(bf16[8,6272]{1,0:T(8,128)(2,1)S(1)} %pack.1), channel_id=1, source_target_pairs={{0,16},{4,20},{8,24},{12,28},{16,0},{20,4},{24,8},{28,12},{1,17},{... | collective-permute-start | bytes 301064 | tf_op jit(solution)/shard_map/ppermute | solution.py:35
  5.6 1.3 %collective-permute-start = (bf16[8,6272]{1,0:T(8,128)(2,1)S(1)}, bf16[8,6272]{1,0:T(8,128)(2,1)S(1)}, u32[]{:S(2)}, u32[]{:S(2)}) collective-permute-start(bf16[8,6272]{1,0:T(8,128)(2,1)S(1)} %pack.1), channel_id=1, source_target_pairs={{0,24},{4,28},{8,16},{12,20},{16,8},{20,12},{24,0},{28,4},{1,25},{... | collective-permute-start | bytes 301064 | tf_op jit(solution)/shard_map/ppermute | solution.py:35
  7.0 2.4 %collective-permute-start.4 = (bf16[8,6272]{1,0:T(8,128)(2,1)S(1)}, bf16[8,6272]{1,0:T(8,128)(2,1)S(1)}, u32[]{:S(2)}, u32[]{:S(2)}) collective-permute-start(bf16[8,6272]{1,0:T(8,128)(2,1)S(1)} %pack.1), channel_id=1, source_target_pairs={{0,3},{1,2},{2,1},{3,0},{4,7},{5,6},{6,5},{7,4},{8,11},{9,10},{10,... | collective-permute-start | bytes 301064 | tf_op jit(solution)/shard_map/ppermute | solution.py:35
  9.4 0.5 %collective-permute-start.3 = (bf16[8,6272]{1,0:T(8,128)(2,1)S(1)}, bf16[8,6272]{1,0:T(8,128)(2,1)S(1)}, u32[]{:S(2)}, u32[]{:S(2)}) collective-permute-start(bf16[8,6272]{1,0:T(8,128)(2,1)S(1)} %pack.1), channel_id=1, source_target_pairs={{0,1},{1,0},{2,3},{3,2},{4,5},{5,4},{6,7},{7,6},{8,9},{9,8},{10,11... | collective-permute-start | bytes 301064 | tf_op jit(solution)/shard_map/ppermute | solution.py:35
  10.0 0.5 %collective-permute-start.2 = (bf16[8,6272]{1,0:T(8,128)(2,1)S(1)}, bf16[8,6272]{1,0:T(8,128)(2,1)S(1)}, u32[]{:S(2)}, u32[]{:S(2)}) collective-permute-start(bf16[8,6272]{1,0:T(8,128)(2,1)S(1)} %pack.1), channel_id=1, source_target_pairs={{0,2},{1,3},{2,0},{3,1},{4,6},{5,7},{6,4},{7,5},{8,10},{9,11},{10,... | collective-permute-start | bytes 301064 | tf_op jit(solution)/shard_map/ppermute | solution.py:35
  10.5 2.8 %weights.1.own_ref.refs_6_ = bf16[3072,768]{1,0:T(8,128)(2,1)S(1)} custom-call(bf16[1,3072,256]{2,1,0:T(8,128)(2,1)} %gate_hbm.1, bf16[1,3072,256]{2,1,0:T(8,128)(2,1)} %up_hbm.1, bf16[1,256,3072]{2,1,0:T(8,128)(2,1)} %down_hbm.1), custom_call_target="tpu_custom_call" | custom-call | bytes 1024 | tf_op jit(solution)/shard_map/weights/pallas_call | solution.py:335
  13.3 0.3 collective-permute-done.1
  13.6 0.0 collective-permute-done
  13.6 0.0 collective-permute-done.4
  13.6 0.6 %collective-permute-done.3 = bf16[8,6272]{1,0:T(8,128)(2,1)S(1)} collective-permute-done((bf16[8,6272]{1,0:T(8,128)(2,1)S(1)}, bf16[8,6272]{1,0:T(8,128)(2,1)S(1)}, u32[]{:S(2)}, u32[]{:S(2)}) %collective-permute-start.3) | collective-permute-done | bytes 100384 | tf_op jit(solution)/shard_map/ppermute | solution.py:35
  14.3 0.3 collective-permute-done.2
  14.6 0.1 collective-permute-start.9
  14.7 1.2 %collective-permute-start.5 = (bf16[32,6272]{1,0:T(8,128)(2,1)S(1)}, bf16[32,6272]{1,0:T(8,128)(2,1)S(1)}, u32[]{:S(2)}, u32[]{:S(2)}) collective-permute-start(bf16[32,6272]{1,0:T(8,128)(2,1)S(1)} %pad_maximum_fusion.refs_0_), channel_id=1, source_target_pairs={{0,8},{4,12},{8,0},{12,4},{16,24},{20,28},{24,16},{28,20},{1,9},{5... | collective-permute-start | bytes 1204232 | tf_op jit(solution)/shard_map/ppermute | solution.py:35
  15.9 2.4 %collective-permute-start.8 = (bf16[16,6272]{1,0:T(8,128)(2,1)S(1)}, bf16[16,6272]{1,0:T(8,128)(2,1)S(1)}, u32[]{:S(2)}, u32[]{:S(2)}) collective-permute-start(bf16[16,6272]{1,0:T(8,128)(2,1)S(1)} %pad_maximum_fusion.1.refs_1_), channel_id=1, source_target_pairs={{0,3},{1,2},{2,1},{3,0},{4,7},{5,6},{6,5},{7,4},{8,11},{9,10},{10,... | collective-permute-start | bytes 602120 | tf_op jit(solution)/shard_map/ppermute | solution.py:35
  18.3 0.5 %collective-permute-start.7 = (bf16[16,6272]{1,0:T(8,128)(2,1)S(1)}, bf16[16,6272]{1,0:T(8,128)(2,1)S(1)}, u32[]{:S(2)}, u32[]{:S(2)}) collective-permute-start(bf16[16,6272]{1,0:T(8,128)(2,1)S(1)} %pad_maximum_fusion.1.refs_1_), channel_id=1, source_target_pairs={{0,2},{1,3},{2,0},{3,1},{4,6},{5,7},{6,4},{7,5},{8,10},{9,11},{10,... | collective-permute-start | bytes 602120 | tf_op jit(solution)/shard_map/ppermute | solution.py:35
  18.8 0.5 %collective-permute-start.6 = (bf16[16,6272]{1,0:T(8,128)(2,1)S(1)}, bf16[16,6272]{1,0:T(8,128)(2,1)S(1)}, u32[]{:S(2)}, u32[]{:S(2)}) collective-permute-start(bf16[16,6272]{1,0:T(8,128)(2,1)S(1)} %pad_maximum_fusion.1.refs_1_), channel_id=1, source_target_pairs={{0,1},{1,0},{2,3},{3,2},{4,5},{5,4},{6,7},{7,6},{8,9},{9,8},{10,11... | collective-permute-start | bytes 602120 | tf_op jit(solution)/shard_map/ppermute | solution.py:35
  19.4 3.2 %collective-permute-done.9.other_ref.refs_7_ = bf16[3072,768]{1,0:T(8,128)(2,1)S(1)} collective-permute-done((bf16[3072,768]{1,0:T(8,128)(2,1)S(1)}, bf16[3072,768]{1,0:T(8,128)(2,1)S(1)}, u32[]{:S(2)}, u32[]{:S(2)}) %collective-permute-start.9) | collective-permute-done | bytes 4718624 | tf_op jit(solution)/shard_map/ppermute | solution.py:35
  22.6 1.8 %back.1.refs_8_ = bf16[1024,3072]{1,0:T(8,128)(2,1)S(1)} custom-call(bf16[3072,768]{1,0:T(8,128)(2,1)S(1)} %weights.1.own_ref.refs_6_, bf16[3072,768]{1,0:T(8,128)(2,1)S(1)} %collective-permute-done.9.other_ref.refs_7_), custom_call_target="tpu_custom_call" | custom-call | tf_op jit(solution)/shard_map/back/pallas_call | solution.py:356
  24.4 0.2 collective-permute-done.8.refs_5_
  24.7 3.5 %collective-permute-done.7.refs_4_ = bf16[16,6272]{1,0:T(8,128)(2,1)S(1)} collective-permute-done((bf16[16,6272]{1,0:T(8,128)(2,1)S(1)}, bf16[16,6272]{1,0:T(8,128)(2,1)S(1)}, u32[]{:S(2)}, u32[]{:S(2)}) %collective-permute-start.7) | collective-permute-done | bytes 200736 | tf_op jit(solution)/shard_map/ppermute | solution.py:35
  28.1 0.1 collective-permute-done.6.refs_3_
  28.2 0.0 collective-permute-done.5.refs_2_
  28.2 2.5 %expert.1 = (f32[32,3200]{1,0:T(8,128)S(1)}, f32[16,3200]{1,0:T(8,128)S(1)}, bf16[32,3200]{1,0:T(8,128)(2,1)S(1)}, bf16[16,3200]{1,0:T(8,128)(2,1)S(1)}, bf16[16...) custom-call(bf16[32,6272]{1,0:T(8,128)(2,1)S(1)} %pad_maximum_fusion, ...), custom_call_target="tpu_custom_call" | custom-call | bytes 1024 | tf_op jit(solution)/shard_map/expert/pallas_call | solution.py:357
  30.7 0.1 collective-permute-start.14
  30.8 1.7 %collective-permute-start.11 = (bf16[16,3200]{1,0:T(8,128)(2,1)S(1)}, bf16[16,3200]{1,0:T(8,128)(2,1)S(1)}, u32[]{:S(2)}, u32[]{:S(2)}) collective-permute-start(bf16[16,3200]{1,0:T(8,128)(2,1)S(1)} %get-tuple-element.38), channel_id=1, source_target_pairs={{0,3},{1,2},{2,1},{3,0},{4,7},{5,6},{6,5},{7,4},{8,11},{9,10},{10,... | collective-permute-start | bytes 307208 | tf_op jit(solution)/shard_map/ppermute | solution.py:35
  32.5 1.2 %collective-permute-start.12 = (bf16[16,3200]{1,0:T(8,128)(2,1)S(1)}, bf16[16,3200]{1,0:T(8,128)(2,1)S(1)}, u32[]{:S(2)}, u32[]{:S(2)}) collective-permute-start(bf16[16,3200]{1,0:T(8,128)(2,1)S(1)} %get-tuple-element.39), channel_id=1, source_target_pairs={{0,1},{1,0},{2,3},{3,2},{4,5},{5,4},{6,7},{7,6},{8,9},{9,8},{10,11... | collective-permute-start | bytes 307208 | tf_op jit(solution)/shard_map/ppermute | solution.py:35
  33.7 0.6 %collective-permute-start.13 = (bf16[16,3200]{1,0:T(8,128)(2,1)S(1)}, bf16[16,3200]{1,0:T(8,128)(2,1)S(1)}, u32[]{:S(2)}, u32[]{:S(2)}) collective-permute-start(bf16[16,3200]{1,0:T(8,128)(2,1)S(1)} %get-tuple-element.40), channel_id=1, source_target_pairs={{0,2},{1,3},{2,0},{3,1},{4,6},{5,7},{6,4},{7,5},{8,10},{9,11},{10,... | collective-permute-start | bytes 307208 | tf_op jit(solution)/shard_map/ppermute | solution.py:35
  34.3 0.8 %collective-permute-start.10 = (bf16[32,3200]{1,0:T(8,128)(2,1)S(1)}, bf16[32,3200]{1,0:T(8,128)(2,1)S(1)}, u32[]{:S(2)}, u32[]{:S(2)}) collective-permute-start(bf16[32,3200]{1,0:T(8,128)(2,1)S(1)} %get-tuple-element.35), channel_id=1, source_target_pairs={{0,8},{4,12},{8,0},{12,4},{16,24},{20,28},{24,16},{28,20},{1,9},{5... | collective-permute-start | bytes 614408 | tf_op jit(solution)/shard_map/ppermute | solution.py:35
  35.2 0.0 collective-permute-done.14.got_ref
  35.2 2.6 %grads.1 = (bf16[1,3072,256]{2,1,0:T(8,128)(2,1)}, bf16[1,3072,256]{2,1,0:T(8,128)(2,1)}, bf16[1,256,3072]{2,1,0:T(8,128)(2,1)}) custom-call(bf16[128,6912]{1,0:T(8,128)(2,1)S(1)} %get-tuple-element.41.pass_ref, bf16[128,6912]{1,0:T(8,128)(2,1)S(1)} %collective-permute-done.14.got_ref, bf16[128,768]{1,0:T(8,128)(2,1)S(1)} %get-tuple-element.42.acts_ref), custom_call_target="tpu_custom_call" | custom-call | bytes 1024 | tf_op jit(solution)/shard_map/grads/pallas_call | solution.py:374
  37.8 0.0 collective-permute-done.11.refs_1_
  37.8 1.3 %collective-permute-done.12.refs_2_ = bf16[16,3200]{1,0:T(8,128)(2,1)S(1)} collective-permute-done((bf16[16,3200]{1,0:T(8,128)(2,1)S(1)}, bf16[16,3200]{1,0:T(8,128)(2,1)S(1)}, u32[]{:S(2)}, u32[]{:S(2)}) %collective-permute-start.12) | collective-permute-done | bytes 102432 | tf_op jit(solution)/shard_map/ppermute | solution.py:35
  39.1 0.0 collective-permute-done.13.refs_3_
  39.2 0.1 sum_far.1
  39.3 2.2 %collective-permute-start.15 = (bf16[8,3200]{1,0:T(8,128)(2,1)S(1)}, bf16[8,3200]{1,0:T(8,128)(2,1)S(1)}, u32[]{:S(2)}, u32[]{:S(2)}) collective-permute-start(bf16[8,3200]{1,0:T(8,128)(2,1)S(1)} %get-tuple-element.47), channel_id=1, source_target_pairs={{0,16},{4,20},{8,24},{12,28},{16,0},{20,4},{24,8},{28,12},{1,17},{... | collective-permute-start | bytes 153608 | tf_op jit(solution)/shard_map/ppermute | solution.py:35
  41.5 1.3 %collective-permute-start.16 = (bf16[8,3200]{1,0:T(8,128)(2,1)S(1)}, bf16[8,3200]{1,0:T(8,128)(2,1)S(1)}, u32[]{:S(2)}, u32[]{:S(2)}) collective-permute-start(bf16[8,3200]{1,0:T(8,128)(2,1)S(1)} %get-tuple-element.48), channel_id=1, source_target_pairs={{0,24},{4,28},{8,16},{12,20},{16,8},{20,12},{24,0},{28,4},{1,25},{... | collective-permute-start | bytes 153608 | tf_op jit(solution)/shard_map/ppermute | solution.py:35
  42.8 0.0 collective-permute-done.10.refs_1_
  42.8 0.1 sum_near.1
  42.9 1.7 %collective-permute-start.17 = (bf16[8,3200]{1,0:T(8,128)(2,1)S(1)}, bf16[8,3200]{1,0:T(8,128)(2,1)S(1)}, u32[]{:S(2)}, u32[]{:S(2)}) collective-permute-start(bf16[8,3200]{1,0:T(8,128)(2,1)S(1)} %get-tuple-element.49), channel_id=1, source_target_pairs={{0,3},{1,2},{2,1},{3,0},{4,7},{5,6},{6,5},{7,4},{8,11},{9,10},{10,... | collective-permute-start | bytes 153608 | tf_op jit(solution)/shard_map/ppermute | solution.py:35
  44.5 1.2 %collective-permute-start.18 = (bf16[8,3200]{1,0:T(8,128)(2,1)S(1)}, bf16[8,3200]{1,0:T(8,128)(2,1)S(1)}, u32[]{:S(2)}, u32[]{:S(2)}) collective-permute-start(bf16[8,3200]{1,0:T(8,128)(2,1)S(1)} %get-tuple-element.50), channel_id=1, source_target_pairs={{0,1},{1,0},{2,3},{3,2},{4,5},{5,4},{6,7},{7,6},{8,9},{9,8},{10,11... | collective-permute-start | bytes 153608 | tf_op jit(solution)/shard_map/ppermute | solution.py:35
  45.8 0.6 %collective-permute-start.19 = (bf16[8,3200]{1,0:T(8,128)(2,1)S(1)}, bf16[8,3200]{1,0:T(8,128)(2,1)S(1)}, u32[]{:S(2)}, u32[]{:S(2)}) collective-permute-start(bf16[8,3200]{1,0:T(8,128)(2,1)S(1)} %get-tuple-element.51), channel_id=1, source_target_pairs={{0,2},{1,3},{2,0},{3,1},{4,6},{5,7},{6,4},{7,5},{8,10},{9,11},{10,... | collective-permute-start | bytes 153608 | tf_op jit(solution)/shard_map/ppermute | solution.py:35
  46.4 0.0 collective-permute-done.15.refs_1_
  46.4 1.0 %collective-permute-done.16.refs_2_ = bf16[8,3200]{1,0:T(8,128)(2,1)S(1)} collective-permute-done((bf16[8,3200]{1,0:T(8,128)(2,1)S(1)}, bf16[8,3200]{1,0:T(8,128)(2,1)S(1)}, u32[]{:S(2)}, u32[]{:S(2)}) %collective-permute-start.16) | collective-permute-done | bytes 51232 | tf_op jit(solution)/shard_map/ppermute | solution.py:35
  47.4 0.0 copy-start
  47.4 1.1 %collective-permute-done.17.refs_1_ = bf16[8,3200]{1,0:T(8,128)(2,1)S(1)} collective-permute-done((bf16[8,3200]{1,0:T(8,128)(2,1)S(1)}, bf16[8,3200]{1,0:T(8,128)(2,1)S(1)}, u32[]{:S(2)}, u32[]{:S(2)}) %collective-permute-start.17) | collective-permute-done | bytes 51232 | tf_op jit(solution)/shard_map/ppermute | solution.py:35
  48.5 0.1 collective-permute-done.18.refs_2_
  48.6 1.2 %collective-permute-done.19.refs_3_ = bf16[8,3200]{1,0:T(8,128)(2,1)S(1)} collective-permute-done((bf16[8,3200]{1,0:T(8,128)(2,1)S(1)}, bf16[8,3200]{1,0:T(8,128)(2,1)S(1)}, u32[]{:S(2)}, u32[]{:S(2)}) %collective-permute-start.19) | collective-permute-done | bytes 51232 | tf_op jit(solution)/shard_map/ppermute | solution.py:35
  49.9 0.0 copy-done
  49.9 0.7 %final.1 = (bf16[8,3072]{1,0:T(8,128)(2,1)}, f32[2,8]{1,0:T(2,128)}) custom-call(f32[8,3200]{1,0:T(8,128)S(1)} %sum_along.1.refs_0_, bf16[8,3200]{1,0:T(8,128)(2,1)S(1)} %collective-permute-done.17.refs_1_, bf16[8,3200]{1,0:T(8,128)(2,1)S(1)} %collective-permute-done.18.refs_2_, bf16[8,3200]{1,0:T(8,128)(2,1)S(1)} %collective-permute-done.19.refs_3_, ...), custom_call_target="tpu_custom_call" | custom-call | bytes 204800 | tf_op jit(solution)/shard_map/final/pallas_call | solution.py:412
  (3 shorter events, 0.1 us)
Async XLA Ops:
  1.5 12.1 %collective-permute-start.1 = (bf16[8,6272]{1,0:T(8,128)(2,1)S(1)}, bf16[8,6272]{1,0:T(8,128)(2,1)S(1)}, u32[]{:S(2)}, u32[]{:S(2)}) collective-permute-start(bf16[8,6272]{1,0:T(8,128)(2,1)S(1)} %pack.1), channel_id=1, source_target_pairs={{0,16},{4,20},{8,24},{12,28},{16,0},{20,4},{24,8},{28,12},{1,17},{... | collective-permute-start | bytes 301064 | tf_op jit(solution)/shard_map/ppermute | solution.py:35
  5.6 8.0 %collective-permute-start = (bf16[8,6272]{1,0:T(8,128)(2,1)S(1)}, bf16[8,6272]{1,0:T(8,128)(2,1)S(1)}, u32[]{:S(2)}, u32[]{:S(2)}) collective-permute-start(bf16[8,6272]{1,0:T(8,128)(2,1)S(1)} %pack.1), channel_id=1, source_target_pairs={{0,24},{4,28},{8,16},{12,20},{16,8},{20,12},{24,0},{28,4},{1,25},{... | collective-permute-start | bytes 301064 | tf_op jit(solution)/shard_map/ppermute | solution.py:35
  7.0 6.6 %collective-permute-start.4 = (bf16[8,6272]{1,0:T(8,128)(2,1)S(1)}, bf16[8,6272]{1,0:T(8,128)(2,1)S(1)}, u32[]{:S(2)}, u32[]{:S(2)}) collective-permute-start(bf16[8,6272]{1,0:T(8,128)(2,1)S(1)} %pack.1), channel_id=1, source_target_pairs={{0,3},{1,2},{2,1},{3,0},{4,7},{5,6},{6,5},{7,4},{8,11},{9,10},{10,... | collective-permute-start | bytes 301064 | tf_op jit(solution)/shard_map/ppermute | solution.py:35
  9.4 4.8 %collective-permute-start.3 = (bf16[8,6272]{1,0:T(8,128)(2,1)S(1)}, bf16[8,6272]{1,0:T(8,128)(2,1)S(1)}, u32[]{:S(2)}, u32[]{:S(2)}) collective-permute-start(bf16[8,6272]{1,0:T(8,128)(2,1)S(1)} %pack.1), channel_id=1, source_target_pairs={{0,1},{1,0},{2,3},{3,2},{4,5},{5,4},{6,7},{7,6},{8,9},{9,8},{10,11... | collective-permute-start | bytes 301064 | tf_op jit(solution)/shard_map/ppermute | solution.py:35
  10.0 4.6 %collective-permute-start.2 = (bf16[8,6272]{1,0:T(8,128)(2,1)S(1)}, bf16[8,6272]{1,0:T(8,128)(2,1)S(1)}, u32[]{:S(2)}, u32[]{:S(2)}) collective-permute-start(bf16[8,6272]{1,0:T(8,128)(2,1)S(1)} %pack.1), channel_id=1, source_target_pairs={{0,2},{1,3},{2,0},{3,1},{4,6},{5,7},{6,4},{7,5},{8,10},{9,11},{10,... | collective-permute-start | bytes 301064 | tf_op jit(solution)/shard_map/ppermute | solution.py:35
  14.6 8.0 %collective-permute-start.9 = (bf16[3072,768]{1,0:T(8,128)(2,1)S(1)}, bf16[3072,768]{1,0:T(8,128)(2,1)S(1)}, u32[]{:S(2)}, u32[]{:S(2)}) collective-permute-start(bf16[3072,768]{1,0:T(8,128)(2,1)S(1)} %weights.1.own_ref.refs_6_), channel_id=1, source_target_pairs={{0,4},{4,0},{8,12},{12,8},{16,20},{20,16},{24,28},{28,24},{1,5},{5... | collective-permute-start | bytes 14155784 | tf_op jit(solution)/shard_map/ppermute | solution.py:35
  14.7 13.5 %collective-permute-start.5 = (bf16[32,6272]{1,0:T(8,128)(2,1)S(1)}, bf16[32,6272]{1,0:T(8,128)(2,1)S(1)}, u32[]{:S(2)}, u32[]{:S(2)}) collective-permute-start(bf16[32,6272]{1,0:T(8,128)(2,1)S(1)} %pad_maximum_fusion.refs_0_), channel_id=1, source_target_pairs={{0,8},{4,12},{8,0},{12,4},{16,24},{20,28},{24,16},{28,20},{1,9},{5... | collective-permute-start | bytes 1204232 | tf_op jit(solution)/shard_map/ppermute | solution.py:35
  15.9 8.8 %collective-permute-start.8 = (bf16[16,6272]{1,0:T(8,128)(2,1)S(1)}, bf16[16,6272]{1,0:T(8,128)(2,1)S(1)}, u32[]{:S(2)}, u32[]{:S(2)}) collective-permute-start(bf16[16,6272]{1,0:T(8,128)(2,1)S(1)} %pad_maximum_fusion.1.refs_1_), channel_id=1, source_target_pairs={{0,3},{1,2},{2,1},{3,0},{4,7},{5,6},{6,5},{7,4},{8,11},{9,10},{10,... | collective-permute-start | bytes 602120 | tf_op jit(solution)/shard_map/ppermute | solution.py:35
  18.3 9.8 %collective-permute-start.7 = (bf16[16,6272]{1,0:T(8,128)(2,1)S(1)}, bf16[16,6272]{1,0:T(8,128)(2,1)S(1)}, u32[]{:S(2)}, u32[]{:S(2)}) collective-permute-start(bf16[16,6272]{1,0:T(8,128)(2,1)S(1)} %pad_maximum_fusion.1.refs_1_), channel_id=1, source_target_pairs={{0,2},{1,3},{2,0},{3,1},{4,6},{5,7},{6,4},{7,5},{8,10},{9,11},{10,... | collective-permute-start | bytes 602120 | tf_op jit(solution)/shard_map/ppermute | solution.py:35
  18.8 9.4 %collective-permute-start.6 = (bf16[16,6272]{1,0:T(8,128)(2,1)S(1)}, bf16[16,6272]{1,0:T(8,128)(2,1)S(1)}, u32[]{:S(2)}, u32[]{:S(2)}) collective-permute-start(bf16[16,6272]{1,0:T(8,128)(2,1)S(1)} %pad_maximum_fusion.1.refs_1_), channel_id=1, source_target_pairs={{0,1},{1,0},{2,3},{3,2},{4,5},{5,4},{6,7},{7,6},{8,9},{9,8},{10,11... | collective-permute-start | bytes 602120 | tf_op jit(solution)/shard_map/ppermute | solution.py:35
  30.7 4.5 %collective-permute-start.14 = (bf16[128,6912]{1,0:T(8,128)(2,1)S(1)}, bf16[128,6912]{1,0:T(8,128)(2,1)S(1)}, u32[]{:S(2)}, u32[]{:S(2)}) collective-permute-start(bf16[128,6912]{1,0:T(8,128)(2,1)S(1)} %get-tuple-element.41.pass_ref), channel_id=1, source_target_pairs={{0,4},{4,0},{8,12},{12,8},{16,20},{20,16},{24,28},{28,24},{1,5},{5... | collective-permute-start | bytes 5308424 | tf_op jit(solution)/shard_map/ppermute | solution.py:35
  30.8 7.1 %collective-permute-start.11 = (bf16[16,3200]{1,0:T(8,128)(2,1)S(1)}, bf16[16,3200]{1,0:T(8,128)(2,1)S(1)}, u32[]{:S(2)}, u32[]{:S(2)}) collective-permute-start(bf16[16,3200]{1,0:T(8,128)(2,1)S(1)} %get-tuple-element.38), channel_id=1, source_target_pairs={{0,3},{1,2},{2,1},{3,0},{4,7},{5,6},{6,5},{7,4},{8,11},{9,10},{10,... | collective-permute-start | bytes 307208 | tf_op jit(solution)/shard_map/ppermute | solution.py:35
  32.5 6.6 %collective-permute-start.12 = (bf16[16,3200]{1,0:T(8,128)(2,1)S(1)}, bf16[16,3200]{1,0:T(8,128)(2,1)S(1)}, u32[]{:S(2)}, u32[]{:S(2)}) collective-permute-start(bf16[16,3200]{1,0:T(8,128)(2,1)S(1)} %get-tuple-element.39), channel_id=1, source_target_pairs={{0,1},{1,0},{2,3},{3,2},{4,5},{5,4},{6,7},{7,6},{8,9},{9,8},{10,11... | collective-permute-start | bytes 307208 | tf_op jit(solution)/shard_map/ppermute | solution.py:35
  33.7 5.4 %collective-permute-start.13 = (bf16[16,3200]{1,0:T(8,128)(2,1)S(1)}, bf16[16,3200]{1,0:T(8,128)(2,1)S(1)}, u32[]{:S(2)}, u32[]{:S(2)}) collective-permute-start(bf16[16,3200]{1,0:T(8,128)(2,1)S(1)} %get-tuple-element.40), channel_id=1, source_target_pairs={{0,2},{1,3},{2,0},{3,1},{4,6},{5,7},{6,4},{7,5},{8,10},{9,11},{10,... | collective-permute-start | bytes 307208 | tf_op jit(solution)/shard_map/ppermute | solution.py:35
  34.3 8.4 %collective-permute-start.10 = (bf16[32,3200]{1,0:T(8,128)(2,1)S(1)}, bf16[32,3200]{1,0:T(8,128)(2,1)S(1)}, u32[]{:S(2)}, u32[]{:S(2)}) collective-permute-start(bf16[32,3200]{1,0:T(8,128)(2,1)S(1)} %get-tuple-element.35), channel_id=1, source_target_pairs={{0,8},{4,12},{8,0},{12,4},{16,24},{20,28},{24,16},{28,20},{1,9},{5... | collective-permute-start | bytes 614408 | tf_op jit(solution)/shard_map/ppermute | solution.py:35
  39.3 7.1 %collective-permute-start.15 = (bf16[8,3200]{1,0:T(8,128)(2,1)S(1)}, bf16[8,3200]{1,0:T(8,128)(2,1)S(1)}, u32[]{:S(2)}, u32[]{:S(2)}) collective-permute-start(bf16[8,3200]{1,0:T(8,128)(2,1)S(1)} %get-tuple-element.47), channel_id=1, source_target_pairs={{0,16},{4,20},{8,24},{12,28},{16,0},{20,4},{24,8},{28,12},{1,17},{... | collective-permute-start | bytes 153608 | tf_op jit(solution)/shard_map/ppermute | solution.py:35
  41.5 5.9 %collective-permute-start.16 = (bf16[8,3200]{1,0:T(8,128)(2,1)S(1)}, bf16[8,3200]{1,0:T(8,128)(2,1)S(1)}, u32[]{:S(2)}, u32[]{:S(2)}) collective-permute-start(bf16[8,3200]{1,0:T(8,128)(2,1)S(1)} %get-tuple-element.48), channel_id=1, source_target_pairs={{0,24},{4,28},{8,16},{12,20},{16,8},{20,12},{24,0},{28,4},{1,25},{... | collective-permute-start | bytes 153608 | tf_op jit(solution)/shard_map/ppermute | solution.py:35
  42.9 5.7 %collective-permute-start.17 = (bf16[8,3200]{1,0:T(8,128)(2,1)S(1)}, bf16[8,3200]{1,0:T(8,128)(2,1)S(1)}, u32[]{:S(2)}, u32[]{:S(2)}) collective-permute-start(bf16[8,3200]{1,0:T(8,128)(2,1)S(1)} %get-tuple-element.49), channel_id=1, source_target_pairs={{0,3},{1,2},{2,1},{3,0},{4,7},{5,6},{6,5},{7,4},{8,11},{9,10},{10,... | collective-permute-start | bytes 153608 | tf_op jit(solution)/shard_map/ppermute | solution.py:35
  44.5 4.1 %collective-permute-start.18 = (bf16[8,3200]{1,0:T(8,128)(2,1)S(1)}, bf16[8,3200]{1,0:T(8,128)(2,1)S(1)}, u32[]{:S(2)}, u32[]{:S(2)}) collective-permute-start(bf16[8,3200]{1,0:T(8,128)(2,1)S(1)} %get-tuple-element.50), channel_id=1, source_target_pairs={{0,1},{1,0},{2,3},{3,2},{4,5},{5,4},{6,7},{7,6},{8,9},{9,8},{10,11... | collective-permute-start | bytes 153608 | tf_op jit(solution)/shard_map/ppermute | solution.py:35
  45.8 4.1 %collective-permute-start.19 = (bf16[8,3200]{1,0:T(8,128)(2,1)S(1)}, bf16[8,3200]{1,0:T(8,128)(2,1)S(1)}, u32[]{:S(2)}, u32[]{:S(2)}) collective-permute-start(bf16[8,3200]{1,0:T(8,128)(2,1)S(1)} %get-tuple-element.51), channel_id=1, source_target_pairs={{0,2},{1,3},{2,0},{3,1},{4,6},{5,7},{6,4},{7,5},{8,10},{9,11},{10,... | collective-permute-start | bytes 153608 | tf_op jit(solution)/shard_map/ppermute | solution.py:35
  47.4 2.5 %copy-start = (s32[8,2]{0,1:T(2,128)S(1)}, s32[8,2]{0,1:T(2,128)}, u32[]{:S(2)}) copy-start(s32[8,2]{0,1:T(2,128)} %param.9) | copy-start | bytes 196
